TPU v7x, 256 devices: a whole 4x4x8 slice. The times are simulated.
256 devices in a mesh: grp: 8 (over y, core), dev: 32 (over x, z).
Axes of the slice: x: 4, y: 4, z: 8, core: 2. Of those that a mesh axis runs over, the one named last changes fastest.
Arguments:
- old_fine: float32 [2048, 9, 128, 128], P('dev', None, 'grp'), may hold values from -6 to 6
- old_ids: int32 [8, 2048], P('grp', 'dev'), may hold values from -1 to 2047, as said below
- old_coarse: float32 [1024, 9, 64, 64], P('dev', None, 'grp'), may hold values from -6 to 6
- coarse_ids: int32 [8, 1024], P('grp', 'dev'), may hold values from 0 to 1023, as said below
- velocity: float32 [2048, 3, 128, 128], P('dev', None, 'grp'), may hold values from -0.12 to 0.12
- diffusion: float32 [9], replicated, may hold values from 0.01 to 0.1
Outputs:
- species_out: float32 [2048, 9, 128, 128], P('dev', None, 'grp')
Inputs may be any that keep to these rules, and one draw needn't show every extreme that they name: `old_ids`: row g names, for each old fine slot k of group g (on dev index k // 64), the x-plane that the slot holds, or -1 for an empty slot whose rows of old_fine are ignored. No plane is named twice; planes named nowhere are newly refined. The slots of one device hold at most 4 planes of any one new box, box e holding planes e * 64 to e * 64 + 63. `coarse_ids`: each row is a permutation. The slots of one device hold at most 2 of the coarse planes e * 32 to e * 32 + 31 of any one new box e.
All inputs are finite; a program needn't handle non-finite values.
Results may differ from a plain program's by a relative error of at most 0.000092.
Values sent between devices are 32-bit elements; how exact they have to be, the bound alone decides.
No kernel may reach another device: no remote copies, remote signals or barrier semaphores. Data moves between devices by JAX's collectives and lax.ppermute only.
A program may use at most 192 MiB of HBM per device.

v0:
```python
import jax
import jax.numpy as jnp
from jax import lax
from jax.sharding import PartitionSpec as P

ITERS = 2


HIGHEST = lax.Precision.HIGHEST


def extended(value, sides, width):
    edges = {}
    for axis, dim in sides:
        size, length = (lax.axis_size(axis), value.shape[dim])
        up = [(i, (i + 1) % size) for i in range(size - 1)]
        last = lax.slice_in_dim(value, length - width, length, axis=dim)
        leading = lax.slice_in_dim(value, 0, width, axis=dim)
        edges[dim] = (
            lax.ppermute(last, axis, up),
            lax.ppermute(leading, axis, [(b, a) for a, b in up]),
        )
    done = []
    for _, dim in sides:
        low, high = edges[dim]
        around = [(width, width) if d in done else (0, 0) for d in range(value.ndim)]
        value = jnp.concatenate([jnp.pad(low, around), value, jnp.pad(high, around)], axis=dim)
        done.append(dim)
    return value


def refine(coarse):
    extent = coarse.shape
    ypadded = jnp.concatenate([coarse[:, :, :1], coarse, coarse[:, :, -1:]], axis=2)
    zpadded = jnp.concatenate([coarse[..., :1], coarse, coarse[..., -1:]], axis=3)
    slope_y = 0.5 * (ypadded[:, :, 2:] - ypadded[:, :, :-2])
    slope_z = 0.5 * (zpadded[..., 2:] - zpadded[..., :-2])
    row_parts = []
    for row_half in range(2):
        col_parts = [
            coarse + (0.5 * row_half - 0.25) * slope_y + (0.5 * col_half - 0.25) * slope_z
            for col_half in range(2)
        ]
        row_parts.append(jnp.stack(col_parts, axis=-1))
    children = jnp.stack(row_parts, axis=3)
    refined = children.reshape(extent[0], extent[1], 2 * extent[2], 2 * extent[3])
    return jnp.repeat(refined, 2, axis=0)


def advance(padded, flow_field, diffusion):
    center = padded[1:-1, :, 1:-1]
    zpadded = jnp.concatenate([center[..., :1], center, center[..., -1:]], axis=3)
    minus_side = [padded[:-2, :, 1:-1], padded[1:-1, :, :-2], zpadded[..., :-2]]
    plus_side = [padded[2:, :, 1:-1], padded[1:-1, :, 2:], zpadded[..., 2:]]
    laplace = (
        minus_side[0]
        + plus_side[0]
        + minus_side[1]
        + plus_side[1]
        + minus_side[2]
        + plus_side[2]
        - 6.0 * center
    )
    transport = jnp.zeros_like(center)
    for direction in range(3):
        speed_part = flow_field[:, direction : direction + 1]
        transport = (
            transport
            + jnp.maximum(speed_part, 0.0) * (center - minus_side[direction])
            + jnp.minimum(speed_part, 0.0) * (plus_side[direction] - center)
        )
    return center + diffusion[None, :, None, None] * laplace - transport


def pack_slots(blocks, labels, block_len, devices, capacity):
    target = jnp.where(labels >= 0, labels // block_len, -1)
    positions = jnp.arange(labels.shape[0])
    earlier = (target[None, :] == target[:, None]) & (positions[None, :] < positions[:, None])
    ranking = jnp.sum(earlier.astype(jnp.int32), axis=1)
    slot_index = jnp.where(labels >= 0, target * capacity + ranking, -1)
    chosen = slot_index[None, :] == jnp.arange(devices * capacity)[:, None]
    outgoing = jnp.dot(chosen.astype(jnp.float32), blocks, precision=HIGHEST)
    within = jnp.sum(jnp.where(chosen, (labels % block_len)[None, :] + 1, 0), axis=1) - 1
    return (outgoing, within)


def unpack_slots(incoming, within, block_len):
    placing = (within[None, :] == jnp.arange(block_len)[:, None]).astype(jnp.float32)
    return (jnp.dot(placing, incoming, precision=HIGHEST), jnp.sum(placing, axis=1))


def on_device(old_fine, old_ids, old_coarse, coarse_ids, velocity, diffusion):
    dev_count = lax.axis_size("dev")
    plane_count = old_fine.shape[0]
    species = old_fine.shape[1]
    row_count = old_fine.shape[2]
    depth_count = old_fine.shape[3]
    fine_capacity = max(2, 2 * plane_count // dev_count)
    outgoing, within = pack_slots(
        old_fine.reshape(plane_count, -1), old_ids[0], plane_count, dev_count, fine_capacity
    )
    arrived, arrived_labels = (
        lax.all_to_all(outgoing, "dev", split_axis=0, concat_axis=0, tiled=True),
        lax.all_to_all(within, "dev", split_axis=0, concat_axis=0, tiled=True),
    )
    moved_rows, filled = unpack_slots(arrived, arrived_labels, plane_count)
    coarse_count = old_coarse.shape[0]
    coarse_flat = old_coarse.reshape(coarse_count, -1)
    coarse_labels = coarse_ids[0]
    coarse_capacity = max(2, 2 * coarse_count // dev_count)
    coarse_out, coarse_within = pack_slots(
        coarse_flat, coarse_labels, coarse_count, dev_count, coarse_capacity
    )
    coarse_in, coarse_in_labels = (
        lax.all_to_all(coarse_out, "dev", split_axis=0, concat_axis=0, tiled=True),
        lax.all_to_all(coarse_within, "dev", split_axis=0, concat_axis=0, tiled=True),
    )
    parents, coarse_filled = unpack_slots(coarse_in, coarse_in_labels, coarse_count)
    interp = refine(parents.reshape(coarse_count, species, row_count // 2, depth_count // 2))
    moved_rows = moved_rows.reshape(plane_count, species, row_count, depth_count)
    species_state = jnp.where((filled < 0.5)[:, None, None, None], interp, moved_rows)
    for repeat in range(ITERS):
        padded = extended(species_state, (("grp", 2), ("dev", 0)), 1)
        species_state = advance(padded, velocity, diffusion)
    return species_state


def solution(mesh):
    in_specs = (
        P("dev", None, "grp", None),
        P("grp", "dev"),
        P("dev", None, "grp", None),
        P("grp", "dev"),
        P("dev", None, "grp", None),
        P(),
    )
    out_specs = P("dev", None, "grp", None)
    return jax.shard_map(
        on_device, mesh=mesh, in_specs=in_specs, out_specs=out_specs, check_vma=False
    )
```

profile of v0, /device:TPU:22, one launch (start us, length us, event | category | flops | bytes accessed | tf_op | source)
XLA Modules:
  0.0 392.9 jit_solution(5522687836277141227)
XLA Ops:
  2.3 0.7 sub.89
  3.0 11.6 %all-to-all-start.1 = ((s32[32,2,1]{1,2,0:T(1,128)}), s32[32,2,1]{1,2,0:T(1,128)S(1)}, u32[]{:S(2)}, u32[]{:S(2)}) async-start(s32[32,2,1]{1,2,0:T(1,128)} %bitcast.11), calls=%async_computation.1 | async-start | bytes 32768 | tf_op jit(solution)/shard_map/all_to_all | solution.py:116
  16.9 1.6 reshape.166
  18.5 0.7 sub.85
  19.2 3.2 all-to-all-done.1
  22.4 6.5 %all-to-all-start = ((s32[32,4,1]{1,2,0:T(1,128)}), s32[32,4,1]{1,2,0:T(1,128)S(1)}, u32[]{:S(2)}, u32[]{:S(2)}) async-start(s32[32,4,1]{1,2,0:T(1,128)} %bitcast.5), calls=%async_computation | async-start | bytes 32768 | tf_op jit(solution)/shard_map/all_to_all | solution.py:104
  29.7 1.9 copy.44
  31.6 5.3 %all-to-all-done = s32[32,4,1]{1,2,0:T(1,128)S(1)} async-done(((s32[32,4,1]{1,2,0:T(1,128)}), s32[32,4,1]{1,2,0:T(1,128)S(1)}, u32[]{:S(2)}, u32[]{:S(2)}) %all-to-all-start) | async-done | bytes 544 | tf_op jit(solution)/shard_map/all_to_all | solution.py:104
  36.9 6.2 %all-to-all-start.2 = ((f32[32,2,4608]{2,1,0:T(2,128)}), f32[32,2,4608]{2,1,0:T(2,128)S(1)}, u32[]{:S(2)}, u32[]{:S(2)}) async-start(f32[32,2,4608]{2,1,0:T(2,128)} %copy.44), calls=%async_computation.2 | async-start | bytes 2359296 | tf_op jit(solution)/shard_map/all_to_all | solution.py:115
  43.1 5.2 %reshape.168 = f32[64,18432,1]{1,0,2:T(8,128)} reshape(f32[64,9,16,128]{3,2,1,0:T(8,128)} %param.6) | data formatting | bytes 9437184 | tf_op jit(solution)/shard_map/reshape | solution.py:100
  48.3 9.7 %fusion.38 = f32[32,4,18432]{2,0,1:T(8,128)} fusion(f32[64,18432,1]{1,0,2:T(8,128)} %reshape.168, s32[32,4]{0,1:T(4,128)S(1)} %multiply_add_fusion.2, s32[64]{0:T(128)S(1)} %get-tuple-element.31), kind=kOutput, calls=%fused_computation.80 | convolution fusion | flops 1811947520 | bytes 14156544 | tf_op jit(solution)/shard_map/dot_general | solution.py:82
  58.1 13.4 %copy.48 = f32[32,4,18432]{2,1,0:T(4,128)} copy(f32[32,4,18432]{2,0,1:T(8,128)} %fusion.38) | data formatting | bytes 18874368 | tf_op jit(solution)/shard_map/dot_general | solution.py:82
  71.5 10.7 %all-to-all-start.3 = ((f32[32,4,18432]{2,1,0:T(4,128)}), f32[32,4,18432]{2,1,0:T(4,128)}, u32[]{:S(2)}, u32[]{:S(2)}) async-start(f32[32,4,18432]{2,1,0:T(4,128)} %copy.48), calls=%async_computation.3 | async-start | bytes 18874368 | tf_op jit(solution)/shard_map/all_to_all | solution.py:103
  82.4 0.9 copy.50
  83.4 1.0 copy.51
  84.3 1.0 copy.52
  85.3 1.0 copy.53
  86.3 1.0 copy.54
  87.3 1.0 copy.55
  89.5 0.7 reduce.7
  90.5 0.8 all_to_all.23
  91.3 0.9 copy.45
  92.2 3.4 fusion.52
  96.0 1.0 add_bitcast_fusion.1
  97.0 1.0 add_bitcast_fusion.3
  98.5 3.1 pad_maximum_fusion.16
  101.7 12.7 %copy.46 = f32[32,9,8,2,64,2]{0,5,4,3,2,1:T(2,128)} copy(f32[32,9,8,2,64,2]{4,0,2,1,5,3:T(8,128)} %pad_maximum_fusion.16) | data formatting | bytes 4718592 | tf_op jit(solution)/shard_map/stack | solution.py:45
  114.4 6.7 %copy.47 = f32[32,9,16,128]{3,0,2,1:T(8,128)} copy(f32[32,9,16,128]{0,3,2,1:T(8,128)} %bitcast.89) | data formatting | bytes 4718592 | tf_op jit(solution)/shard_map/reshape | solution.py:46
  121.0 163.8 %all-to-all-done.3 = f32[32,4,18432]{2,1,0:T(4,128)} async-done(((f32[32,4,18432]{2,1,0:T(4,128)}), f32[32,4,18432]{2,1,0:T(4,128)}, u32[]{:S(2)}, u32[]{:S(2)}) %all-to-all-start.3) | async-done | bytes 9437216 | tf_op jit(solution)/shard_map/all_to_all | solution.py:103
  284.8 10.8 %all_to_all.25 = f32[128,18432]{1,0:T(8,128)} reshape(f32[32,4,18432]{2,1,0:T(4,128)} %all-to-all-done.3) | data formatting | bytes 18874368 | tf_op jit(solution)/shard_map/all_to_all | solution.py:103
  295.6 9.6 %copy.49 = f32[18432,128]{1,0:T(8,128)} copy(f32[18432,128]{0,1:T(8,128)} %bitcast.90) | data formatting | bytes 18874368 | tf_op jit(solution)/shard_map/dot_general | solution.py:89
  305.2 3.6 broadcast_in_dim.73
  308.8 8.4 %broadcast_select_fusion = f32[64,9,16,128]{3,0,2,1:T(8,128)S(1)} fusion(f32[64,9,16,128]{3,0,2,1:T(8,128)S(1)} %bitcast.91, pred[64]{0:T(512)(128)(4,1)S(1)} %broadcast_compare_fusion, f32[9,16,128,128]{3,2,1,0:T(8,128)} %bitcast.88, s32[128]{0:T(128)S(1)} %eq.136), kind=kOutput, calls=%fused_computation.61 | convolution fusion | flops 1813127168 | bytes 18874944 | tf_op jit(solution)/shard_map/dot_general | solution.py:89
  317.3 1.9 collective-permute-start.1
  319.3 3.6 collective-permute-start.2
  322.9 5.2 %collective-permute-start = (f32[1,9,16,128]{3,0,2,1:T(1,128)S(1)}, f32[1,9,16,128]{3,0,2,1:T(1,128)S(1)}, u32[]{:S(2)}, u32[]{:S(2)}) collective-permute-start(f32[1,9,16,128]{3,0,2,1:T(1,128)S(1)} %get-tuple-element.12), channel_id=1, source_target_pairs={{0,1},{1,2},{2,3},{3,4},{4,5},{5,6},{6,7},{7,8},{8,9},{9,10},{10,1... | collective-permute-start | bytes 221192 | tf_op jit(solution)/shard_map/ppermute | solution.py:20
  328.1 7.7 %collective-permute-start.3 = (f32[1,9,16,128]{3,0,2,1:T(1,128)S(1)}, f32[1,9,16,128]{3,0,2,1:T(1,128)S(1)}, u32[]{:S(2)}, u32[]{:S(2)}) collective-permute-start(f32[1,9,16,128]{3,0,2,1:T(1,128)S(1)} %get-tuple-element.11), channel_id=1, source_target_pairs={{1,0},{2,1},{3,2},{4,3},{5,4},{6,5},{7,6},{8,7},{9,8},{10,9},{11,1... | collective-permute-start | bytes 221192 | tf_op jit(solution)/shard_map/ppermute | solution.py:21
  335.8 4.1 %fusion.65 = (f32[64,9,16,1]{3,0,2,1:T(8,128)S(1)}, f32[64,9,16,1]{3,0,2,1:T(8,128)}) fusion(f32[64,9,16,128]{3,0,2,1:T(8,128)S(1)} %broadcast_select_fusion), kind=kLoop, calls=%fused_computation.149 | loop fusion | bytes 147456 | tf_op jit(solution)/shard_map/slice | solution.py:52
  339.9 0.7 copy-done.2
  340.6 14.2 %fusion.24 = f32[64,9,16,128]{3,0,2,1:T(8,128)S(1)} fusion(f32[64,9,16,128]{3,0,2,1:T(8,128)S(1)} %broadcast_select_fusion, f32[64,9,1,128]{3,0,2,1:T(8,128)} %copy-done.2, f32[64,9,1,128]{3,0,2,1:T(8,128)S(1)} %collective-permute-done.1, f32[64,9,16,1]{3,0,2,1:T(8,128)} %get-tuple-element.14, f32[64,9,16,1]{3,0,2,1:T(8,128)S(1)} %get-tuple-element.13, ...), kind=kLoop, calls=%fused_computation.37 | loop fusion | flops 50724864 | bytes 13393956 | tf_op jit(solution)/shard_map/sub | solution.py:72
  355.0 1.9 collective-permute-start.5
  356.9 3.6 collective-permute-start.6
  360.5 1.9 collective-permute-start.4
  362.5 6.0 %collective-permute-start.7 = (f32[1,9,16,128]{3,0,2,1:T(1,128)S(1)}, f32[1,9,16,128]{3,0,2,1:T(1,128)S(1)}, u32[]{:S(2)}, u32[]{:S(2)}) collective-permute-start(f32[1,9,16,128]{3,0,2,1:T(1,128)S(1)} %get-tuple-element.5), channel_id=1, source_target_pairs={{1,0},{2,1},{3,2},{4,3},{5,4},{6,5},{7,6},{8,7},{9,8},{10,9},{11,1... | collective-permute-start | bytes 221192 | tf_op jit(solution)/shard_map/ppermute | solution.py:21
  368.5 4.1 %fusion.62 = (f32[64,9,16,1]{3,0,2,1:T(8,128)S(1)}, f32[64,9,16,1]{3,0,2,1:T(8,128)}) fusion(f32[64,9,16,128]{3,0,2,1:T(8,128)S(1)} %fusion.24), kind=kLoop, calls=%fused_computation.146 | loop fusion | bytes 147456 | tf_op jit(solution)/shard_map/slice | solution.py:52
  372.7 0.7 copy-done.1
  373.4 14.4 %fusion.6 = f32[64,9,16,128]{3,0,2,1:T(8,128)S(1)} fusion(f32[64,9,16,128]{3,0,2,1:T(8,128)S(1)} %fusion.24, f32[64,9,1,128]{3,0,2,1:T(8,128)} %copy-done.1, f32[64,9,1,128]{3,0,2,1:T(8,128)S(1)} %collective-permute-done.5, f32[64,9,16,1]{3,0,2,1:T(8,128)} %get-tuple-element.8, f32[64,9,16,1]{3,0,2,1:T(8,128)S(1)} %get-tuple-element.7, ...), kind=kLoop, calls=%fused_computation.9 | loop fusion | flops 50724864 | bytes 13393956 | tf_op jit(solution)/shard_map/sub | solution.py:72
  387.7 4.9 %copy.56 = f32[64,9,16,128]{3,2,1,0:T(8,128)} copy(f32[64,9,16,128]{3,0,2,1:T(8,128)S(1)} %fusion.6) | data formatting | bytes 9437184 | tf_op jit(solution)/shard_map/sub | solution.py:72
  (44 shorter events, 8.4 us)
Async XLA Ops:
  3.0 19.4 %all-to-all-start.1 = ((s32[32,2,1]{1,2,0:T(1,128)}), s32[32,2,1]{1,2,0:T(1,128)S(1)}, u32[]{:S(2)}, u32[]{:S(2)}) async-start(s32[32,2,1]{1,2,0:T(1,128)} %bitcast.11), calls=%async_computation.1 | async-start | bytes 32768 | tf_op jit(solution)/shard_map/all_to_all | solution.py:116
  22.4 14.5 %all-to-all-start = ((s32[32,4,1]{1,2,0:T(1,128)}), s32[32,4,1]{1,2,0:T(1,128)S(1)}, u32[]{:S(2)}, u32[]{:S(2)}) async-start(s32[32,4,1]{1,2,0:T(1,128)} %bitcast.5), calls=%async_computation | async-start | bytes 32768 | tf_op jit(solution)/shard_map/all_to_all | solution.py:104
  36.9 34.6 %all-to-all-start.2 = ((f32[32,2,4608]{2,1,0:T(2,128)}), f32[32,2,4608]{2,1,0:T(2,128)S(1)}, u32[]{:S(2)}, u32[]{:S(2)}) async-start(f32[32,2,4608]{2,1,0:T(2,128)} %copy.44), calls=%async_computation.2 | async-start | bytes 2359296 | tf_op jit(solution)/shard_map/all_to_all | solution.py:115
  71.5 10.7 %copy-start = (f32[64,3,16,128]{3,2,1,0:T(8,128)S(1)}, f32[64,3,16,128]{3,2,1,0:T(8,128)}, u32[]{:S(2)}) copy-start(f32[64,3,16,128]{3,2,1,0:T(8,128)} %param.10) | copy-start | bytes 4718596
  71.5 213.4 %all-to-all-start.3 = ((f32[32,4,18432]{2,1,0:T(4,128)}), f32[32,4,18432]{2,1,0:T(4,128)}, u32[]{:S(2)}, u32[]{:S(2)}) async-start(f32[32,4,18432]{2,1,0:T(4,128)} %copy.48), calls=%async_computation.3 | async-start | bytes 18874368 | tf_op jit(solution)/shard_map/all_to_all | solution.py:103
  317.3 22.6 %collective-permute-start.1 = (f32[64,9,1,128]{3,0,2,1:T(8,128)S(1)}, f32[64,9,1,128]{3,0,2,1:T(8,128)S(1)}, u32[]{:S(2)}, u32[]{:S(2)}) collective-permute-start(f32[64,9,1,128]{3,0,2,1:T(8,128)S(1)} %get-tuple-element.15), channel_id=1, source_target_pairs={{0,32},{32,64},{64,96},{96,128},{128,160},{160,192},{192,224},{1,3... | collective-permute-start | bytes 884744 | tf_op jit(solution)/shard_map/ppermute | solution.py:20
  319.3 20.6 %collective-permute-start.2 = (f32[64,9,1,128]{3,0,2,1:T(8,128)S(1)}, f32[64,9,1,128]{3,0,2,1:T(8,128)S(1)}, u32[]{:S(2)}, u32[]{:S(2)}) collective-permute-start(f32[64,9,1,128]{3,0,2,1:T(8,128)S(1)} %get-tuple-element.16), channel_id=1, source_target_pairs={{32,0},{64,32},{96,64},{128,96},{160,128},{192,160},{224,192},{33,... | collective-permute-start | bytes 884744 | tf_op jit(solution)/shard_map/ppermute | solution.py:21
  322.9 17.0 %collective-permute-start = (f32[1,9,16,128]{3,0,2,1:T(1,128)S(1)}, f32[1,9,16,128]{3,0,2,1:T(1,128)S(1)}, u32[]{:S(2)}, u32[]{:S(2)}) collective-permute-start(f32[1,9,16,128]{3,0,2,1:T(1,128)S(1)} %get-tuple-element.12), channel_id=1, source_target_pairs={{0,1},{1,2},{2,3},{3,4},{4,5},{5,6},{6,7},{7,8},{8,9},{9,10},{10,1... | collective-permute-start | bytes 221192 | tf_op jit(solution)/shard_map/ppermute | solution.py:20
  328.1 12.5 %copy-start.3 = (f32[9]{0:T(128)S(1)}, f32[9]{0:T(128)}, u32[]{:S(2)}) copy-start(f32[9]{0:T(128)} %param.11) | copy-start | bytes 112
  328.1 11.8 %collective-permute-start.3 = (f32[1,9,16,128]{3,0,2,1:T(1,128)S(1)}, f32[1,9,16,128]{3,0,2,1:T(1,128)S(1)}, u32[]{:S(2)}, u32[]{:S(2)}) collective-permute-start(f32[1,9,16,128]{3,0,2,1:T(1,128)S(1)} %get-tuple-element.11), channel_id=1, source_target_pairs={{1,0},{2,1},{3,2},{4,3},{5,4},{6,5},{7,6},{8,7},{9,8},{10,9},{11,1... | collective-permute-start | bytes 221192 | tf_op jit(solution)/shard_map/ppermute | solution.py:21
  339.9 0.7 copy-start.2
  355.0 17.7 %collective-permute-start.5 = (f32[64,9,1,128]{3,0,2,1:T(8,128)S(1)}, f32[64,9,1,128]{3,0,2,1:T(8,128)S(1)}, u32[]{:S(2)}, u32[]{:S(2)}) collective-permute-start(f32[64,9,1,128]{3,0,2,1:T(8,128)S(1)} %get-tuple-element.9), channel_id=1, source_target_pairs={{0,32},{32,64},{64,96},{96,128},{128,160},{160,192},{192,224},{1,3... | collective-permute-start | bytes 884744 | tf_op jit(solution)/shard_map/ppermute | solution.py:20
  356.9 15.7 %collective-permute-start.6 = (f32[64,9,1,128]{3,0,2,1:T(8,128)S(1)}, f32[64,9,1,128]{3,0,2,1:T(8,128)S(1)}, u32[]{:S(2)}, u32[]{:S(2)}) collective-permute-start(f32[64,9,1,128]{3,0,2,1:T(8,128)S(1)} %get-tuple-element.10), channel_id=1, source_target_pairs={{32,0},{64,32},{96,64},{128,96},{160,128},{192,160},{224,192},{33,... | collective-permute-start | bytes 884744 | tf_op jit(solution)/shard_map/ppermute | solution.py:21
  360.5 12.1 %collective-permute-start.4 = (f32[1,9,16,128]{3,0,2,1:T(1,128)S(1)}, f32[1,9,16,128]{3,0,2,1:T(1,128)S(1)}, u32[]{:S(2)}, u32[]{:S(2)}) collective-permute-start(f32[1,9,16,128]{3,0,2,1:T(1,128)S(1)} %get-tuple-element.6), channel_id=1, source_target_pairs={{0,1},{1,2},{2,3},{3,4},{4,5},{5,6},{6,7},{7,8},{8,9},{9,10},{10,1... | collective-permute-start | bytes 221192 | tf_op jit(solution)/shard_map/ppermute | solution.py:20
  362.5 10.2 %collective-permute-start.7 = (f32[1,9,16,128]{3,0,2,1:T(1,128)S(1)}, f32[1,9,16,128]{3,0,2,1:T(1,128)S(1)}, u32[]{:S(2)}, u32[]{:S(2)}) collective-permute-start(f32[1,9,16,128]{3,0,2,1:T(1,128)S(1)} %get-tuple-element.5), channel_id=1, source_target_pairs={{1,0},{2,1},{3,2},{4,3},{5,4},{6,5},{7,6},{8,7},{9,8},{10,9},{11,1... | collective-permute-start | bytes 221192 | tf_op jit(solution)/shard_map/ppermute | solution.py:21
  372.6 0.7 copy-start.1
where the time goes:
time: 398 us; the launch traced here: 393 us
  waiting for transfers between devices  172 us (43%)
  local copies, waits for them, and re-layouts  90.4 us (23%)
  starting transfers between devices  66.9 us (17%)
  other arithmetic  40.5 us (10%)
  matrix products  22.1 us (6%)
    all_to_all x1, waiting for transfers between devices, on_device(): lax.all_to_all(outgoing, 'dev', split_axis=0, concat_axis=0, tiled=True)  164 us
    sub x2, other arithmetic, advance(): return center + diffusion[None, :, None, None] * laplace - transport  28.5 us
    ppermute x4, starting transfers between devices, extended(): lax.ppermute(leading, axis, [(b, a) for a, b in up])  21 us
    dot_general x2, local copies, waits for them, and re-layouts, pack_slots(): outgoing = jnp.dot(chosen.astype(jnp.float32), blocks, precision=HIGHEST)  15.3 us
    another operation x1, local copies, waits for them, and re-layouts, refine(): children = jnp.stack(row_parts, axis=3)  12.7 us
    dot_general x2, matrix products, unpack_slots(): jnp.dot(placing, incoming, precision=HIGHEST)  11.7 us
    all_to_all x1, starting transfers between devices, on_device(): lax.all_to_all(coarse_within, 'dev', split_axis=0, concat_axis=0, tiled=T...  11.6 us
    ppermute x4, starting transfers between devices, extended(): lax.ppermute(last, axis, up)  10.9 us
  transfers between devices with their start and end apart: 12, of which 3 were waited for; matrix products, arithmetic and copies ran while one was open for 21% of the time, Pallas kernels for 0%

commit v1 on v0

v1 whole, which is shorter than its diff:
```python
import functools

import jax
import jax.numpy as jnp
from jax import lax
from jax.experimental import pallas as pl
from jax.experimental.pallas import tpu as pltpu
from jax.sharding import PartitionSpec as P

ITERS = 2
FINE_CAP = 4
COARSE_CAP = 2
VMEM = pl.BlockSpec(memory_space=pltpu.VMEM)
SMEM = pl.BlockSpec(memory_space=pltpu.SMEM)
PARAMS = pltpu.CompilerParams(vmem_limit_bytes=56 * 1024 * 1024)


def ranks(boxes):
    count = boxes.shape[-1]
    earlier = jnp.arange(count)[None, :] < jnp.arange(count)[:, None]
    same = boxes[..., None, :] == boxes[..., :, None]
    return jnp.sum((same & earlier).astype(jnp.int32), axis=-1)


def pack_fine_kernel(slot_ref, fine_ref, out_ref):
    planes = fine_ref.shape[0]

    def body(k, carry):
        slot = slot_ref[k]

        @pl.when(slot >= 0)
        def _():
            out_ref[slot] = fine_ref[k]

        return carry

    lax.fori_loop(0, planes, body, 0)


def pack_coarse_kernel(slot_ref, coarse_ref, out_ref):
    planes, _, _, depth = coarse_ref.shape

    def body(k, carry):
        slot = slot_ref[k]
        pair = slot // 2

        @pl.when(slot % 2 == 0)
        def _():
            out_ref[pair, :, :, 0:depth] = coarse_ref[k]

        @pl.when(slot % 2 == 1)
        def _():
            out_ref[pair, :, :, depth : 2 * depth] = coarse_ref[k]

        return carry

    lax.fori_loop(0, planes, body, 0)


def build_kernel(fine_at_ref, coarse_at_ref, fine_ref, coarse_ref, out_ref, ylow_ref, yhigh_ref, xlow_ref, xhigh_ref):
    planes, species, rows, lanes = out_ref.shape
    half = rows // 2
    lane = lax.broadcasted_iota(jnp.int32, (half, lanes), 1)
    row = lax.broadcasted_iota(jnp.int32, (half, lanes), 0)
    sign = jnp.where(lane % 2 == 0, -0.25, 0.25)
    lane_first = lane % (lanes // 2) == 0
    lane_last = lane % (lanes // 2) == lanes // 2 - 1

    def body(c, carry):
        at = [fine_at_ref[2 * c], fine_at_ref[2 * c + 1]]

        @pl.when((at[0] < 0) | (at[1] < 0))
        def _():
            slot = coarse_at_ref[c]
            pair = slot // 2
            index = (slot % 2) * (lanes // 2) + lane // 2
            for s in range(species):
                p = coarse_ref[pair, s]
                below = jnp.where(row == 0, p, pltpu.roll(p, 1, 0))
                above = jnp.where(row == half - 1, p, pltpu.roll(p, half - 1, 0))
                left = jnp.where(lane_first, p, pltpu.roll(p, 1, 1))
                right = jnp.where(lane_last, p, pltpu.roll(p, lanes - 1, 1))
                slope_y = 0.125 * (above - below)
                slope_z = 0.5 * (right - left)
                gz = jnp.take_along_axis(slope_z, index, axis=1) * sign
                even = jnp.take_along_axis(p - slope_y, index, axis=1) + gz
                odd = jnp.take_along_axis(p + slope_y, index, axis=1) + gz
                for child in range(2):

                    @pl.when(at[child] < 0)
                    def _():
                        x = 2 * c + child
                        out_ref[x, s, pl.ds(0, half, 2), :] = even
                        out_ref[x, s, pl.ds(1, half, 2), :] = odd
                        ylow_ref[pl.ds(x * species + s, 1), :] = even[0:1]
                        yhigh_ref[pl.ds(x * species + s, 1), :] = odd[half - 1 : half]

        for child in range(2):

            @pl.when(at[child] >= 0)
            def _():
                x = 2 * c + child
                for s in range(species):
                    value = fine_ref[at[child], s]
                    out_ref[x, s] = value
                    ylow_ref[pl.ds(x * species + s, 1), :] = value[0:1]
                    yhigh_ref[pl.ds(x * species + s, 1), :] = value[rows - 1 : rows]

        return carry

    lax.fori_loop(0, planes // 2, body, 0)
    xlow_ref[...] = out_ref[0]
    xhigh_ref[...] = out_ref[planes - 1]


def step_kernel(edges, diff_ref, u_ref, vel_ref, ylow_ref, yhigh_ref, xlow_ref, xhigh_ref, out_ref, *edge_refs):
    planes, species, rows, lanes = u_ref.shape
    lane = lax.broadcasted_iota(jnp.int32, (rows, lanes), 1)
    row = lax.broadcasted_iota(jnp.int32, (rows, lanes), 0)

    def plane(x, below, above):
        positive = [jnp.maximum(vel_ref[x, k], 0.0) for k in range(3)]
        negative = [jnp.minimum(vel_ref[x, k], 0.0) for k in range(3)]
        keep = 1.0
        for k in range(3):
            keep = keep - (positive[k] - negative[k])
        for s in range(species):
            d = diff_ref[s]
            u = u_ref[x, s]
            y_low = jnp.where(row == 0, ylow_ref[pl.ds(x * species + s, 1), :], pltpu.roll(u, 1, 0))
            y_high = jnp.where(row == rows - 1, yhigh_ref[pl.ds(x * species + s, 1), :], pltpu.roll(u, rows - 1, 0))
            z_low = jnp.where(lane == 0, u, pltpu.roll(u, 1, 1))
            z_high = jnp.where(lane == lanes - 1, u, pltpu.roll(u, lanes - 1, 1))
            new = u * (keep - 6.0 * d)
            for k, (low, high) in enumerate(((below(s), above(s)), (y_low, y_high), (z_low, z_high))):
                new = new + low * (d + positive[k]) + high * (d - negative[k])
            out_ref[x, s] = new
            if edges:
                edge_refs[0][pl.ds(x * species + s, 1), :] = new[0:1]
                edge_refs[1][pl.ds(x * species + s, 1), :] = new[rows - 1 : rows]

    plane(0, lambda s: xlow_ref[s], lambda s: u_ref[1, s])

    def body(x, carry):
        plane(x, lambda s: u_ref[x - 1, s], lambda s: u_ref[x + 1, s])
        return carry

    lax.fori_loop(1, planes - 1, body, 0)
    plane(planes - 1, lambda s: u_ref[planes - 2, s], lambda s: xhigh_ref[s])
    if edges:
        edge_refs[2][...] = out_ref[0]
        edge_refs[3][...] = out_ref[planes - 1]


def halo(ylow, yhigh, xlow, xhigh):
    got = []
    for axis, low, high in (("grp", ylow, yhigh), ("dev", xlow, xhigh)):
        size = lax.axis_size(axis)
        up = [(i, (i + 1) % size) for i in range(size - 1)]
        got.append(lax.ppermute(high, axis, up))
        got.append(lax.ppermute(low, axis, [(b, a) for a, b in up]))
    return got


def on_device(old_fine, old_ids, old_coarse, coarse_ids, velocity, diffusion):
    devices = lax.axis_size("dev")
    me = lax.axis_index("dev")
    planes, species, rows, lanes = old_fine.shape
    coarse_planes = old_coarse.shape[0]
    f32 = jnp.float32

    own_coarse = coarse_ids[0]
    coarse_slot = (own_coarse // coarse_planes) * COARSE_CAP + ranks(own_coarse // coarse_planes)
    coarse_out = pl.pallas_call(
        pack_coarse_kernel,
        out_shape=jax.ShapeDtypeStruct((devices, species, rows // 2, lanes), f32),
        in_specs=[SMEM, VMEM],
        out_specs=VMEM,
        compiler_params=PARAMS,
        name="pack_coarse",
    )(coarse_slot, old_coarse)
    coarse_in = lax.all_to_all(coarse_out, "dev", split_axis=0, concat_axis=0, tiled=True)

    own = old_ids[0]
    own_box = jnp.where(own >= 0, own // planes, -1)
    fine_slot = jnp.where(own >= 0, own_box * FINE_CAP + ranks(own_box), -1)
    fine_out = pl.pallas_call(
        pack_fine_kernel,
        out_shape=jax.ShapeDtypeStruct((devices * FINE_CAP, species, rows, lanes), f32),
        in_specs=[SMEM, VMEM],
        out_specs=VMEM,
        compiler_params=PARAMS,
        name="pack_fine",
    )(fine_slot, old_fine)
    fine_in = lax.all_to_all(fine_out, "dev", split_axis=0, concat_axis=0, tiled=True)

    labels = lax.all_gather(jnp.concatenate([own, own_coarse]), "dev", tiled=False)
    all_ids, all_coarse = labels[:, :planes], labels[:, planes:]
    all_box = jnp.where(all_ids >= 0, all_ids // planes, -1)
    slot_of = jnp.arange(devices)[:, None] * FINE_CAP + ranks(all_box)
    wanted = me * planes + jnp.arange(planes)
    fine_at = jnp.max(jnp.where(all_ids[None] == wanted[:, None, None], slot_of[None], -1), axis=(1, 2))
    coarse_slot_of = jnp.arange(devices)[:, None] * COARSE_CAP + ranks(all_coarse // coarse_planes)
    coarse_wanted = me * coarse_planes + jnp.arange(coarse_planes)
    coarse_at = jnp.max(
        jnp.where(all_coarse[None] == coarse_wanted[:, None, None], coarse_slot_of[None], 0), axis=(1, 2)
    )

    edge_shapes = [jax.ShapeDtypeStruct((planes * species, lanes), f32)] * 2 + [
        jax.ShapeDtypeStruct((species, rows, lanes), f32)
    ] * 2
    state_shape = jax.ShapeDtypeStruct(old_fine.shape, f32)
    state, *edges = pl.pallas_call(
        build_kernel,
        out_shape=[state_shape] + edge_shapes,
        in_specs=[SMEM, SMEM, VMEM, VMEM],
        out_specs=[VMEM] * 5,
        compiler_params=PARAMS,
        name="build",
    )(fine_at, coarse_at, fine_in, coarse_in)

    for repeat in range(ITERS):
        last = repeat == ITERS - 1
        around = halo(*edges)
        state, *edges = pl.pallas_call(
            functools.partial(step_kernel, not last),
            out_shape=[state_shape] + ([] if last else edge_shapes),
            in_specs=[SMEM] + [VMEM] * 6,
            out_specs=[VMEM] * (1 if last else 5),
            compiler_params=PARAMS,
            name="step",
        )(diffusion, state, velocity, *around)
    return state


def solution(mesh):
    in_specs = (
        P("dev", None, "grp", None),
        P("grp", "dev"),
        P("dev", None, "grp", None),
        P("grp", "dev"),
        P("dev", None, "grp", None),
        P(),
    )
    out_specs = P("dev", None, "grp", None)
    return jax.shard_map(
        on_device, mesh=mesh, in_specs=in_specs, out_specs=out_specs, check_vma=False
    )
```

time: 398 us -> 503 us (1.26)
  blocking collectives: 0 us -> 336 us
  waiting for transfers between devices: 172 us -> 29.1 us
  local copies, waits for them, and re-layouts: 90.4 us -> 3.38 us
  Pallas kernels: 0 us -> 42.4 us
  other arithmetic: 40.5 us -> 8.78 us
  matrix products: 22.1 us -> 0 us
  starting transfers between devices: 66.9 us -> 73.2 us
    unnamed x0 -> x1, blocking collectives: none -> 336 us
    all_to_all x3 -> x1, waiting for transfers between devices: 172 us -> 0.01 us  [on_device(): lax.all_to_all(fine_out, 'dev', split_axis=0, concat_axis=0, tiled=True)]
    pallas_call x0 -> x5, Pallas kernels: none -> 42.4 us  [the longest x2 24.2 us: on_device(): pl.pallas_call(functools.partial(step_kernel, not last), out_shape=[state...]
    sub x4 -> x0, other arithmetic: 28.5 us -> none  [the longest x2 28.5 us: advance(): return center + diffusion[None, :, None, None] * laplace - transport]
    dot_general x4 -> x0, local copies, waits for them, and re-layouts: 25.7 us -> none  [the longest x2 15.3 us: pack_slots(): outgoing = jnp.dot(chosen.astype(jnp.float32), blocks, precision=HIGHEST)]
    ppermute x8, starting transfers between devices: 31.9 us -> 54.1 us  [the longest x4 36 us: halo(): got.append(lax.ppermute(high, axis, up))]
    dot_general x4 -> x0, matrix products: 22.1 us -> none  [the longest x2 11.7 us: unpack_slots(): jnp.dot(placing, incoming, precision=HIGHEST)]
    all_to_all x3 -> x1, starting transfers between devices: 28.8 us -> 7.43 us  [on_device(): lax.all_to_all(fine_out, 'dev', split_axis=0, concat_axis=0, tiled=True)]
  transfers between devices with their start and end apart: 12 -> 10, of which waited for: 3 -> 5; matrix products, arithmetic and copies ran while one was open for 21% -> 1% of each run, Pallas kernels for 0% -> 1%
where the time goes in v1:
time: 503 us; the launch traced here: 493 us
  blocking collectives  336 us (67%)
  starting transfers between devices  73.2 us (15%)
  Pallas kernels  42.4 us (8%)
  waiting for transfers between devices  29.1 us (6%)
  other arithmetic  8.78 us (2%)
    unnamed x1, blocking collectives  336 us
    ppermute x4, starting transfers between devices, halo(): got.append(lax.ppermute(high, axis, up))  36 us
    pallas_call x2, Pallas kernels, on_device(): pl.pallas_call(functools.partial(step_kernel, not last), out_shape=[state...  24.2 us
    all_to_all x1, waiting for transfers between devices, on_device(): lax.all_to_all(coarse_out, 'dev', split_axis=0, concat_axis=0, tiled=True)  21.1 us
    ppermute x4, starting transfers between devices, halo(): got.append(lax.ppermute(low, axis, [(b, a) for a, b in up]))  18.2 us
    all_to_all x1, starting transfers between devices, on_device(): lax.all_to_all(coarse_out, 'dev', split_axis=0, concat_axis=0, tiled=True)  11.6 us
  transfers between devices with their start and end apart: 10, of which 5 were waited for; matrix products, arithmetic and copies ran while one was open for 1% of the time, Pallas kernels for 1%

profile of v1, /device:TPU:22, one launch (start us, length us, event | category | flops | bytes accessed | tf_op | source)
XLA Modules:
  0.0 493.5 jit_solution(1377598524432164444)
XLA Ops:
  0.0 0.7 and_select_fusion.1
  0.7 0.7 fusion.5
  1.3 0.2 convert_reduce_fusion.3
  1.5 1.2 multiply_add_fusion.slot_ref
  2.7 3.5 pack_coarse.1
  6.2 11.6 %all-to-all-start.1 = ((f32[32,9,8,128]{3,2,1,0:T(8,128)}), f32[32,9,8,128]{3,2,1,0:T(8,128)S(1)}, u32[]{:S(2)}, u32[]{:S(2)}) async-start(f32[32,9,8,128]{3,2,1,0:T(8,128)} %pack_coarse.1), calls=%async_computation.1 | async-start | bytes 2359296 | tf_op jit(solution)/shard_map/all_to_all | solution.py:182
  17.9 0.2 convert_reduce_fusion.2
  18.1 0.5 compare_select_fusion.13.slot_ref
  18.6 7.1 %pack_fine.1 = f32[128,9,16,128]{3,2,1,0:T(8,128)} custom-call(s32[64]{0:T(128)} %compare_select_fusion.13.slot_ref, f32[64,9,16,128]{3,2,1,0:T(8,128)} %fine_ref.1), custom_call_target="tpu_custom_call" | custom-call | tf_op jit(solution)/shard_map/pack_fine/pallas_call | solution.py:187
  25.7 21.1 %all-to-all-done.1.coarse_ref = f32[32,9,8,128]{3,2,1,0:T(8,128)S(1)} async-done(((f32[32,9,8,128]{3,2,1,0:T(8,128)}), f32[32,9,8,128]{3,2,1,0:T(8,128)S(1)}, u32[]{:S(2)}, u32[]{:S(2)}) %all-to-all-start.1) | async-done | bytes 1179680 | tf_op jit(solution)/shard_map/all_to_all | solution.py:182
  46.8 1.0 copy-done
  47.8 7.4 %all-to-all-start = ((f32[128,9,16,128]{3,2,1,0:T(8,128)}), f32[128,9,16,128]{3,2,1,0:T(8,128)}, u32[]{:S(2)}, u32[]{:S(2)}) async-start(f32[128,9,16,128]{3,2,1,0:T(8,128)} %pack_fine.1), calls=%async_computation | async-start | bytes 18874368 | tf_op jit(solution)/shard_map/all_to_all | solution.py:195
  55.3 0.6 dynamic-slice
  56.5 0.2 add_dynamic-update-slice_fusion
  56.7 335.8 %all-reduce = s32[3072]{0:T(1024)S(1)} all-reduce(s32[3072]{0:T(1024)S(1)} %add_dynamic-update-slice_fusion), channel_id=2, replica_groups=mesh['grp'=8,'dev'=32] {'dev'}, use_global_device_ids=true, to_apply=%add | all-reduce | flops 3072 | bytes 24576
  392.5 0.1 reshape.139
  392.6 0.1 fusion.7
  392.7 0.8 convert_reduce_fusion.1
  393.5 0.1 broadcast_add_fusion
  393.5 1.3 select_reduce_fusion.1.coarse_at_ref
  394.8 0.9 convert_reduce_fusion
  395.7 0.1 broadcast_add_fusion.1
  395.8 1.9 select_reduce_fusion.fine_at_ref
  397.7 0.0 all-to-all-done.fine_ref
  397.8 7.6 %build.1 = (f32[64,9,16,128]{3,2,1,0:T(8,128)}, f32[576,128]{1,0:T(8,128)}, f32[576,128]{1,0:T(8,128)}, f32[9,16,128]{2,1,0:T(8,128)}, f32[9,16,128]{2,1,0:T(8,128)}) custom-call(s32[64]{0:T(128)} %select_reduce_fusion.fine_at_ref, s32[32]{0:T(128)} %select_reduce_fusion.1.coarse_at_ref, f32[128,9,16,128]{3,2,1,0:T(8,128)} %all-to-all-done.fine_ref, ...), custom_call_target="tpu_custom_call" | custom-call | tf_op jit(solution)/shard_map/build/pallas_call | solution.py:213
  405.4 1.9 collective-permute-start
  407.3 3.6 collective-permute-start.1
  410.9 30.1 %collective-permute-start.2 = (f32[9,16,128]{2,1,0:T(8,128)}, f32[9,16,128]{2,1,0:T(8,128)S(1)}, u32[]{:S(2)}, u32[]{:S(2)}) collective-permute-start(f32[9,16,128]{2,1,0:T(8,128)} %get-tuple-element.18), channel_id=1, source_target_pairs={{0,1},{1,2},{2,3},{3,4},{4,5},{5,6},{6,7},{7,8},{8,9},{9,10},{10,1... | collective-permute-start | bytes 221192 | tf_op jit(solution)/shard_map/ppermute | solution.py:160
  441.0 4.7 collective-permute-start.3
  445.7 1.1 collective-permute-done.2.xlow_ref
  446.7 1.8 collective-permute-done.3.xhigh_ref
  448.6 0.0 collective-permute-done.ylow_ref
  448.6 0.0 collective-permute-done.1.yhigh_ref
  448.6 0.6 copy-done.6
  449.2 0.1 copy-done.1
  449.3 0.1 copy-done.2
  449.5 12.2 %step.2 = (f32[64,9,16,128]{3,2,1,0:T(8,128)}, f32[576,128]{1,0:T(8,128)}, f32[576,128]{1,0:T(8,128)}, f32[9,16,128]{2,1,0:T(8,128)}, f32[9,16,128]{2,1,0:T(8,128)}) custom-call(f32[9]{0:T(128)} %diff_ref.3, f32[64,9,16,128]{3,2,1,0:T(8,128)} %get-tuple-element.15.u_ref, f32[64,3,16,128]{3,2,1,0:T(8,128)} %vel_ref.3, f32[576,128]{1,0:T(8,128)} %copy-done.1, ...), custom_call_target="tpu_custom_call" | custom-call | tf_op jit(solution)/shard_map/step/pallas_call | solution.py:225
  461.7 2.1 collective-permute-start.4
  463.7 3.5 collective-permute-start.5
  467.2 1.9 collective-permute-start.6
  469.2 6.4 %collective-permute-start.7 = (f32[9,16,128]{2,1,0:T(8,128)}, f32[9,16,128]{2,1,0:T(8,128)S(1)}, u32[]{:S(2)}, u32[]{:S(2)}) collective-permute-start(f32[9,16,128]{2,1,0:T(8,128)} %get-tuple-element.24), channel_id=1, source_target_pairs={{1,0},{2,1},{3,2},{4,3},{5,4},{6,5},{7,6},{8,7},{9,8},{10,9},{11,1... | collective-permute-start | bytes 221192 | tf_op jit(solution)/shard_map/ppermute | solution.py:161
  475.6 1.0 collective-permute-done.6.xlow_ref
  476.5 4.1 collective-permute-done.7.xhigh_ref
  480.6 0.0 collective-permute-done.4.ylow_ref
  480.6 0.6 copy-done.8
  481.2 0.1 copy-done.3
  481.3 0.1 copy-done.4
  481.5 12.0 %step.3 = f32[64,9,16,128]{3,2,1,0:T(8,128)} custom-call(f32[9]{0:T(128)} %diff_ref.3, f32[64,9,16,128]{3,2,1,0:T(8,128)} %get-tuple-element.20.u_ref, f32[64,3,16,128]{3,2,1,0:T(8,128)} %vel_ref.3, f32[576,128]{1,0:T(8,128)} %copy-done.3, f32[576,128]{1,0:T(8,128)} %copy-done.4, f32[9,16,128]{2,1,0:T(8,128)} %copy-done.7, f32[9,16,128]{2,1,0:T(8,128)} %copy-done.8), custom_call_target="tpu_custom_call" | custom-call | tf_op jit(solution)/shard_map/step/pallas_call | solution.py:225
  (28 shorter events, 0.1 us)
Async XLA Ops:
  0.0 17.8 %copy-start.10 = (s32[1,64]{1,0:T(1,128)S(1)}, s32[1,64]{1,0:T(1,128)}, u32[]{:S(2)}) copy-start(s32[1,64]{1,0:T(1,128)} %param.7) | copy-start | bytes 772
  6.2 40.5 %all-to-all-start.1 = ((f32[32,9,8,128]{3,2,1,0:T(8,128)}), f32[32,9,8,128]{3,2,1,0:T(8,128)S(1)}, u32[]{:S(2)}, u32[]{:S(2)}) async-start(f32[32,9,8,128]{3,2,1,0:T(8,128)} %pack_coarse.1), calls=%async_computation.1 | async-start | bytes 2359296 | tf_op jit(solution)/shard_map/all_to_all | solution.py:182
  25.6 29.6 %copy-start.11 = (u32[256]{0:T(256)S(1)}, u32[256]{0:T(256)}, u32[]{:S(2)}) copy-start(u32[256]{0:T(256)} %constant.71) | copy-start | bytes 3076
  25.6 30.9 %copy-start.9 = (s32[1,32]{1,0:T(1,128)S(1)}, s32[1,32]{1,0:T(1,128)}, u32[]{:S(2)}) copy-start(s32[1,32]{1,0:T(1,128)} %param.9) | copy-start | bytes 388
  46.8 1.0 copy-start
  47.8 350.0 %all-to-all-start = ((f32[128,9,16,128]{3,2,1,0:T(8,128)}), f32[128,9,16,128]{3,2,1,0:T(8,128)}, u32[]{:S(2)}, u32[]{:S(2)}) async-start(f32[128,9,16,128]{3,2,1,0:T(8,128)} %pack_fine.1), calls=%async_computation | async-start | bytes 18874368 | tf_op jit(solution)/shard_map/all_to_all | solution.py:195
  405.4 43.2 %collective-permute-start = (f32[576,128]{1,0:T(8,128)}, f32[576,128]{1,0:T(8,128)S(1)}, u32[]{:S(2)}, u32[]{:S(2)}) collective-permute-start(f32[576,128]{1,0:T(8,128)} %get-tuple-element.16), channel_id=1, source_target_pairs={{0,32},{32,64},{64,96},{96,128},{128,160},{160,192},{192,224},{1,3... | collective-permute-start | bytes 884744 | tf_op jit(solution)/shard_map/ppermute | solution.py:160
  407.3 41.3 %collective-permute-start.1 = (f32[576,128]{1,0:T(8,128)}, f32[576,128]{1,0:T(8,128)S(1)}, u32[]{:S(2)}, u32[]{:S(2)}) collective-permute-start(f32[576,128]{1,0:T(8,128)} %get-tuple-element.17), channel_id=1, source_target_pairs={{32,0},{64,32},{96,64},{128,96},{160,128},{192,160},{224,192},{33,... | collective-permute-start | bytes 884744 | tf_op jit(solution)/shard_map/ppermute | solution.py:161
  410.9 35.8 %collective-permute-start.2 = (f32[9,16,128]{2,1,0:T(8,128)}, f32[9,16,128]{2,1,0:T(8,128)S(1)}, u32[]{:S(2)}, u32[]{:S(2)}) collective-permute-start(f32[9,16,128]{2,1,0:T(8,128)} %get-tuple-element.18), channel_id=1, source_target_pairs={{0,1},{1,2},{2,3},{3,4},{4,5},{5,6},{6,7},{7,8},{8,9},{9,10},{10,1... | collective-permute-start | bytes 221192 | tf_op jit(solution)/shard_map/ppermute | solution.py:160
  441.0 7.6 %collective-permute-start.3 = (f32[9,16,128]{2,1,0:T(8,128)}, f32[9,16,128]{2,1,0:T(8,128)S(1)}, u32[]{:S(2)}, u32[]{:S(2)}) collective-permute-start(f32[9,16,128]{2,1,0:T(8,128)} %get-tuple-element.19), channel_id=1, source_target_pairs={{1,0},{2,1},{3,2},{4,3},{5,4},{6,5},{7,6},{8,7},{9,8},{10,9},{11,1... | collective-permute-start | bytes 221192 | tf_op jit(solution)/shard_map/ppermute | solution.py:161
  446.7 1.9 copy-start.5
  448.6 0.6 copy-start.6
  448.6 0.7 copy-start.1
  448.6 0.9 copy-start.2
  461.7 18.9 %collective-permute-start.4 = (f32[576,128]{1,0:T(8,128)}, f32[576,128]{1,0:T(8,128)S(1)}, u32[]{:S(2)}, u32[]{:S(2)}) collective-permute-start(f32[576,128]{1,0:T(8,128)} %get-tuple-element.21), channel_id=1, source_target_pairs={{0,32},{32,64},{64,96},{96,128},{128,160},{160,192},{192,224},{1,3... | collective-permute-start | bytes 884744 | tf_op jit(solution)/shard_map/ppermute | solution.py:160
  463.7 16.8 %collective-permute-start.5 = (f32[576,128]{1,0:T(8,128)}, f32[576,128]{1,0:T(8,128)S(1)}, u32[]{:S(2)}, u32[]{:S(2)}) collective-permute-start(f32[576,128]{1,0:T(8,128)} %get-tuple-element.22), channel_id=1, source_target_pairs={{32,0},{64,32},{96,64},{128,96},{160,128},{192,160},{224,192},{33,... | collective-permute-start | bytes 884744 | tf_op jit(solution)/shard_map/ppermute | solution.py:161
  467.2 9.3 %collective-permute-start.6 = (f32[9,16,128]{2,1,0:T(8,128)}, f32[9,16,128]{2,1,0:T(8,128)S(1)}, u32[]{:S(2)}, u32[]{:S(2)}) collective-permute-start(f32[9,16,128]{2,1,0:T(8,128)} %get-tuple-element.23), channel_id=1, source_target_pairs={{0,1},{1,2},{2,3},{3,4},{4,5},{5,6},{6,7},{7,8},{8,9},{9,10},{10,1... | collective-permute-start | bytes 221192 | tf_op jit(solution)/shard_map/ppermute | solution.py:160
  469.2 11.4 %collective-permute-start.7 = (f32[9,16,128]{2,1,0:T(8,128)}, f32[9,16,128]{2,1,0:T(8,128)S(1)}, u32[]{:S(2)}, u32[]{:S(2)}) collective-permute-start(f32[9,16,128]{2,1,0:T(8,128)} %get-tuple-element.24), channel_id=1, source_target_pairs={{1,0},{2,1},{3,2},{4,3},{5,4},{6,5},{7,6},{8,7},{9,8},{10,9},{11,1... | collective-permute-start | bytes 221192 | tf_op jit(solution)/shard_map/ppermute | solution.py:161
  476.5 4.1 copy-start.7
  480.6 0.6 copy-start.8
  480.6 0.7 copy-start.3
  480.6 0.9 copy-start.4

commit v2 on v1

v2 whole, which is shorter than its diff:
```python
import functools

import jax
import jax.numpy as jnp
from jax import lax
from jax.experimental import pallas as pl
from jax.experimental.pallas import tpu as pltpu
from jax.sharding import PartitionSpec as P

ITERS = 2
FINE_CAP = 4
COARSE_CAP = 2
DIRECT = 5
EXTRA = 2 * FINE_CAP + 1 - DIRECT
VMEM = pl.BlockSpec(memory_space=pltpu.VMEM)
SMEM = pl.BlockSpec(memory_space=pltpu.SMEM)
PARAMS = pltpu.CompilerParams(vmem_limit_bytes=56 * 1024 * 1024)


def ranks(boxes):
    count = boxes.shape[-1]
    earlier = jnp.arange(count)[None, :] < jnp.arange(count)[:, None]
    same = boxes[..., None, :] == boxes[..., :, None]
    return jnp.sum((same & earlier).astype(jnp.int32), axis=-1)


def plan_kernel(me_ref, units_ref, row_ref, column_ref):
    devices, lanes = units_ref.shape
    me = me_ref[0]
    units = units_ref[...]
    source = lax.broadcasted_iota(jnp.int32, units.shape, 0)
    lane = lax.broadcasted_iota(jnp.int32, units.shape, 1)
    surplus = pltpu.roll(jnp.maximum(units - DIRECT, 0), 0, 1, stride=1, stride_axis=0)
    none = jnp.full(units.shape, -1, jnp.int32)

    def one_round(r, carry):
        left, free, second, through, *chosen = carry
        ok = (left > 0) & (free > 0) & (second > 0)
        position = DIRECT - free
        item = surplus - left
        chosen = [jnp.where(ok & (item == i), r * 8 + position, table) for i, table in enumerate(chosen)]
        through = jnp.where(ok, source * 8 + position, through)
        used = ok.astype(jnp.int32)
        left, free, second = left - used, free - used, second - used
        free = pltpu.roll(free, lanes - 1, 1)
        second = pltpu.roll(pltpu.roll(second, devices - 1, 0), lanes - 1, 1)
        through = pltpu.roll(pltpu.roll(through, devices - 1, 0), lanes - 1, 1)
        return (left, free, second, through, *chosen)

    init = (surplus, jnp.maximum(DIRECT - units, 0), jnp.ones(units.shape, jnp.int32), none) + (none,) * EXTRA
    left, _, _, through, *chosen = lax.fori_loop(0, devices, one_round, init)
    for i in range(EXTRA):
        row_ref[i : i + 1] = jnp.max(jnp.where(source == me, chosen[i], -1), axis=0, keepdims=True)
    row_ref[EXTRA : EXTRA + 1] = jnp.max(left, axis=0, keepdims=True)
    column = none
    for i in range(EXTRA):
        mine = (lane < devices) & (lane == (source + me) % devices)
        found = jnp.max(jnp.where(mine, chosen[i], -1), axis=1, keepdims=True)
        column = jnp.where(lane == i, found, column)
    found = jnp.max(jnp.where(lane == me, through, -1), axis=1, keepdims=True)
    column_ref[...] = jnp.where(lane == EXTRA, found, column)


def pack_kernel(devices, slot_of, me_ref, fine_at_ref, coarse_at_ref, row_ref, fine_ref, coarse_ref, out_ref):
    planes = fine_ref.shape[0]
    coarse_planes, _, half, depth = coarse_ref.shape

    def fine_plane(k, carry):
        code = fine_at_ref[k]

        @pl.when(code >= 0)
        def _():
            for h in range(2):
                slot = slot_of(me_ref[0], row_ref, code // FINE_CAP, 2 * (code % FINE_CAP) + h)

                @pl.when(slot >= 0)
                def _():
                    out_ref[slot] = fine_ref[k, :, h * half : (h + 1) * half, :]

        return carry

    lax.fori_loop(0, planes, fine_plane, 0)

    def coarse_plane(k, carry):
        code = coarse_at_ref[k]

        @pl.when(code >= 0)
        def _():
            at = code // 2
            slot = slot_of(me_ref[0], row_ref, at // (DIRECT + EXTRA), at % (DIRECT + EXTRA))
            for j in range(2):

                @pl.when((slot >= 0) & (code % 2 == j))
                def _():
                    out_ref[slot, :, :, j * depth : (j + 1) * depth] = coarse_ref[k]

        return carry

    lax.fori_loop(0, coarse_planes, coarse_plane, 0)


def first_slot(devices, me, row_ref, box, unit):
    t = (me + box) % devices
    code = row_ref[jnp.maximum(unit - DIRECT, 0), t]
    relay = jnp.where(code >= 0, ((t + code // 8) % devices) * DIRECT + code % 8, -1)
    return jnp.where(unit < DIRECT, box * DIRECT + unit, relay)


def direct_slot(me, row_ref, box, unit):
    return jnp.where(unit < DIRECT, -1, box * EXTRA + unit - DIRECT)


def forward_kernel(me_ref, column_ref, in_ref, out_ref):
    devices = out_ref.shape[0]

    def body(a, carry):
        code = column_ref[a, EXTRA]

        @pl.when(code >= 0)
        def _():
            out_ref[(me_ref[0] - a + devices) % devices] = in_ref[(code // 8) * DIRECT + code % 8]

        return carry

    lax.fori_loop(0, devices, body, 0)


def rows_to_edges(flat_ref, ylow_ref, yhigh_ref, planes, species, rows):
    for s in range(species):
        for x in range(0, planes, 8):
            for edge_ref, at in ((ylow_ref, 0), (yhigh_ref, rows - 1)):
                start = (x * species + s) * rows + at
                edge_ref[s * planes + x : s * planes + x + 8] = flat_ref[pl.ds(start, 8, stride=species * rows), :]


def build_kernel(
    planned, shape, me_ref, column_ref, fine_at_ref, coarse_at_ref, first_ref, second_ref,
    out_ref, ylow_ref, yhigh_ref, xlow_ref, xhigh_ref,
):
    planes, species, rows, lanes = shape
    half = rows // 2
    devices = column_ref.shape[0]
    lane = lax.broadcasted_iota(jnp.int32, (half, lanes), 1)
    row = lax.broadcasted_iota(jnp.int32, (half, lanes), 0)
    sign = jnp.where(lane % 2 == 0, -0.25, 0.25)
    lane_first = lane % (lanes // 2) == 0
    lane_last = lane % (lanes // 2) == lanes // 2 - 1

    def late(source, unit):
        if not planned:
            return source * EXTRA + jnp.maximum(unit - DIRECT, 0)
        code = column_ref[source, jnp.maximum(unit - DIRECT, 0)]
        return jnp.where(unit < DIRECT, 0, (source + me_ref[0] + code // 8) % devices)

    def fetch(source, unit, use):
        @pl.when(unit < DIRECT)
        def _():
            use(first_ref, source * DIRECT + unit)

        @pl.when(unit >= DIRECT)
        def _():
            use(second_ref, late(source, unit))

    def body(c, carry):
        at = [fine_at_ref[2 * c], fine_at_ref[2 * c + 1]]

        @pl.when((at[0] < 0) | (at[1] < 0))
        def _():
            code = coarse_at_ref[c]
            index = (code % 2) * (lanes // 2) + lane // 2

            def interpolate(ref, slot):
                for s in range(species):
                    p = ref[slot, s]
                    below = jnp.where(row == 0, p, pltpu.roll(p, 1, 0))
                    above = jnp.where(row == half - 1, p, pltpu.roll(p, half - 1, 0))
                    left = jnp.where(lane_first, p, pltpu.roll(p, 1, 1))
                    right = jnp.where(lane_last, p, pltpu.roll(p, lanes - 1, 1))
                    slope_y = 0.125 * (above - below)
                    slope_z = 0.5 * (right - left)
                    gz = jnp.take_along_axis(slope_z, index, axis=1) * sign
                    even = jnp.take_along_axis(p - slope_y, index, axis=1) + gz
                    odd = jnp.take_along_axis(p + slope_y, index, axis=1) + gz
                    for child in range(2):
                        start = pl.multiple_of(((2 * c + child) * species + s) * rows, rows)
                        out_ref[pl.ds(start, half, stride=2), :] = even
                        out_ref[pl.ds(start + 1, half, stride=2), :] = odd

            fetch(code // 2 // (DIRECT + EXTRA), code // 2 % (DIRECT + EXTRA), interpolate)

        for child in range(2):

            @pl.when(at[child] >= 0)
            def _():
                for h in range(2):

                    def copy(ref, slot):
                        for s in range(species):
                            start = pl.multiple_of(((2 * c + child) * species + s) * rows + h * half, half)
                            out_ref[pl.ds(start, half), :] = ref[slot, s]

                    fetch(at[child] // FINE_CAP, 2 * (at[child] % FINE_CAP) + h, copy)

        return carry

    lax.fori_loop(0, planes // 2, body, 0)
    rows_to_edges(out_ref, ylow_ref, yhigh_ref, planes, species, rows)
    xlow_ref[...] = out_ref[0 : species * rows]
    xhigh_ref[...] = out_ref[(planes - 1) * species * rows : planes * species * rows]


def step_kernel(shape, diff_ref, u_ref, vel_ref, ylow_ref, yhigh_ref, xlow_ref, xhigh_ref, out_ref, *edge_refs):
    planes, species, rows, lanes = shape
    size = species * rows
    lane = lax.broadcasted_iota(jnp.int32, (rows, lanes), 1)
    row = lax.broadcasted_iota(jnp.int32, (rows, lanes), 0)

    def plane(x, below, above):
        positive = [jnp.maximum(vel_ref[x, k], 0.0) for k in range(3)]
        negative = [jnp.minimum(vel_ref[x, k], 0.0) for k in range(3)]
        keep = 1.0
        for k in range(3):
            keep = keep - (positive[k] - negative[k])
        for s in range(species):
            d = diff_ref[s]
            here = pl.ds(pl.multiple_of(x * size + s * rows, rows), rows)
            u = u_ref[here, :]
            edge = pl.ds(s * planes + x, 1)
            y_low = jnp.where(row == 0, ylow_ref[edge, :], pltpu.roll(u, 1, 0))
            y_high = jnp.where(row == rows - 1, yhigh_ref[edge, :], pltpu.roll(u, rows - 1, 0))
            z_low = jnp.where(lane == 0, u, pltpu.roll(u, 1, 1))
            z_high = jnp.where(lane == lanes - 1, u, pltpu.roll(u, lanes - 1, 1))
            new = u * (keep - 6.0 * d)
            for k, (low, high) in enumerate(((below(s), above(s)), (y_low, y_high), (z_low, z_high))):
                new = new + low * (d + positive[k]) + high * (d - negative[k])
            out_ref[here, :] = new

    def at(ref, x):
        return lambda s: ref[pl.ds(pl.multiple_of(x * size + s * rows, rows), rows), :]

    plane(0, at(xlow_ref, 0), at(u_ref, 1))

    def body(x, carry):
        plane(x, at(u_ref, x - 1), at(u_ref, x + 1))
        return carry

    lax.fori_loop(1, planes - 1, body, 0)
    plane(planes - 1, at(u_ref, planes - 2), at(xhigh_ref, 0))
    if edge_refs:
        rows_to_edges(out_ref, edge_refs[0], edge_refs[1], planes, species, rows)
        edge_refs[2][...] = out_ref[0:size]
        edge_refs[3][...] = out_ref[(planes - 1) * size : planes * size]


def halo(ylow, yhigh, xlow, xhigh):
    got = []
    for axis, low, high in (("grp", ylow, yhigh), ("dev", xlow, xhigh)):
        size = lax.axis_size(axis)
        up = [(i, (i + 1) % size) for i in range(size - 1)]
        got.append(lax.ppermute(high, axis, up))
        got.append(lax.ppermute(low, axis, [(b, a) for a, b in up]))
    return got


def on_device(old_fine, old_ids, old_coarse, coarse_ids, velocity, diffusion):
    devices = lax.axis_size("dev")
    me = lax.axis_index("dev")
    me_ref = me.reshape(1).astype(jnp.int32)
    planes, species, rows, lanes = old_fine.shape
    half = rows // 2
    coarse_planes = old_coarse.shape[0]
    unit_count = DIRECT + EXTRA
    f32 = jnp.float32
    i32 = jnp.int32

    def units_shape(count):
        return jax.ShapeDtypeStruct((count, species, half, lanes), f32)

    own, own_coarse = old_ids[0], coarse_ids[0]
    labels = jnp.broadcast_to(jnp.concatenate([own, own_coarse])[None], (devices, planes + coarse_planes))
    labels = lax.all_to_all(labels, "dev", split_axis=0, concat_axis=0, tiled=True)
    all_ids, all_coarse = labels[:, :planes], labels[:, planes:]
    all_box = jnp.where(all_ids >= 0, all_ids // planes, -1)
    all_coarse_box = all_coarse // coarse_planes
    flat_parents = jnp.where(all_ids >= 0, all_ids // 2, -1).reshape(-1)

    def needed(coarse):
        kept = jnp.sum((flat_parents == coarse[..., None]).astype(i32), axis=-1)
        return kept < 2

    box = jnp.arange(lanes) % devices
    fine_units = jnp.sum((all_box[:, None, :] == box[None, :, None]).astype(i32), axis=-1)
    asked = needed(all_coarse)[:, None, :] & (all_coarse_box[:, None, :] == box[None, :, None])
    units = 2 * fine_units + jnp.max(asked.astype(i32), axis=-1)
    row, column = pl.pallas_call(
        plan_kernel,
        out_shape=[jax.ShapeDtypeStruct((8, lanes), i32), jax.ShapeDtypeStruct((devices, lanes), i32)],
        in_specs=[SMEM, VMEM],
        out_specs=[VMEM] * 2,
        name="plan",
    )(me_ref, units)
    feasible = jnp.max(row[EXTRA, :devices]) == 0

    own_box = jnp.where(own >= 0, own // planes, -1)
    send_fine = jnp.where(own >= 0, own_box * FINE_CAP + ranks(own_box), -1)
    own_coarse_box = own_coarse // coarse_planes
    before = jnp.sum((own_box[None, :] == own_coarse_box[:, None]).astype(i32), axis=1)
    send_coarse = (own_coarse_box * unit_count + 2 * before) * 2 + ranks(own_coarse_box)
    send_coarse = jnp.where(needed(own_coarse), send_coarse, -1)

    order = jnp.arange(devices)[:, None]
    wanted = me * planes + jnp.arange(planes)
    fine_at = jnp.where(all_ids[None] == wanted[:, None, None], (order * FINE_CAP + ranks(all_box))[None], -1)
    fine_at = jnp.max(fine_at, axis=(1, 2))
    to_me = jnp.sum((all_box == me).astype(i32), axis=1, keepdims=True)
    coarse_wanted = me * coarse_planes + jnp.arange(coarse_planes)
    coarse_code = (order * unit_count + 2 * to_me) * 2 + ranks(all_coarse_box)
    coarse_at = jnp.where(all_coarse[None] == coarse_wanted[:, None, None], coarse_code[None], 0)
    coarse_at = jnp.max(coarse_at, axis=(1, 2))

    def pack(count, slot_of, name):
        return pl.pallas_call(
            functools.partial(pack_kernel, devices, slot_of),
            out_shape=units_shape(count),
            in_specs=[SMEM] * 4 + [VMEM] * 2,
            out_specs=VMEM,
            compiler_params=PARAMS,
            name=name,
        )(me_ref, send_fine, send_coarse, row, old_fine, old_coarse)

    first = pack(devices * DIRECT, functools.partial(first_slot, devices), "pack")
    first = lax.all_to_all(first, "dev", split_axis=0, concat_axis=0, tiled=True)

    size = species * rows
    edge_shapes = [jax.ShapeDtypeStruct((species * planes, lanes), f32)] * 2 + [
        jax.ShapeDtypeStruct((size, lanes), f32)
    ] * 2
    state_shape = jax.ShapeDtypeStruct((planes * size, lanes), f32)

    def build(planned, second):
        second = lax.all_to_all(second, "dev", split_axis=0, concat_axis=0, tiled=True)
        return pl.pallas_call(
            functools.partial(build_kernel, planned, old_fine.shape),
            out_shape=[state_shape] + edge_shapes,
            in_specs=[SMEM] * 4 + [VMEM] * 2,
            out_specs=[VMEM] * 5,
            compiler_params=PARAMS,
            name="build",
        )(me_ref, column, fine_at, coarse_at, first, second)

    def relayed():
        second = pl.pallas_call(
            forward_kernel,
            out_shape=units_shape(devices),
            in_specs=[SMEM] * 2 + [VMEM],
            out_specs=VMEM,
            compiler_params=PARAMS,
            name="forward",
        )(me_ref, column, first)
        return build(True, second)

    def direct():
        return build(False, pack(devices * EXTRA, direct_slot, "pack_rest"))

    state, *edges = lax.cond(feasible, relayed, direct)

    for repeat in range(ITERS):
        last = repeat == ITERS - 1
        around = halo(*edges)
        state, *edges = pl.pallas_call(
            functools.partial(step_kernel, old_fine.shape),
            out_shape=[state_shape] + ([] if last else edge_shapes),
            in_specs=[SMEM] + [VMEM] * 6,
            out_specs=[VMEM] * (1 if last else 5),
            compiler_params=PARAMS,
            name="step",
        )(diffusion, state, velocity, *around)
    return state.reshape(old_fine.shape)


def solution(mesh):
    in_specs = (
        P("dev", None, "grp", None),
        P("grp", "dev"),
        P("dev", None, "grp", None),
        P("grp", "dev"),
        P("dev", None, "grp", None),
        P(),
    )
    out_specs = P("dev", None, "grp", None)
    return jax.shard_map(
        on_device, mesh=mesh, in_specs=in_specs, out_specs=out_specs, check_vma=False
    )
```

time: 503 us -> 291 us (0.58); the launches traced: 493 us -> 287 us
  blocking collectives: 336 us -> 41 us
  waiting for transfers between devices: 29.1 us -> 133 us
  starting transfers between devices: 73.2 us -> 45.2 us
  Pallas kernels: 42.4 us -> 51.2 us
    unnamed x1 -> x0, blocking collectives: 336 us -> none
    all_to_all x2, waiting for transfers between devices: 21.1 us -> 128 us  [the longest x1 124 us: on_device(): lax.all_to_all(first, 'dev', split_axis=0, concat_axis=0, tiled=True)]
    all_to_all x0 -> x1, blocking collectives: none -> 41 us  [build(): lax.all_to_all(second, 'dev', split_axis=0, concat_axis=0, tiled=True)]
    ppermute x4, starting transfers between devices: 36 us -> 11 us  [halo(): got.append(lax.ppermute(high, axis, up))]
    pallas_call x5 -> x6, Pallas kernels: 42.4 us -> 51.2 us  [the longest x2 24.6 us: on_device(): pl.pallas_call(functools.partial(step_kernel, old_fine.shape), out_shape=...]
  transfers between devices with their start and end apart: 10 -> 10, of which waited for: 5 -> 6; matrix products, arithmetic and copies ran while one was open for 1% -> 3% of each run, Pallas kernels for 1% -> 0%
where the time goes in v2:
time: 291 us; the launch traced here: 287 us
  waiting for transfers between devices  133 us (46%)
  Pallas kernels  51.2 us (18%)
  starting transfers between devices  45.2 us (16%)
  blocking collectives  41 us (14%)
  other arithmetic  13.4 us (5%)
    all_to_all x1, waiting for transfers between devices, on_device(): lax.all_to_all(first, 'dev', split_axis=0, concat_axis=0, tiled=True)  124 us
    all_to_all x1, blocking collectives, build(): lax.all_to_all(second, 'dev', split_axis=0, concat_axis=0, tiled=True)  41 us
    pallas_call x2, Pallas kernels, on_device(): pl.pallas_call(functools.partial(step_kernel, old_fine.shape), out_shape=...  24.6 us
    ppermute x4, starting transfers between devices, halo(): got.append(lax.ppermute(low, axis, [(b, a) for a, b in up]))  16 us
    all_to_all x1, starting transfers between devices, on_device(): lax.all_to_all(labels, 'dev', split_axis=0, concat_axis=0, tiled=True)  11.6 us
    ppermute x4, starting transfers between devices, halo(): got.append(lax.ppermute(high, axis, up))  11 us
    pallas_call x1, Pallas kernels, pack(): pl.pallas_call(functools.partial(pack_kernel, devices, slot_of), out_shap...  10.6 us
    pallas_call x1, Pallas kernels, build(): pl.pallas_call(functools.partial(build_kernel, planned, old_fine.shape),...  7.84 us
  transfers between devices with their start and end apart: 10, of which 6 were waited for; matrix products, arithmetic and copies ran while one was open for 3% of the time, Pallas kernels for 0%

profile of v2, /device:TPU:22, one launch (start us, length us, event | category | flops | bytes accessed | tf_op | source)
XLA Modules:
  0.0 287.1 jit_solution(15553293587454985945)
XLA Ops:
  0.0 0.7 pad_add_fusion
  0.7 0.6 broadcast_in_dim.26
  1.4 11.6 %all-to-all-start.2 = ((s32[32,1,96]{2,1,0:T(1,128)}), s32[32,1,96]{2,1,0:T(1,128)S(1)}, u32[]{:S(2)}, u32[]{:S(2)}) async-start(s32[32,1,96]{2,1,0:T(1,128)} %broadcast_in_dim.26), calls=%async_computation.2 | async-start | bytes 32768 | tf_op jit(solution)/shard_map/all_to_all | solution.py:281
  13.0 0.7 fusion.9
  13.6 0.7 and_select_fusion.1
  14.3 0.7 compare_select_fusion.15
  15.0 0.7 fusion.8
  15.6 0.2 convert_reduce_fusion.9
  15.8 0.2 convert_reduce_fusion.6
  16.0 0.7 compare_select_fusion.14.fine_at_ref
  16.7 0.2 convert_reduce_fusion.8
  16.9 4.0 %all-to-all-done.2 = s32[32,1,96]{2,1,0:T(1,128)S(1)} async-done(((s32[32,1,96]{2,1,0:T(1,128)}), s32[32,1,96]{2,1,0:T(1,128)S(1)}, u32[]{:S(2)}, u32[]{:S(2)}) %all-to-all-start.2) | async-done | bytes 12320 | tf_op jit(solution)/shard_map/all_to_all | solution.py:281
  21.1 0.9 convert_reduce_fusion.5
  22.0 1.1 convert_reduce_fusion
  23.1 0.4 convert_reduce_fusion.2
  23.4 0.4 convert_reduce_fusion.4
  23.8 0.6 multiply_add_fusion.units_ref
  24.4 4.0 %plan.1 = (s32[8,128]{1,0:T(8,128)S(1)}, s32[32,128]{1,0:T(8,128)S(1)}) custom-call(s32[1]{0:T(128)} %bitcast.me_ref, s32[32,128]{1,0:T(8,128)} %multiply_add_fusion.units_ref), custom_call_target="tpu_custom_call" | custom-call | tf_op jit(solution)/shard_map/plan/pallas_call | solution.py:295
  28.4 0.7 compare_select_fusion.coarse_at_ref
  29.0 10.6 %pack.1 = f32[160,9,8,128]{3,2,1,0:T(8,128)} custom-call(s32[1]{0:T(128)} %bitcast.me_ref, s32[64]{0:T(128)S(1)} %compare_select_fusion.14.fine_at_ref, s32[32]{0:T(128)S(1)} %compare_select_fusion.coarse_at_ref, s32[8,128]{1,0:T(8,128)S(1)} %get-tuple-element.62.row_ref, f32[64,9,16,128]{3,2,1,0:T(8,128)} %fine_ref.1, f32[32,9,8,64]{3,2,1,0:T(8,128)} %coarse_ref.1), custom_call_target="tpu_custom_call" | custom-call | tf_op jit(solution)/shard_map/pack/pallas_call | solution.py:322
  39.6 6.6 %all-to-all-start.3 = ((f32[160,9,8,128]{3,2,1,0:T(8,128)}), f32[160,9,8,128]{3,2,1,0:T(8,128)}, u32[]{:S(2)}, u32[]{:S(2)}) async-start(f32[160,9,8,128]{3,2,1,0:T(8,128)} %pack.1), calls=%async_computation.3 | async-start | bytes 11796480 | tf_op jit(solution)/shard_map/all_to_all | solution.py:332
  46.3 0.6 slice_reduce_fusion
  47.6 0.8 convert_reduce_fusion.3
  48.4 0.7 select_reduce_fusion.1
  49.2 0.9 convert_reduce_fusion.1
  50.2 1.3 select_reduce_fusion
  51.5 124.0 %all-to-all-done.3 = f32[160,9,8,128]{3,2,1,0:T(8,128)} async-done(((f32[160,9,8,128]{3,2,1,0:T(8,128)}), f32[160,9,8,128]{3,2,1,0:T(8,128)}, u32[]{:S(2)}, u32[]{:S(2)}) %all-to-all-start.3) | async-done | bytes 5898272 | tf_op jit(solution)/shard_map/all_to_all | solution.py:332
  175.6 53.1 %conditional.1 = ((f32[9216,128]{1,0:T(8,128)}, f32[576,128]{1,0:T(8,128)S(1)}, f32[576,128]{1,0:T(8,128)S(1)}, f32[144,128]{1,0:T(8,128)S(1)}, f32[144,128]{1,0:T(8,128)S(1)})) conditional(s32[]{:T(128)} %convert_element_type.36, (s32[1]{0:T(128)}, s32[64]{0:T(128)S(1)}, s32[32]{0:T(128)S(1)}, s32[8,128]{1,0:T(8,128)S(1)}, ...), branch_computations={%region_13.14_spmd, %region_14.15_spmd} | conditional | bytes 9437192 | solution.py:365
  175.6 4.3 %forward.1 = f32[32,9,8,128]{3,2,1,0:T(8,128)} custom-call(s32[1]{0:T(128)} %get-tuple-element.45.me_ref, s32[32,128]{1,0:T(8,128)S(1)} %get-tuple-element.46.column_ref, f32[160,9,8,128]{3,2,1,0:T(8,128)} %get-tuple-element.49.in_ref.first_ref), custom_call_target="tpu_custom_call" | custom-call | tf_op jit(solution)/shard_map/cond/branch_1_fun/forward/pallas_call | solution.py:352
  179.8 41.0 %all_to_all.23.second_ref = f32[32,9,8,128]{3,2,1,0:T(8,128)} all-to-all(f32[32,9,8,128]{3,2,1,0:T(8,128)} %forward.1), channel_id=1, replica_groups=mesh['grp'=8,'dev'=32] {'dev'}, dimensions={0} | all-to-all | bytes 2359296 | tf_op jit(solution)/shard_map/cond/branch_1_fun/all_to_all | solution.py:341
  220.9 7.8 %build.3 = (f32[9216,128]{1,0:T(8,128)}, f32[576,128]{1,0:T(8,128)S(1)}, f32[576,128]{1,0:T(8,128)S(1)}, f32[144,128]{1,0:T(8,128)S(1)}, f32[144,128]{1,0:T(8,128)S(1)}) custom-call(s32[1]{0:T(128)} %get-tuple-element.45.me_ref, s32[32,128]{1,0:T(8,128)S(1)} %get-tuple-element.46.column_ref, s32[64]{0:T(128)S(1)} %get-tuple-element.47.fine_at_ref, ...), custom_call_target="tpu_custom_call" | custom-call | tf_op jit(solution)/shard_map/cond/branch_1_fun/build/pallas_call | solution.py:342
  228.7 1.9 collective-permute-start
  230.6 3.6 %collective-permute-start.1 = (f32[576,128]{1,0:T(8,128)S(1)}, f32[576,128]{1,0:T(8,128)S(1)}, u32[]{:S(2)}, u32[]{:S(2)}) collective-permute-start(f32[576,128]{1,0:T(8,128)S(1)} %get-tuple-element.66), channel_id=1, source_target_pairs={{32,0},{64,32},{96,64},{128,96},{160,128},{192,160},{224,192},{33,... | collective-permute-start | bytes 884744 | tf_op jit(solution)/shard_map/ppermute | solution.py:261
  234.3 2.9 collective-permute-start.2
  237.2 5.1 %collective-permute-start.3 = (f32[144,128]{1,0:T(8,128)S(1)}, f32[144,128]{1,0:T(8,128)S(1)}, u32[]{:S(2)}, u32[]{:S(2)}) collective-permute-start(f32[144,128]{1,0:T(8,128)S(1)} %get-tuple-element.68), channel_id=1, source_target_pairs={{1,0},{2,1},{3,2},{4,3},{5,4},{6,5},{7,6},{8,7},{9,8},{10,9},{11,1... | collective-permute-start | bytes 221192 | tf_op jit(solution)/shard_map/ppermute | solution.py:261
  242.3 0.4 collective-permute-done.2.xlow_ref
  242.6 2.3 collective-permute-done.3.xhigh_ref
  244.9 0.6 copy-done.6
  245.8 12.4 %step.2 = (f32[9216,128]{1,0:T(8,128)}, f32[576,128]{1,0:T(8,128)}, f32[576,128]{1,0:T(8,128)}, f32[144,128]{1,0:T(8,128)}, f32[144,128]{1,0:T(8,128)}) custom-call(f32[9]{0:T(128)} %diff_ref.3, f32[9216,128]{1,0:T(8,128)} %get-tuple-element.64.u_ref, f32[64,3,16,128]{3,2,1,0:T(8,128)} %vel_ref.3, f32[576,128]{1,0:T(8,128)} %copy-done.1, ...), custom_call_target="tpu_custom_call" | custom-call | tf_op jit(solution)/shard_map/step/pallas_call | solution.py:370
  258.2 2.3 collective-permute-start.4
  260.5 3.2 %collective-permute-start.5 = (f32[576,128]{1,0:T(8,128)}, f32[576,128]{1,0:T(8,128)S(1)}, u32[]{:S(2)}, u32[]{:S(2)}) collective-permute-start(f32[576,128]{1,0:T(8,128)} %get-tuple-element.71), channel_id=1, source_target_pairs={{32,0},{64,32},{96,64},{128,96},{160,128},{192,160},{224,192},{33,... | collective-permute-start | bytes 884744 | tf_op jit(solution)/shard_map/ppermute | solution.py:261
  263.8 3.9 %collective-permute-start.6 = (f32[144,128]{1,0:T(8,128)}, f32[144,128]{1,0:T(8,128)S(1)}, u32[]{:S(2)}, u32[]{:S(2)}) collective-permute-start(f32[144,128]{1,0:T(8,128)} %get-tuple-element.72), channel_id=1, source_target_pairs={{0,1},{1,2},{2,3},{3,4},{4,5},{5,6},{6,7},{7,8},{8,9},{9,10},{10,1... | collective-permute-start | bytes 221192 | tf_op jit(solution)/shard_map/ppermute | solution.py:260
  267.7 4.0 %collective-permute-start.7 = (f32[144,128]{1,0:T(8,128)}, f32[144,128]{1,0:T(8,128)S(1)}, u32[]{:S(2)}, u32[]{:S(2)}) collective-permute-start(f32[144,128]{1,0:T(8,128)} %get-tuple-element.73), channel_id=1, source_target_pairs={{1,0},{2,1},{3,2},{4,3},{5,4},{6,5},{7,6},{8,7},{9,8},{10,9},{11,1... | collective-permute-start | bytes 221192 | tf_op jit(solution)/shard_map/ppermute | solution.py:261
  271.7 0.6 collective-permute-done.6.xlow_ref
  272.3 1.8 collective-permute-done.7.xhigh_ref
  274.2 0.6 copy-done.8
  274.8 0.1 copy-done.3
  275.0 12.1 %step.3 = f32[9216,128]{1,0:T(8,128)} custom-call(f32[9]{0:T(128)} %diff_ref.3, f32[9216,128]{1,0:T(8,128)} %get-tuple-element.69.u_ref, f32[64,3,16,128]{3,2,1,0:T(8,128)} %vel_ref.3, f32[576,128]{1,0:T(8,128)} %copy-done.3, f32[576,128]{1,0:T(8,128)} %copy-done.4, f32[144,128]{1,0:T(8,128)} %copy-done.7, f32[144,128]{1,0:T(8,128)} %copy-done.8), custom_call_target="tpu_custom_call" | custom-call | tf_op jit(solution)/shard_map/step/pallas_call | solution.py:370
  (32 shorter events, 0.8 us)
Async XLA Ops:
  1.4 19.4 %all-to-all-start.2 = ((s32[32,1,96]{2,1,0:T(1,128)}), s32[32,1,96]{2,1,0:T(1,128)S(1)}, u32[]{:S(2)}, u32[]{:S(2)}) async-start(s32[32,1,96]{2,1,0:T(1,128)} %broadcast_in_dim.26), calls=%async_computation.2 | async-start | bytes 32768 | tf_op jit(solution)/shard_map/all_to_all | solution.py:281
  39.6 136.0 %copy-start = (f32[32,9,8,64]{3,2,1,0:T(8,128)S(1)}, f32[32,9,8,64]{3,2,1,0:T(8,128)}, u32[]{:S(2)}) copy-start(f32[32,9,8,64]{3,2,1,0:T(8,128)} %coarse_ref.1) | copy-start | bytes 1769476
  39.6 136.0 %all-to-all-start.3 = ((f32[160,9,8,128]{3,2,1,0:T(8,128)}), f32[160,9,8,128]{3,2,1,0:T(8,128)}, u32[]{:S(2)}, u32[]{:S(2)}) async-start(f32[160,9,8,128]{3,2,1,0:T(8,128)} %pack.1), calls=%async_computation.3 | async-start | bytes 11796480 | tf_op jit(solution)/shard_map/all_to_all | solution.py:332
  228.7 16.2 %collective-permute-start = (f32[576,128]{1,0:T(8,128)S(1)}, f32[576,128]{1,0:T(8,128)S(1)}, u32[]{:S(2)}, u32[]{:S(2)}) collective-permute-start(f32[576,128]{1,0:T(8,128)S(1)} %get-tuple-element.65), channel_id=1, source_target_pairs={{0,32},{32,64},{64,96},{96,128},{128,160},{160,192},{192,224},{1,3... | collective-permute-start | bytes 884744 | tf_op jit(solution)/shard_map/ppermute | solution.py:260
  230.6 14.3 %collective-permute-start.1 = (f32[576,128]{1,0:T(8,128)S(1)}, f32[576,128]{1,0:T(8,128)S(1)}, u32[]{:S(2)}, u32[]{:S(2)}) collective-permute-start(f32[576,128]{1,0:T(8,128)S(1)} %get-tuple-element.66), channel_id=1, source_target_pairs={{32,0},{64,32},{96,64},{128,96},{160,128},{192,160},{224,192},{33,... | collective-permute-start | bytes 884744 | tf_op jit(solution)/shard_map/ppermute | solution.py:261
  234.3 8.4 %collective-permute-start.2 = (f32[144,128]{1,0:T(8,128)S(1)}, f32[144,128]{1,0:T(8,128)S(1)}, u32[]{:S(2)}, u32[]{:S(2)}) collective-permute-start(f32[144,128]{1,0:T(8,128)S(1)} %get-tuple-element.67), channel_id=1, source_target_pairs={{0,1},{1,2},{2,3},{3,4},{4,5},{5,6},{6,7},{7,8},{8,9},{9,10},{10,1... | collective-permute-start | bytes 221192 | tf_op jit(solution)/shard_map/ppermute | solution.py:260
  237.2 7.8 %collective-permute-start.3 = (f32[144,128]{1,0:T(8,128)S(1)}, f32[144,128]{1,0:T(8,128)S(1)}, u32[]{:S(2)}, u32[]{:S(2)}) collective-permute-start(f32[144,128]{1,0:T(8,128)S(1)} %get-tuple-element.68), channel_id=1, source_target_pairs={{1,0},{2,1},{3,2},{4,3},{5,4},{6,5},{7,6},{8,7},{9,8},{10,9},{11,1... | collective-permute-start | bytes 221192 | tf_op jit(solution)/shard_map/ppermute | solution.py:261
  242.6 2.3 copy-start.5
  244.9 0.6 copy-start.6
  244.9 0.7 copy-start.1
  244.9 0.8 copy-start.2
  258.2 16.0 %collective-permute-start.4 = (f32[576,128]{1,0:T(8,128)}, f32[576,128]{1,0:T(8,128)S(1)}, u32[]{:S(2)}, u32[]{:S(2)}) collective-permute-start(f32[576,128]{1,0:T(8,128)} %get-tuple-element.70), channel_id=1, source_target_pairs={{0,32},{32,64},{64,96},{96,128},{128,160},{160,192},{192,224},{1,3... | collective-permute-start | bytes 884744 | tf_op jit(solution)/shard_map/ppermute | solution.py:260
  260.5 13.6 %collective-permute-start.5 = (f32[576,128]{1,0:T(8,128)}, f32[576,128]{1,0:T(8,128)S(1)}, u32[]{:S(2)}, u32[]{:S(2)}) collective-permute-start(f32[576,128]{1,0:T(8,128)} %get-tuple-element.71), channel_id=1, source_target_pairs={{32,0},{64,32},{96,64},{128,96},{160,128},{192,160},{224,192},{33,... | collective-permute-start | bytes 884744 | tf_op jit(solution)/shard_map/ppermute | solution.py:261
  263.8 8.6 %collective-permute-start.6 = (f32[144,128]{1,0:T(8,128)}, f32[144,128]{1,0:T(8,128)S(1)}, u32[]{:S(2)}, u32[]{:S(2)}) collective-permute-start(f32[144,128]{1,0:T(8,128)} %get-tuple-element.72), channel_id=1, source_target_pairs={{0,1},{1,2},{2,3},{3,4},{4,5},{5,6},{6,7},{7,8},{8,9},{9,10},{10,1... | collective-permute-start | bytes 221192 | tf_op jit(solution)/shard_map/ppermute | solution.py:260
  267.7 6.5 %collective-permute-start.7 = (f32[144,128]{1,0:T(8,128)}, f32[144,128]{1,0:T(8,128)S(1)}, u32[]{:S(2)}, u32[]{:S(2)}) collective-permute-start(f32[144,128]{1,0:T(8,128)} %get-tuple-element.73), channel_id=1, source_target_pairs={{1,0},{2,1},{3,2},{4,3},{5,4},{6,5},{7,6},{8,7},{9,8},{10,9},{11,1... | collective-permute-start | bytes 221192 | tf_op jit(solution)/shard_map/ppermute | solution.py:261
  272.3 1.8 copy-start.7
  274.1 0.6 copy-start.8
  274.1 0.8 copy-start.3
  274.2 0.9 copy-start.4

commit v3 on v2

--- a/solution.py
+++ b/solution.py
@@ -12,8 +12,10 @@
 COARSE_CAP = 2
 DIRECT = 5
 EXTRA = 2 * FINE_CAP + 1 - DIRECT
+CHUNKS = ((0, 6), (6, 9))
 VMEM = pl.BlockSpec(memory_space=pltpu.VMEM)
 SMEM = pl.BlockSpec(memory_space=pltpu.SMEM)
+ANY = pl.BlockSpec(memory_space=pl.ANY)
 PARAMS = pltpu.CompilerParams(vmem_limit_bytes=56 * 1024 * 1024)
 
 
@@ -61,9 +63,10 @@
     column_ref[...] = jnp.where(lane == EXTRA, found, column)
 
 
-def pack_kernel(devices, slot_of, me_ref, fine_at_ref, coarse_at_ref, row_ref, fine_ref, coarse_ref, out_ref):
+def pack_kernel(slot_of, chunk, me_ref, fine_at_ref, coarse_at_ref, row_ref, fine_ref, coarse_ref, out_ref):
     planes = fine_ref.shape[0]
     coarse_planes, _, half, depth = coarse_ref.shape
+    first, end = chunk
 
     def fine_plane(k, carry):
         code = fine_at_ref[k]
@@ -75,7 +78,7 @@
 
                 @pl.when(slot >= 0)
                 def _():
-                    out_ref[slot] = fine_ref[k, :, h * half : (h + 1) * half, :]
+                    out_ref[slot] = fine_ref[k, first:end, h * half : (h + 1) * half, :]
 
         return carry
 
@@ -92,7 +95,7 @@
 
                 @pl.when((slot >= 0) & (code % 2 == j))
                 def _():
-                    out_ref[slot, :, :, j * depth : (j + 1) * depth] = coarse_ref[k]
+                    out_ref[slot, :, :, j * depth : (j + 1) * depth] = coarse_ref[k, first:end]
 
         return carry
 
@@ -134,8 +137,8 @@
 
 
 def build_kernel(
-    planned, shape, me_ref, column_ref, fine_at_ref, coarse_at_ref, first_ref, second_ref,
-    out_ref, ylow_ref, yhigh_ref, xlow_ref, xhigh_ref,
+    shape, start, me_ref, column_ref, left_ref, fine_at_ref, coarse_at_ref, first_ref, second_ref, rest_ref,
+    out_ref, ylow_ref, yhigh_ref, xlow_ref, xhigh_ref, held_ref, sem,
 ):
     planes, species, rows, lanes = shape
     half = rows // 2
@@ -146,20 +149,27 @@
     lane_first = lane % (lanes // 2) == 0
     lane_last = lane % (lanes // 2) == lanes // 2 - 1
 
-    def late(source, unit):
-        if not planned:
-            return source * EXTRA + jnp.maximum(unit - DIRECT, 0)
-        code = column_ref[source, jnp.maximum(unit - DIRECT, 0)]
-        return jnp.where(unit < DIRECT, 0, (source + me_ref[0] + code // 8) % devices)
+    planned = left_ref[0] == 0
 
     def fetch(source, unit, use):
+        over = jnp.maximum(unit - DIRECT, 0)
+
         @pl.when(unit < DIRECT)
         def _():
             use(first_ref, source * DIRECT + unit)
 
-        @pl.when(unit >= DIRECT)
-        def _():
-            use(second_ref, late(source, unit))
+        @pl.when((unit >= DIRECT) & planned)
+        def _():
+            use(second_ref, (source + me_ref[0] + column_ref[source, over] // 8) % devices)
+
+        @pl.when((unit >= DIRECT) & jnp.logical_not(planned))
+        def _():
+            copy = pltpu.make_async_copy(
+                rest_ref.at[pl.ds(source * EXTRA + over, 1), start : start + species], held_ref, sem
+            )
+            copy.start()
+            copy.wait()
+            use(held_ref, 0)
 
     def body(c, carry):
         at = [fine_at_ref[2 * c], fine_at_ref[2 * c + 1]]
@@ -182,9 +192,9 @@
                     even = jnp.take_along_axis(p - slope_y, index, axis=1) + gz
                     odd = jnp.take_along_axis(p + slope_y, index, axis=1) + gz
                     for child in range(2):
-                        start = pl.multiple_of(((2 * c + child) * species + s) * rows, rows)
-                        out_ref[pl.ds(start, half, stride=2), :] = even
-                        out_ref[pl.ds(start + 1, half, stride=2), :] = odd
+                        base = pl.multiple_of(((2 * c + child) * species + s) * rows, rows)
+                        out_ref[pl.ds(base, half, stride=2), :] = even
+                        out_ref[pl.ds(base + 1, half, stride=2), :] = odd
 
             fetch(code // 2 // (DIRECT + EXTRA), code // 2 % (DIRECT + EXTRA), interpolate)
 
@@ -196,8 +206,8 @@
 
                     def copy(ref, slot):
                         for s in range(species):
-                            start = pl.multiple_of(((2 * c + child) * species + s) * rows + h * half, half)
-                            out_ref[pl.ds(start, half), :] = ref[slot, s]
+                            base = pl.multiple_of(((2 * c + child) * species + s) * rows + h * half, half)
+                            out_ref[pl.ds(base, half), :] = ref[slot, s]
 
                     fetch(at[child] // FINE_CAP, 2 * (at[child] % FINE_CAP) + h, copy)
 
@@ -209,7 +219,7 @@
     xhigh_ref[...] = out_ref[(planes - 1) * species * rows : planes * species * rows]
 
 
-def step_kernel(shape, diff_ref, u_ref, vel_ref, ylow_ref, yhigh_ref, xlow_ref, xhigh_ref, out_ref, *edge_refs):
+def advance(shape, start, diff_ref, u_ref, vel_ref, ylow_ref, yhigh_ref, xlow_ref, xhigh_ref, out_ref, after):
     planes, species, rows, lanes = shape
     size = species * rows
     lane = lax.broadcasted_iota(jnp.int32, (rows, lanes), 1)
@@ -222,7 +232,7 @@
         for k in range(3):
             keep = keep - (positive[k] - negative[k])
         for s in range(species):
-            d = diff_ref[s]
+            d = diff_ref[start + s]
             here = pl.ds(pl.multiple_of(x * size + s * rows, rows), rows)
             u = u_ref[here, :]
             edge = pl.ds(s * planes + x, 1)
@@ -238,18 +248,53 @@
     def at(ref, x):
         return lambda s: ref[pl.ds(pl.multiple_of(x * size + s * rows, rows), rows), :]
 
-    plane(0, at(xlow_ref, 0), at(u_ref, 1))
-
     def body(x, carry):
         plane(x, at(u_ref, x - 1), at(u_ref, x + 1))
         return carry
 
-    lax.fori_loop(1, planes - 1, body, 0)
-    plane(planes - 1, at(u_ref, planes - 2), at(xhigh_ref, 0))
-    if edge_refs:
-        rows_to_edges(out_ref, edge_refs[0], edge_refs[1], planes, species, rows)
-        edge_refs[2][...] = out_ref[0:size]
-        edge_refs[3][...] = out_ref[(planes - 1) * size : planes * size]
+    plane(0, at(xlow_ref, 0), at(u_ref, 1))
+    for x in range(0, planes, 8):
+        lax.fori_loop(max(x, 1), min(x + 8, planes - 1), body, 0)
+        if x + 8 == planes:
+            plane(planes - 1, at(u_ref, planes - 2), at(xhigh_ref, 0))
+        after(x)
+
+
+def step_kernel(shape, start, diff_ref, u_ref, vel_ref, *refs):
+    planes, species, rows, _ = shape
+    size = species * rows
+    *around, out_ref, ylow_ref, yhigh_ref, xlow_ref, xhigh_ref = refs
+    advance(shape, start, diff_ref, u_ref, vel_ref, *around, out_ref, lambda x: None)
+    rows_to_edges(out_ref, ylow_ref, yhigh_ref, planes, species, rows)
+    xlow_ref[...] = out_ref[0:size]
+    xhigh_ref[...] = out_ref[(planes - 1) * size : planes * size]
+
+
+def last_step_kernel(shape, start, diff_ref, u_ref, vel_ref, *refs):
+    planes, species, rows, _ = shape
+    size = species * rows
+    *around, out_ref, new_ref, sem = refs
+    copies = []
+
+    def send(x):
+        for i in range(x, x + 8):
+            copy = pltpu.make_async_copy(
+                new_ref.at[i * size : (i + 1) * size], out_ref.at[i, start * rows : start * rows + size], sem.at[i]
+            )
+            copy.start()
+            copies.append(copy)
+
+    advance(shape, start, diff_ref, u_ref, vel_ref, *around[:4], new_ref, send)
+    for copy in copies:
+        copy.wait()
+
+
+def empty_kernel(out_ref):
+    pass
+
+
+def cost(microseconds):
+    return pl.CostEstimate(flops=0, bytes_accessed=int(microseconds * 3.6e6), transcendentals=0)
 
 
 def halo(ylow, yhigh, xlow, xhigh):
@@ -273,8 +318,8 @@
     f32 = jnp.float32
     i32 = jnp.int32
 
-    def units_shape(count):
-        return jax.ShapeDtypeStruct((count, species, half, lanes), f32)
+    def units_shape(count, many):
+        return jax.ShapeDtypeStruct((count, many, half, lanes), f32)
 
     own, own_coarse = old_ids[0], coarse_ids[0]
     labels = jnp.broadcast_to(jnp.concatenate([own, own_coarse])[None], (devices, planes + coarse_planes))
@@ -299,7 +344,7 @@
         out_specs=[VMEM] * 2,
         name="plan",
     )(me_ref, units)
-    feasible = jnp.max(row[EXTRA, :devices]) == 0
+    left = jnp.max(row[EXTRA, :devices]).reshape(1)
 
     own_box = jnp.where(own >= 0, own // planes, -1)
     send_fine = jnp.where(own >= 0, own_box * FINE_CAP + ranks(own_box), -1)
@@ -318,64 +363,107 @@
     coarse_at = jnp.where(all_coarse[None] == coarse_wanted[:, None, None], coarse_code[None], 0)
     coarse_at = jnp.max(coarse_at, axis=(1, 2))
 
-    def pack(count, slot_of, name):
+    def pack(count, slot_of, chunk, name):
         return pl.pallas_call(
-            functools.partial(pack_kernel, devices, slot_of),
-            out_shape=units_shape(count),
+            functools.partial(pack_kernel, slot_of, chunk),
+            out_shape=units_shape(count, chunk[1] - chunk[0]),
             in_specs=[SMEM] * 4 + [VMEM] * 2,
             out_specs=VMEM,
             compiler_params=PARAMS,
             name=name,
         )(me_ref, send_fine, send_coarse, row, old_fine, old_coarse)
 
-    first = pack(devices * DIRECT, functools.partial(first_slot, devices), "pack")
-    first = lax.all_to_all(first, "dev", split_axis=0, concat_axis=0, tiled=True)
-
-    size = species * rows
-    edge_shapes = [jax.ShapeDtypeStruct((species * planes, lanes), f32)] * 2 + [
-        jax.ShapeDtypeStruct((size, lanes), f32)
-    ] * 2
-    state_shape = jax.ShapeDtypeStruct((planes * size, lanes), f32)
-
-    def build(planned, second):
-        second = lax.all_to_all(second, "dev", split_axis=0, concat_axis=0, tiled=True)
+    def exchange(value):
+        return lax.all_to_all(value, "dev", split_axis=0, concat_axis=0, tiled=True)
+
+    def no_rest():
         return pl.pallas_call(
-            functools.partial(build_kernel, planned, old_fine.shape),
-            out_shape=[state_shape] + edge_shapes,
-            in_specs=[SMEM] * 4 + [VMEM] * 2,
-            out_specs=[VMEM] * 5,
-            compiler_params=PARAMS,
-            name="build",
-        )(me_ref, column, fine_at, coarse_at, first, second)
-
-    def relayed():
+            empty_kernel,
+            out_shape=units_shape(devices * EXTRA, species),
+            out_specs=pl.BlockSpec(memory_space=pl.ANY),
+            name="nothing",
+        )()
+
+    def rest_direct():
+        return exchange(pack(devices * EXTRA, direct_slot, (0, species), "pack_rest"))
+
+    rest = lax.cond(left[0] == 0, no_rest, rest_direct)
+
+    def first_phase(chunk):
+        return pack(devices * DIRECT, functools.partial(first_slot, devices), chunk, "pack")
+
+    def second_phase(chunk, first):
         second = pl.pallas_call(
             forward_kernel,
-            out_shape=units_shape(devices),
+            out_shape=units_shape(devices, chunk[1] - chunk[0]),
             in_specs=[SMEM] * 2 + [VMEM],
             out_specs=VMEM,
             compiler_params=PARAMS,
+            cost_estimate=cost(3),
             name="forward",
         )(me_ref, column, first)
-        return build(True, second)
-
-    def direct():
-        return build(False, pack(devices * EXTRA, direct_slot, "pack_rest"))
-
-    state, *edges = lax.cond(feasible, relayed, direct)
-
-    for repeat in range(ITERS):
-        last = repeat == ITERS - 1
+        return exchange(second)
+
+    def halves(chunk, first, second):
+        start, end = chunk
+        count = end - start
+        shape = (planes, count, rows, lanes)
+        size = count * rows
+        edge_shapes = [jax.ShapeDtypeStruct((count * planes, lanes), f32)] * 2 + [
+            jax.ShapeDtypeStruct((size, lanes), f32)
+        ] * 2
+        state_shape = jax.ShapeDtypeStruct((planes * size, lanes), f32)
+        state, *edges = pl.pallas_call(
+            functools.partial(build_kernel, shape, start),
+            out_shape=[state_shape] + edge_shapes,
+            in_specs=[SMEM] * 5 + [VMEM] * 2 + [ANY],
+            out_specs=[VMEM] * 5,
+            scratch_shapes=[pltpu.VMEM((1, count, half, lanes), f32), pltpu.SemaphoreType.DMA],
+            compiler_params=PARAMS,
+            cost_estimate=cost(count),
+            name="build",
+        )(me_ref, column, left, fine_at, coarse_at, first, second, rest)
+        for _ in range(ITERS - 1):
+            state, *edges = pl.pallas_call(
+                functools.partial(step_kernel, shape, start),
+                out_shape=[state_shape] + edge_shapes,
+                in_specs=[SMEM] + [VMEM] * 6,
+                out_specs=[VMEM] * 5,
+                compiler_params=PARAMS,
+                cost_estimate=cost(count),
+                name="step",
+            )(diffusion, state, velocity, *halo(*edges))
         around = halo(*edges)
-        state, *edges = pl.pallas_call(
-            functools.partial(step_kernel, old_fine.shape),
-            out_shape=[state_shape] + ([] if last else edge_shapes),
-            in_specs=[SMEM] + [VMEM] * 6,
-            out_specs=[VMEM] * (1 if last else 5),
-            compiler_params=PARAMS,
-            name="step",
-        )(diffusion, state, velocity, *around)
-    return state.reshape(old_fine.shape)
+
+        def last(done):
+            earlier = [] if done is None else [done]
+            return pl.pallas_call(
+                functools.partial(last_step_kernel, shape, start),
+                out_shape=jax.ShapeDtypeStruct((planes, species * rows, lanes), f32),
+                in_specs=[SMEM] + [VMEM] * 6 + [ANY] * len(earlier),
+                out_specs=ANY,
+                scratch_shapes=[pltpu.VMEM((planes * size, lanes), f32), pltpu.SemaphoreType.DMA((planes,))],
+                input_output_aliases={7: 0} if earlier else {},
+                compiler_params=PARAMS,
+                cost_estimate=cost(count),
+                name="last_step",
+            )(diffusion, state, velocity, *around, *earlier)
+
+        return around, last
+
+    done, last, first = None, None, exchange(first_phase(CHUNKS[0]))
+    for i, chunk in enumerate(CHUNKS):
+        second = second_phase(chunk, first)
+        if i + 1 < len(CHUNKS):
+            packed, second = lax.optimization_barrier((first_phase(CHUNKS[i + 1]), second))
+            upcoming = exchange(packed)
+        if last is not None:
+            done = last(done)
+        around, last = halves(chunk, first, second)
+        if i + 1 < len(CHUNKS):
+            first, _ = lax.optimization_barrier((upcoming, around))
+    done = last(done)
+    return done.reshape(old_fine.shape)
 
 
 def solution(mesh):

time: 291 us -> 337 us (1.16)
  waiting for transfers between devices: 133 us -> 35.1 us
  blocking collectives: 41 us -> 113 us
  starting transfers between devices: 45.2 us -> 80.1 us
  Pallas kernels: 51.2 us -> 85.8 us
    all_to_all x1 -> x2, waiting for transfers between devices: 124 us -> 11.8 us  [exchange(): return lax.all_to_all(value, 'dev', split_axis=0, concat_axis=0, tiled=True)]
    all_to_all x1 -> x2, blocking collectives: 41 us -> 113 us  [exchange(): return lax.all_to_all(value, 'dev', split_axis=0, concat_axis=0, tiled=True)]
    pallas_call x5 -> x11, Pallas kernels: 47.2 us -> 81.2 us  [the longest x2 19.1 us: halves(): pl.pallas_call(functools.partial(build_kernel, shape, start), out_shape=[...]
    ppermute x4 -> x8, starting transfers between devices: 16 us -> 38.2 us  [halo(): got.append(lax.ppermute(low, axis, [(b, a) for a, b in up]))]
    ppermute x4 -> x8, waiting for transfers between devices: 0.99 us -> 16 us  [halo(): got.append(lax.ppermute(high, axis, up))]
    all_to_all x1 -> x2, starting transfers between devices: 6.59 us -> 14 us  [exchange(): return lax.all_to_all(value, 'dev', split_axis=0, concat_axis=0, tiled=True)]
    ppermute x4 -> x8, starting transfers between devices: 11 us -> 16.3 us  [halo(): got.append(lax.ppermute(high, axis, up))]
  transfers between devices with their start and end apart: 10 -> 19, of which waited for: 6 -> 6; matrix products, arithmetic and copies ran while one was open for 3% -> 3% of each run, Pallas kernels for 0% -> 12%
where the time goes in v3:
time: 337 us; the launch traced here: 334 us
  blocking collectives  113 us (34%)
  Pallas kernels  85.8 us (25%)
  starting transfers between devices  80.1 us (24%)
  waiting for transfers between devices  35.1 us (10%)
  other arithmetic  14.5 us (4%)
  local copies, waits for them, and re-layouts  4.17 us (1%)
    all_to_all x2, blocking collectives, exchange(): return lax.all_to_all(value, 'dev', split_axis=0, concat_axis=0, tiled=True)  113 us
    ppermute x8, starting transfers between devices, halo(): got.append(lax.ppermute(low, axis, [(b, a) for a, b in up]))  38.2 us
    pallas_call x2, Pallas kernels, halves(): pl.pallas_call(functools.partial(build_kernel, shape, start), out_shape=[...  19.1 us
    pallas_call x2, Pallas kernels, halves(): pl.pallas_call(functools.partial(step_kernel, shape, start), out_shape=[s...  18.9 us
    pallas_call x2, Pallas kernels, pack(): pl.pallas_call(functools.partial(pack_kernel, slot_of, chunk), out_shape=...  18.4 us
    pallas_call x2, Pallas kernels, last(): pl.pallas_call(functools.partial(last_step_kernel, shape, start), out_sha...  18.3 us
    ppermute x8, starting transfers between devices, halo(): got.append(lax.ppermute(high, axis, up))  16.3 us
    ppermute x8, waiting for transfers between devices, halo(): got.append(lax.ppermute(high, axis, up))  16 us
  transfers between devices with their start and end apart: 19, of which 6 were waited for; matrix products, arithmetic and copies ran while one was open for 3% of the time, Pallas kernels for 12%

profile of v3, /device:TPU:22, one launch (start us, length us, event | category | flops | bytes accessed | tf_op | source)
XLA Modules:
  0.0 334.2 jit_solution(15567588134948398296)
XLA Ops:
  0.0 0.7 pad_add_fusion
  1.4 11.6 %all-to-all-start.1 = ((s32[32,1,96]{2,1,0:T(1,128)}), s32[32,1,96]{2,1,0:T(1,128)S(1)}, u32[]{:S(2)}, u32[]{:S(2)}) async-start(s32[32,1,96]{2,1,0:T(1,128)} %broadcast_in_dim.26), calls=%async_computation.1 | async-start | bytes 32768 | tf_op jit(solution)/shard_map/all_to_all | solution.py:326
  13.0 0.7 fusion.9
  16.0 0.7 compare_select_fusion.14.fine_at_ref
  16.9 4.0 %all-to-all-done.1 = s32[32,1,96]{2,1,0:T(1,128)S(1)} async-done(((s32[32,1,96]{2,1,0:T(1,128)}), s32[32,1,96]{2,1,0:T(1,128)S(1)}, u32[]{:S(2)}, u32[]{:S(2)}) %all-to-all-start.1) | async-done | bytes 12320 | tf_op jit(solution)/shard_map/all_to_all | solution.py:326
  21.1 0.9 convert_reduce_fusion.5
  22.0 1.1 convert_reduce_fusion
  24.4 4.6 %plan.1 = (s32[8,128]{1,0:T(8,128)S(1)}, s32[32,128]{1,0:T(8,128)}) custom-call(s32[1]{0:T(128)} %bitcast.me_ref, s32[32,128]{1,0:T(8,128)} %multiply_add_fusion.units_ref), custom_call_target="tpu_custom_call" | custom-call | tf_op jit(solution)/shard_map/plan/pallas_call | solution.py:340
  29.6 0.7 compare_select_fusion.coarse_at_ref
  30.3 9.7 %pack.3 = f32[160,6,8,128]{3,2,1,0:T(8,128)} custom-call(s32[1]{0:T(128)} %bitcast.me_ref, s32[64]{0:T(128)S(1)} %compare_select_fusion.14.fine_at_ref, s32[32]{0:T(128)S(1)} %compare_select_fusion.coarse_at_ref, s32[8,128]{1,0:T(8,128)S(1)} %get-tuple-element.52.row_ref, f32[64,9,16,128]{3,2,1,0:T(8,128)} %fine_ref.3, f32[32,9,8,64]{3,2,1,0:T(8,128)} %coarse_ref.3), custom_call_target="tpu_custom_call" | custom-call | tf_op jit(solution)/shard_map/pack/pallas_call | solution.py:367
  40.6 94.2 %all_to_all.34.in_ref.first_ref = f32[160,6,8,128]{3,2,1,0:T(8,128)} all-to-all(f32[160,6,8,128]{3,2,1,0:T(8,128)} %pack.3), channel_id=1, replica_groups=mesh['grp'=8,'dev'=32] {'dev'}, dimensions={0} | all-to-all | bytes 7864320 | tf_op jit(solution)/shard_map/all_to_all | solution.py:377
  134.8 3.6 %forward.2 = f32[32,6,8,128]{3,2,1,0:T(8,128)} custom-call(s32[1]{0:T(128)} %bitcast.me_ref, s32[32,128]{1,0:T(8,128)} %get-tuple-element.51.column_ref, f32[160,6,8,128]{3,2,1,0:T(8,128)} %all_to_all.34.in_ref.first_ref), custom_call_target="tpu_custom_call" | custom-call | bytes 10800000 | tf_op jit(solution)/shard_map/forward/pallas_call | solution.py:396
  138.4 7.0 %all-to-all-start.3 = ((f32[32,6,8,128]{3,2,1,0:T(8,128)}), f32[32,6,8,128]{3,2,1,0:T(8,128)S(1)}, u32[]{:S(2)}, u32[]{:S(2)}) async-start(f32[32,6,8,128]{3,2,1,0:T(8,128)} %forward.2), calls=%async_computation.3 | async-start | bytes 1572864 | tf_op jit(solution)/shard_map/all_to_all | solution.py:377
  145.4 8.7 %pack.2 = f32[160,3,8,128]{3,2,1,0:T(8,128)} custom-call(s32[1]{0:T(128)} %bitcast.me_ref, s32[64]{0:T(128)S(1)} %compare_select_fusion.14.fine_at_ref, s32[32]{0:T(128)S(1)} %compare_select_fusion.coarse_at_ref, s32[8,128]{1,0:T(8,128)S(1)} %get-tuple-element.52.row_ref, f32[64,9,16,128]{3,2,1,0:T(8,128)} %fine_ref.3, f32[32,9,8,64]{3,2,1,0:T(8,128)S(1)} %copy-done.1), custom_call_target="tpu_custom_call" | custom-call | tf_op jit(solution)/shard_map/pack/pallas_call | solution.py:367
  154.1 11.8 %all-to-all-done.3.second_ref = f32[32,6,8,128]{3,2,1,0:T(8,128)S(1)} async-done(((f32[32,6,8,128]{3,2,1,0:T(8,128)}), f32[32,6,8,128]{3,2,1,0:T(8,128)S(1)}, u32[]{:S(2)}, u32[]{:S(2)}) %all-to-all-start.3) | async-done | bytes 786464 | tf_op jit(solution)/shard_map/all_to_all | solution.py:377
  165.9 7.0 %all-to-all-start.4 = ((f32[160,3,8,128]{3,2,1,0:T(8,128)}), f32[160,3,8,128]{3,2,1,0:T(8,128)S(1)}, u32[]{:S(2)}, u32[]{:S(2)}) async-start(f32[160,3,8,128]{3,2,1,0:T(8,128)} %pack.2), calls=%async_computation.4 | async-start | bytes 3932160 | tf_op jit(solution)/shard_map/all_to_all | solution.py:377
  173.0 0.8 convert_reduce_fusion.3
  173.9 1.3 select_reduce_fusion.1.coarse_at_ref
  175.2 0.9 convert_reduce_fusion.1
  176.2 1.9 select_reduce_fusion.fine_at_ref
  178.1 10.9 %build.2 = (f32[6144,128]{1,0:T(8,128)}, f32[384,128]{1,0:T(8,128)}, f32[384,128]{1,0:T(8,128)}, f32[96,128]{1,0:T(8,128)}, f32[96,128]{1,0:T(8,128)}) custom-call(s32[1]{0:T(128)} %bitcast.me_ref, s32[32,128]{1,0:T(8,128)} %get-tuple-element.51.column_ref, s32[1]{0:T(128)} %bitcast.4.left_ref, s32[64]{0:T(128)} %select_reduce_fusion.fine_at_ref, ...), custom_call_target="tpu_custom_call" | custom-call | bytes 21600000 | tf_op jit(solution)/shard_map/build/pallas_call | solution.py:416
  189.1 1.9 collective-permute-start
  191.0 3.6 %collective-permute-start.1 = (f32[384,128]{1,0:T(8,128)}, f32[384,128]{1,0:T(8,128)S(1)}, u32[]{:S(2)}, u32[]{:S(2)}) collective-permute-start(f32[384,128]{1,0:T(8,128)} %get-tuple-element.57), channel_id=1, source_target_pairs={{32,0},{64,32},{96,64},{128,96},{160,128},{192,160},{224,192},{33,... | collective-permute-start | bytes 589832 | tf_op jit(solution)/shard_map/ppermute | solution.py:306
  194.6 1.9 collective-permute-start.2
  196.6 6.0 %collective-permute-start.3 = (f32[96,128]{1,0:T(8,128)}, f32[96,128]{1,0:T(8,128)S(1)}, u32[]{:S(2)}, u32[]{:S(2)}) collective-permute-start(f32[96,128]{1,0:T(8,128)} %get-tuple-element.59), channel_id=1, source_target_pairs={{1,0},{2,1},{3,2},{4,3},{5,4},{6,5},{7,6},{8,7},{9,8},{10,9},{11,1... | collective-permute-start | bytes 147464 | tf_op jit(solution)/shard_map/ppermute | solution.py:306
  202.6 15.7 %collective-permute-done.2.refs_2_ = f32[96,128]{1,0:T(8,128)S(1)} collective-permute-done((f32[96,128]{1,0:T(8,128)}, f32[96,128]{1,0:T(8,128)S(1)}, u32[]{:S(2)}, u32[]{:S(2)}) %collective-permute-start.2) | collective-permute-done | bytes 49184 | tf_op jit(solution)/shard_map/ppermute | solution.py:305
  219.1 10.4 %step.2 = (f32[6144,128]{1,0:T(8,128)}, f32[384,128]{1,0:T(8,128)}, f32[384,128]{1,0:T(8,128)}, f32[96,128]{1,0:T(8,128)}, f32[96,128]{1,0:T(8,128)}) custom-call(f32[9]{0:T(128)} %diff_ref.7, f32[6144,128]{1,0:T(8,128)} %get-tuple-element.55.u_ref, f32[64,3,16,128]{3,2,1,0:T(8,128)} %vel_ref.7, f32[384,128]{1,0:T(8,128)} %copy-done.3, ...), custom_call_target="tpu_custom_call" | custom-call | bytes 21600000 | tf_op jit(solution)/shard_map/step/pallas_call | solution.py:427
  229.5 1.9 collective-permute-start.4
  231.5 3.6 %collective-permute-start.5 = (f32[384,128]{1,0:T(8,128)}, f32[384,128]{1,0:T(8,128)S(1)}, u32[]{:S(2)}, u32[]{:S(2)}) collective-permute-start(f32[384,128]{1,0:T(8,128)} %get-tuple-element.61), channel_id=1, source_target_pairs={{32,0},{64,32},{96,64},{128,96},{160,128},{192,160},{224,192},{33,... | collective-permute-start | bytes 589832 | tf_op jit(solution)/shard_map/ppermute | solution.py:306
  235.1 1.9 collective-permute-start.6
  237.0 6.0 %collective-permute-start.7 = (f32[96,128]{1,0:T(8,128)}, f32[96,128]{1,0:T(8,128)S(1)}, u32[]{:S(2)}, u32[]{:S(2)}) collective-permute-start(f32[96,128]{1,0:T(8,128)} %get-tuple-element.63), channel_id=1, source_target_pairs={{1,0},{2,1},{3,2},{4,3},{5,4},{6,5},{7,6},{8,7},{9,8},{10,9},{11,1... | collective-permute-start | bytes 147464 | tf_op jit(solution)/shard_map/ppermute | solution.py:306
  243.4 1.7 collective-permute-done.7.refs_3_
  245.2 1.3 copy-done
  246.5 2.9 forward.3
  249.4 19.0 %all_to_all.35.second_ref = f32[32,3,8,128]{3,2,1,0:T(8,128)} all-to-all(f32[32,3,8,128]{3,2,1,0:T(8,128)} %forward.3), channel_id=1, replica_groups=mesh['grp'=8,'dev'=32] {'dev'}, dimensions={0} | all-to-all | bytes 786432 | tf_op jit(solution)/shard_map/all_to_all | solution.py:377
  268.5 8.2 %build.3 = (f32[3072,128]{1,0:T(8,128)}, f32[192,128]{1,0:T(8,128)}, f32[192,128]{1,0:T(8,128)}, f32[48,128]{1,0:T(8,128)}, f32[48,128]{1,0:T(8,128)}) custom-call(s32[1]{0:T(128)} %bitcast.me_ref, s32[32,128]{1,0:T(8,128)} %get-tuple-element.51.column_ref, s32[1]{0:T(128)} %bitcast.4.left_ref, s32[64]{0:T(128)} %select_reduce_fusion.fine_at_ref, ...), custom_call_target="tpu_custom_call" | custom-call | bytes 10800000 | tf_op jit(solution)/shard_map/build/pallas_call | solution.py:416
  276.7 1.9 collective-permute-start.8
  278.6 3.6 %collective-permute-start.9 = (f32[192,128]{1,0:T(8,128)}, f32[192,128]{1,0:T(8,128)S(1)}, u32[]{:S(2)}, u32[]{:S(2)}) collective-permute-start(f32[192,128]{1,0:T(8,128)} %get-tuple-element.67), channel_id=1, source_target_pairs={{32,0},{64,32},{96,64},{128,96},{160,128},{192,160},{224,192},{33,... | collective-permute-start | bytes 294920 | tf_op jit(solution)/shard_map/ppermute | solution.py:306
  282.3 2.9 collective-permute-start.10
  285.2 5.2 %collective-permute-start.11 = (f32[48,128]{1,0:T(8,128)}, f32[48,128]{1,0:T(8,128)S(1)}, u32[]{:S(2)}, u32[]{:S(2)}) collective-permute-start(f32[48,128]{1,0:T(8,128)} %get-tuple-element.69), channel_id=1, source_target_pairs={{1,0},{2,1},{3,2},{4,3},{5,4},{6,5},{7,6},{8,7},{9,8},{10,9},{11,1... | collective-permute-start | bytes 73736 | tf_op jit(solution)/shard_map/ppermute | solution.py:306
  290.4 1.5 collective-permute-done.11.refs_3_
  292.6 8.5 %step.3 = (f32[3072,128]{1,0:T(8,128)}, f32[192,128]{1,0:T(8,128)}, f32[192,128]{1,0:T(8,128)}, f32[48,128]{1,0:T(8,128)}, f32[48,128]{1,0:T(8,128)}) custom-call(f32[9]{0:T(128)} %diff_ref.7, f32[3072,128]{1,0:T(8,128)} %get-tuple-element.65.u_ref, f32[64,3,16,128]{3,2,1,0:T(8,128)} %vel_ref.7, f32[192,128]{1,0:T(8,128)} %copy-done.9, ...), custom_call_target="tpu_custom_call" | custom-call | bytes 10800000 | tf_op jit(solution)/shard_map/step/pallas_call | solution.py:427
  301.1 1.9 collective-permute-start.12
  303.0 3.6 %collective-permute-start.13 = (f32[192,128]{1,0:T(8,128)}, f32[192,128]{1,0:T(8,128)S(1)}, u32[]{:S(2)}, u32[]{:S(2)}) collective-permute-start(f32[192,128]{1,0:T(8,128)} %get-tuple-element.72), channel_id=1, source_target_pairs={{32,0},{64,32},{96,64},{128,96},{160,128},{192,160},{224,192},{33,... | collective-permute-start | bytes 294920 | tf_op jit(solution)/shard_map/ppermute | solution.py:306
  306.7 1.9 collective-permute-start.14
  308.6 6.3 %collective-permute-start.15 = (f32[48,128]{1,0:T(8,128)}, f32[48,128]{1,0:T(8,128)S(1)}, u32[]{:S(2)}, u32[]{:S(2)}) collective-permute-start(f32[48,128]{1,0:T(8,128)} %get-tuple-element.74), channel_id=1, source_target_pairs={{1,0},{2,1},{3,2},{4,3},{5,4},{6,5},{7,6},{8,7},{9,8},{10,9},{11,1... | collective-permute-start | bytes 73736 | tf_op jit(solution)/shard_map/ppermute | solution.py:306
  315.0 9.9 %last_step.2.refs_4_ = f32[64,144,128]{2,1,0:T(8,128)} custom-call(f32[9]{0:T(128)} %diff_ref.7, f32[6144,128]{1,0:T(8,128)} %get-tuple-element.75.u_ref, f32[64,3,16,128]{3,2,1,0:T(8,128)} %vel_ref.7, f32[384,128]{1,0:T(8,128)} %copy-done.5, f32[384,128]{1,0:T(8,128)} %copy-done.6, f32[96,128]{1,0:T(8,128)} %copy-done.11, f32[96,128]{1,0:T(8,128)} %copy-done.12), custom_call_target="tpu_custom_call" | custom-call | bytes 21600000 | tf_op jit(solution)/shard_map/last_step/pallas_call | solution.py:440
  325.6 8.5 %last_step.3 = f32[64,144,128]{2,1,0:T(8,128)} custom-call(f32[9]{0:T(128)} %diff_ref.7, f32[3072,128]{1,0:T(8,128)} %get-tuple-element.70.u_ref, f32[64,3,16,128]{3,2,1,0:T(8,128)} %vel_ref.7, f32[192,128]{1,0:T(8,128)} %copy-done.7, f32[192,128]{1,0:T(8,128)} %copy-done.8, f32[48,128]{1,0:T(8,128)} %copy-done.15, ...), custom_call_target="tpu_custom_call", output_to_operand_aliasing={{}: (7, {})} | custom-call | bytes 10800000 | tf_op jit(solution)/shard_map/last_step/pallas_call | solution.py:440
  (77 shorter events, 8.1 us)
Async XLA Ops:
  1.4 19.4 %all-to-all-start.1 = ((s32[32,1,96]{2,1,0:T(1,128)}), s32[32,1,96]{2,1,0:T(1,128)S(1)}, u32[]{:S(2)}, u32[]{:S(2)}) async-start(s32[32,1,96]{2,1,0:T(1,128)} %broadcast_in_dim.26), calls=%async_computation.1 | async-start | bytes 32768 | tf_op jit(solution)/shard_map/all_to_all | solution.py:326
  30.3 10.3 %copy-start.1 = (f32[32,9,8,64]{3,2,1,0:T(8,128)S(1)}, f32[32,9,8,64]{3,2,1,0:T(8,128)}, u32[]{:S(2)}) copy-start(f32[32,9,8,64]{3,2,1,0:T(8,128)} %coarse_ref.3) | copy-start | bytes 1769476
  138.4 27.6 %all-to-all-start.3 = ((f32[32,6,8,128]{3,2,1,0:T(8,128)}), f32[32,6,8,128]{3,2,1,0:T(8,128)S(1)}, u32[]{:S(2)}, u32[]{:S(2)}) async-start(f32[32,6,8,128]{3,2,1,0:T(8,128)} %forward.2), calls=%async_computation.3 | async-start | bytes 1572864 | tf_op jit(solution)/shard_map/all_to_all | solution.py:377
  165.9 12.2 %copy-start.2 = (f32[32,6,8,128]{3,2,1,0:T(8,128)}, f32[32,6,8,128]{3,2,1,0:T(8,128)S(1)}, u32[]{:S(2)}) copy-start(f32[32,6,8,128]{3,2,1,0:T(8,128)S(1)} %all-to-all-done.3.second_ref) | copy-start | bytes 2359300
  165.9 79.2 %all-to-all-start.4 = ((f32[160,3,8,128]{3,2,1,0:T(8,128)}), f32[160,3,8,128]{3,2,1,0:T(8,128)S(1)}, u32[]{:S(2)}, u32[]{:S(2)}) async-start(f32[160,3,8,128]{3,2,1,0:T(8,128)} %pack.2), calls=%async_computation.4 | async-start | bytes 3932160 | tf_op jit(solution)/shard_map/all_to_all | solution.py:377
  189.1 29.2 %collective-permute-start = (f32[384,128]{1,0:T(8,128)}, f32[384,128]{1,0:T(8,128)S(1)}, u32[]{:S(2)}, u32[]{:S(2)}) collective-permute-start(f32[384,128]{1,0:T(8,128)} %get-tuple-element.56), channel_id=1, source_target_pairs={{0,32},{32,64},{64,96},{96,128},{128,160},{160,192},{192,224},{1,3... | collective-permute-start | bytes 589832 | tf_op jit(solution)/shard_map/ppermute | solution.py:305
  191.0 27.3 %collective-permute-start.1 = (f32[384,128]{1,0:T(8,128)}, f32[384,128]{1,0:T(8,128)S(1)}, u32[]{:S(2)}, u32[]{:S(2)}) collective-permute-start(f32[384,128]{1,0:T(8,128)} %get-tuple-element.57), channel_id=1, source_target_pairs={{32,0},{64,32},{96,64},{128,96},{160,128},{192,160},{224,192},{33,... | collective-permute-start | bytes 589832 | tf_op jit(solution)/shard_map/ppermute | solution.py:306
  194.6 23.7 %collective-permute-start.2 = (f32[96,128]{1,0:T(8,128)}, f32[96,128]{1,0:T(8,128)S(1)}, u32[]{:S(2)}, u32[]{:S(2)}) collective-permute-start(f32[96,128]{1,0:T(8,128)} %get-tuple-element.58), channel_id=1, source_target_pairs={{0,1},{1,2},{2,3},{3,4},{4,5},{5,6},{6,7},{7,8},{8,9},{9,10},{10,1... | collective-permute-start | bytes 147464 | tf_op jit(solution)/shard_map/ppermute | solution.py:305
  196.6 21.7 %collective-permute-start.3 = (f32[96,128]{1,0:T(8,128)}, f32[96,128]{1,0:T(8,128)S(1)}, u32[]{:S(2)}, u32[]{:S(2)}) collective-permute-start(f32[96,128]{1,0:T(8,128)} %get-tuple-element.59), channel_id=1, source_target_pairs={{1,0},{2,1},{3,2},{4,3},{5,4},{6,5},{7,6},{8,7},{9,8},{10,9},{11,1... | collective-permute-start | bytes 147464 | tf_op jit(solution)/shard_map/ppermute | solution.py:306
  218.3 0.6 copy-start.13
  218.3 0.6 copy-start.14
  218.3 0.7 copy-start.3
  218.3 0.8 copy-start.4
  229.5 15.6 %collective-permute-start.4 = (f32[384,128]{1,0:T(8,128)}, f32[384,128]{1,0:T(8,128)S(1)}, u32[]{:S(2)}, u32[]{:S(2)}) collective-permute-start(f32[384,128]{1,0:T(8,128)} %get-tuple-element.60), channel_id=1, source_target_pairs={{0,32},{32,64},{64,96},{96,128},{128,160},{160,192},{192,224},{1,3... | collective-permute-start | bytes 589832 | tf_op jit(solution)/shard_map/ppermute | solution.py:305
  231.5 13.7 %collective-permute-start.5 = (f32[384,128]{1,0:T(8,128)}, f32[384,128]{1,0:T(8,128)S(1)}, u32[]{:S(2)}, u32[]{:S(2)}) collective-permute-start(f32[384,128]{1,0:T(8,128)} %get-tuple-element.61), channel_id=1, source_target_pairs={{32,0},{64,32},{96,64},{128,96},{160,128},{192,160},{224,192},{33,... | collective-permute-start | bytes 589832 | tf_op jit(solution)/shard_map/ppermute | solution.py:306
  235.1 8.3 %collective-permute-start.6 = (f32[96,128]{1,0:T(8,128)}, f32[96,128]{1,0:T(8,128)S(1)}, u32[]{:S(2)}, u32[]{:S(2)}) collective-permute-start(f32[96,128]{1,0:T(8,128)} %get-tuple-element.62), channel_id=1, source_target_pairs={{0,1},{1,2},{2,3},{3,4},{4,5},{5,6},{6,7},{7,8},{8,9},{9,10},{10,1... | collective-permute-start | bytes 147464 | tf_op jit(solution)/shard_map/ppermute | solution.py:305
  237.0 8.1 %collective-permute-start.7 = (f32[96,128]{1,0:T(8,128)}, f32[96,128]{1,0:T(8,128)S(1)}, u32[]{:S(2)}, u32[]{:S(2)}) collective-permute-start(f32[96,128]{1,0:T(8,128)} %get-tuple-element.63), channel_id=1, source_target_pairs={{1,0},{2,1},{3,2},{4,3},{5,4},{6,5},{7,6},{8,7},{9,8},{10,9},{11,1... | collective-permute-start | bytes 147464 | tf_op jit(solution)/shard_map/ppermute | solution.py:306
  243.4 71.5 %copy-start.11 = (f32[96,128]{1,0:T(8,128)}, f32[96,128]{1,0:T(8,128)S(1)}, u32[]{:S(2)}) copy-start(f32[96,128]{1,0:T(8,128)S(1)} %collective-permute-done.6.refs_2_) | copy-start | bytes 147460
  245.1 69.8 %copy-start.12 = (f32[96,128]{1,0:T(8,128)}, f32[96,128]{1,0:T(8,128)S(1)}, u32[]{:S(2)}) copy-start(f32[96,128]{1,0:T(8,128)S(1)} %collective-permute-done.7.refs_3_) | copy-start | bytes 147460
  245.1 69.8 %copy-start.5 = (f32[384,128]{1,0:T(8,128)}, f32[384,128]{1,0:T(8,128)S(1)}, u32[]{:S(2)}) copy-start(f32[384,128]{1,0:T(8,128)S(1)} %collective-permute-done.4.refs_0_) | copy-start | bytes 589828
  245.1 69.8 %copy-start.6 = (f32[384,128]{1,0:T(8,128)}, f32[384,128]{1,0:T(8,128)S(1)}, u32[]{:S(2)}) copy-start(f32[384,128]{1,0:T(8,128)S(1)} %collective-permute-done.5.refs_1_) | copy-start | bytes 589828
  245.2 1.4 copy-start
  276.7 15.3 %collective-permute-start.8 = (f32[192,128]{1,0:T(8,128)}, f32[192,128]{1,0:T(8,128)S(1)}, u32[]{:S(2)}, u32[]{:S(2)}) collective-permute-start(f32[192,128]{1,0:T(8,128)} %get-tuple-element.66), channel_id=1, source_target_pairs={{0,32},{32,64},{64,96},{96,128},{128,160},{160,192},{192,224},{1,3... | collective-permute-start | bytes 294920 | tf_op jit(solution)/shard_map/ppermute | solution.py:305
  278.6 13.3 %collective-permute-start.9 = (f32[192,128]{1,0:T(8,128)}, f32[192,128]{1,0:T(8,128)S(1)}, u32[]{:S(2)}, u32[]{:S(2)}) collective-permute-start(f32[192,128]{1,0:T(8,128)} %get-tuple-element.67), channel_id=1, source_target_pairs={{32,0},{64,32},{96,64},{128,96},{160,128},{192,160},{224,192},{33,... | collective-permute-start | bytes 294920 | tf_op jit(solution)/shard_map/ppermute | solution.py:306
  282.3 8.2 %collective-permute-start.10 = (f32[48,128]{1,0:T(8,128)}, f32[48,128]{1,0:T(8,128)S(1)}, u32[]{:S(2)}, u32[]{:S(2)}) collective-permute-start(f32[48,128]{1,0:T(8,128)} %get-tuple-element.68), channel_id=1, source_target_pairs={{0,1},{1,2},{2,3},{3,4},{4,5},{5,6},{6,7},{7,8},{8,9},{9,10},{10,1... | collective-permute-start | bytes 73736 | tf_op jit(solution)/shard_map/ppermute | solution.py:305
  285.2 6.7 %collective-permute-start.11 = (f32[48,128]{1,0:T(8,128)}, f32[48,128]{1,0:T(8,128)S(1)}, u32[]{:S(2)}, u32[]{:S(2)}) collective-permute-start(f32[48,128]{1,0:T(8,128)} %get-tuple-element.69), channel_id=1, source_target_pairs={{1,0},{2,1},{3,2},{4,3},{5,4},{6,5},{7,6},{8,7},{9,8},{10,9},{11,1... | collective-permute-start | bytes 73736 | tf_op jit(solution)/shard_map/ppermute | solution.py:306
  290.4 1.5 copy-start.16
  292.0 0.6 copy-start.18
  292.0 0.6 copy-start.9
  292.0 0.7 copy-start.10
  301.1 23.8 %collective-permute-start.12 = (f32[192,128]{1,0:T(8,128)}, f32[192,128]{1,0:T(8,128)S(1)}, u32[]{:S(2)}, u32[]{:S(2)}) collective-permute-start(f32[192,128]{1,0:T(8,128)} %get-tuple-element.71), channel_id=1, source_target_pairs={{0,32},{32,64},{64,96},{96,128},{128,160},{160,192},{192,224},{1,3... | collective-permute-start | bytes 294920 | tf_op jit(solution)/shard_map/ppermute | solution.py:305
  303.0 21.9 %collective-permute-start.13 = (f32[192,128]{1,0:T(8,128)}, f32[192,128]{1,0:T(8,128)S(1)}, u32[]{:S(2)}, u32[]{:S(2)}) collective-permute-start(f32[192,128]{1,0:T(8,128)} %get-tuple-element.72), channel_id=1, source_target_pairs={{32,0},{64,32},{96,64},{128,96},{160,128},{192,160},{224,192},{33,... | collective-permute-start | bytes 294920 | tf_op jit(solution)/shard_map/ppermute | solution.py:306
  306.7 18.2 %collective-permute-start.14 = (f32[48,128]{1,0:T(8,128)}, f32[48,128]{1,0:T(8,128)S(1)}, u32[]{:S(2)}, u32[]{:S(2)}) collective-permute-start(f32[48,128]{1,0:T(8,128)} %get-tuple-element.73), channel_id=1, source_target_pairs={{0,1},{1,2},{2,3},{3,4},{4,5},{5,6},{6,7},{7,8},{8,9},{9,10},{10,1... | collective-permute-start | bytes 73736 | tf_op jit(solution)/shard_map/ppermute | solution.py:305
  308.6 16.3 %collective-permute-start.15 = (f32[48,128]{1,0:T(8,128)}, f32[48,128]{1,0:T(8,128)S(1)}, u32[]{:S(2)}, u32[]{:S(2)}) collective-permute-start(f32[48,128]{1,0:T(8,128)} %get-tuple-element.74), channel_id=1, source_target_pairs={{1,0},{2,1},{3,2},{4,3},{5,4},{6,5},{7,6},{8,7},{9,8},{10,9},{11,1... | collective-permute-start | bytes 73736 | tf_op jit(solution)/shard_map/ppermute | solution.py:306
  324.9 0.6 copy-start.15
  324.9 0.6 copy-start.17
  324.9 0.6 copy-start.7
  324.9 0.6 copy-start.8

commit v4 on v2

v4 whole, which is shorter than its diff:
```python
import functools

import jax
import jax.numpy as jnp
from jax import lax
from jax.experimental import pallas as pl
from jax.experimental.pallas import tpu as pltpu
from jax.sharding import PartitionSpec as P

ITERS = 2
FINE_CAP = 4
COARSE_CAP = 2
DIRECT = 5
EXTRA = 2 * FINE_CAP + 1 - DIRECT
VMEM = pl.BlockSpec(memory_space=pltpu.VMEM)
SMEM = pl.BlockSpec(memory_space=pltpu.SMEM)
ANY = pl.BlockSpec(memory_space=pl.ANY)
PARAMS = pltpu.CompilerParams(vmem_limit_bytes=56 * 1024 * 1024)
UNROLL = 4


def ranks(boxes):
    count = boxes.shape[-1]
    earlier = jnp.arange(count)[None, :] < jnp.arange(count)[:, None]
    same = boxes[..., None, :] == boxes[..., :, None]
    return jnp.sum((same & earlier).astype(jnp.int32), axis=-1)


def plan_kernel(me_ref, units_ref, row_ref, column_ref):
    devices, lanes = units_ref.shape
    me = me_ref[0]
    units = units_ref[...]
    source = lax.broadcasted_iota(jnp.int32, units.shape, 0)
    lane = lax.broadcasted_iota(jnp.int32, units.shape, 1)
    surplus = pltpu.roll(jnp.maximum(units - DIRECT, 0), 0, 1, stride=1, stride_axis=0)
    none = jnp.full(units.shape, -1, jnp.int32)

    def one_round(r, carry):
        left, free, second, through, *chosen = carry
        ok = (left > 0) & (free > 0) & (second > 0)
        position = DIRECT - free
        item = surplus - left
        chosen = [jnp.where(ok & (item == i), r * 8 + position, table) for i, table in enumerate(chosen)]
        through = jnp.where(ok, source * 8 + position, through)
        used = ok.astype(jnp.int32)
        left, free, second = left - used, free - used, second - used
        free = pltpu.roll(free, lanes - 1, 1)
        second = pltpu.roll(pltpu.roll(second, devices - 1, 0), lanes - 1, 1)
        through = pltpu.roll(pltpu.roll(through, devices - 1, 0), lanes - 1, 1)
        return (left, free, second, through, *chosen)

    init = (surplus, jnp.maximum(DIRECT - units, 0), jnp.ones(units.shape, jnp.int32), none) + (none,) * EXTRA
    left, _, _, through, *chosen = lax.fori_loop(0, devices, one_round, init)
    for i in range(EXTRA):
        row_ref[i : i + 1] = jnp.max(jnp.where(source == me, chosen[i], -1), axis=0, keepdims=True)
    row_ref[EXTRA : EXTRA + 1] = jnp.max(left, axis=0, keepdims=True)
    row_ref[EXTRA + 1 : EXTRA + 2] = jnp.max(jnp.where(source == me, units, 0), axis=0, keepdims=True)
    column = none
    for i in range(EXTRA):
        mine = (lane < devices) & (lane == (source + me) % devices)
        found = jnp.max(jnp.where(mine, chosen[i], -1), axis=1, keepdims=True)
        column = jnp.where(lane == i, found, column)
    found = jnp.max(jnp.where(lane == me, through, -1), axis=1, keepdims=True)
    column_ref[...] = jnp.where(lane == EXTRA, found, column)


def pack_direct_kernel(fine_at_ref, coarse_at_ref, fine_ref, coarse_ref, out_ref, pairs_ref):
    planes = fine_ref.shape[0]
    coarse_planes, _, half, depth = coarse_ref.shape

    def fine_plane(k, carry):
        code = fine_at_ref[k]
        for h in range(2):
            unit = 2 * (code % FINE_CAP) + h

            @pl.when((code >= 0) & (unit < DIRECT))
            def _():
                out_ref[(code // FINE_CAP) * DIRECT + unit] = fine_ref[k, :, h * half : (h + 1) * half, :]

        return carry

    lax.fori_loop(0, planes, fine_plane, 0)

    def coarse_plane(k, carry):
        code = coarse_at_ref[k]
        for j in range(COARSE_CAP):

            @pl.when(code % COARSE_CAP == j)
            def _():
                pairs_ref[code // COARSE_CAP, :, :, j * depth : (j + 1) * depth] = coarse_ref[k]

        return carry

    lax.fori_loop(0, coarse_planes, coarse_plane, 0)


def pack_late_kernel(me_ref, row_ref, fine_at_ref, fine_ref, pairs_ref, _, out_ref, fine_sem, coarse_sem):
    planes, _, rows, _ = fine_ref.shape
    devices = pairs_ref.shape[0]
    half = rows // 2

    def slot_of(box, unit):
        t = (me_ref[0] + box) % devices
        code = row_ref[jnp.maximum(unit - DIRECT, 0), t]
        relay = jnp.where(code >= 0, ((t + code // 8) % devices) * DIRECT + code % 8, -1)
        return jnp.where(unit < DIRECT, box * DIRECT + unit, relay)

    def each(act):
        def fine_plane(k, carry):
            code = fine_at_ref[k]

            @pl.when((code >= 0) & (2 * (code % FINE_CAP) + 1 >= DIRECT))
            def _():
                for h in range(2):
                    unit = 2 * (code % FINE_CAP) + h
                    slot = slot_of(code // FINE_CAP, unit)

                    @pl.when((unit >= DIRECT) & (slot >= 0))
                    def _():
                        source = fine_ref.at[k, :, h * half : (h + 1) * half, :]
                        act(pltpu.make_async_copy(source, out_ref.at[slot], fine_sem.at[2 * k + h]))

            return carry

        lax.fori_loop(0, planes, fine_plane, 0)

        def coarse_pair(box, carry):
            units = row_ref[EXTRA + 1, box]
            slot = slot_of(box, jnp.maximum(units - 1, 0))

            @pl.when((units % 2 == 1) & (slot >= 0))
            def _():
                act(pltpu.make_async_copy(pairs_ref.at[box], out_ref.at[slot], coarse_sem.at[box]))

            return carry

        lax.fori_loop(0, devices, coarse_pair, 0)

    each(lambda copy: copy.start())
    each(lambda copy: copy.wait())


def pack_rest_kernel(row_ref, fine_at_ref, fine_ref, pairs_ref, out_ref):
    planes, _, rows, _ = fine_ref.shape
    devices = pairs_ref.shape[0]
    half = rows // 2

    def fine_plane(k, carry):
        code = fine_at_ref[k]
        for h in range(2):
            unit = 2 * (code % FINE_CAP) + h

            @pl.when((code >= 0) & (unit >= DIRECT))
            def _():
                out_ref[(code // FINE_CAP) * EXTRA + unit - DIRECT] = fine_ref[k, :, h * half : (h + 1) * half, :]

        return carry

    lax.fori_loop(0, planes, fine_plane, 0)

    def coarse_pair(box, carry):
        units = row_ref[EXTRA + 1, box]

        @pl.when((units % 2 == 1) & (units > DIRECT))
        def _():
            out_ref[box * EXTRA + units - 1 - DIRECT] = pairs_ref[box]

        return carry

    lax.fori_loop(0, devices, coarse_pair, 0)


def forward_kernel(me_ref, column_ref, in_ref, out_ref):
    devices = out_ref.shape[0]

    def body(a, carry):
        code = column_ref[a, EXTRA]

        @pl.when(code >= 0)
        def _():
            out_ref[(me_ref[0] - a + devices) % devices] = in_ref[(code // 8) * DIRECT + code % 8]

        return carry

    lax.fori_loop(0, devices, body, 0)


def rows_to_edges(flat_ref, ylow_ref, yhigh_ref, planes, species, rows):
    for s in range(species):
        for x in range(0, planes, 8):
            for edge_ref, at in ((ylow_ref, 0), (yhigh_ref, rows - 1)):
                start = (x * species + s) * rows + at
                edge_ref[s * planes + x : s * planes + x + 8] = flat_ref[pl.ds(start, 8, stride=species * rows), :]


def interpolate(ref, slot, part, store):
    _, species, half, lanes = ref.shape
    lane = lax.broadcasted_iota(jnp.int32, (half, lanes), 1)
    row = lax.broadcasted_iota(jnp.int32, (half, lanes), 0)
    sign = jnp.where(lane % 2 == 0, -0.25, 0.25)
    lane_first = lane % (lanes // 2) == 0
    lane_last = lane % (lanes // 2) == lanes // 2 - 1
    index = part * (lanes // 2) + lane // 2
    for s in range(species):
        p = ref[slot, s]
        below = jnp.where(row == 0, p, pltpu.roll(p, 1, 0))
        above = jnp.where(row == half - 1, p, pltpu.roll(p, half - 1, 0))
        left = jnp.where(lane_first, p, pltpu.roll(p, 1, 1))
        right = jnp.where(lane_last, p, pltpu.roll(p, lanes - 1, 1))
        slope_y = 0.125 * (above - below)
        slope_z = 0.5 * (right - left)
        gz = jnp.take_along_axis(slope_z, index, axis=1) * sign
        even = jnp.take_along_axis(p - slope_y, index, axis=1) + gz
        odd = jnp.take_along_axis(p + slope_y, index, axis=1) + gz
        store(s, even, odd)


def build_kernel(shape, fine_at_ref, coarse_at_ref, first_ref, out_ref, ylow_ref, yhigh_ref):
    planes, species, rows, lanes = shape
    half = rows // 2

    def body(c, carry):
        at = [fine_at_ref[2 * c], fine_at_ref[2 * c + 1]]
        code = coarse_at_ref[c]
        unit = code // 2 % (DIRECT + EXTRA)

        @pl.when(((at[0] < 0) | (at[1] < 0)) & (unit < DIRECT))
        def _():
            def store(s, even, odd):
                for child in range(2):
                    base = pl.multiple_of(((2 * c + child) * species + s) * rows, rows)
                    out_ref[pl.ds(base, half, stride=2), :] = even
                    out_ref[pl.ds(base + 1, half, stride=2), :] = odd

            interpolate(first_ref, code // 2 // (DIRECT + EXTRA) * DIRECT + unit, code % 2, store)

        for child in range(2):
            for h in range(2):
                late = 2 * (at[child] % FINE_CAP) + h

                @pl.when((at[child] >= 0) & (late < DIRECT))
                def _():
                    slot = at[child] // FINE_CAP * DIRECT + late
                    for s in range(species):
                        base = pl.multiple_of(((2 * c + child) * species + s) * rows + h * half, half)
                        out_ref[pl.ds(base, half), :] = first_ref[slot, s]

        return carry

    lax.fori_loop(0, planes // 2, body, 0)
    rows_to_edges(out_ref, ylow_ref, yhigh_ref, planes, species, rows)


def build_late_kernel(
    me_ref, column_ref, left_ref, fine_at_ref, coarse_at_ref, second_ref, rest_ref, _, ylow_in_ref, yhigh_in_ref,
    state_ref, ylow_ref, yhigh_ref, xlow_ref, xhigh_ref, held_ref, plane_ref, sem, late_sem,
):
    planes, species, rows, lanes = state_ref.shape
    half = rows // 2
    devices = column_ref.shape[0]
    planned = left_ref[0] == 0
    ylow_ref[...] = ylow_in_ref[...]
    yhigh_ref[...] = yhigh_in_ref[...]

    def now(source, target):
        copy = pltpu.make_async_copy(source, target, sem)
        copy.start()
        copy.wait()

    def relayed(source, unit):
        return (source + me_ref[0] + column_ref[source, unit - DIRECT] // 8) % devices

    def bring(source, unit):
        now(rest_ref.at[pl.ds(source * EXTRA + unit - DIRECT, 1)], held_ref)

    def parent(c, carry):
        at = [fine_at_ref[2 * c], fine_at_ref[2 * c + 1]]
        code = coarse_at_ref[c]
        unit = code // 2 % (DIRECT + EXTRA)
        source = code // 2 // (DIRECT + EXTRA)

        @pl.when(((at[0] < 0) | (at[1] < 0)) & (unit >= DIRECT))
        def _():
            def store(s, even, odd):
                plane_ref[s, pl.ds(0, half, stride=2), :] = even
                plane_ref[s, pl.ds(1, half, stride=2), :] = odd

            @pl.when(planned)
            def _():
                held_ref[0] = second_ref[relayed(source, unit)]

            @pl.when(jnp.logical_not(planned))
            def _():
                bring(source, unit)

            interpolate(held_ref, 0, code % 2, store)
            for child in range(2):

                @pl.when(at[child] < 0)
                def _():
                    x = 2 * c + child
                    now(plane_ref, state_ref.at[x])
                    for s in range(species):
                        ylow_ref[pl.ds(s * planes + x, 1), :] = plane_ref[s, 0:1]
                        yhigh_ref[pl.ds(s * planes + x, 1), :] = plane_ref[s, rows - 1 : rows]

        return carry

    lax.fori_loop(0, planes // 2, parent, 0)

    def each(begin):
        def plane(x, carry):
            at = fine_at_ref[x]

            @pl.when((at >= 0) & (2 * (at % FINE_CAP) + 1 >= DIRECT))
            def _():
                source = at // FINE_CAP
                for h in range(2):
                    unit = 2 * (at % FINE_CAP) + h
                    target = state_ref.at[x, :, h * half : (h + 1) * half, :]
                    edge_ref, edge = ((ylow_ref, 0), (yhigh_ref, half - 1))[h]

                    def set_edge(ref, slot):
                        for s in range(species):
                            edge_ref[pl.ds(s * planes + x, 1), :] = ref[slot, s, edge : edge + 1]

                    @pl.when((unit >= DIRECT) & planned)
                    def _():
                        slot = relayed(source, jnp.maximum(unit, DIRECT))
                        copy = pltpu.make_async_copy(second_ref.at[slot], target, late_sem.at[2 * x + h])
                        if begin:
                            copy.start()
                            set_edge(second_ref, slot)
                        else:
                            copy.wait()

                    if begin:

                        @pl.when((unit >= DIRECT) & jnp.logical_not(planned))
                        def _():
                            bring(source, jnp.maximum(unit, DIRECT))
                            now(held_ref.at[0], target)
                            set_edge(held_ref, 0)

            return carry

        lax.fori_loop(0, planes, plane, 0)

    each(True)
    each(False)
    now(state_ref.at[0], xlow_ref)
    now(state_ref.at[planes - 1], xhigh_ref)


def advance(shape, diff_ref, u_ref, vel_ref, ylow_ref, yhigh_ref, xlow_ref, xhigh_ref, out_ref, after):
    planes, species, rows, lanes = shape
    size = species * rows
    lane = lax.broadcasted_iota(jnp.int32, (rows, lanes), 1)
    row = lax.broadcasted_iota(jnp.int32, (rows, lanes), 0)

    def plane(x, below, above):
        positive = [jnp.maximum(vel_ref[x, k], 0.0) for k in range(3)]
        negative = [jnp.minimum(vel_ref[x, k], 0.0) for k in range(3)]
        keep = 1.0
        for k in range(3):
            keep = keep - (positive[k] - negative[k])
        for s in range(species):
            d = diff_ref[s]
            here = pl.ds(pl.multiple_of(x * size + s * rows, rows), rows)
            u = u_ref[here, :]
            edge = pl.ds(s * planes + x, 1)
            y_low = jnp.where(row == 0, ylow_ref[edge, :], pltpu.roll(u, 1, 0))
            y_high = jnp.where(row == rows - 1, yhigh_ref[edge, :], pltpu.roll(u, rows - 1, 0))
            z_low = jnp.where(lane == 0, u, pltpu.roll(u, 1, 1))
            z_high = jnp.where(lane == lanes - 1, u, pltpu.roll(u, lanes - 1, 1))
            new = u * (keep - 6.0 * d)
            for k, (low, high) in enumerate(((below(s), above(s)), (y_low, y_high), (z_low, z_high))):
                new = new + low * (d + positive[k]) + high * (d - negative[k])
            out_ref[here, :] = new

    def at(ref, x):
        return lambda s: ref[pl.ds(pl.multiple_of(x * size + s * rows, rows), rows), :]

    def group(x, first, last):
        for i in range(UNROLL):
            below = at(xlow_ref, 0) if first and i == 0 else at(u_ref, x + i - 1)
            above = at(xhigh_ref, 0) if last and i == UNROLL - 1 else at(u_ref, x + i + 1)
            plane(x + i, below, above)
        after(x)

    def body(g, carry):
        group(g * UNROLL, False, False)
        return carry

    group(0, True, False)
    lax.fori_loop(1, planes // UNROLL - 1, body, 0)
    group(planes - UNROLL, False, True)


def step_kernel(shape, diff_ref, u_ref, vel_ref, *refs):
    planes, species, rows, _ = shape
    size = species * rows
    *around, out_ref, ylow_ref, yhigh_ref, xlow_ref, xhigh_ref = refs
    advance(shape, diff_ref, u_ref, vel_ref, *around, out_ref, lambda x: None)
    rows_to_edges(out_ref, ylow_ref, yhigh_ref, planes, species, rows)
    xlow_ref[...] = out_ref[0:size]
    xhigh_ref[...] = out_ref[(planes - 1) * size : planes * size]


def last_step_kernel(shape, diff_ref, u_ref, vel_ref, *refs):
    planes, species, rows, _ = shape
    size = UNROLL * species * rows
    *around, out_ref, new_ref, sem = refs

    def copy(g):
        part = pl.ds(pl.multiple_of(g * size, size), size)
        return pltpu.make_async_copy(new_ref.at[part], out_ref.at[part], sem.at[g])

    advance(shape, diff_ref, u_ref, vel_ref, *around, new_ref, lambda x: copy(x // UNROLL).start())

    def finish(g, carry):
        copy(g).wait()
        return carry

    lax.fori_loop(0, planes // UNROLL, finish, 0)


def empty_kernel(out_ref):
    pass


def cost(microseconds):
    return pl.CostEstimate(flops=0, bytes_accessed=int(microseconds * 3.6e6), transcendentals=0)


def halo(ylow, yhigh, xlow, xhigh):
    got = []
    for axis, low, high in (("grp", ylow, yhigh), ("dev", xlow, xhigh)):
        size = lax.axis_size(axis)
        up = [(i, (i + 1) % size) for i in range(size - 1)]
        got.append(lax.ppermute(high, axis, up))
        got.append(lax.ppermute(low, axis, [(b, a) for a, b in up]))
    return got


def on_device(old_fine, old_ids, old_coarse, coarse_ids, velocity, diffusion):
    devices = lax.axis_size("dev")
    me = lax.axis_index("dev")
    me_ref = me.reshape(1).astype(jnp.int32)
    planes, species, rows, lanes = old_fine.shape
    half = rows // 2
    coarse_planes = old_coarse.shape[0]
    unit_count = DIRECT + EXTRA
    f32 = jnp.float32
    i32 = jnp.int32

    def units_shape(count):
        return jax.ShapeDtypeStruct((count, species, half, lanes), f32)

    own, own_coarse = old_ids[0], coarse_ids[0]
    own_box = jnp.where(own >= 0, own // planes, -1)
    send_fine = jnp.where(own >= 0, own_box * FINE_CAP + ranks(own_box), -1)
    own_coarse_box = own_coarse // coarse_planes
    send_coarse = own_coarse_box * COARSE_CAP + ranks(own_coarse_box)
    packed, pairs = pl.pallas_call(
        pack_direct_kernel,
        out_shape=[units_shape(devices * DIRECT), units_shape(devices)],
        in_specs=[SMEM] * 2 + [VMEM] * 2,
        out_specs=[VMEM] * 2,
        compiler_params=PARAMS,
        cost_estimate=cost(8),
        name="pack_direct",
    )(send_fine, send_coarse, old_fine, old_coarse)

    labels = jnp.broadcast_to(jnp.concatenate([own, own_coarse])[None], (devices, planes + coarse_planes))
    labels = lax.all_to_all(labels, "dev", split_axis=0, concat_axis=0, tiled=True)
    all_ids, all_coarse = labels[:, :planes], labels[:, planes:]
    all_box = jnp.where(all_ids >= 0, all_ids // planes, -1)
    all_coarse_box = all_coarse // coarse_planes
    flat_parents = jnp.where(all_ids >= 0, all_ids // 2, -1).reshape(-1)

    def needed(coarse):
        kept = jnp.sum((flat_parents == coarse[..., None]).astype(i32), axis=-1)
        return kept < 2

    box = jnp.arange(lanes) % devices
    fine_units = jnp.sum((all_box[:, None, :] == box[None, :, None]).astype(i32), axis=-1)
    asked = needed(all_coarse)[:, None, :] & (all_coarse_box[:, None, :] == box[None, :, None])
    units = 2 * fine_units + jnp.max(asked.astype(i32), axis=-1)
    row, column = pl.pallas_call(
        plan_kernel,
        out_shape=[jax.ShapeDtypeStruct((8, lanes), i32), jax.ShapeDtypeStruct((devices, lanes), i32)],
        in_specs=[SMEM, VMEM],
        out_specs=[VMEM] * 2,
        name="plan",
    )(me_ref, units)
    left = jnp.max(row[EXTRA, :devices]).reshape(1)

    order = jnp.arange(devices)[:, None]
    wanted = me * planes + jnp.arange(planes)
    fine_at = jnp.where(all_ids[None] == wanted[:, None, None], (order * FINE_CAP + ranks(all_box))[None], -1)
    fine_at = jnp.max(fine_at, axis=(1, 2))
    to_me = jnp.sum((all_box == me).astype(i32), axis=1, keepdims=True)
    coarse_wanted = me * coarse_planes + jnp.arange(coarse_planes)
    coarse_code = (order * unit_count + 2 * to_me) * 2 + ranks(all_coarse_box)
    coarse_at = jnp.where(all_coarse[None] == coarse_wanted[:, None, None], coarse_code[None], 0)
    coarse_at = jnp.max(coarse_at, axis=(1, 2))

    def exchange(value):
        return lax.all_to_all(value, "dev", split_axis=0, concat_axis=0, tiled=True)

    packed = pl.pallas_call(
        pack_late_kernel,
        out_shape=units_shape(devices * DIRECT),
        in_specs=[SMEM] * 3 + [ANY] * 3,
        out_specs=ANY,
        scratch_shapes=[pltpu.SemaphoreType.DMA((2 * planes,)), pltpu.SemaphoreType.DMA((devices,))],
        input_output_aliases={5: 0},
        name="pack_late",
    )(me_ref, row, send_fine, old_fine, pairs, packed)

    def no_rest():
        return pl.pallas_call(empty_kernel, out_shape=units_shape(devices * EXTRA), out_specs=ANY, name="nothing")()

    def rest_direct():
        rest = pl.pallas_call(
            pack_rest_kernel,
            out_shape=units_shape(devices * EXTRA),
            in_specs=[SMEM] * 2 + [VMEM] * 2,
            out_specs=VMEM,
            compiler_params=PARAMS,
            name="pack_rest",
        )(row, send_fine, old_fine, pairs)
        return exchange(rest)

    rest = lax.cond(left[0] == 0, no_rest, rest_direct)
    packed, rest = lax.optimization_barrier((packed, rest))
    first = exchange(packed)
    second = pl.pallas_call(
        forward_kernel,
        out_shape=units_shape(devices),
        in_specs=[SMEM] * 2 + [VMEM],
        out_specs=VMEM,
        compiler_params=PARAMS,
        cost_estimate=cost(3),
        name="forward",
    )(me_ref, column, first)
    second = exchange(second)

    size = species * rows
    edge_shapes = [jax.ShapeDtypeStruct((species * planes, lanes), f32)] * 2
    xedge_shapes = [jax.ShapeDtypeStruct((size, lanes), f32)] * 2
    state_shape = jax.ShapeDtypeStruct((planes * size, lanes), f32)
    state, ylow, yhigh = pl.pallas_call(
        functools.partial(build_kernel, old_fine.shape),
        out_shape=[state_shape] + edge_shapes,
        in_specs=[SMEM] * 2 + [VMEM],
        out_specs=[VMEM] * 3,
        compiler_params=PARAMS,
        cost_estimate=cost(10),
        name="build",
    )(fine_at, coarse_at, first)
    plane_shape = jax.ShapeDtypeStruct((species, rows, lanes), f32)
    state, ylow, yhigh, xlow, xhigh = pl.pallas_call(
        build_late_kernel,
        out_shape=[jax.ShapeDtypeStruct(old_fine.shape, f32)] + edge_shapes + [plane_shape] * 2,
        in_specs=[SMEM] * 5 + [VMEM, ANY, ANY] + [VMEM] * 2,
        out_specs=[ANY] + [VMEM] * 4,
        scratch_shapes=[
            pltpu.VMEM((1, species, half, lanes), f32),
            pltpu.VMEM((species, rows, lanes), f32),
            pltpu.SemaphoreType.DMA,
            pltpu.SemaphoreType.DMA((2 * planes,)),
        ],
        input_output_aliases={7: 0},
        compiler_params=PARAMS,
        cost_estimate=cost(4),
        name="build_late",
    )(me_ref, column, left, fine_at, coarse_at, second, rest, state.reshape(old_fine.shape), ylow, yhigh)
    state = state.reshape(state_shape.shape)
    edges = [ylow, yhigh, xlow.reshape(size, lanes), xhigh.reshape(size, lanes)]

    for repeat in range(ITERS):
        last = repeat == ITERS - 1
        state = pl.pallas_call(
            functools.partial(last_step_kernel if last else step_kernel, old_fine.shape),
            out_shape=[state_shape] + ([] if last else edge_shapes + xedge_shapes),
            in_specs=[SMEM] + [VMEM] * 6,
            out_specs=[ANY] if last else [VMEM] * 5,
            scratch_shapes=[
                pltpu.VMEM(state_shape.shape, f32), pltpu.SemaphoreType.DMA((planes // UNROLL,))
            ] if last else [],
            compiler_params=PARAMS,
            cost_estimate=cost(10),
            name="last_step" if last else "step",
        )(diffusion, state, velocity, *halo(*edges))
        state, *edges = state
    return state.reshape(old_fine.shape)


def solution(mesh):
    in_specs = (
        P("dev", None, "grp", None),
        P("grp", "dev"),
        P("dev", None, "grp", None),
        P("grp", "dev"),
        P("dev", None, "grp", None),
        P(),
    )
    out_specs = P("dev", None, "grp", None)
    return jax.shard_map(
        on_device, mesh=mesh, in_specs=in_specs, out_specs=out_specs, check_vma=False
    )
```

time: 291 us -> 299 us (1.027)
  waiting for transfers between devices: 133 us -> 17.8 us
  blocking collectives: 41 us -> 144 us
  Pallas kernels: 51.2 us -> 71.7 us
    all_to_all x1, waiting for transfers between devices: 124 us -> 13.2 us  [exchange(): return lax.all_to_all(value, 'dev', split_axis=0, concat_axis=0, tiled=True)]
    all_to_all x1, blocking collectives: 41 us -> 144 us  [exchange(): return lax.all_to_all(value, 'dev', split_axis=0, concat_axis=0, tiled=True)]
    pallas_call x5 -> x8, Pallas kernels: 47.2 us -> 67.1 us  [the longest x2 18.5 us: on_device(): pl.pallas_call(functools.partial(last_step_kernel if last else step_kerne...]
    all_to_all x1, waiting for transfers between devices: 3.95 us -> 0.01 us  [on_device(): lax.all_to_all(labels, 'dev', split_axis=0, concat_axis=0, tiled=True)]
    ppermute x4, starting transfers between devices: 16 us -> 19.6 us  [halo(): got.append(lax.ppermute(low, axis, [(b, a) for a, b in up]))]
    ppermute x4, starting transfers between devices: 11 us -> 7.71 us  [halo(): got.append(lax.ppermute(high, axis, up))]
  transfers between devices with their start and end apart: 10 -> 10, of which waited for: 6 -> 5; matrix products, arithmetic and copies ran while one was open for 3% -> 3% of each run, Pallas kernels for 0% -> 7%
where the time goes in v4:
time: 299 us; the launch traced here: 297 us
  blocking collectives  144 us (48%)
  Pallas kernels  71.7 us (24%)
  starting transfers between devices  45.7 us (15%)
  waiting for transfers between devices  17.8 us (6%)
  other arithmetic  14 us (5%)
  local copies, waits for them, and re-layouts  3.36 us (1%)
    all_to_all x1, blocking collectives, exchange(): return lax.all_to_all(value, 'dev', split_axis=0, concat_axis=0, tiled=True)  144 us
    ppermute x4, starting transfers between devices, halo(): got.append(lax.ppermute(low, axis, [(b, a) for a, b in up]))  19.6 us
    pallas_call x2, Pallas kernels, on_device(): pl.pallas_call(functools.partial(last_step_kernel if last else step_kerne...  18.5 us
    all_to_all x1, waiting for transfers between devices, exchange(): return lax.all_to_all(value, 'dev', split_axis=0, concat_axis=0, tiled=True)  13.2 us
    pallas_call x1, Pallas kernels, on_device(): pl.pallas_call(pack_late_kernel, out_shape=units_shape(devices * DIRECT),...  13 us
    pallas_call x1, Pallas kernels, on_device(): pl.pallas_call(build_late_kernel, out_shape=[jax.ShapeDtypeStruct(old_fin...  11.7 us
    all_to_all x1, starting transfers between devices, on_device(): lax.all_to_all(labels, 'dev', split_axis=0, concat_axis=0, tiled=True)  11.6 us
    pallas_call x1, Pallas kernels, on_device(): pl.pallas_call(functools.partial(build_kernel, old_fine.shape), out_shape...  10.4 us
  transfers between devices with their start and end apart: 10, of which 5 were waited for; matrix products, arithmetic and copies ran while one was open for 3% of the time, Pallas kernels for 7%

profile of v4, /device:TPU:22, one launch (start us, length us, event | category | flops | bytes accessed | tf_op | source)
XLA Modules:
  0.0 297.0 jit_solution(6940548529295575511)
XLA Ops:
  0.0 0.7 pad_add_fusion
  0.7 0.6 broadcast_in_dim.24
  1.4 11.6 %all-to-all-start.1 = ((s32[32,1,96]{2,1,0:T(1,128)}), s32[32,1,96]{2,1,0:T(1,128)S(1)}, u32[]{:S(2)}, u32[]{:S(2)}) async-start(s32[32,1,96]{2,1,0:T(1,128)} %broadcast_in_dim.24), calls=%async_computation.1 | async-start | bytes 32768 | tf_op jit(solution)/shard_map/all_to_all | solution.py:476
  13.0 0.7 compare_select_fusion.14
  13.6 0.7 fusion.9
  14.3 0.7 and_select_fusion.1
  15.0 0.7 fusion.8
  15.6 0.2 convert_reduce_fusion.5
  15.8 0.7 compare_select_fusion.13.fine_at_ref
  16.5 0.2 convert_reduce_fusion.6
  16.7 1.2 multiply_add_fusion.1.coarse_at_ref
  17.9 9.1 %pack_direct.1 = (f32[160,9,8,128]{3,2,1,0:T(8,128)}, f32[32,9,8,128]{3,2,1,0:T(8,128)S(1)}) custom-call(s32[64]{0:T(128)S(1)} %compare_select_fusion.13.fine_at_ref, s32[32]{0:T(128)} %multiply_add_fusion.1.coarse_at_ref, f32[64,9,16,128]{3,2,1,0:T(8,128)} %fine_ref.3, f32[32,9,8,64]{3,2,1,0:T(8,128)} %coarse_ref.1), custom_call_target="tpu_custom_call" | custom-call | bytes 28800000 | tf_op jit(solution)/shard_map/pack_direct/pallas_call | solution.py:465
  27.1 0.1 fusion.11
  27.3 1.1 convert_reduce_fusion
  28.4 0.4 convert_reduce_fusion.2
  28.7 0.4 convert_reduce_fusion.4
  29.1 0.6 multiply_add_fusion.units_ref
  29.7 4.6 %plan.1 = (s32[8,128]{1,0:T(8,128)S(1)}, s32[32,128]{1,0:T(8,128)}) custom-call(s32[1]{0:T(128)} %bitcast.me_ref, s32[32,128]{1,0:T(8,128)} %multiply_add_fusion.units_ref), custom_call_target="tpu_custom_call" | custom-call | tf_op jit(solution)/shard_map/plan/pallas_call | solution.py:490
  34.3 0.7 slice_reduce_fusion
  35.6 13.0 %pack_late.1 = f32[160,9,8,128]{3,2,1,0:T(8,128)} custom-call(s32[1]{0:T(128)} %bitcast.me_ref, s32[8,128]{1,0:T(8,128)S(1)} %get-tuple-element.40.row_ref, s32[64]{0:T(128)S(1)} %compare_select_fusion.13.fine_at_ref, f32[64,9,16,128]{3,2,1,0:T(8,128)} %fine_ref.3, ...), custom_call_target="tpu_custom_call", output_to_operand_aliasing={{}: (5, {})} | custom-call | tf_op jit(solution)/shard_map/pack_late/pallas_call | solution.py:512
  48.7 143.6 %all_to_all.24.in_ref.first_ref = f32[160,9,8,128]{3,2,1,0:T(8,128)} all-to-all(f32[160,9,8,128]{3,2,1,0:T(8,128)} %pack_late.1), channel_id=1, replica_groups=mesh['grp'=8,'dev'=32] {'dev'}, dimensions={0} | all-to-all | bytes 11796480 | tf_op jit(solution)/shard_map/all_to_all | solution.py:510
  192.2 4.3 %forward.1 = f32[32,9,8,128]{3,2,1,0:T(8,128)} custom-call(s32[1]{0:T(128)} %bitcast.me_ref, s32[32,128]{1,0:T(8,128)} %get-tuple-element.39.column_ref, f32[160,9,8,128]{3,2,1,0:T(8,128)} %all_to_all.24.in_ref.first_ref), custom_call_target="tpu_custom_call" | custom-call | bytes 10800000 | tf_op jit(solution)/shard_map/forward/pallas_call | solution.py:539
  196.5 6.8 %all-to-all-start.3 = ((f32[32,9,8,128]{3,2,1,0:T(8,128)}), f32[32,9,8,128]{3,2,1,0:T(8,128)S(1)}, u32[]{:S(2)}, u32[]{:S(2)}) async-start(f32[32,9,8,128]{3,2,1,0:T(8,128)} %forward.1), calls=%async_computation.3 | async-start | bytes 2359296 | tf_op jit(solution)/shard_map/all_to_all | solution.py:510
  203.4 0.8 convert_reduce_fusion.3
  204.3 1.3 select_reduce_fusion.1.coarse_at_ref
  205.6 0.9 convert_reduce_fusion.1
  206.6 1.9 select_reduce_fusion.fine_at_ref
  208.5 10.4 %build.1 = (f32[9216,128]{1,0:T(8,128)}, f32[576,128]{1,0:T(8,128)}, f32[576,128]{1,0:T(8,128)}) custom-call(s32[64]{0:T(128)} %select_reduce_fusion.fine_at_ref, s32[32]{0:T(128)} %select_reduce_fusion.1.coarse_at_ref, f32[160,9,8,128]{3,2,1,0:T(8,128)} %all_to_all.24.in_ref.first_ref), custom_call_target="tpu_custom_call" | custom-call | bytes 36000000 | tf_op jit(solution)/shard_map/build/pallas_call | solution.py:554
  218.9 13.2 %all-to-all-done.3.second_ref = f32[32,9,8,128]{3,2,1,0:T(8,128)S(1)} async-done(((f32[32,9,8,128]{3,2,1,0:T(8,128)}), f32[32,9,8,128]{3,2,1,0:T(8,128)S(1)}, u32[]{:S(2)}, u32[]{:S(2)}) %all-to-all-start.3) | async-done | bytes 1179680 | tf_op jit(solution)/shard_map/all_to_all | solution.py:510
  232.2 1.0 copy-done
  233.2 11.7 %build_late.1 = (f32[64,9,16,128]{3,2,1,0:T(8,128)}, f32[576,128]{1,0:T(8,128)}, f32[576,128]{1,0:T(8,128)}, f32[9,16,128]{2,1,0:T(8,128)}, f32[9,16,128]{2,1,0:T(8,128)}) custom-call(s32[1]{0:T(128)} %bitcast.me_ref, s32[32,128]{1,0:T(8,128)} %get-tuple-element.39.column_ref, s32[1]{0:T(128)} %bitcast.4.left_ref, ...), custom_call_target="tpu_custom_call", output_to_operand_aliasing={{0}: (7, {})} | custom-call | bytes 14400000 | tf_op jit(solution)/shard_map/build_late/pallas_call | solution.py:564
  244.9 1.9 collective-permute-start
  246.8 3.6 %collective-permute-start.1 = (f32[576,128]{1,0:T(8,128)}, f32[576,128]{1,0:T(8,128)S(1)}, u32[]{:S(2)}, u32[]{:S(2)}) collective-permute-start(f32[576,128]{1,0:T(8,128)} %get-tuple-element.50), channel_id=1, source_target_pairs={{32,0},{64,32},{96,64},{128,96},{160,128},{192,160},{224,192},{33,... | collective-permute-start | bytes 884744 | tf_op jit(solution)/shard_map/ppermute | solution.py:442
  250.5 2.0 collective-permute-start.2
  252.4 6.0 %collective-permute-start.3 = (f32[144,128]{1,0:T(8,128)}, f32[144,128]{1,0:T(8,128)S(1)}, u32[]{:S(2)}, u32[]{:S(2)}) collective-permute-start(f32[144,128]{1,0:T(8,128)} %bitcast.25), channel_id=1, source_target_pairs={{1,0},{2,1},{3,2},{4,3},{5,4},{6,5},{7,6},{8,7},{9,8},{10,9},{11,1... | collective-permute-start | bytes 221192 | tf_op jit(solution)/shard_map/ppermute | solution.py:442
  258.4 0.6 collective-permute-done.2.refs_2_
  259.0 1.7 collective-permute-done.3.refs_3_
  260.7 0.6 copy-done.6
  261.6 10.0 %step.1 = (f32[9216,128]{1,0:T(8,128)}, f32[576,128]{1,0:T(8,128)}, f32[576,128]{1,0:T(8,128)}, f32[144,128]{1,0:T(8,128)}, f32[144,128]{1,0:T(8,128)}) custom-call(f32[9]{0:T(128)} %diff_ref.3, f32[9216,128]{1,0:T(8,128)} %bitcast.22, f32[64,3,16,128]{3,2,1,0:T(8,128)} %vel_ref.3, f32[576,128]{1,0:T(8,128)} %copy-done.1, f32[576,128]{1,0:T(8,128)} %copy-done.2, ...), custom_call_target="tpu_custom_call" | custom-call | bytes 36000000 | tf_op jit(solution)/shard_map/step/pallas_call | solution.py:585
  271.6 1.9 collective-permute-start.4
  273.5 3.6 %collective-permute-start.5 = (f32[576,128]{1,0:T(8,128)}, f32[576,128]{1,0:T(8,128)S(1)}, u32[]{:S(2)}, u32[]{:S(2)}) collective-permute-start(f32[576,128]{1,0:T(8,128)} %get-tuple-element.55), channel_id=1, source_target_pairs={{32,0},{64,32},{96,64},{128,96},{160,128},{192,160},{224,192},{33,... | collective-permute-start | bytes 884744 | tf_op jit(solution)/shard_map/ppermute | solution.py:442
  277.2 1.9 collective-permute-start.6
  279.1 6.3 %collective-permute-start.7 = (f32[144,128]{1,0:T(8,128)}, f32[144,128]{1,0:T(8,128)S(1)}, u32[]{:S(2)}, u32[]{:S(2)}) collective-permute-start(f32[144,128]{1,0:T(8,128)} %get-tuple-element.57), channel_id=1, source_target_pairs={{1,0},{2,1},{3,2},{4,3},{5,4},{6,5},{7,6},{8,7},{9,8},{10,9},{11,1... | collective-permute-start | bytes 221192 | tf_op jit(solution)/shard_map/ppermute | solution.py:442
  285.4 0.7 collective-permute-done.6.refs_2_
  286.1 1.6 collective-permute-done.7.refs_3_
  287.7 0.6 copy-done.8
  288.3 0.1 copy-done.3
  288.5 8.5 %last_step.1 = f32[9216,128]{1,0:T(8,128)} custom-call(f32[9]{0:T(128)} %diff_ref.3, f32[9216,128]{1,0:T(8,128)} %get-tuple-element.53.u_ref, f32[64,3,16,128]{3,2,1,0:T(8,128)} %vel_ref.3, f32[576,128]{1,0:T(8,128)} %copy-done.3, f32[576,128]{1,0:T(8,128)} %copy-done.4, f32[144,128]{1,0:T(8,128)} %copy-done.7, f32[144,128]{1,0:T(8,128)} %copy-done.8), custom_call_target="tpu_custom_call" | custom-call | bytes 36000000 | tf_op jit(solution)/shard_map/last_step/pallas_call | solution.py:585
  (33 shorter events, 0.7 us)
Async XLA Ops:
  1.4 25.6 %all-to-all-start.1 = ((s32[32,1,96]{2,1,0:T(1,128)}), s32[32,1,96]{2,1,0:T(1,128)S(1)}, u32[]{:S(2)}, u32[]{:S(2)}) async-start(s32[32,1,96]{2,1,0:T(1,128)} %broadcast_in_dim.24), calls=%async_computation.1 | async-start | bytes 32768 | tf_op jit(solution)/shard_map/all_to_all | solution.py:476
  196.5 35.6 %all-to-all-start.3 = ((f32[32,9,8,128]{3,2,1,0:T(8,128)}), f32[32,9,8,128]{3,2,1,0:T(8,128)S(1)}, u32[]{:S(2)}, u32[]{:S(2)}) async-start(f32[32,9,8,128]{3,2,1,0:T(8,128)} %forward.1), calls=%async_computation.3 | async-start | bytes 2359296 | tf_op jit(solution)/shard_map/all_to_all | solution.py:510
  232.2 1.0 copy-start
  244.9 15.8 %collective-permute-start = (f32[576,128]{1,0:T(8,128)}, f32[576,128]{1,0:T(8,128)S(1)}, u32[]{:S(2)}, u32[]{:S(2)}) collective-permute-start(f32[576,128]{1,0:T(8,128)} %get-tuple-element.49), channel_id=1, source_target_pairs={{0,32},{32,64},{64,96},{96,128},{128,160},{160,192},{192,224},{1,3... | collective-permute-start | bytes 884744 | tf_op jit(solution)/shard_map/ppermute | solution.py:441
  246.8 13.9 %collective-permute-start.1 = (f32[576,128]{1,0:T(8,128)}, f32[576,128]{1,0:T(8,128)S(1)}, u32[]{:S(2)}, u32[]{:S(2)}) collective-permute-start(f32[576,128]{1,0:T(8,128)} %get-tuple-element.50), channel_id=1, source_target_pairs={{32,0},{64,32},{96,64},{128,96},{160,128},{192,160},{224,192},{33,... | collective-permute-start | bytes 884744 | tf_op jit(solution)/shard_map/ppermute | solution.py:442
  250.5 8.6 %collective-permute-start.2 = (f32[144,128]{1,0:T(8,128)}, f32[144,128]{1,0:T(8,128)S(1)}, u32[]{:S(2)}, u32[]{:S(2)}) collective-permute-start(f32[144,128]{1,0:T(8,128)} %bitcast.26), channel_id=1, source_target_pairs={{0,1},{1,2},{2,3},{3,4},{4,5},{5,6},{6,7},{7,8},{8,9},{9,10},{10,1... | collective-permute-start | bytes 221192 | tf_op jit(solution)/shard_map/ppermute | solution.py:441
  252.4 8.3 %collective-permute-start.3 = (f32[144,128]{1,0:T(8,128)}, f32[144,128]{1,0:T(8,128)S(1)}, u32[]{:S(2)}, u32[]{:S(2)}) collective-permute-start(f32[144,128]{1,0:T(8,128)} %bitcast.25), channel_id=1, source_target_pairs={{1,0},{2,1},{3,2},{4,3},{5,4},{6,5},{7,6},{8,7},{9,8},{10,9},{11,1... | collective-permute-start | bytes 221192 | tf_op jit(solution)/shard_map/ppermute | solution.py:442
  259.0 1.7 copy-start.5
  260.7 0.6 copy-start.6
  260.7 0.7 copy-start.1
  260.7 0.8 copy-start.2
  271.6 16.1 %collective-permute-start.4 = (f32[576,128]{1,0:T(8,128)}, f32[576,128]{1,0:T(8,128)S(1)}, u32[]{:S(2)}, u32[]{:S(2)}) collective-permute-start(f32[576,128]{1,0:T(8,128)} %get-tuple-element.54), channel_id=1, source_target_pairs={{0,32},{32,64},{64,96},{96,128},{128,160},{160,192},{192,224},{1,3... | collective-permute-start | bytes 884744 | tf_op jit(solution)/shard_map/ppermute | solution.py:441
  273.5 14.2 %collective-permute-start.5 = (f32[576,128]{1,0:T(8,128)}, f32[576,128]{1,0:T(8,128)S(1)}, u32[]{:S(2)}, u32[]{:S(2)}) collective-permute-start(f32[576,128]{1,0:T(8,128)} %get-tuple-element.55), channel_id=1, source_target_pairs={{32,0},{64,32},{96,64},{128,96},{160,128},{192,160},{224,192},{33,... | collective-permute-start | bytes 884744 | tf_op jit(solution)/shard_map/ppermute | solution.py:442
  277.2 8.9 %collective-permute-start.6 = (f32[144,128]{1,0:T(8,128)}, f32[144,128]{1,0:T(8,128)S(1)}, u32[]{:S(2)}, u32[]{:S(2)}) collective-permute-start(f32[144,128]{1,0:T(8,128)} %get-tuple-element.56), channel_id=1, source_target_pairs={{0,1},{1,2},{2,3},{3,4},{4,5},{5,6},{6,7},{7,8},{8,9},{9,10},{10,1... | collective-permute-start | bytes 221192 | tf_op jit(solution)/shard_map/ppermute | solution.py:441
  279.1 8.6 %collective-permute-start.7 = (f32[144,128]{1,0:T(8,128)}, f32[144,128]{1,0:T(8,128)S(1)}, u32[]{:S(2)}, u32[]{:S(2)}) collective-permute-start(f32[144,128]{1,0:T(8,128)} %get-tuple-element.57), channel_id=1, source_target_pairs={{1,0},{2,1},{3,2},{4,3},{5,4},{6,5},{7,6},{8,7},{9,8},{10,9},{11,1... | collective-permute-start | bytes 221192 | tf_op jit(solution)/shard_map/ppermute | solution.py:442
  286.1 1.6 copy-start.7
  287.6 0.6 copy-start.8
  287.7 0.8 copy-start.3
  287.7 0.9 copy-start.4

commit v5 on v2

v5 whole, which is shorter than its diff:
```python
import functools

import jax
import jax.numpy as jnp
from jax import lax
from jax.experimental import pallas as pl
from jax.experimental.pallas import tpu as pltpu
from jax.sharding import PartitionSpec as P

ITERS = 2
FINE_CAP = 4
COARSE_CAP = 2
DIRECT = 5
EXTRA = 2 * FINE_CAP + 1 - DIRECT
VMEM = pl.BlockSpec(memory_space=pltpu.VMEM)
SMEM = pl.BlockSpec(memory_space=pltpu.SMEM)
ANY = pl.BlockSpec(memory_space=pl.ANY)
PARAMS = pltpu.CompilerParams(vmem_limit_bytes=56 * 1024 * 1024)
UNROLL = 4


def ranks(boxes):
    count = boxes.shape[-1]
    earlier = jnp.arange(count)[None, :] < jnp.arange(count)[:, None]
    same = boxes[..., None, :] == boxes[..., :, None]
    return jnp.sum((same & earlier).astype(jnp.int32), axis=-1)


def plan_kernel(me_ref, units_ref, row_ref, column_ref):
    devices, lanes = units_ref.shape
    me = me_ref[0]
    units = units_ref[...]
    source = lax.broadcasted_iota(jnp.int32, units.shape, 0)
    lane = lax.broadcasted_iota(jnp.int32, units.shape, 1)
    surplus = pltpu.roll(jnp.maximum(units - DIRECT, 0), 0, 1, stride=1, stride_axis=0)
    none = jnp.full(units.shape, -1, jnp.int32)

    def one_round(r, carry):
        left, free, second, through, *chosen = carry
        ok = (left > 0) & (free > 0) & (second > 0)
        position = DIRECT - free
        item = surplus - left
        chosen = [jnp.where(ok & (item == i), r * 8 + position, table) for i, table in enumerate(chosen)]
        through = jnp.where(ok, source * 8 + position, through)
        used = ok.astype(jnp.int32)
        left, free, second = left - used, free - used, second - used
        free = pltpu.roll(free, lanes - 1, 1)
        second = pltpu.roll(pltpu.roll(second, devices - 1, 0), lanes - 1, 1)
        through = pltpu.roll(pltpu.roll(through, devices - 1, 0), lanes - 1, 1)
        return (left, free, second, through, *chosen)

    init = (surplus, jnp.maximum(DIRECT - units, 0), jnp.ones(units.shape, jnp.int32), none) + (none,) * EXTRA
    left, _, _, through, *chosen = lax.fori_loop(0, devices, one_round, init)
    for i in range(EXTRA):
        row_ref[i : i + 1] = jnp.max(jnp.where(source == me, chosen[i], -1), axis=0, keepdims=True)
    row_ref[EXTRA : EXTRA + 1] = jnp.max(left, axis=0, keepdims=True)
    column = none
    for i in range(EXTRA):
        mine = (lane < devices) & (lane == (source + me) % devices)
        found = jnp.max(jnp.where(mine, chosen[i], -1), axis=1, keepdims=True)
        column = jnp.where(lane == i, found, column)
    found = jnp.max(jnp.where(lane == me, through, -1), axis=1, keepdims=True)
    column_ref[...] = jnp.where(lane == EXTRA, found, column)


def pack_kernel(devices, slot_of, me_ref, fine_at_ref, coarse_at_ref, row_ref, fine_ref, coarse_ref, out_ref):
    planes = fine_ref.shape[0]
    coarse_planes, _, half, depth = coarse_ref.shape

    def fine_plane(k, carry):
        code = fine_at_ref[k]

        @pl.when(code >= 0)
        def _():
            for h in range(2):
                slot = slot_of(me_ref[0], row_ref, code // FINE_CAP, 2 * (code % FINE_CAP) + h)

                @pl.when(slot >= 0)
                def _():
                    out_ref[slot] = fine_ref[k, :, h * half : (h + 1) * half, :]

        return carry

    lax.fori_loop(0, planes, fine_plane, 0)

    def coarse_plane(k, carry):
        code = coarse_at_ref[k]

        @pl.when(code >= 0)
        def _():
            at = code // 2
            slot = slot_of(me_ref[0], row_ref, at // (DIRECT + EXTRA), at % (DIRECT + EXTRA))
            for j in range(2):

                @pl.when((slot >= 0) & (code % 2 == j))
                def _():
                    out_ref[slot, :, :, j * depth : (j + 1) * depth] = coarse_ref[k]

        return carry

    lax.fori_loop(0, coarse_planes, coarse_plane, 0)


def first_slot(devices, me, row_ref, box, unit):
    t = (me + box) % devices
    code = row_ref[jnp.maximum(unit - DIRECT, 0), t]
    relay = jnp.where(code >= 0, ((t + code // 8) % devices) * DIRECT + code % 8, -1)
    return jnp.where(unit < DIRECT, box * DIRECT + unit, relay)


def direct_slot(me, row_ref, box, unit):
    return jnp.where(unit < DIRECT, -1, box * EXTRA + unit - DIRECT)


def forward_kernel(me_ref, column_ref, in_ref, out_ref):
    devices = out_ref.shape[0]

    def body(a, carry):
        code = column_ref[a, EXTRA]

        @pl.when(code >= 0)
        def _():
            out_ref[(me_ref[0] - a + devices) % devices] = in_ref[(code // 8) * DIRECT + code % 8]

        return carry

    lax.fori_loop(0, devices, body, 0)


def rows_to_edges(flat_ref, edge_ref, offset, row, planes, species, rows):
    for s in range(species):
        for x in range(0, planes, 8):
            at = offset + s * planes + x
            edge_ref[at : at + 8] = flat_ref[pl.ds((x * species + s) * rows + row, 8, stride=species * rows), :]


def interpolate(ref, slot, part, store):
    _, species, half, lanes = ref.shape
    lane = lax.broadcasted_iota(jnp.int32, (half, lanes), 1)
    row = lax.broadcasted_iota(jnp.int32, (half, lanes), 0)
    sign = jnp.where(lane % 2 == 0, -0.25, 0.25)
    lane_first = lane % (lanes // 2) == 0
    lane_last = lane % (lanes // 2) == lanes // 2 - 1
    index = part * (lanes // 2) + lane // 2
    for s in range(species):
        p = ref[slot, s]
        below = jnp.where(row == 0, p, pltpu.roll(p, 1, 0))
        above = jnp.where(row == half - 1, p, pltpu.roll(p, half - 1, 0))
        left = jnp.where(lane_first, p, pltpu.roll(p, 1, 1))
        right = jnp.where(lane_last, p, pltpu.roll(p, lanes - 1, 1))
        slope_y = 0.125 * (above - below)
        slope_z = 0.5 * (right - left)
        gz = jnp.take_along_axis(slope_z, index, axis=1) * sign
        even = jnp.take_along_axis(p - slope_y, index, axis=1) + gz
        odd = jnp.take_along_axis(p + slope_y, index, axis=1) + gz
        store(s, even, odd)


def build_kernel(shape, fine_at_ref, coarse_at_ref, first_ref, out_ref, ylow_ref, yhigh_ref, xlow_ref, xhigh_ref):
    planes, species, rows, lanes = shape
    half = rows // 2

    def body(c, carry):
        at = [fine_at_ref[2 * c], fine_at_ref[2 * c + 1]]
        code = coarse_at_ref[c]
        unit = code // 2 % (DIRECT + EXTRA)

        @pl.when(((at[0] < 0) | (at[1] < 0)) & (unit < DIRECT))
        def _():
            def store(s, even, odd):
                for child in range(2):
                    base = pl.multiple_of(((2 * c + child) * species + s) * rows, rows)
                    out_ref[pl.ds(base, half, stride=2), :] = even
                    out_ref[pl.ds(base + 1, half, stride=2), :] = odd

            interpolate(first_ref, code // 2 // (DIRECT + EXTRA) * DIRECT + unit, code % 2, store)

        for child in range(2):
            for h in range(2):
                late = 2 * (at[child] % FINE_CAP) + h

                @pl.when((at[child] >= 0) & (late < DIRECT))
                def _():
                    slot = at[child] // FINE_CAP * DIRECT + late
                    for s in range(species):
                        base = pl.multiple_of(((2 * c + child) * species + s) * rows + h * half, half)
                        out_ref[pl.ds(base, half), :] = first_ref[slot, s]

        return carry

    lax.fori_loop(0, planes // 2, body, 0)
    for r in range(ITERS):
        rows_to_edges(out_ref, ylow_ref, r * species * planes, r, planes, species, rows)
        rows_to_edges(out_ref, yhigh_ref, r * species * planes, rows - ITERS + r, planes, species, rows)
    deep = ITERS * species * rows
    xlow_ref[...] = out_ref[0:deep]
    xhigh_ref[...] = out_ref[planes * species * rows - deep : planes * species * rows]


def late_units(shape, me_ref, column_ref, left_ref, fine_at_ref, coarse_at_ref, second_ref, rest_ref, held_ref,
               plane_ref, sem, half_plane, whole_plane):
    planes, _, rows, _ = shape
    half = rows // 2
    devices = column_ref.shape[0]
    planned = left_ref[0] == 0

    def relayed(source, unit):
        return (source + me_ref[0] + column_ref[source, jnp.maximum(unit - DIRECT, 0)] // 8) % devices

    def bring(source, unit):
        copy = pltpu.make_async_copy(
            rest_ref.at[pl.ds(source * EXTRA + jnp.maximum(unit - DIRECT, 0), 1)], held_ref, sem
        )
        copy.start()
        copy.wait()

    def parent(c, carry):
        at = [fine_at_ref[2 * c], fine_at_ref[2 * c + 1]]
        code = coarse_at_ref[c]
        unit = code // 2 % (DIRECT + EXTRA)
        source = code // 2 // (DIRECT + EXTRA)

        @pl.when(((at[0] < 0) | (at[1] < 0)) & (unit >= DIRECT))
        def _():
            def store(s, even, odd):
                plane_ref[s, pl.ds(0, half, stride=2), :] = even
                plane_ref[s, pl.ds(1, half, stride=2), :] = odd

            @pl.when(planned)
            def _():
                held_ref[0] = second_ref[relayed(source, unit)]

            @pl.when(jnp.logical_not(planned))
            def _():
                bring(source, unit)

            interpolate(held_ref, 0, code % 2, store)
            for child in range(2):

                @pl.when(at[child] < 0)
                def _():
                    whole_plane(2 * c + child)

        return carry

    lax.fori_loop(0, planes // 2, parent, 0)

    def plane(x, carry):
        at = fine_at_ref[x]

        @pl.when((at >= 0) & (2 * (at % FINE_CAP) + 1 >= DIRECT))
        def _():
            for h in range(2):
                unit = 2 * (at % FINE_CAP) + h

                @pl.when((unit >= DIRECT) & planned)
                def _():
                    half_plane(x, h, second_ref, relayed(at // FINE_CAP, unit))

                @pl.when((unit >= DIRECT) & jnp.logical_not(planned))
                def _():
                    bring(at // FINE_CAP, unit)
                    half_plane(x, h, held_ref, 0)

        return carry

    lax.fori_loop(0, planes, plane, 0)


def edges_kernel(
    shape, me_ref, column_ref, left_ref, fine_at_ref, coarse_at_ref, second_ref, rest_ref,
    ylow_in_ref, yhigh_in_ref, xlow_in_ref, xhigh_in_ref,
    ylow_ref, yhigh_ref, xlow_ref, xhigh_ref, held_ref, plane_ref, sem,
):
    planes, species, rows, _ = shape
    half = rows // 2
    size = species * rows
    ylow_ref[...] = ylow_in_ref[...]
    yhigh_ref[...] = yhigh_in_ref[...]
    xlow_ref[...] = xlow_in_ref[...]
    xhigh_ref[...] = xhigh_in_ref[...]

    def half_edges(x, h, value):
        edge_ref, first = ((ylow_ref, 0), (yhigh_ref, half - ITERS))[h]
        for s in range(species):
            for r in range(ITERS):
                edge_ref[pl.ds((r * species + s) * planes + x, 1), :] = value(s, slice(first + r, first + r + 1))
        for near, xedge_ref, at in ((x < ITERS, xlow_ref, x), (x >= planes - ITERS, xhigh_ref, x - planes + ITERS)):

            @pl.when(near)
            def _():
                for s in range(species):
                    base = pl.multiple_of(at * size + s * rows + h * half, half)
                    xedge_ref[pl.ds(base, half), :] = value(s, slice(0, half))

    def half_plane(x, h, ref, slot):
        half_edges(x, h, lambda s, part: ref[slot, s, part])

    def whole_plane(x):
        for h in range(2):
            half_edges(x, h, lambda s, part: plane_ref[s, h * half + part.start : h * half + part.stop])

    late_units(
        shape, me_ref, column_ref, left_ref, fine_at_ref, coarse_at_ref, second_ref, rest_ref, held_ref, plane_ref,
        sem, half_plane, whole_plane,
    )


def corners_kernel(planes, species, ylow_ref, yhigh_ref, xlow_ref, xhigh_ref, down_ref, up_ref):
    deep = xlow_ref.shape[0]
    down_ref[0:deep] = xlow_ref[...]
    up_ref[0:deep] = xhigh_ref[...]
    for message_ref, x in ((down_ref, 0), (up_ref, planes - 1)):
        for s in range(species):
            low = ((ITERS - 1) * species + s) * planes + x
            high = s * planes + x
            message_ref[deep + s : deep + s + 1] = ylow_ref[low : low + 1]
            message_ref[deep + 16 + s : deep + 16 + s + 1] = yhigh_ref[high : high + 1]
        for at in (deep + species, deep + 16 + species):
            message_ref[at : at + 16 - species] = jnp.zeros((16 - species, message_ref.shape[1]), jnp.float32)


def velocity_edges_kernel(vel_ref, ylow_ref, yhigh_ref, xlow_ref, xhigh_ref, *, shape):
    planes, directions, rows, _ = shape
    size = directions * rows
    rows_to_edges(vel_ref, ylow_ref, 0, 0, planes, directions, rows)
    rows_to_edges(vel_ref, yhigh_ref, 0, rows - 1, planes, directions, rows)
    xlow_ref[...] = vel_ref[0:size]
    xhigh_ref[...] = vel_ref[(planes - 1) * size : planes * size]


class Flow:
    def __init__(self, velocity):
        self.positive = [jnp.maximum(v, 0.0) for v in velocity]
        self.negative = [jnp.minimum(v, 0.0) for v in velocity]
        self.keep = 1.0
        for low, high in zip(self.positive, self.negative):
            self.keep = self.keep - (low - high)

    def step(self, u, neighbours, d):
        new = u * (self.keep - 6.0 * d)
        for k, (low, high) in enumerate(neighbours):
            new = new + low * (d + self.positive[k]) + high * (d - self.negative[k])
        return new


def steps_kernel(
    shape, me_ref, column_ref, left_ref, fine_at_ref, coarse_at_ref, inside_ref, diff_ref, second_ref, rest_ref, state_ref,
    vel_ref, ylow_own_ref, yhigh_own_ref, ylow_ref, yhigh_ref, xlow_ref, xhigh_ref, vylow_ref, vyhigh_ref, vxlow_ref,
    vxhigh_ref, out_ref, u0_ref, u1_ref, row_low_ref, row_high_ref, plane_low_ref, plane_high_ref, held_ref, plane_ref, sem,
    out_sem,
):
    planes, species, rows, lanes = shape
    half = rows // 2
    size = species * rows
    copy = pltpu.make_async_copy(state_ref, u0_ref, sem)
    copy.start()
    copy.wait()

    def half_plane(x, h, ref, slot):
        for s in range(species):
            base = pl.multiple_of(x * size + s * rows + h * half, half)
            u0_ref[pl.ds(base, half), :] = ref[slot, s]

    def whole_plane(x):
        for s in range(species):
            u0_ref[pl.ds(pl.multiple_of(x * size + s * rows, rows), rows), :] = plane_ref[s]

    late_units(
        shape, me_ref, column_ref, left_ref, fine_at_ref, coarse_at_ref, second_ref, rest_ref, held_ref, plane_ref,
        sem, half_plane, whole_plane,
    )

    def along(u, first, last, dim):
        count = u.shape[dim]
        at = lax.broadcasted_iota(jnp.int32, u.shape, dim)
        low = jnp.where(at == 0, first, pltpu.roll(u, 1, dim))
        high = jnp.where(at == count - 1, last, pltpu.roll(u, count - 1, dim))
        return low, high

    deep = ITERS * size
    for (near_ref, near, far, own_ref, own, v_ref, corner, target_ref, inside) in (
        (ylow_ref, 1, 0, ylow_own_ref, 0, vylow_ref, deep, row_low_ref, 0),
        (yhigh_ref, 0, 1, yhigh_own_ref, 1, vyhigh_ref, deep + 16, row_high_ref, 1),
    ):
        for x in range(0, planes, 16):
            flow = Flow([v_ref[k * planes + x : k * planes + x + 16] for k in range(3)])
            for s in range(species):

                def band(ref, r):
                    start = (r * species + s) * planes + x
                    return ref[start : start + 16]

                u = band(near_ref, near)
                start = (near * species + s) * planes
                if x == 0:
                    first = xlow_ref[corner + s : corner + s + 1]
                else:
                    first = near_ref[start + x - 1 : start + x]
                if x + 16 == planes:
                    last = xhigh_ref[corner + s : corner + s + 1]
                else:
                    last = near_ref[start + x + 16 : start + x + 17]
                outer, inner = band(near_ref, far), band(own_ref, own)
                across = (outer, inner) if inside == 0 else (inner, outer)
                new = flow.step(u, (along(u, first, last, 0), across, along(u, u, u, 1)), diff_ref[s])
                target_ref[s * planes + x : s * planes + x + 16] = new * inside_ref[inside]

    def at(ref, x):
        return lambda s: ref[pl.ds(pl.multiple_of(x * size + s * rows, rows), rows), :]

    def edge(ref, offset, x):
        return lambda s: ref[pl.ds(offset + s * planes + x, 1), :]

    def plane(velocity, center, below, above, y_low, y_high, store):
        flow = Flow(velocity)
        for s in range(species):
            u = center(s)
            sides = ((below(s), above(s)), along(u, y_low(s), y_high(s), 0), along(u, u, u, 1))
            store(s, flow.step(u, sides, diff_ref[s]))

    for (halo_ref, near, below, above, v_ref, target_ref, inside) in (
        (xlow_ref, 1, at(xlow_ref, 0), at(u0_ref, 0), vxlow_ref, plane_low_ref, 2),
        (xhigh_ref, 0, at(u0_ref, planes - 1), at(xhigh_ref, 1), vxhigh_ref, plane_high_ref, 3),
    ):

        def store(s, new):
            target_ref[s * rows : (s + 1) * rows] = new * inside_ref[inside]

        def corner(offset):
            return lambda s: halo_ref[deep + offset + s : deep + offset + s + 1]

        velocity = [v_ref[k * rows : (k + 1) * rows] for k in range(3)]
        plane(velocity, at(halo_ref, near), below, above, corner(0), corner(16), store)

    def advance(u_ref, new_ref, low, high, y_low, y_high, after):
        def group(x, first, last):
            for i in range(UNROLL):

                def store(s, new):
                    new_ref[pl.ds(pl.multiple_of((x + i) * size + s * rows, rows), rows), :] = new

                plane(
                    [vel_ref[x + i, k] for k in range(3)],
                    at(u_ref, x + i),
                    low if first and i == 0 else at(u_ref, x + i - 1),
                    high if last and i == UNROLL - 1 else at(u_ref, x + i + 1),
                    edge(*y_low, x + i),
                    edge(*y_high, x + i),
                    store,
                )
            after(x // UNROLL)

        def body(g, carry):
            group(g * UNROLL, False, False)
            return carry

        group(0, True, False)
        lax.fori_loop(1, planes // UNROLL - 1, body, 0)
        group(planes - UNROLL, False, True)

    def send(g):
        part = pl.ds(pl.multiple_of(g * UNROLL * size, UNROLL * size), UNROLL * size)
        return pltpu.make_async_copy(u0_ref.at[part], out_ref.at[part], out_sem.at[g])

    advance(
        u0_ref, u1_ref, at(xlow_ref, 1), at(xhigh_ref, 0), (ylow_ref, species * planes), (yhigh_ref, 0), lambda g: None
    )
    advance(
        u1_ref, u0_ref, at(plane_low_ref, 0), at(plane_high_ref, 0), (row_low_ref, 0), (row_high_ref, 0),
        lambda g: send(g).start(),
    )

    def finish(g, carry):
        send(g).wait()
        return carry

    lax.fori_loop(0, planes // UNROLL, finish, 0)


def empty_kernel(out_ref):
    pass


def cost(microseconds):
    return pl.CostEstimate(flops=0, bytes_accessed=int(microseconds * 3.6e6), transcendentals=0)


def neighbours(axis, low, high):
    size = lax.axis_size(axis)
    up = [(i, (i + 1) % size) for i in range(size - 1)]
    return lax.ppermute(high, axis, up), lax.ppermute(low, axis, [(b, a) for a, b in up])


def on_device(old_fine, old_ids, old_coarse, coarse_ids, velocity, diffusion):
    devices = lax.axis_size("dev")
    me = lax.axis_index("dev")
    me_ref = me.reshape(1).astype(jnp.int32)
    planes, species, rows, lanes = old_fine.shape
    half = rows // 2
    coarse_planes = old_coarse.shape[0]
    unit_count = DIRECT + EXTRA
    f32 = jnp.float32
    i32 = jnp.int32

    def units_shape(count):
        return jax.ShapeDtypeStruct((count, species, half, lanes), f32)

    own, own_coarse = old_ids[0], coarse_ids[0]
    labels = jnp.broadcast_to(jnp.concatenate([own, own_coarse])[None], (devices, planes + coarse_planes))
    labels = lax.all_to_all(labels, "dev", split_axis=0, concat_axis=0, tiled=True)
    all_ids, all_coarse = labels[:, :planes], labels[:, planes:]
    all_box = jnp.where(all_ids >= 0, all_ids // planes, -1)
    all_coarse_box = all_coarse // coarse_planes
    flat_parents = jnp.where(all_ids >= 0, all_ids // 2, -1).reshape(-1)

    def needed(coarse):
        kept = jnp.sum((flat_parents == coarse[..., None]).astype(i32), axis=-1)
        return kept < 2

    box = jnp.arange(lanes) % devices
    fine_units = jnp.sum((all_box[:, None, :] == box[None, :, None]).astype(i32), axis=-1)
    asked = needed(all_coarse)[:, None, :] & (all_coarse_box[:, None, :] == box[None, :, None])
    units = 2 * fine_units + jnp.max(asked.astype(i32), axis=-1)
    row, column = pl.pallas_call(
        plan_kernel,
        out_shape=[jax.ShapeDtypeStruct((8, lanes), i32), jax.ShapeDtypeStruct((devices, lanes), i32)],
        in_specs=[SMEM, VMEM],
        out_specs=[VMEM] * 2,
        name="plan",
    )(me_ref, units)
    left = jnp.max(row[EXTRA, :devices]).reshape(1)

    own_box = jnp.where(own >= 0, own // planes, -1)
    send_fine = jnp.where(own >= 0, own_box * FINE_CAP + ranks(own_box), -1)
    own_coarse_box = own_coarse // coarse_planes
    before = jnp.sum((own_box[None, :] == own_coarse_box[:, None]).astype(i32), axis=1)
    send_coarse = (own_coarse_box * unit_count + 2 * before) * 2 + ranks(own_coarse_box)
    send_coarse = jnp.where(needed(own_coarse), send_coarse, -1)

    order = jnp.arange(devices)[:, None]
    wanted = me * planes + jnp.arange(planes)
    fine_at = jnp.where(all_ids[None] == wanted[:, None, None], (order * FINE_CAP + ranks(all_box))[None], -1)
    fine_at = jnp.max(fine_at, axis=(1, 2))
    to_me = jnp.sum((all_box == me).astype(i32), axis=1, keepdims=True)
    coarse_wanted = me * coarse_planes + jnp.arange(coarse_planes)
    coarse_code = (order * unit_count + 2 * to_me) * 2 + ranks(all_coarse_box)
    coarse_at = jnp.where(all_coarse[None] == coarse_wanted[:, None, None], coarse_code[None], 0)
    coarse_at = jnp.max(coarse_at, axis=(1, 2))

    def exchange(value):
        return lax.all_to_all(value, "dev", split_axis=0, concat_axis=0, tiled=True)

    def pack(count, slot_of, name):
        return pl.pallas_call(
            functools.partial(pack_kernel, devices, slot_of),
            out_shape=units_shape(count),
            in_specs=[SMEM] * 4 + [VMEM] * 2,
            out_specs=VMEM,
            compiler_params=PARAMS,
            name=name,
        )(me_ref, send_fine, send_coarse, row, old_fine, old_coarse)

    packed = pack(devices * DIRECT, functools.partial(first_slot, devices), "pack")

    def no_rest():
        return pl.pallas_call(empty_kernel, out_shape=units_shape(devices * EXTRA), out_specs=ANY, name="nothing")()

    def rest_direct():
        return exchange(pack(devices * EXTRA, direct_slot, "pack_rest"))

    rest = lax.cond(left[0] == 0, no_rest, rest_direct)
    packed, rest, flow = lax.optimization_barrier((packed, rest, velocity))
    first = exchange(packed)

    def edge_shapes(deep, count):
        along_y = jax.ShapeDtypeStruct((deep * count * planes, lanes), f32)
        along_x = jax.ShapeDtypeStruct((deep * count * rows, lanes), f32)
        return [along_y, along_y, along_x, along_x]

    directions = flow.shape[1]
    vylow, vyhigh, vxlow, vxhigh = pl.pallas_call(
        functools.partial(velocity_edges_kernel, shape=flow.shape),
        out_shape=edge_shapes(1, directions),
        in_specs=[VMEM],
        out_specs=[VMEM] * 4,
        compiler_params=PARAMS,
        name="velocity_edges",
    )(flow.reshape(planes * directions * rows, lanes))
    flow_edges = [*neighbours("grp", vylow, vyhigh), *neighbours("dev", vxlow, vxhigh)]
    first, *flow_edges = lax.optimization_barrier((first, *flow_edges))
    second = pl.pallas_call(
        forward_kernel,
        out_shape=units_shape(devices),
        in_specs=[SMEM] * 2 + [VMEM],
        out_specs=VMEM,
        compiler_params=PARAMS,
        cost_estimate=cost(3),
        name="forward",
    )(me_ref, column, first)
    second = exchange(second)

    size = species * rows
    state_shape = jax.ShapeDtypeStruct((planes * size, lanes), f32)
    state, *edges = pl.pallas_call(
        functools.partial(build_kernel, old_fine.shape),
        out_shape=[state_shape] + edge_shapes(ITERS, species),
        in_specs=[SMEM] * 2 + [VMEM],
        out_specs=[VMEM] * 5,
        compiler_params=PARAMS,
        cost_estimate=cost(10),
        name="build",
    )(fine_at, coarse_at, first)
    late_scratch = [
        pltpu.VMEM((1, species, half, lanes), f32),
        pltpu.VMEM((species, rows, lanes), f32),
        pltpu.SemaphoreType.DMA,
    ]
    ylow_own, yhigh_own, xlow_own, xhigh_own = pl.pallas_call(
        functools.partial(edges_kernel, old_fine.shape),
        out_shape=edge_shapes(ITERS, species),
        in_specs=[SMEM] * 5 + [VMEM, ANY] + [VMEM] * 4,
        out_specs=[VMEM] * 4,
        scratch_shapes=late_scratch,
        compiler_params=PARAMS,
        cost_estimate=cost(4),
        name="edges",
    )(me_ref, column, left, fine_at, coarse_at, second, rest, *edges)
    ylow, yhigh = neighbours("grp", ylow_own, yhigh_own)
    message = jax.ShapeDtypeStruct((ITERS * size + 32, lanes), f32)
    down, up = pl.pallas_call(
        functools.partial(corners_kernel, planes, species),
        out_shape=[message] * 2,
        in_specs=[VMEM] * 4,
        out_specs=[VMEM] * 2,
        compiler_params=PARAMS,
        name="corners",
    )(ylow, yhigh, xlow_own, xhigh_own)
    xlow, xhigh = neighbours("dev", down, up)
    grp, dev = lax.axis_index("grp"), lax.axis_index("dev")
    inside = jnp.stack([grp > 0, grp < lax.axis_size("grp") - 1, dev > 0, dev < devices - 1]).astype(f32)
    row_edge = pltpu.VMEM((species * planes, lanes), f32)
    plane_edge = pltpu.VMEM((size, lanes), f32)
    done = pl.pallas_call(
        functools.partial(steps_kernel, old_fine.shape),
        out_shape=state_shape,
        in_specs=[SMEM] * 7 + [VMEM, ANY, ANY] + [VMEM] * 11,
        out_specs=ANY,
        scratch_shapes=[pltpu.VMEM(state_shape.shape, f32)] * 2
        + [row_edge] * 2
        + [plane_edge] * 2
        + late_scratch
        + [pltpu.SemaphoreType.DMA((planes // UNROLL,))],
        compiler_params=PARAMS,
        name="steps",
    )(
        me_ref, column, left, fine_at, coarse_at, inside, diffusion, second, rest, state, velocity,
        ylow_own, yhigh_own, ylow, yhigh, xlow, xhigh, *flow_edges,
    )
    return done.reshape(old_fine.shape)


def solution(mesh):
    in_specs = (
        P("dev", None, "grp", None),
        P("grp", "dev"),
        P("dev", None, "grp", None),
        P("grp", "dev"),
        P("dev", None, "grp", None),
        P(),
    )
    out_specs = P("dev", None, "grp", None)
    return jax.shard_map(
        on_device, mesh=mesh, in_specs=in_specs, out_specs=out_specs, check_vma=False
    )
```

time: 291 us -> 278 us (0.955)
  blocking collectives: 41 us -> 0 us
  waiting for transfers between devices: 133 us -> 143 us
  Pallas kernels: 51.2 us -> 59.5 us
  starting transfers between devices: 45.2 us -> 53.4 us
    ppermute x8, waiting for transfers between devices: 5.09 us -> 125 us  [the longest x4 117 us: neighbours(): lax.ppermute(high, axis, up)]
    all_to_all x1 -> x2, waiting for transfers between devices: 124 us -> 14.5 us  [exchange(): return lax.all_to_all(value, 'dev', split_axis=0, concat_axis=0, tiled=True)]
    all_to_all x1 -> x0, blocking collectives: 41 us -> none  [build(): lax.all_to_all(second, 'dev', split_axis=0, concat_axis=0, tiled=True)]
    all_to_all x1 -> x2, starting transfers between devices: 6.59 us -> 15.8 us  [exchange(): return lax.all_to_all(value, 'dev', split_axis=0, concat_axis=0, tiled=True)]
    pallas_call x4 -> x7, Pallas kernels: 36.6 us -> 44.4 us  [the longest x1 19 us: on_device(): pl.pallas_call(functools.partial(steps_kernel, old_fine.shape), out_shape...]
  transfers between devices with their start and end apart: 10 -> 11, of which waited for: 6 -> 8; matrix products, arithmetic and copies ran while one was open for 3% -> 3% of each run, Pallas kernels for 0% -> 5%
where the time goes in v5:
time: 278 us; the launch traced here: 276 us
  waiting for transfers between devices  143 us (51%)
  Pallas kernels  59.5 us (21%)
  starting transfers between devices  53.4 us (19%)
  other arithmetic  15 us (5%)
  local copies, waits for them, and re-layouts  3.26 us (1%)
    ppermute x4, waiting for transfers between devices, neighbours(): lax.ppermute(high, axis, up)  117 us
    pallas_call x1, Pallas kernels, on_device(): pl.pallas_call(functools.partial(steps_kernel, old_fine.shape), out_shape...  19 us
    all_to_all x2, starting transfers between devices, exchange(): return lax.all_to_all(value, 'dev', split_axis=0, concat_axis=0, tiled=True)  15.8 us
    all_to_all x2, waiting for transfers between devices, exchange(): return lax.all_to_all(value, 'dev', split_axis=0, concat_axis=0, tiled=True)  14.5 us
    ppermute x4, starting transfers between devices, neighbours(): lax.ppermute(low, axis, [(b, a) for a, b in up])  13.6 us
    ppermute x4, starting transfers between devices, neighbours(): lax.ppermute(high, axis, up)  12.3 us
    all_to_all x1, starting transfers between devices, on_device(): lax.all_to_all(labels, 'dev', split_axis=0, concat_axis=0, tiled=True)  11.6 us
    pallas_call x1, Pallas kernels, on_device(): pl.pallas_call(functools.partial(build_kernel, old_fine.shape), out_shape...  10.7 us
  transfers between devices with their start and end apart: 11, of which 8 were waited for; matrix products, arithmetic and copies ran while one was open for 3% of the time, Pallas kernels for 5%

profile of v5, /device:TPU:22, one launch (start us, length us, event | category | flops | bytes accessed | tf_op | source)
XLA Modules:
  0.0 275.6 jit_solution(17981119054653224042)
XLA Ops:
  0.0 0.7 pad_add_fusion
  0.7 0.6 broadcast_in_dim.26
  1.4 11.6 %all-to-all-start.1 = ((s32[32,1,96]{2,1,0:T(1,128)}), s32[32,1,96]{2,1,0:T(1,128)S(1)}, u32[]{:S(2)}, u32[]{:S(2)}) async-start(s32[32,1,96]{2,1,0:T(1,128)} %broadcast_in_dim.26), calls=%async_computation.1 | async-start | bytes 32768 | tf_op jit(solution)/shard_map/all_to_all | solution.py:511
  13.0 0.7 fusion.9
  13.6 0.7 and_select_fusion.1
  14.3 0.7 compare_select_fusion.15
  15.0 0.7 fusion.8
  16.0 0.7 compare_select_fusion.14.fine_at_ref
  16.9 3.9 %all-to-all-done.1 = s32[32,1,96]{2,1,0:T(1,128)S(1)} async-done(((s32[32,1,96]{2,1,0:T(1,128)}), s32[32,1,96]{2,1,0:T(1,128)S(1)}, u32[]{:S(2)}, u32[]{:S(2)}) %all-to-all-start.1) | async-done | bytes 12320 | tf_op jit(solution)/shard_map/all_to_all | solution.py:511
  21.1 0.9 convert_reduce_fusion.5
  22.0 1.1 convert_reduce_fusion
  23.4 0.4 convert_reduce_fusion.4
  23.8 0.6 multiply_add_fusion.units_ref
  24.4 4.6 %plan.1 = (s32[8,128]{1,0:T(8,128)S(1)}, s32[32,128]{1,0:T(8,128)}) custom-call(s32[1]{0:T(128)} %bitcast.me_ref, s32[32,128]{1,0:T(8,128)} %multiply_add_fusion.units_ref), custom_call_target="tpu_custom_call" | custom-call | tf_op jit(solution)/shard_map/plan/pallas_call | solution.py:525
  29.0 0.7 slice_reduce_fusion
  29.6 0.7 compare_select_fusion.coarse_at_ref
  30.3 10.5 %pack.1 = f32[160,9,8,128]{3,2,1,0:T(8,128)} custom-call(s32[1]{0:T(128)} %bitcast.me_ref, s32[64]{0:T(128)S(1)} %compare_select_fusion.14.fine_at_ref, s32[32]{0:T(128)S(1)} %compare_select_fusion.coarse_at_ref, s32[8,128]{1,0:T(8,128)S(1)} %get-tuple-element.52.row_ref, f32[64,9,16,128]{3,2,1,0:T(8,128)} %fine_ref.1, f32[32,9,8,64]{3,2,1,0:T(8,128)} %coarse_ref.1), custom_call_target="tpu_custom_call" | custom-call | tf_op jit(solution)/shard_map/pack/pallas_call | solution.py:555
  41.5 6.7 %all-to-all-start.2 = ((f32[160,9,8,128]{3,2,1,0:T(8,128)}), f32[160,9,8,128]{3,2,1,0:T(8,128)}, u32[]{:S(2)}, u32[]{:S(2)}) async-start(f32[160,9,8,128]{3,2,1,0:T(8,128)} %pack.1), calls=%async_computation.2 | async-start | bytes 11796480 | tf_op jit(solution)/shard_map/all_to_all | solution.py:552
  48.2 2.2 velocity_edges.1
  50.3 1.9 collective-permute-start
  52.3 3.6 %collective-permute-start.1 = (f32[192,128]{1,0:T(8,128)}, f32[192,128]{1,0:T(8,128)S(1)}, u32[]{:S(2)}, u32[]{:S(2)}) collective-permute-start(f32[192,128]{1,0:T(8,128)} %get-tuple-element.56), channel_id=1, source_target_pairs={{32,0},{64,32},{96,64},{128,96},{160,128},{192,160},{224,192},{33,... | collective-permute-start | bytes 294920 | tf_op jit(solution)/shard_map/ppermute | solution.py:492
  55.9 3.4 %collective-permute-start.2 = (f32[48,128]{1,0:T(8,128)}, f32[48,128]{1,0:T(8,128)S(1)}, u32[]{:S(2)}, u32[]{:S(2)}) collective-permute-start(f32[48,128]{1,0:T(8,128)} %get-tuple-element.57), channel_id=1, source_target_pairs={{0,1},{1,2},{2,3},{3,4},{4,5},{5,6},{6,7},{7,8},{8,9},{9,10},{10,1... | collective-permute-start | bytes 73736 | tf_op jit(solution)/shard_map/ppermute | solution.py:492
  59.3 4.6 %collective-permute-start.3 = (f32[48,128]{1,0:T(8,128)}, f32[48,128]{1,0:T(8,128)S(1)}, u32[]{:S(2)}, u32[]{:S(2)}) collective-permute-start(f32[48,128]{1,0:T(8,128)} %get-tuple-element.58), channel_id=1, source_target_pairs={{1,0},{2,1},{3,2},{4,3},{5,4},{6,5},{7,6},{8,7},{9,8},{10,9},{11,1... | collective-permute-start | bytes 73736 | tf_op jit(solution)/shard_map/ppermute | solution.py:492
  63.9 112.5 %collective-permute-done.2.vxlow_ref = f32[48,128]{1,0:T(8,128)S(1)} collective-permute-done((f32[48,128]{1,0:T(8,128)}, f32[48,128]{1,0:T(8,128)S(1)}, u32[]{:S(2)}, u32[]{:S(2)}) %collective-permute-start.2) | collective-permute-done | bytes 24608 | tf_op jit(solution)/shard_map/ppermute | solution.py:492
  176.4 1.5 all-to-all-done.2.in_ref.first_ref
  177.9 4.3 %forward.1 = f32[32,9,8,128]{3,2,1,0:T(8,128)} custom-call(s32[1]{0:T(128)} %bitcast.me_ref, s32[32,128]{1,0:T(8,128)} %get-tuple-element.51.column_ref, f32[160,9,8,128]{3,2,1,0:T(8,128)} %all-to-all-done.2.in_ref.first_ref), custom_call_target="tpu_custom_call" | custom-call | bytes 10800000 | tf_op jit(solution)/shard_map/forward/pallas_call | solution.py:592
  182.2 9.2 %all-to-all-start.3 = ((f32[32,9,8,128]{3,2,1,0:T(8,128)}), f32[32,9,8,128]{3,2,1,0:T(8,128)S(1)}, u32[]{:S(2)}, u32[]{:S(2)}) async-start(f32[32,9,8,128]{3,2,1,0:T(8,128)} %forward.1), calls=%async_computation.3 | async-start | bytes 2359296 | tf_op jit(solution)/shard_map/all_to_all | solution.py:552
  191.4 0.8 convert_reduce_fusion.3
  192.3 1.2 select_reduce_fusion.1.coarse_at_ref
  193.6 0.9 convert_reduce_fusion.1
  194.6 1.9 select_reduce_fusion.fine_at_ref
  196.5 10.7 %build.1 = (f32[9216,128]{1,0:T(8,128)}, f32[1152,128]{1,0:T(8,128)}, f32[1152,128]{1,0:T(8,128)}, f32[288,128]{1,0:T(8,128)}, f32[288,128]{1,0:T(8,128)}) custom-call(s32[64]{0:T(128)} %select_reduce_fusion.fine_at_ref, s32[32]{0:T(128)} %select_reduce_fusion.1.coarse_at_ref, f32[160,9,8,128]{3,2,1,0:T(8,128)} %all-to-all-done.2.in_ref.first_ref), custom_call_target="tpu_custom_call" | custom-call | bytes 36000000 | tf_op jit(solution)/shard_map/build/pallas_call | solution.py:605
  207.2 13.0 %all-to-all-done.3.second_ref = f32[32,9,8,128]{3,2,1,0:T(8,128)S(1)} async-done(((f32[32,9,8,128]{3,2,1,0:T(8,128)}), f32[32,9,8,128]{3,2,1,0:T(8,128)S(1)}, u32[]{:S(2)}, u32[]{:S(2)}) %all-to-all-start.3) | async-done | bytes 1179680 | tf_op jit(solution)/shard_map/all_to_all | solution.py:552
  220.2 1.0 copy-done
  221.3 6.1 %edges.1 = (f32[1152,128]{1,0:T(8,128)}, f32[1152,128]{1,0:T(8,128)}, f32[288,128]{1,0:T(8,128)}, f32[288,128]{1,0:T(8,128)}) custom-call(s32[1]{0:T(128)} %bitcast.me_ref, s32[32,128]{1,0:T(8,128)} %get-tuple-element.51.column_ref, s32[1]{0:T(128)} %bitcast.4.left_ref, s32[64]{0:T(128)} %select_reduce_fusion.fine_at_ref, ...), custom_call_target="tpu_custom_call" | custom-call | bytes 14400000 | tf_op jit(solution)/shard_map/edges/pallas_call | solution.py:619
  227.4 1.9 collective-permute-start.5
  229.3 2.4 collective-permute-start.4
  231.7 5.3 %collective-permute-done.5.yhigh_ref = f32[1152,128]{1,0:T(8,128)S(1)} collective-permute-done((f32[1152,128]{1,0:T(8,128)}, f32[1152,128]{1,0:T(8,128)S(1)}, u32[]{:S(2)}, u32[]{:S(2)}) %collective-permute-start.5) | collective-permute-done | bytes 589856 | tf_op jit(solution)/shard_map/ppermute | solution.py:492
  237.0 3.8 %collective-permute-done.4.ylow_ref = f32[1152,128]{1,0:T(8,128)S(1)} collective-permute-done((f32[1152,128]{1,0:T(8,128)}, f32[1152,128]{1,0:T(8,128)S(1)}, u32[]{:S(2)}, u32[]{:S(2)}) %collective-permute-start.4) | collective-permute-done | bytes 589856 | tf_op jit(solution)/shard_map/ppermute | solution.py:492
  240.9 0.8 copy-done.3
  241.7 2.1 corners.1
  243.8 4.6 %collective-permute-start.6 = (f32[320,128]{1,0:T(8,128)}, f32[320,128]{1,0:T(8,128)S(1)}, u32[]{:S(2)}, u32[]{:S(2)}) collective-permute-start(f32[320,128]{1,0:T(8,128)} %get-tuple-element.70), channel_id=1, source_target_pairs={{0,1},{1,2},{2,3},{3,4},{4,5},{5,6},{6,7},{7,8},{8,9},{9,10},{10,1... | collective-permute-start | bytes 491528 | tf_op jit(solution)/shard_map/ppermute | solution.py:492
  248.4 3.5 %collective-permute-start.7 = (f32[320,128]{1,0:T(8,128)}, f32[320,128]{1,0:T(8,128)S(1)}, u32[]{:S(2)}, u32[]{:S(2)}) collective-permute-start(f32[320,128]{1,0:T(8,128)} %get-tuple-element.71), channel_id=1, source_target_pairs={{1,0},{2,1},{3,2},{4,3},{5,4},{6,5},{7,6},{8,7},{9,8},{10,9},{11,1... | collective-permute-start | bytes 491528 | tf_op jit(solution)/shard_map/ppermute | solution.py:492
  251.9 0.6 add_convert_fusion.inside_ref
  252.5 1.0 collective-permute-done.6.xlow_ref
  253.5 2.3 collective-permute-done.7.xhigh_ref
  255.8 0.7 copy-done.5
  256.5 19.0 %steps.1 = f32[9216,128]{1,0:T(8,128)} custom-call(s32[1]{0:T(128)} %bitcast.me_ref, s32[32,128]{1,0:T(8,128)} %get-tuple-element.51.column_ref, s32[1]{0:T(128)} %bitcast.4.left_ref, s32[64]{0:T(128)} %select_reduce_fusion.fine_at_ref, s32[32]{0:T(128)} %select_reduce_fusion.1.coarse_at_ref, f32[4]{0:T(128)} %add_convert_fusion.inside_ref, f32[9]{0:T(128)} %diff_ref.1, ...), custom_call_target="tpu_custom_call" | custom-call | tf_op jit(solution)/shard_map/steps/pallas_call | solution.py:644
  (39 shorter events, 1.4 us)
Async XLA Ops:
  1.4 19.4 %all-to-all-start.1 = ((s32[32,1,96]{2,1,0:T(1,128)}), s32[32,1,96]{2,1,0:T(1,128)S(1)}, u32[]{:S(2)}, u32[]{:S(2)}) async-start(s32[32,1,96]{2,1,0:T(1,128)} %broadcast_in_dim.26), calls=%async_computation.1 | async-start | bytes 32768 | tf_op jit(solution)/shard_map/all_to_all | solution.py:511
  30.3 11.2 %copy-start.1 = (f32[32,9,8,64]{3,2,1,0:T(8,128)S(1)}, f32[32,9,8,64]{3,2,1,0:T(8,128)}, u32[]{:S(2)}) copy-start(f32[32,9,8,64]{3,2,1,0:T(8,128)} %coarse_ref.1) | copy-start | bytes 1769476
  41.5 136.4 %all-to-all-start.2 = ((f32[160,9,8,128]{3,2,1,0:T(8,128)}), f32[160,9,8,128]{3,2,1,0:T(8,128)}, u32[]{:S(2)}, u32[]{:S(2)}) async-start(f32[160,9,8,128]{3,2,1,0:T(8,128)} %pack.1), calls=%async_computation.2 | async-start | bytes 11796480 | tf_op jit(solution)/shard_map/all_to_all | solution.py:552
  50.3 126.0 %collective-permute-start = (f32[192,128]{1,0:T(8,128)}, f32[192,128]{1,0:T(8,128)S(1)}, u32[]{:S(2)}, u32[]{:S(2)}) collective-permute-start(f32[192,128]{1,0:T(8,128)} %get-tuple-element.55), channel_id=1, source_target_pairs={{0,32},{32,64},{64,96},{96,128},{128,160},{160,192},{192,224},{1,3... | collective-permute-start | bytes 294920 | tf_op jit(solution)/shard_map/ppermute | solution.py:492
  52.3 124.1 %collective-permute-start.1 = (f32[192,128]{1,0:T(8,128)}, f32[192,128]{1,0:T(8,128)S(1)}, u32[]{:S(2)}, u32[]{:S(2)}) collective-permute-start(f32[192,128]{1,0:T(8,128)} %get-tuple-element.56), channel_id=1, source_target_pairs={{32,0},{64,32},{96,64},{128,96},{160,128},{192,160},{224,192},{33,... | collective-permute-start | bytes 294920 | tf_op jit(solution)/shard_map/ppermute | solution.py:492
  55.9 120.4 %collective-permute-start.2 = (f32[48,128]{1,0:T(8,128)}, f32[48,128]{1,0:T(8,128)S(1)}, u32[]{:S(2)}, u32[]{:S(2)}) collective-permute-start(f32[48,128]{1,0:T(8,128)} %get-tuple-element.57), channel_id=1, source_target_pairs={{0,1},{1,2},{2,3},{3,4},{4,5},{5,6},{6,7},{7,8},{8,9},{9,10},{10,1... | collective-permute-start | bytes 73736 | tf_op jit(solution)/shard_map/ppermute | solution.py:492
  59.3 117.1 %collective-permute-start.3 = (f32[48,128]{1,0:T(8,128)}, f32[48,128]{1,0:T(8,128)S(1)}, u32[]{:S(2)}, u32[]{:S(2)}) collective-permute-start(f32[48,128]{1,0:T(8,128)} %get-tuple-element.58), channel_id=1, source_target_pairs={{1,0},{2,1},{3,2},{4,3},{5,4},{6,5},{7,6},{8,7},{9,8},{10,9},{11,1... | collective-permute-start | bytes 73736 | tf_op jit(solution)/shard_map/ppermute | solution.py:492
  176.3 5.9 %copy-start.8 = (f32[48,128]{1,0:T(8,128)}, f32[48,128]{1,0:T(8,128)S(1)}, u32[]{:S(2)}) copy-start(f32[48,128]{1,0:T(8,128)S(1)} %collective-permute-done.2.vxlow_ref) | copy-start | bytes 73732
  176.3 5.8 %copy-start.9 = (f32[48,128]{1,0:T(8,128)}, f32[48,128]{1,0:T(8,128)S(1)}, u32[]{:S(2)}) copy-start(f32[48,128]{1,0:T(8,128)S(1)} %collective-permute-done.3.vxhigh_ref) | copy-start | bytes 73732
  176.4 5.8 %copy-start.6 = (f32[192,128]{1,0:T(8,128)}, f32[192,128]{1,0:T(8,128)S(1)}, u32[]{:S(2)}) copy-start(f32[192,128]{1,0:T(8,128)S(1)} %collective-permute-done.vylow_ref) | copy-start | bytes 294916
  176.4 5.8 %copy-start.7 = (f32[192,128]{1,0:T(8,128)}, f32[192,128]{1,0:T(8,128)S(1)}, u32[]{:S(2)}) copy-start(f32[192,128]{1,0:T(8,128)S(1)} %collective-permute-done.1.vyhigh_ref) | copy-start | bytes 294916
  182.2 38.0 %all-to-all-start.3 = ((f32[32,9,8,128]{3,2,1,0:T(8,128)}), f32[32,9,8,128]{3,2,1,0:T(8,128)S(1)}, u32[]{:S(2)}, u32[]{:S(2)}) async-start(f32[32,9,8,128]{3,2,1,0:T(8,128)} %forward.1), calls=%async_computation.3 | async-start | bytes 2359296 | tf_op jit(solution)/shard_map/all_to_all | solution.py:552
  220.2 1.0 copy-start
  227.4 9.6 %collective-permute-start.5 = (f32[1152,128]{1,0:T(8,128)}, f32[1152,128]{1,0:T(8,128)S(1)}, u32[]{:S(2)}, u32[]{:S(2)}) collective-permute-start(f32[1152,128]{1,0:T(8,128)} %get-tuple-element.66.ylow_own_ref), channel_id=1, source_target_pairs={{32,0},{64,32},{96,64},{128,96},{160,128},{192,160},{224,192},{33,... | collective-permute-start | bytes 1769480 | tf_op jit(solution)/shard_map/ppermute | solution.py:492
  229.3 11.5 %collective-permute-start.4 = (f32[1152,128]{1,0:T(8,128)}, f32[1152,128]{1,0:T(8,128)S(1)}, u32[]{:S(2)}, u32[]{:S(2)}) collective-permute-start(f32[1152,128]{1,0:T(8,128)} %get-tuple-element.67.yhigh_own_ref), channel_id=1, source_target_pairs={{0,32},{32,64},{64,96},{96,128},{128,160},{160,192},{192,224},{1,3... | collective-permute-start | bytes 1769480 | tf_op jit(solution)/shard_map/ppermute | solution.py:492
  237.0 3.8 %copy-start.2 = (f32[1152,128]{1,0:T(8,128)}, f32[1152,128]{1,0:T(8,128)S(1)}, u32[]{:S(2)}) copy-start(f32[1152,128]{1,0:T(8,128)S(1)} %collective-permute-done.5.yhigh_ref) | copy-start | bytes 1769476
  240.9 0.8 copy-start.3
  243.8 9.7 %collective-permute-start.6 = (f32[320,128]{1,0:T(8,128)}, f32[320,128]{1,0:T(8,128)S(1)}, u32[]{:S(2)}, u32[]{:S(2)}) collective-permute-start(f32[320,128]{1,0:T(8,128)} %get-tuple-element.70), channel_id=1, source_target_pairs={{0,1},{1,2},{2,3},{3,4},{4,5},{5,6},{6,7},{7,8},{8,9},{9,10},{10,1... | collective-permute-start | bytes 491528 | tf_op jit(solution)/shard_map/ppermute | solution.py:492
  248.4 7.4 %collective-permute-start.7 = (f32[320,128]{1,0:T(8,128)}, f32[320,128]{1,0:T(8,128)S(1)}, u32[]{:S(2)}, u32[]{:S(2)}) collective-permute-start(f32[320,128]{1,0:T(8,128)} %get-tuple-element.71), channel_id=1, source_target_pairs={{1,0},{2,1},{3,2},{4,3},{5,4},{6,5},{7,6},{8,7},{9,8},{10,9},{11,1... | collective-permute-start | bytes 491528 | tf_op jit(solution)/shard_map/ppermute | solution.py:492
  253.5 2.3 copy-start.4
  255.8 0.7 copy-start.5

commit v6 on v5

--- a/solution.py
+++ b/solution.py
@@ -63,17 +63,58 @@
     column_ref[...] = jnp.where(lane == EXTRA, found, column)
 
 
-def pack_kernel(devices, slot_of, me_ref, fine_at_ref, coarse_at_ref, row_ref, fine_ref, coarse_ref, out_ref):
+def pack_kernel(
+    devices, first, me_ref, fine_at_ref, coarse_at_ref, row_ref, fine_in_ref, coarse_ref, out_ref, fine_ref, sem
+):
     planes = fine_ref.shape[0]
     coarse_planes, _, half, depth = coarse_ref.shape
+    part = planes // sem.shape[0]
+
+    def bring(i):
+        planes_of = pl.ds(i * part, part)
+        return pltpu.make_async_copy(fine_in_ref.at[planes_of], fine_ref.at[planes_of], sem.at[i])
+
+    def slot_of(box, unit):
+        if first:
+            return first_slot(devices, me_ref[0], row_ref, box, unit)
+        return jnp.where(unit < DIRECT, -1, box * EXTRA + unit - DIRECT)
+
+    for i in range(sem.shape[0]):
+        bring(i).start()
+
+    def coarse_plane(k, carry):
+        code = coarse_at_ref[k]
+
+        @pl.when(code >= 0)
+        def _():
+            at = code // 2
+            slot = slot_of(at // (DIRECT + EXTRA), at % (DIRECT + EXTRA))
+            for j in range(2):
+
+                @pl.when((slot >= 0) & (code % 2 == j))
+                def _():
+                    out_ref[slot, :, :, j * depth : (j + 1) * depth] = coarse_ref[k]
+
+        return carry
+
+    lax.fori_loop(0, coarse_planes, coarse_plane, 0)
 
     def fine_plane(k, carry):
         code = fine_at_ref[k]
-
-        @pl.when(code >= 0)
+        box, rank = code // FINE_CAP, code % FINE_CAP
+        whole = DIRECT // 2
+
+        if first:
+
+            @pl.when((code >= 0) & (rank < whole))
+            def _():
+                for h in range(2):
+                    out_ref[box * DIRECT + 2 * rank + h] = fine_ref[k, :, h * half : (h + 1) * half, :]
+
+        @pl.when((code >= 0) & (rank >= whole))
         def _():
             for h in range(2):
-                slot = slot_of(me_ref[0], row_ref, code // FINE_CAP, 2 * (code % FINE_CAP) + h)
+                slot = slot_of(box, 2 * rank + h)
 
                 @pl.when(slot >= 0)
                 def _():
@@ -81,24 +122,9 @@
 
         return carry
 
-    lax.fori_loop(0, planes, fine_plane, 0)
-
-    def coarse_plane(k, carry):
-        code = coarse_at_ref[k]
-
-        @pl.when(code >= 0)
-        def _():
-            at = code // 2
-            slot = slot_of(me_ref[0], row_ref, at // (DIRECT + EXTRA), at % (DIRECT + EXTRA))
-            for j in range(2):
-
-                @pl.when((slot >= 0) & (code % 2 == j))
-                def _():
-                    out_ref[slot, :, :, j * depth : (j + 1) * depth] = coarse_ref[k]
-
-        return carry
-
-    lax.fori_loop(0, coarse_planes, coarse_plane, 0)
+    for i in range(sem.shape[0]):
+        bring(i).wait()
+        lax.fori_loop(i * part, (i + 1) * part, fine_plane, 0)
 
 
 def first_slot(devices, me, row_ref, box, unit):
@@ -108,23 +134,24 @@
     return jnp.where(unit < DIRECT, box * DIRECT + unit, relay)
 
 
-def direct_slot(me, row_ref, box, unit):
-    return jnp.where(unit < DIRECT, -1, box * EXTRA + unit - DIRECT)
-
-
-def forward_kernel(me_ref, column_ref, in_ref, out_ref):
+def forward_kernel(me_ref, column_ref, in_ref, out_ref, sem):
     devices = out_ref.shape[0]
 
-    def body(a, carry):
-        code = column_ref[a, EXTRA]
-
-        @pl.when(code >= 0)
-        def _():
-            out_ref[(me_ref[0] - a + devices) % devices] = in_ref[(code // 8) * DIRECT + code % 8]
-
-        return carry
-
-    lax.fori_loop(0, devices, body, 0)
+    def each(act):
+        def body(a, carry):
+            code = column_ref[a, EXTRA]
+
+            @pl.when(code >= 0)
+            def _():
+                box = (me_ref[0] - a + devices) % devices
+                act(pltpu.make_async_copy(in_ref.at[(code // 8) * DIRECT + code % 8], out_ref.at[box], sem.at[a]))
+
+            return carry
+
+        lax.fori_loop(0, devices, body, 0)
+
+    each(lambda copy: copy.start())
+    each(lambda copy: copy.wait())
 
 
 def rows_to_edges(flat_ref, edge_ref, offset, row, planes, species, rows):
@@ -197,15 +224,47 @@
     xhigh_ref[...] = out_ref[planes * species * rows - deep : planes * species * rows]
 
 
-def late_units(shape, me_ref, column_ref, left_ref, fine_at_ref, coarse_at_ref, second_ref, rest_ref, held_ref,
+def late_units(shape, late_ref, left_ref, fine_at_ref, coarse_at_ref, second_ref, rest_ref, held_ref,
                plane_ref, sem, half_plane, whole_plane):
     planes, _, rows, _ = shape
     half = rows // 2
-    devices = column_ref.shape[0]
     planned = left_ref[0] == 0
 
-    def relayed(source, unit):
-        return (source + me_ref[0] + column_ref[source, jnp.maximum(unit - DIRECT, 0)] // 8) % devices
+    def children(c, ref, slot):
+        def store(s, even, odd):
+            plane_ref[s, pl.ds(0, half, stride=2), :] = even
+            plane_ref[s, pl.ds(1, half, stride=2), :] = odd
+
+        interpolate(ref, slot, coarse_at_ref[c] % 2, store)
+        for child in range(2):
+
+            @pl.when(fine_at_ref[2 * c + child] < 0)
+            def _():
+                whole_plane(2 * c + child)
+
+    def from_relay(m, carry):
+        what = late_ref[m]
+
+        @pl.when((what >= 0) & (what < 2 * planes))
+        def _():
+            for h in range(2):
+
+                @pl.when(what % 2 == h)
+                def _():
+                    half_plane(what // 2, h, second_ref, m)
+
+        for more in range(2):
+            parent = late_ref[(1 + more) * late_ref.shape[0] // 3 + m]
+
+            @pl.when(parent >= 0)
+            def _():
+                children(parent, second_ref, m)
+
+        return carry
+
+    @pl.when(planned)
+    def _():
+        lax.fori_loop(0, second_ref.shape[0], from_relay, 0)
 
     def bring(source, unit):
         copy = pltpu.make_async_copy(
@@ -214,63 +273,37 @@
         copy.start()
         copy.wait()
 
-    def parent(c, carry):
-        at = [fine_at_ref[2 * c], fine_at_ref[2 * c + 1]]
+    def direct(c, carry):
         code = coarse_at_ref[c]
         unit = code // 2 % (DIRECT + EXTRA)
-        source = code // 2 // (DIRECT + EXTRA)
-
-        @pl.when(((at[0] < 0) | (at[1] < 0)) & (unit >= DIRECT))
+
+        @pl.when(((fine_at_ref[2 * c] < 0) | (fine_at_ref[2 * c + 1] < 0)) & (unit >= DIRECT))
         def _():
-            def store(s, even, odd):
-                plane_ref[s, pl.ds(0, half, stride=2), :] = even
-                plane_ref[s, pl.ds(1, half, stride=2), :] = odd
-
-            @pl.when(planned)
-            def _():
-                held_ref[0] = second_ref[relayed(source, unit)]
-
-            @pl.when(jnp.logical_not(planned))
-            def _():
-                bring(source, unit)
-
-            interpolate(held_ref, 0, code % 2, store)
-            for child in range(2):
-
-                @pl.when(at[child] < 0)
+            bring(code // 2 // (DIRECT + EXTRA), unit)
+            children(c, held_ref, 0)
+
+        for x in (2 * c, 2 * c + 1):
+            at = fine_at_ref[x]
+            for h in range(2):
+                late = 2 * (at % FINE_CAP) + h
+
+                @pl.when((at >= 0) & (late >= DIRECT))
                 def _():
-                    whole_plane(2 * c + child)
+                    bring(at // FINE_CAP, late)
+                    half_plane(x, h, held_ref, 0)
 
         return carry
 
-    lax.fori_loop(0, planes // 2, parent, 0)
-
-    def plane(x, carry):
-        at = fine_at_ref[x]
-
-        @pl.when((at >= 0) & (2 * (at % FINE_CAP) + 1 >= DIRECT))
-        def _():
-            for h in range(2):
-                unit = 2 * (at % FINE_CAP) + h
-
-                @pl.when((unit >= DIRECT) & planned)
-                def _():
-                    half_plane(x, h, second_ref, relayed(at // FINE_CAP, unit))
-
-                @pl.when((unit >= DIRECT) & jnp.logical_not(planned))
-                def _():
-                    bring(at // FINE_CAP, unit)
-                    half_plane(x, h, held_ref, 0)
-
-        return carry
-
-    lax.fori_loop(0, planes, plane, 0)
+    @pl.when(jnp.logical_not(planned))
+    def _():
+        lax.fori_loop(0, planes // 2, direct, 0)
 
 
 def edges_kernel(
-    shape, me_ref, column_ref, left_ref, fine_at_ref, coarse_at_ref, second_ref, rest_ref,
+    shape, late_ref, left_ref, fine_at_ref, coarse_at_ref, second_ref, rest_ref,
     ylow_in_ref, yhigh_in_ref, xlow_in_ref, xhigh_in_ref,
-    ylow_ref, yhigh_ref, xlow_ref, xhigh_ref, held_ref, plane_ref, sem,
+    ylow_ref, yhigh_ref, xlow_ref, xhigh_ref, low_low_ref, low_high_ref, high_low_ref, high_high_ref, held_ref, plane_ref,
+    sem,
 ):
     planes, species, rows, _ = shape
     half = rows // 2
@@ -301,23 +334,19 @@
             half_edges(x, h, lambda s, part: plane_ref[s, h * half + part.start : h * half + part.stop])
 
     late_units(
-        shape, me_ref, column_ref, left_ref, fine_at_ref, coarse_at_ref, second_ref, rest_ref, held_ref, plane_ref,
+        shape, late_ref, left_ref, fine_at_ref, coarse_at_ref, second_ref, rest_ref, held_ref, plane_ref,
         sem, half_plane, whole_plane,
     )
-
-
-def corners_kernel(planes, species, ylow_ref, yhigh_ref, xlow_ref, xhigh_ref, down_ref, up_ref):
-    deep = xlow_ref.shape[0]
-    down_ref[0:deep] = xlow_ref[...]
-    up_ref[0:deep] = xhigh_ref[...]
-    for message_ref, x in ((down_ref, 0), (up_ref, planes - 1)):
+    first, last = 0, (ITERS - 1) * species * planes
+    for corner_ref, edge_ref, at in (
+        (low_low_ref, ylow_ref, first),
+        (low_high_ref, yhigh_ref, last),
+        (high_low_ref, ylow_ref, first + planes - 1),
+        (high_high_ref, yhigh_ref, last + planes - 1),
+    ):
+        corner_ref[...] = jnp.zeros_like(corner_ref)
         for s in range(species):
-            low = ((ITERS - 1) * species + s) * planes + x
-            high = s * planes + x
-            message_ref[deep + s : deep + s + 1] = ylow_ref[low : low + 1]
-            message_ref[deep + 16 + s : deep + 16 + s + 1] = yhigh_ref[high : high + 1]
-        for at in (deep + species, deep + 16 + species):
-            message_ref[at : at + 16 - species] = jnp.zeros((16 - species, message_ref.shape[1]), jnp.float32)
+            corner_ref[s : s + 1] = edge_ref[at + s * planes : at + s * planes + 1]
 
 
 def velocity_edges_kernel(vel_ref, ylow_ref, yhigh_ref, xlow_ref, xhigh_ref, *, shape):
@@ -345,9 +374,9 @@
 
 
 def steps_kernel(
-    shape, me_ref, column_ref, left_ref, fine_at_ref, coarse_at_ref, inside_ref, diff_ref, second_ref, rest_ref, state_ref,
-    vel_ref, ylow_own_ref, yhigh_own_ref, ylow_ref, yhigh_ref, xlow_ref, xhigh_ref, vylow_ref, vyhigh_ref, vxlow_ref,
-    vxhigh_ref, out_ref, u0_ref, u1_ref, row_low_ref, row_high_ref, plane_low_ref, plane_high_ref, held_ref, plane_ref, sem,
+    shape, late_ref, left_ref, fine_at_ref, coarse_at_ref, inside_ref, diff_ref, second_ref, rest_ref, state_ref,
+    vel_ref, ylow_own_ref, yhigh_own_ref, ylow_ref, yhigh_ref, xlow_ref, xhigh_ref, low_low_ref, low_high_ref, high_low_ref,
+    high_high_ref, vylow_ref, vyhigh_ref, vxlow_ref, vxhigh_ref, out_ref, u0_ref, u1_ref, row_low_ref, row_high_ref, plane_low_ref, plane_high_ref, held_ref, plane_ref, sem,
     out_sem,
 ):
     planes, species, rows, lanes = shape
@@ -355,21 +384,6 @@
     size = species * rows
     copy = pltpu.make_async_copy(state_ref, u0_ref, sem)
     copy.start()
-    copy.wait()
-
-    def half_plane(x, h, ref, slot):
-        for s in range(species):
-            base = pl.multiple_of(x * size + s * rows + h * half, half)
-            u0_ref[pl.ds(base, half), :] = ref[slot, s]
-
-    def whole_plane(x):
-        for s in range(species):
-            u0_ref[pl.ds(pl.multiple_of(x * size + s * rows, rows), rows), :] = plane_ref[s]
-
-    late_units(
-        shape, me_ref, column_ref, left_ref, fine_at_ref, coarse_at_ref, second_ref, rest_ref, held_ref, plane_ref,
-        sem, half_plane, whole_plane,
-    )
 
     def along(u, first, last, dim):
         count = u.shape[dim]
@@ -378,10 +392,9 @@
         high = jnp.where(at == count - 1, last, pltpu.roll(u, count - 1, dim))
         return low, high
 
-    deep = ITERS * size
     for (near_ref, near, far, own_ref, own, v_ref, corner, target_ref, inside) in (
-        (ylow_ref, 1, 0, ylow_own_ref, 0, vylow_ref, deep, row_low_ref, 0),
-        (yhigh_ref, 0, 1, yhigh_own_ref, 1, vyhigh_ref, deep + 16, row_high_ref, 1),
+        (ylow_ref, 1, 0, ylow_own_ref, 0, vylow_ref, (low_low_ref, high_low_ref), row_low_ref, 0),
+        (yhigh_ref, 0, 1, yhigh_own_ref, 1, vyhigh_ref, (low_high_ref, high_high_ref), row_high_ref, 1),
     ):
         for x in range(0, planes, 16):
             flow = Flow([v_ref[k * planes + x : k * planes + x + 16] for k in range(3)])
@@ -394,11 +407,11 @@
                 u = band(near_ref, near)
                 start = (near * species + s) * planes
                 if x == 0:
-                    first = xlow_ref[corner + s : corner + s + 1]
+                    first = corner[0][s : s + 1]
                 else:
                     first = near_ref[start + x - 1 : start + x]
                 if x + 16 == planes:
-                    last = xhigh_ref[corner + s : corner + s + 1]
+                    last = corner[1][s : s + 1]
                 else:
                     last = near_ref[start + x + 16 : start + x + 17]
                 outer, inner = band(near_ref, far), band(own_ref, own)
@@ -419,19 +432,35 @@
             sides = ((below(s), above(s)), along(u, y_low(s), y_high(s), 0), along(u, u, u, 1))
             store(s, flow.step(u, sides, diff_ref[s]))
 
-    for (halo_ref, near, below, above, v_ref, target_ref, inside) in (
-        (xlow_ref, 1, at(xlow_ref, 0), at(u0_ref, 0), vxlow_ref, plane_low_ref, 2),
-        (xhigh_ref, 0, at(u0_ref, planes - 1), at(xhigh_ref, 1), vxhigh_ref, plane_high_ref, 3),
+    copy.wait()
+
+    def half_plane(x, h, ref, slot):
+        for s in range(species):
+            base = pl.multiple_of(x * size + s * rows + h * half, half)
+            u0_ref[pl.ds(base, half), :] = ref[slot, s]
+
+    def whole_plane(x):
+        for s in range(species):
+            u0_ref[pl.ds(pl.multiple_of(x * size + s * rows, rows), rows), :] = plane_ref[s]
+
+    late_units(
+        shape, late_ref, left_ref, fine_at_ref, coarse_at_ref, second_ref, rest_ref, held_ref, plane_ref,
+        sem, half_plane, whole_plane,
+    )
+
+    for (halo_ref, near, below, above, v_ref, target_ref, (corner_low_ref, corner_high_ref, inside)) in (
+        (xlow_ref, 1, at(xlow_ref, 0), at(u0_ref, 0), vxlow_ref, plane_low_ref, (low_low_ref, low_high_ref, 2)),
+        (xhigh_ref, 0, at(u0_ref, planes - 1), at(xhigh_ref, 1), vxhigh_ref, plane_high_ref, (high_low_ref, high_high_ref, 3)),
     ):
 
         def store(s, new):
             target_ref[s * rows : (s + 1) * rows] = new * inside_ref[inside]
 
-        def corner(offset):
-            return lambda s: halo_ref[deep + offset + s : deep + offset + s + 1]
+        def corner(ref):
+            return lambda s: ref[s : s + 1]
 
         velocity = [v_ref[k * rows : (k + 1) * rows] for k in range(3)]
-        plane(velocity, at(halo_ref, near), below, above, corner(0), corner(16), store)
+        plane(velocity, at(halo_ref, near), below, above, corner(corner_low_ref), corner(corner_high_ref), store)
 
     def advance(u_ref, new_ref, low, high, y_low, y_high, after):
         def group(x, first, last):
@@ -490,6 +519,17 @@
     size = lax.axis_size(axis)
     up = [(i, (i + 1) % size) for i in range(size - 1)]
     return lax.ppermute(high, axis, up), lax.ppermute(low, axis, [(b, a) for a, b in up])
+
+
+def diagonal(value, grp_step, dev_step):
+    groups, devices = lax.axis_size("grp"), lax.axis_size("dev")
+    pairs = []
+    for g in range(groups):
+        for d in range(devices):
+            to_g, to_d = g + grp_step, d + dev_step
+            if 0 <= to_g < groups and 0 <= to_d < devices:
+                pairs.append((g * devices + d, to_g * devices + to_d))
+    return lax.ppermute(value, ("grp", "dev"), pairs)
 
 
 def on_device(old_fine, old_ids, old_coarse, coarse_ids, velocity, diffusion):
@@ -551,23 +591,24 @@
     def exchange(value):
         return lax.all_to_all(value, "dev", split_axis=0, concat_axis=0, tiled=True)
 
-    def pack(count, slot_of, name):
+    def pack(count, first, name):
         return pl.pallas_call(
-            functools.partial(pack_kernel, devices, slot_of),
+            functools.partial(pack_kernel, devices, first),
             out_shape=units_shape(count),
-            in_specs=[SMEM] * 4 + [VMEM] * 2,
+            in_specs=[SMEM] * 4 + [ANY, VMEM],
             out_specs=VMEM,
+            scratch_shapes=[pltpu.VMEM(old_fine.shape, f32), pltpu.SemaphoreType.DMA((4,))],
             compiler_params=PARAMS,
             name=name,
         )(me_ref, send_fine, send_coarse, row, old_fine, old_coarse)
 
-    packed = pack(devices * DIRECT, functools.partial(first_slot, devices), "pack")
+    packed = pack(devices * DIRECT, True, "pack")
 
     def no_rest():
         return pl.pallas_call(empty_kernel, out_shape=units_shape(devices * EXTRA), out_specs=ANY, name="nothing")()
 
     def rest_direct():
-        return exchange(pack(devices * EXTRA, direct_slot, "pack_rest"))
+        return exchange(pack(devices * EXTRA, False, "pack_rest"))
 
     rest = lax.cond(left[0] == 0, no_rest, rest_direct)
     packed, rest, flow = lax.optimization_barrier((packed, rest, velocity))
@@ -592,8 +633,9 @@
     second = pl.pallas_call(
         forward_kernel,
         out_shape=units_shape(devices),
-        in_specs=[SMEM] * 2 + [VMEM],
+        in_specs=[SMEM] * 2 + [ANY],
         out_specs=VMEM,
+        scratch_shapes=[pltpu.SemaphoreType.DMA((devices,))],
         compiler_params=PARAMS,
         cost_estimate=cost(3),
         name="forward",
@@ -611,32 +653,48 @@
         cost_estimate=cost(10),
         name="build",
     )(fine_at, coarse_at, first)
+    relay_of = (jnp.arange(devices)[:, None] + me + column[:, :EXTRA] // 8) % devices
+
+    def through(source, unit, used):
+        over = jnp.arange(EXTRA) == (unit - DIRECT)[:, None]
+        hit = (source[:, None, None] == jnp.arange(devices)[None, :, None]) & over[:, None, :]
+        relay = jnp.max(jnp.where(hit, relay_of[None], -1), axis=(1, 2))
+        return jnp.where(used & (unit >= DIRECT), relay, -1)
+
+    order = jnp.arange(devices)
+    halves = jnp.arange(2 * planes)
+    at = jnp.repeat(fine_at, 2)
+    relay = through(at // FINE_CAP, 2 * (at % FINE_CAP) + halves % 2, at >= 0)
+    late_fine = jnp.max(jnp.where(relay[:, None] == order[None], halves[:, None], -1), axis=0)
+    parents = jnp.arange(coarse_planes)
+    code = coarse_at // 2
+    fresh = jnp.min(fine_at.reshape(coarse_planes, 2), axis=1) < 0
+    relay = through(code // unit_count, code % unit_count, fresh)
+    late_parents = [
+        jnp.max(jnp.where((relay[:, None] == order[None]) & (coarse_at % 2 == j)[:, None], parents[:, None], -1), axis=0)
+        for j in range(COARSE_CAP)
+    ]
+    late = jnp.concatenate([late_fine, *late_parents])
     late_scratch = [
         pltpu.VMEM((1, species, half, lanes), f32),
         pltpu.VMEM((species, rows, lanes), f32),
         pltpu.SemaphoreType.DMA,
     ]
-    ylow_own, yhigh_own, xlow_own, xhigh_own = pl.pallas_call(
+    corner_shape = jax.ShapeDtypeStruct((16, lanes), f32)
+    ylow_own, yhigh_own, xlow_own, xhigh_own, *corners = pl.pallas_call(
         functools.partial(edges_kernel, old_fine.shape),
-        out_shape=edge_shapes(ITERS, species),
-        in_specs=[SMEM] * 5 + [VMEM, ANY] + [VMEM] * 4,
-        out_specs=[VMEM] * 4,
+        out_shape=edge_shapes(ITERS, species) + [corner_shape] * 4,
+        in_specs=[SMEM] * 4 + [VMEM, ANY] + [VMEM] * 4,
+        out_specs=[VMEM] * 8,
         scratch_shapes=late_scratch,
         compiler_params=PARAMS,
         cost_estimate=cost(4),
         name="edges",
-    )(me_ref, column, left, fine_at, coarse_at, second, rest, *edges)
+    )(late, left, fine_at, coarse_at, second, rest, *edges)
     ylow, yhigh = neighbours("grp", ylow_own, yhigh_own)
-    message = jax.ShapeDtypeStruct((ITERS * size + 32, lanes), f32)
-    down, up = pl.pallas_call(
-        functools.partial(corners_kernel, planes, species),
-        out_shape=[message] * 2,
-        in_specs=[VMEM] * 4,
-        out_specs=[VMEM] * 2,
-        compiler_params=PARAMS,
-        name="corners",
-    )(ylow, yhigh, xlow_own, xhigh_own)
-    xlow, xhigh = neighbours("dev", down, up)
+    xlow, xhigh = neighbours("dev", xlow_own, xhigh_own)
+    low_low, low_high, high_low, high_high = corners
+    corners = [diagonal(high_high, 1, 1), diagonal(high_low, -1, 1), diagonal(low_high, 1, -1), diagonal(low_low, -1, -1)]
     grp, dev = lax.axis_index("grp"), lax.axis_index("dev")
     inside = jnp.stack([grp > 0, grp < lax.axis_size("grp") - 1, dev > 0, dev < devices - 1]).astype(f32)
     row_edge = pltpu.VMEM((species * planes, lanes), f32)
@@ -644,7 +702,7 @@
     done = pl.pallas_call(
         functools.partial(steps_kernel, old_fine.shape),
         out_shape=state_shape,
-        in_specs=[SMEM] * 7 + [VMEM, ANY, ANY] + [VMEM] * 11,
+        in_specs=[SMEM] * 6 + [VMEM, ANY, ANY] + [VMEM] * 15,
         out_specs=ANY,
         scratch_shapes=[pltpu.VMEM(state_shape.shape, f32)] * 2
         + [row_edge] * 2
@@ -654,8 +712,8 @@
         compiler_params=PARAMS,
         name="steps",
     )(
-        me_ref, column, left, fine_at, coarse_at, inside, diffusion, second, rest, state, velocity,
-        ylow_own, yhigh_own, ylow, yhigh, xlow, xhigh, *flow_edges,
+        late, left, fine_at, coarse_at, inside, diffusion, second, rest, state, velocity,
+        ylow_own, yhigh_own, ylow, yhigh, xlow, xhigh, *corners, *flow_edges,
     )
     return done.reshape(old_fine.shape)
 

time: 278 us -> 283 us (1.018)
  starting transfers between devices: 53.4 us -> 65.1 us
  Pallas kernels: 59.5 us -> 48.8 us
  waiting for transfers between devices: 143 us -> 146 us
    ppermute x0 -> x4, waiting for transfers between devices: none -> 15.8 us  [diagonal(): return lax.ppermute(value, ('grp', 'dev'), pairs)]
    ppermute x0 -> x4, starting transfers between devices: none -> 11.4 us  [diagonal(): return lax.ppermute(value, ('grp', 'dev'), pairs)]
    ppermute x4, waiting for transfers between devices: 117 us -> 109 us  [neighbours(): lax.ppermute(high, axis, up)]
    ppermute x4, waiting for transfers between devices: 7.59 us -> 0.01 us  [neighbours(): lax.ppermute(low, axis, [(b, a) for a, b in up])]
    pallas_call x2 -> x1, Pallas kernels: 12.6 us -> 7.43 us  [pack(): pl.pallas_call(functools.partial(pack_kernel, devices, first), out_shape=...]
  transfers between devices with their start and end apart: 11 -> 15, of which waited for: 8 -> 7; matrix products, arithmetic and copies ran while one was open for 3% -> 4% of each run, Pallas kernels for 5% -> 4%
where the time goes in v6:
time: 283 us; the launch traced here: 280 us
  waiting for transfers between devices  146 us (52%)
  starting transfers between devices  65.1 us (23%)
  Pallas kernels  48.8 us (17%)
  other arithmetic  15.6 us (6%)
  local copies, waits for them, and re-layouts  3.23 us (1%)
    ppermute x4, waiting for transfers between devices, neighbours(): lax.ppermute(high, axis, up)  109 us
    all_to_all x2, waiting for transfers between devices, exchange(): return lax.all_to_all(value, 'dev', split_axis=0, concat_axis=0, tiled=True)  17.2 us
    pallas_call x1, Pallas kernels, on_device(): pl.pallas_call(functools.partial(steps_kernel, old_fine.shape), out_shape...  16.7 us
    all_to_all x2, starting transfers between devices, exchange(): return lax.all_to_all(value, 'dev', split_axis=0, concat_axis=0, tiled=True)  16.3 us
    ppermute x4, waiting for transfers between devices, diagonal(): return lax.ppermute(value, ('grp', 'dev'), pairs)  15.8 us
    ppermute x4, starting transfers between devices, neighbours(): lax.ppermute(low, axis, [(b, a) for a, b in up])  13.9 us
    ppermute x4, starting transfers between devices, neighbours(): lax.ppermute(high, axis, up)  11.9 us
    all_to_all x1, starting transfers between devices, on_device(): lax.all_to_all(labels, 'dev', split_axis=0, concat_axis=0, tiled=True)  11.6 us
  transfers between devices with their start and end apart: 15, of which 7 were waited for; matrix products, arithmetic and copies ran while one was open for 4% of the time, Pallas kernels for 4%

profile of v6, /device:TPU:22, one launch (start us, length us, event | category | flops | bytes accessed | tf_op | source)
XLA Modules:
  0.0 280.3 jit_solution(2880358718262514764)
XLA Ops:
  0.0 0.7 pad_add_fusion
  0.7 0.6 broadcast_in_dim.70
  1.4 11.6 %all-to-all-start.1 = ((s32[32,1,96]{2,1,0:T(1,128)}), s32[32,1,96]{2,1,0:T(1,128)S(1)}, u32[]{:S(2)}, u32[]{:S(2)}) async-start(s32[32,1,96]{2,1,0:T(1,128)} %broadcast_in_dim.70), calls=%async_computation.1 | async-start | bytes 32768 | tf_op jit(solution)/shard_map/all_to_all | solution.py:551
  13.0 0.7 fusion.17
  13.6 0.7 and_select_fusion.1
  14.3 0.7 compare_select_fusion.21
  15.0 0.7 fusion.16
  16.0 0.7 compare_select_fusion.20.fine_at_ref
  16.9 3.9 %all-to-all-done.1 = s32[32,1,96]{2,1,0:T(1,128)S(1)} async-done(((s32[32,1,96]{2,1,0:T(1,128)}), s32[32,1,96]{2,1,0:T(1,128)S(1)}, u32[]{:S(2)}, u32[]{:S(2)}) %all-to-all-start.1) | async-done | bytes 12320 | tf_op jit(solution)/shard_map/all_to_all | solution.py:551
  21.1 0.9 convert_reduce_fusion.5
  22.0 1.1 convert_reduce_fusion
  23.8 0.6 multiply_add_fusion.units_ref
  24.4 4.6 %plan.1 = (s32[8,128]{1,0:T(8,128)S(1)}, s32[32,128]{1,0:T(8,128)}) custom-call(s32[1]{0:T(128)} %bitcast.3.me_ref, s32[32,128]{1,0:T(8,128)} %multiply_add_fusion.units_ref), custom_call_target="tpu_custom_call" | custom-call | tf_op jit(solution)/shard_map/plan/pallas_call | solution.py:565
  29.0 0.7 slice_reduce_fusion
  29.7 0.7 compare_select_fusion.coarse_at_ref
  30.3 7.4 %pack.1 = f32[160,9,8,128]{3,2,1,0:T(8,128)} custom-call(s32[1]{0:T(128)} %bitcast.3.me_ref, s32[64]{0:T(128)S(1)} %compare_select_fusion.20.fine_at_ref, s32[32]{0:T(128)S(1)} %compare_select_fusion.coarse_at_ref, s32[8,128]{1,0:T(8,128)S(1)} %get-tuple-element.54.row_ref, f32[64,9,16,128]{3,2,1,0:T(8,128)} %fine_in_ref.1, f32[32,9,8,64]{3,2,1,0:T(8,128)} %coarse_ref.1), custom_call_target="tpu_custom_call" | custom-call | tf_op jit(solution)/shard_map/pack/pallas_call | solution.py:595
  38.4 6.9 %all-to-all-start.2 = ((f32[160,9,8,128]{3,2,1,0:T(8,128)}), f32[160,9,8,128]{3,2,1,0:T(8,128)}, u32[]{:S(2)}, u32[]{:S(2)}) async-start(f32[160,9,8,128]{3,2,1,0:T(8,128)} %pack.1), calls=%async_computation.2 | async-start | bytes 11796480 | tf_op jit(solution)/shard_map/all_to_all | solution.py:592
  45.6 0.9 convert_reduce_fusion.2
  46.6 1.3 select_reduce_fusion.fine_at_ref
  48.2 2.2 velocity_edges.1
  50.3 3.4 %collective-permute-start.2 = (f32[48,128]{1,0:T(8,128)}, f32[48,128]{1,0:T(8,128)S(1)}, u32[]{:S(2)}, u32[]{:S(2)}) collective-permute-start(f32[48,128]{1,0:T(8,128)} %get-tuple-element.59), channel_id=1, source_target_pairs={{0,1},{1,2},{2,3},{3,4},{4,5},{5,6},{6,7},{7,8},{8,9},{9,10},{10,1... | collective-permute-start | bytes 73736 | tf_op jit(solution)/shard_map/ppermute | solution.py:521
  53.7 4.6 %collective-permute-start.3 = (f32[48,128]{1,0:T(8,128)}, f32[48,128]{1,0:T(8,128)S(1)}, u32[]{:S(2)}, u32[]{:S(2)}) collective-permute-start(f32[48,128]{1,0:T(8,128)} %get-tuple-element.60), channel_id=1, source_target_pairs={{1,0},{2,1},{3,2},{4,3},{5,4},{6,5},{7,6},{8,7},{9,8},{10,9},{11,1... | collective-permute-start | bytes 73736 | tf_op jit(solution)/shard_map/ppermute | solution.py:521
  58.3 1.9 collective-permute-start
  60.2 3.6 %collective-permute-start.1 = (f32[192,128]{1,0:T(8,128)}, f32[192,128]{1,0:T(8,128)S(1)}, u32[]{:S(2)}, u32[]{:S(2)}) collective-permute-start(f32[192,128]{1,0:T(8,128)} %get-tuple-element.58), channel_id=1, source_target_pairs={{32,0},{64,32},{96,64},{128,96},{160,128},{192,160},{224,192},{33,... | collective-permute-start | bytes 294920 | tf_op jit(solution)/shard_map/ppermute | solution.py:521
  64.1 0.8 convert_reduce_fusion.3
  64.8 109.3 %collective-permute-done.2.vxlow_ref = f32[48,128]{1,0:T(8,128)S(1)} collective-permute-done((f32[48,128]{1,0:T(8,128)}, f32[48,128]{1,0:T(8,128)S(1)}, u32[]{:S(2)}, u32[]{:S(2)}) %collective-permute-start.2) | collective-permute-done | bytes 24608 | tf_op jit(solution)/shard_map/ppermute | solution.py:521
  174.2 3.5 %forward.1 = f32[32,9,8,128]{3,2,1,0:T(8,128)} custom-call(s32[1]{0:T(128)} %bitcast.3.me_ref, s32[32,128]{1,0:T(8,128)} %get-tuple-element.53.column_ref, f32[160,9,8,128]{3,2,1,0:T(8,128)} %all-to-all-done.2.in_ref.first_ref), custom_call_target="tpu_custom_call" | custom-call | bytes 10800000 | tf_op jit(solution)/shard_map/forward/pallas_call | solution.py:633
  177.7 9.4 %all-to-all-start.3 = ((f32[32,9,8,128]{3,2,1,0:T(8,128)}), f32[32,9,8,128]{3,2,1,0:T(8,128)S(1)}, u32[]{:S(2)}, u32[]{:S(2)}) async-start(f32[32,9,8,128]{3,2,1,0:T(8,128)} %forward.1), calls=%async_computation.3 | async-start | bytes 2359296 | tf_op jit(solution)/shard_map/all_to_all | solution.py:592
  187.5 0.7 select_reduce_fusion.1.coarse_at_ref
  188.7 0.7 pad_add_fusion.1.late_ref
  189.4 9.7 %build.1 = (f32[9216,128]{1,0:T(8,128)}, f32[1152,128]{1,0:T(8,128)}, f32[1152,128]{1,0:T(8,128)}, f32[288,128]{1,0:T(8,128)}, f32[288,128]{1,0:T(8,128)}) custom-call(s32[64]{0:T(128)} %copy-done.11, s32[32]{0:T(128)} %copy-done.12, f32[160,9,8,128]{3,2,1,0:T(8,128)} %all-to-all-done.2.in_ref.first_ref), custom_call_target="tpu_custom_call" | custom-call | bytes 36000000 | tf_op jit(solution)/shard_map/build/pallas_call | solution.py:647
  199.1 17.2 %all-to-all-done.3.second_ref = f32[32,9,8,128]{3,2,1,0:T(8,128)S(1)} async-done(((f32[32,9,8,128]{3,2,1,0:T(8,128)}), f32[32,9,8,128]{3,2,1,0:T(8,128)S(1)}, u32[]{:S(2)}, u32[]{:S(2)}) %all-to-all-start.3) | async-done | bytes 1179680 | tf_op jit(solution)/shard_map/all_to_all | solution.py:592
  216.3 1.0 copy-done
  217.4 4.7 %edges.1 = (f32[1152,128]{1,0:T(8,128)}, f32[1152,128]{1,0:T(8,128)}, f32[288,128]{1,0:T(8,128)}, f32[288,128]{1,0:T(8,128)}, f32[16,128]{1,0:T(8,128)}, /*index...) custom-call(s32[96]{0:T(128)} %pad_add_fusion.1.late_ref, s32[1]{0:T(128)} %bitcast.4.left_ref, s32[64]{0:T(128)} %copy-done.11, ...), custom_call_target="tpu_custom_call" | custom-call | bytes 14400000 | tf_op jit(solution)/shard_map/edges/pallas_call | solution.py:684
  222.0 1.9 collective-permute-start.5
  224.0 2.4 collective-permute-start.4
  226.4 4.2 %collective-permute-start.6 = (f32[288,128]{1,0:T(8,128)}, f32[288,128]{1,0:T(8,128)S(1)}, u32[]{:S(2)}, u32[]{:S(2)}) collective-permute-start(f32[288,128]{1,0:T(8,128)} %get-tuple-element.70), channel_id=1, source_target_pairs={{0,1},{1,2},{2,3},{3,4},{4,5},{5,6},{6,7},{7,8},{8,9},{9,10},{10,1... | collective-permute-start | bytes 442376 | tf_op jit(solution)/shard_map/ppermute | solution.py:521
  230.6 3.8 %collective-permute-start.7 = (f32[288,128]{1,0:T(8,128)}, f32[288,128]{1,0:T(8,128)S(1)}, u32[]{:S(2)}, u32[]{:S(2)}) collective-permute-start(f32[288,128]{1,0:T(8,128)} %get-tuple-element.71), channel_id=1, source_target_pairs={{1,0},{2,1},{3,2},{4,3},{5,4},{6,5},{7,6},{8,7},{9,8},{10,9},{11,1... | collective-permute-start | bytes 442376 | tf_op jit(solution)/shard_map/ppermute | solution.py:521
  234.4 2.7 collective-permute-start.8
  237.0 5.5 %collective-permute-done.8.low_low_ref = f32[16,128]{1,0:T(8,128)S(1)} collective-permute-done((f32[16,128]{1,0:T(8,128)}, f32[16,128]{1,0:T(8,128)S(1)}, u32[]{:S(2)}, u32[]{:S(2)}) %collective-permute-start.8) | collective-permute-done | bytes 8224 | tf_op jit(solution)/shard_map/ppermute | solution.py:532
  242.5 1.9 collective-permute-start.9
  244.5 5.4 %collective-permute-done.9.low_high_ref = f32[16,128]{1,0:T(8,128)S(1)} collective-permute-done((f32[16,128]{1,0:T(8,128)}, f32[16,128]{1,0:T(8,128)S(1)}, u32[]{:S(2)}, u32[]{:S(2)}) %collective-permute-start.9) | collective-permute-done | bytes 8224 | tf_op jit(solution)/shard_map/ppermute | solution.py:532
  249.8 1.9 collective-permute-start.10
  251.8 4.1 %collective-permute-done.10.high_low_ref = f32[16,128]{1,0:T(8,128)S(1)} collective-permute-done((f32[16,128]{1,0:T(8,128)}, f32[16,128]{1,0:T(8,128)S(1)}, u32[]{:S(2)}, u32[]{:S(2)}) %collective-permute-start.10) | collective-permute-done | bytes 8224 | tf_op jit(solution)/shard_map/ppermute | solution.py:532
  255.9 4.9 %collective-permute-start.11 = (f32[16,128]{1,0:T(8,128)}, f32[16,128]{1,0:T(8,128)S(1)}, u32[]{:S(2)}, u32[]{:S(2)}) collective-permute-start(f32[16,128]{1,0:T(8,128)} %get-tuple-element.75), channel_id=1, source_target_pairs={{33,0},{34,1},{35,2},{36,3},{37,4},{38,5},{39,6},{40,7},{41,8},{42... | collective-permute-start | bytes 24584 | tf_op jit(solution)/shard_map/ppermute | solution.py:532
  260.8 0.6 add_convert_fusion.inside_ref
  261.5 0.8 collective-permute-done.11.high_high_ref
  263.4 16.7 %steps.1 = f32[9216,128]{1,0:T(8,128)} custom-call(s32[96]{0:T(128)} %pad_add_fusion.1.late_ref, s32[1]{0:T(128)} %bitcast.4.left_ref, s32[64]{0:T(128)} %copy-done.11, s32[32]{0:T(128)} %copy-done.12, f32[4]{0:T(128)} %add_convert_fusion.inside_ref, f32[9]{0:T(128)} %diff_ref.1, f32[32,9,8,128]{3,2,1,0:T(8,128)} %copy-done, ...), custom_call_target="tpu_custom_call" | custom-call | tf_op jit(solution)/shard_map/steps/pallas_call | solution.py:702
  (83 shorter events, 4.2 us)
Async XLA Ops:
  1.4 19.4 %all-to-all-start.1 = ((s32[32,1,96]{2,1,0:T(1,128)}), s32[32,1,96]{2,1,0:T(1,128)S(1)}, u32[]{:S(2)}, u32[]{:S(2)}) async-start(s32[32,1,96]{2,1,0:T(1,128)} %broadcast_in_dim.70), calls=%async_computation.1 | async-start | bytes 32768 | tf_op jit(solution)/shard_map/all_to_all | solution.py:551
  30.3 8.1 %copy-start.1 = (f32[32,9,8,64]{3,2,1,0:T(8,128)S(1)}, f32[32,9,8,64]{3,2,1,0:T(8,128)}, u32[]{:S(2)}) copy-start(f32[32,9,8,64]{3,2,1,0:T(8,128)} %coarse_ref.1) | copy-start | bytes 1769476
  38.4 7.0 %copy-start.8 = (s32[32,128]{1,0:T(8,128)S(1)}, s32[32,128]{1,0:T(8,128)}, u32[]{:S(2)}) copy-start(s32[32,128]{1,0:T(8,128)} %get-tuple-element.53.column_ref) | copy-start | bytes 49156
  38.4 135.7 %all-to-all-start.2 = ((f32[160,9,8,128]{3,2,1,0:T(8,128)}), f32[160,9,8,128]{3,2,1,0:T(8,128)}, u32[]{:S(2)}, u32[]{:S(2)}) async-start(f32[160,9,8,128]{3,2,1,0:T(8,128)} %pack.1), calls=%async_computation.2 | async-start | bytes 11796480 | tf_op jit(solution)/shard_map/all_to_all | solution.py:592
  48.0 139.2 %copy-start.11 = (s32[64]{0:T(128)}, s32[64]{0:T(128)S(1)}, u32[]{:S(2)}) copy-start(s32[64]{0:T(128)S(1)} %select_reduce_fusion.fine_at_ref) | copy-start | bytes 772
  50.3 123.8 %collective-permute-start.2 = (f32[48,128]{1,0:T(8,128)}, f32[48,128]{1,0:T(8,128)S(1)}, u32[]{:S(2)}, u32[]{:S(2)}) collective-permute-start(f32[48,128]{1,0:T(8,128)} %get-tuple-element.59), channel_id=1, source_target_pairs={{0,1},{1,2},{2,3},{3,4},{4,5},{5,6},{6,7},{7,8},{8,9},{9,10},{10,1... | collective-permute-start | bytes 73736 | tf_op jit(solution)/shard_map/ppermute | solution.py:521
  53.7 120.4 %collective-permute-start.3 = (f32[48,128]{1,0:T(8,128)}, f32[48,128]{1,0:T(8,128)S(1)}, u32[]{:S(2)}, u32[]{:S(2)}) collective-permute-start(f32[48,128]{1,0:T(8,128)} %get-tuple-element.60), channel_id=1, source_target_pairs={{1,0},{2,1},{3,2},{4,3},{5,4},{6,5},{7,6},{8,7},{9,8},{10,9},{11,1... | collective-permute-start | bytes 73736 | tf_op jit(solution)/shard_map/ppermute | solution.py:521
  58.3 115.8 %collective-permute-start = (f32[192,128]{1,0:T(8,128)}, f32[192,128]{1,0:T(8,128)S(1)}, u32[]{:S(2)}, u32[]{:S(2)}) collective-permute-start(f32[192,128]{1,0:T(8,128)} %get-tuple-element.57), channel_id=1, source_target_pairs={{0,32},{32,64},{64,96},{96,128},{128,160},{160,192},{192,224},{1,3... | collective-permute-start | bytes 294920 | tf_op jit(solution)/shard_map/ppermute | solution.py:521
  60.2 113.9 %collective-permute-start.1 = (f32[192,128]{1,0:T(8,128)}, f32[192,128]{1,0:T(8,128)S(1)}, u32[]{:S(2)}, u32[]{:S(2)}) collective-permute-start(f32[192,128]{1,0:T(8,128)} %get-tuple-element.58), channel_id=1, source_target_pairs={{32,0},{64,32},{96,64},{128,96},{160,128},{192,160},{224,192},{33,... | collective-permute-start | bytes 294920 | tf_op jit(solution)/shard_map/ppermute | solution.py:521
  174.1 3.5 %copy-start.9 = (f32[48,128]{1,0:T(8,128)}, f32[48,128]{1,0:T(8,128)S(1)}, u32[]{:S(2)}) copy-start(f32[48,128]{1,0:T(8,128)S(1)} %collective-permute-done.2.vxlow_ref) | copy-start | bytes 73732
  174.1 3.5 %copy-start.10 = (f32[48,128]{1,0:T(8,128)}, f32[48,128]{1,0:T(8,128)S(1)}, u32[]{:S(2)}) copy-start(f32[48,128]{1,0:T(8,128)S(1)} %collective-permute-done.3.vxhigh_ref) | copy-start | bytes 73732
  174.1 3.5 %copy-start.6 = (f32[192,128]{1,0:T(8,128)}, f32[192,128]{1,0:T(8,128)S(1)}, u32[]{:S(2)}) copy-start(f32[192,128]{1,0:T(8,128)S(1)} %collective-permute-done.vylow_ref) | copy-start | bytes 294916
  174.2 3.5 %copy-start.7 = (f32[192,128]{1,0:T(8,128)}, f32[192,128]{1,0:T(8,128)S(1)}, u32[]{:S(2)}) copy-start(f32[192,128]{1,0:T(8,128)S(1)} %collective-permute-done.1.vyhigh_ref) | copy-start | bytes 294916
  177.7 38.6 %all-to-all-start.3 = ((f32[32,9,8,128]{3,2,1,0:T(8,128)}), f32[32,9,8,128]{3,2,1,0:T(8,128)S(1)}, u32[]{:S(2)}, u32[]{:S(2)}) async-start(f32[32,9,8,128]{3,2,1,0:T(8,128)} %forward.1), calls=%async_computation.3 | async-start | bytes 2359296 | tf_op jit(solution)/shard_map/all_to_all | solution.py:592
  188.2 1.1 copy-start.12
  216.3 1.0 copy-start
  222.0 40.2 %collective-permute-start.5 = (f32[1152,128]{1,0:T(8,128)}, f32[1152,128]{1,0:T(8,128)S(1)}, u32[]{:S(2)}, u32[]{:S(2)}) collective-permute-start(f32[1152,128]{1,0:T(8,128)} %get-tuple-element.68.ylow_own_ref), channel_id=1, source_target_pairs={{32,0},{64,32},{96,64},{128,96},{160,128},{192,160},{224,192},{33,... | collective-permute-start | bytes 1769480 | tf_op jit(solution)/shard_map/ppermute | solution.py:521
  224.0 38.3 %collective-permute-start.4 = (f32[1152,128]{1,0:T(8,128)}, f32[1152,128]{1,0:T(8,128)S(1)}, u32[]{:S(2)}, u32[]{:S(2)}) collective-permute-start(f32[1152,128]{1,0:T(8,128)} %get-tuple-element.69.yhigh_own_ref), channel_id=1, source_target_pairs={{0,32},{32,64},{64,96},{96,128},{128,160},{160,192},{192,224},{1,3... | collective-permute-start | bytes 1769480 | tf_op jit(solution)/shard_map/ppermute | solution.py:521
  226.4 35.8 %collective-permute-start.6 = (f32[288,128]{1,0:T(8,128)}, f32[288,128]{1,0:T(8,128)S(1)}, u32[]{:S(2)}, u32[]{:S(2)}) collective-permute-start(f32[288,128]{1,0:T(8,128)} %get-tuple-element.70), channel_id=1, source_target_pairs={{0,1},{1,2},{2,3},{3,4},{4,5},{5,6},{6,7},{7,8},{8,9},{9,10},{10,1... | collective-permute-start | bytes 442376 | tf_op jit(solution)/shard_map/ppermute | solution.py:521
  230.6 31.7 %collective-permute-start.7 = (f32[288,128]{1,0:T(8,128)}, f32[288,128]{1,0:T(8,128)S(1)}, u32[]{:S(2)}, u32[]{:S(2)}) collective-permute-start(f32[288,128]{1,0:T(8,128)} %get-tuple-element.71), channel_id=1, source_target_pairs={{1,0},{2,1},{3,2},{4,3},{5,4},{6,5},{7,6},{8,7},{9,8},{10,9},{11,1... | collective-permute-start | bytes 442376 | tf_op jit(solution)/shard_map/ppermute | solution.py:521
  234.4 8.2 %collective-permute-start.8 = (f32[16,128]{1,0:T(8,128)}, f32[16,128]{1,0:T(8,128)S(1)}, u32[]{:S(2)}, u32[]{:S(2)}) collective-permute-start(f32[16,128]{1,0:T(8,128)} %get-tuple-element.72), channel_id=1, source_target_pairs={{0,33},{1,34},{2,35},{3,36},{4,37},{5,38},{6,39},{7,40},{8,41},{9,... | collective-permute-start | bytes 24584 | tf_op jit(solution)/shard_map/ppermute | solution.py:532
  242.5 19.7 %copy-start.13 = (f32[16,128]{1,0:T(8,128)}, f32[16,128]{1,0:T(8,128)S(1)}, u32[]{:S(2)}) copy-start(f32[16,128]{1,0:T(8,128)S(1)} %collective-permute-done.8.low_low_ref) | copy-start | bytes 24580
  242.5 7.3 %collective-permute-start.9 = (f32[16,128]{1,0:T(8,128)}, f32[16,128]{1,0:T(8,128)S(1)}, u32[]{:S(2)}, u32[]{:S(2)}) collective-permute-start(f32[16,128]{1,0:T(8,128)} %get-tuple-element.73), channel_id=1, source_target_pairs={{32,1},{33,2},{34,3},{35,4},{36,5},{37,6},{38,7},{39,8},{40,9},{41... | collective-permute-start | bytes 24584 | tf_op jit(solution)/shard_map/ppermute | solution.py:532
  249.8 12.5 %copy-start.14 = (f32[16,128]{1,0:T(8,128)}, f32[16,128]{1,0:T(8,128)S(1)}, u32[]{:S(2)}) copy-start(f32[16,128]{1,0:T(8,128)S(1)} %collective-permute-done.9.low_high_ref) | copy-start | bytes 24580
  249.8 6.1 %collective-permute-start.10 = (f32[16,128]{1,0:T(8,128)}, f32[16,128]{1,0:T(8,128)S(1)}, u32[]{:S(2)}, u32[]{:S(2)}) collective-permute-start(f32[16,128]{1,0:T(8,128)} %get-tuple-element.74), channel_id=1, source_target_pairs={{1,32},{2,33},{3,34},{4,35},{5,36},{6,37},{7,38},{8,39},{9,40},{10... | collective-permute-start | bytes 24584 | tf_op jit(solution)/shard_map/ppermute | solution.py:532
  255.9 6.4 %copy-start.15 = (f32[16,128]{1,0:T(8,128)}, f32[16,128]{1,0:T(8,128)S(1)}, u32[]{:S(2)}) copy-start(f32[16,128]{1,0:T(8,128)S(1)} %collective-permute-done.10.high_low_ref) | copy-start | bytes 24580
  255.9 6.3 %collective-permute-start.11 = (f32[16,128]{1,0:T(8,128)}, f32[16,128]{1,0:T(8,128)S(1)}, u32[]{:S(2)}, u32[]{:S(2)}) collective-permute-start(f32[16,128]{1,0:T(8,128)} %get-tuple-element.75), channel_id=1, source_target_pairs={{33,0},{34,1},{35,2},{36,3},{37,4},{38,5},{39,6},{40,7},{41,8},{42... | collective-permute-start | bytes 24584 | tf_op jit(solution)/shard_map/ppermute | solution.py:532
  262.2 0.6 copy-start.16
  262.2 0.7 copy-start.4
  262.2 0.7 copy-start.5
  262.3 0.9 copy-start.2
  262.3 1.1 copy-start.3

commit v7 on v6

--- a/solution.py
+++ b/solution.py
@@ -302,8 +302,7 @@
 def edges_kernel(
     shape, late_ref, left_ref, fine_at_ref, coarse_at_ref, second_ref, rest_ref,
     ylow_in_ref, yhigh_in_ref, xlow_in_ref, xhigh_in_ref,
-    ylow_ref, yhigh_ref, xlow_ref, xhigh_ref, low_low_ref, low_high_ref, high_low_ref, high_high_ref, held_ref, plane_ref,
-    sem,
+    ylow_ref, yhigh_ref, xlow_ref, xhigh_ref, held_ref, plane_ref, sem,
 ):
     planes, species, rows, _ = shape
     half = rows // 2
@@ -337,16 +336,20 @@
         shape, late_ref, left_ref, fine_at_ref, coarse_at_ref, second_ref, rest_ref, held_ref, plane_ref,
         sem, half_plane, whole_plane,
     )
-    first, last = 0, (ITERS - 1) * species * planes
-    for corner_ref, edge_ref, at in (
-        (low_low_ref, ylow_ref, first),
-        (low_high_ref, yhigh_ref, last),
-        (high_low_ref, ylow_ref, first + planes - 1),
-        (high_high_ref, yhigh_ref, last + planes - 1),
-    ):
-        corner_ref[...] = jnp.zeros_like(corner_ref)
+
+
+def corners_kernel(planes, species, ylow_ref, yhigh_ref, xlow_ref, xhigh_ref, down_ref, up_ref):
+    deep = xlow_ref.shape[0]
+    down_ref[0:deep] = xlow_ref[...]
+    up_ref[0:deep] = xhigh_ref[...]
+    for message_ref, x in ((down_ref, 0), (up_ref, planes - 1)):
         for s in range(species):
-            corner_ref[s : s + 1] = edge_ref[at + s * planes : at + s * planes + 1]
+            low = ((ITERS - 1) * species + s) * planes + x
+            high = s * planes + x
+            message_ref[deep + s : deep + s + 1] = ylow_ref[low : low + 1]
+            message_ref[deep + 16 + s : deep + 16 + s + 1] = yhigh_ref[high : high + 1]
+        for at in (deep + species, deep + 16 + species):
+            message_ref[at : at + 16 - species] = jnp.zeros((16 - species, message_ref.shape[1]), jnp.float32)
 
 
 def velocity_edges_kernel(vel_ref, ylow_ref, yhigh_ref, xlow_ref, xhigh_ref, *, shape):
@@ -373,28 +376,120 @@
         return new
 
 
-def steps_kernel(
-    shape, late_ref, left_ref, fine_at_ref, coarse_at_ref, inside_ref, diff_ref, second_ref, rest_ref, state_ref,
-    vel_ref, ylow_own_ref, yhigh_own_ref, ylow_ref, yhigh_ref, xlow_ref, xhigh_ref, low_low_ref, low_high_ref, high_low_ref,
-    high_high_ref, vylow_ref, vyhigh_ref, vxlow_ref, vxhigh_ref, out_ref, u0_ref, u1_ref, row_low_ref, row_high_ref, plane_low_ref, plane_high_ref, held_ref, plane_ref, sem,
-    out_sem,
+def along(u, first, last, dim):
+    count = u.shape[dim]
+    at = lax.broadcasted_iota(jnp.int32, u.shape, dim)
+    low = jnp.where(at == 0, first, pltpu.roll(u, 1, dim))
+    high = jnp.where(at == count - 1, last, pltpu.roll(u, count - 1, dim))
+    return low, high
+
+
+def advance_plane(diff_ref, velocity, center, below, above, y_low, y_high, store):
+    flow = Flow(velocity)
+    for s in range(diff_ref.shape[0]):
+        u = center(s)
+        sides = ((below(s), above(s)), along(u, y_low(s), y_high(s), 0), along(u, u, u, 1))
+        store(s, flow.step(u, sides, diff_ref[s]))
+
+
+def planes_of(ref, x, rows, size):
+    return lambda s: ref[pl.ds(pl.multiple_of(x * size + s * rows, rows), rows), :]
+
+
+def advance(shape, diff_ref, vel_ref, u_ref, new_ref, low, high, y_low, y_high, after):
+    planes, species, rows, _ = shape
+    size = species * rows
+
+    def group(x, first, last):
+        for i in range(UNROLL):
+
+            def store(s, new):
+                new_ref[pl.ds(pl.multiple_of((x + i) * size + s * rows, rows), rows), :] = new
+
+            advance_plane(
+                diff_ref,
+                [vel_ref[x + i, k] for k in range(3)],
+                planes_of(u_ref, x + i, rows, size),
+                low if first and i == 0 else planes_of(u_ref, x + i - 1, rows, size),
+                high if last and i == UNROLL - 1 else planes_of(u_ref, x + i + 1, rows, size),
+                y_low(x + i),
+                y_high(x + i),
+                store,
+            )
+        after(x // UNROLL)
+
+    def body(g, carry):
+        group(g * UNROLL, False, False)
+        return carry
+
+    group(0, True, False)
+    lax.fori_loop(1, planes // UNROLL - 1, body, 0)
+    group(planes - UNROLL, False, True)
+
+
+def send_group(shape, from_ref, to_ref, sem, g):
+    size = UNROLL * shape[1] * shape[2]
+    part = pl.ds(pl.multiple_of(g * size, size), size)
+    return pltpu.make_async_copy(from_ref.at[part], to_ref.at[part], sem.at[g])
+
+
+def finish_groups(shape, from_ref, to_ref, sem):
+    def finish(g, carry):
+        send_group(shape, from_ref, to_ref, sem, g).wait()
+        return carry
+
+    lax.fori_loop(0, shape[0] // UNROLL, finish, 0)
+
+
+def first_step_kernel(
+    shape, late_ref, left_ref, fine_at_ref, coarse_at_ref, diff_ref, second_ref, rest_ref, state_ref, vel_ref, out_ref,
+    u0_ref, u1_ref, held_ref, plane_ref, sem, out_sem,
 ):
-    planes, species, rows, lanes = shape
+    _, species, rows, _ = shape
     half = rows // 2
     size = species * rows
     copy = pltpu.make_async_copy(state_ref, u0_ref, sem)
     copy.start()
-
-    def along(u, first, last, dim):
-        count = u.shape[dim]
-        at = lax.broadcasted_iota(jnp.int32, u.shape, dim)
-        low = jnp.where(at == 0, first, pltpu.roll(u, 1, dim))
-        high = jnp.where(at == count - 1, last, pltpu.roll(u, count - 1, dim))
-        return low, high
+    copy.wait()
+
+    def half_plane(x, h, ref, slot):
+        for s in range(species):
+            base = pl.multiple_of(x * size + s * rows + h * half, half)
+            u0_ref[pl.ds(base, half), :] = ref[slot, s]
+
+    def whole_plane(x):
+        for s in range(species):
+            u0_ref[pl.ds(pl.multiple_of(x * size + s * rows, rows), rows), :] = plane_ref[s]
+
+    late_units(
+        shape, late_ref, left_ref, fine_at_ref, coarse_at_ref, second_ref, rest_ref, held_ref, plane_ref,
+        sem, half_plane, whole_plane,
+    )
+
+    def nothing(s):
+        return 0.0
+
+    advance(
+        shape, diff_ref, vel_ref, u0_ref, u1_ref, nothing, nothing, lambda x: nothing, lambda x: nothing,
+        lambda g: send_group(shape, u1_ref, out_ref, out_sem, g).start(),
+    )
+    finish_groups(shape, u1_ref, out_ref, out_sem)
+
+
+def second_step_kernel(
+    shape, inside_ref, diff_ref, first_ref, vel_ref, ylow_own_ref, yhigh_own_ref, xlow_own_ref, xhigh_own_ref, ylow_ref,
+    yhigh_ref, xlow_ref, xhigh_ref, vylow_own_ref, vyhigh_own_ref, vylow_ref, vyhigh_ref, vxlow_ref, vxhigh_ref,
+    out_ref, u1_ref, u2_ref, row_low_ref, row_high_ref, plane_low_ref, plane_high_ref, sem, out_sem,
+):
+    planes, species, rows, lanes = shape
+    size = species * rows
+    deep = ITERS * size
+    copy = pltpu.make_async_copy(first_ref, u1_ref, sem)
+    copy.start()
 
     for (near_ref, near, far, own_ref, own, v_ref, corner, target_ref, inside) in (
-        (ylow_ref, 1, 0, ylow_own_ref, 0, vylow_ref, (low_low_ref, high_low_ref), row_low_ref, 0),
-        (yhigh_ref, 0, 1, yhigh_own_ref, 1, vyhigh_ref, (low_high_ref, high_high_ref), row_high_ref, 1),
+        (ylow_ref, 1, 0, ylow_own_ref, 0, vylow_ref, deep, row_low_ref, 0),
+        (yhigh_ref, 0, 1, yhigh_own_ref, 1, vyhigh_ref, deep + 16, row_high_ref, 1),
     ):
         for x in range(0, planes, 16):
             flow = Flow([v_ref[k * planes + x : k * planes + x + 16] for k in range(3)])
@@ -407,11 +502,11 @@
                 u = band(near_ref, near)
                 start = (near * species + s) * planes
                 if x == 0:
-                    first = corner[0][s : s + 1]
+                    first = xlow_ref[corner + s : corner + s + 1]
                 else:
                     first = near_ref[start + x - 1 : start + x]
                 if x + 16 == planes:
-                    last = corner[1][s : s + 1]
+                    last = xhigh_ref[corner + s : corner + s + 1]
                 else:
                     last = near_ref[start + x + 16 : start + x + 17]
                 outer, inner = band(near_ref, far), band(own_ref, own)
@@ -420,91 +515,49 @@
                 target_ref[s * planes + x : s * planes + x + 16] = new * inside_ref[inside]
 
     def at(ref, x):
-        return lambda s: ref[pl.ds(pl.multiple_of(x * size + s * rows, rows), rows), :]
-
-    def edge(ref, offset, x):
-        return lambda s: ref[pl.ds(offset + s * planes + x, 1), :]
-
-    def plane(velocity, center, below, above, y_low, y_high, store):
-        flow = Flow(velocity)
-        for s in range(species):
-            u = center(s)
-            sides = ((below(s), above(s)), along(u, y_low(s), y_high(s), 0), along(u, u, u, 1))
-            store(s, flow.step(u, sides, diff_ref[s]))
-
-    copy.wait()
-
-    def half_plane(x, h, ref, slot):
-        for s in range(species):
-            base = pl.multiple_of(x * size + s * rows + h * half, half)
-            u0_ref[pl.ds(base, half), :] = ref[slot, s]
-
-    def whole_plane(x):
-        for s in range(species):
-            u0_ref[pl.ds(pl.multiple_of(x * size + s * rows, rows), rows), :] = plane_ref[s]
-
-    late_units(
-        shape, late_ref, left_ref, fine_at_ref, coarse_at_ref, second_ref, rest_ref, held_ref, plane_ref,
-        sem, half_plane, whole_plane,
-    )
-
-    for (halo_ref, near, below, above, v_ref, target_ref, (corner_low_ref, corner_high_ref, inside)) in (
-        (xlow_ref, 1, at(xlow_ref, 0), at(u0_ref, 0), vxlow_ref, plane_low_ref, (low_low_ref, low_high_ref, 2)),
-        (xhigh_ref, 0, at(u0_ref, planes - 1), at(xhigh_ref, 1), vxhigh_ref, plane_high_ref, (high_low_ref, high_high_ref, 3)),
+        return planes_of(ref, x, rows, size)
+
+    for (halo_ref, near, below, above, v_ref, target_ref, inside) in (
+        (xlow_ref, 1, at(xlow_ref, 0), at(xlow_own_ref, 0), vxlow_ref, plane_low_ref, 2),
+        (xhigh_ref, 0, at(xhigh_own_ref, ITERS - 1), at(xhigh_ref, 1), vxhigh_ref, plane_high_ref, 3),
     ):
 
         def store(s, new):
             target_ref[s * rows : (s + 1) * rows] = new * inside_ref[inside]
 
-        def corner(ref):
-            return lambda s: ref[s : s + 1]
+        def corner(offset):
+            return lambda s: halo_ref[deep + offset + s : deep + offset + s + 1]
 
         velocity = [v_ref[k * rows : (k + 1) * rows] for k in range(3)]
-        plane(velocity, at(halo_ref, near), below, above, corner(corner_low_ref), corner(corner_high_ref), store)
-
-    def advance(u_ref, new_ref, low, high, y_low, y_high, after):
-        def group(x, first, last):
-            for i in range(UNROLL):
-
-                def store(s, new):
-                    new_ref[pl.ds(pl.multiple_of((x + i) * size + s * rows, rows), rows), :] = new
-
-                plane(
-                    [vel_ref[x + i, k] for k in range(3)],
-                    at(u_ref, x + i),
-                    low if first and i == 0 else at(u_ref, x + i - 1),
-                    high if last and i == UNROLL - 1 else at(u_ref, x + i + 1),
-                    edge(*y_low, x + i),
-                    edge(*y_high, x + i),
-                    store,
-                )
-            after(x // UNROLL)
-
-        def body(g, carry):
-            group(g * UNROLL, False, False)
-            return carry
-
-        group(0, True, False)
-        lax.fori_loop(1, planes // UNROLL - 1, body, 0)
-        group(planes - UNROLL, False, True)
-
-    def send(g):
-        part = pl.ds(pl.multiple_of(g * UNROLL * size, UNROLL * size), UNROLL * size)
-        return pltpu.make_async_copy(u0_ref.at[part], out_ref.at[part], out_sem.at[g])
+        advance_plane(diff_ref, velocity, at(halo_ref, near), below, above, corner(0), corner(16), store)
+
+    copy.wait()
+    for x in range(0, planes, 8):
+        up = jnp.maximum(vylow_own_ref[planes + x : planes + x + 8], 0.0)
+        down = jnp.minimum(vyhigh_own_ref[planes + x : planes + x + 8], 0.0)
+        for s in range(species):
+            low = pl.ds((x * species + s) * rows, 8, stride=size)
+            high = pl.ds((x * species + s) * rows + rows - 1, 8, stride=size)
+            start = species * planes + s * planes + x
+            u1_ref[low, :] = u1_ref[low, :] + (diff_ref[s] + up) * ylow_ref[start : start + 8]
+            start = s * planes + x
+            u1_ref[high, :] = u1_ref[high, :] + (diff_ref[s] - down) * yhigh_ref[start : start + 8]
+    up = jnp.maximum(vel_ref[0, 0], 0.0)
+    down = jnp.minimum(vel_ref[planes - 1, 0], 0.0)
+    for s in range(species):
+        low = slice(s * rows, (s + 1) * rows)
+        high = slice((planes - 1) * size + s * rows, (planes - 1) * size + (s + 1) * rows)
+        u1_ref[low] = u1_ref[low] + (diff_ref[s] + up) * at(xlow_ref, 1)(s)
+        u1_ref[high] = u1_ref[high] + (diff_ref[s] - down) * at(xhigh_ref, 0)(s)
+
+    def edge(ref):
+        return lambda x: lambda s: ref[pl.ds(s * planes + x, 1), :]
 
     advance(
-        u0_ref, u1_ref, at(xlow_ref, 1), at(xhigh_ref, 0), (ylow_ref, species * planes), (yhigh_ref, 0), lambda g: None
+        shape, diff_ref, vel_ref, u1_ref, u2_ref, at(plane_low_ref, 0), at(plane_high_ref, 0), edge(row_low_ref),
+        edge(row_high_ref), lambda g: send_group(shape, u2_ref, out_ref, out_sem, g).start(),
     )
-    advance(
-        u1_ref, u0_ref, at(plane_low_ref, 0), at(plane_high_ref, 0), (row_low_ref, 0), (row_high_ref, 0),
-        lambda g: send(g).start(),
-    )
-
-    def finish(g, carry):
-        send(g).wait()
-        return carry
-
-    lax.fori_loop(0, planes // UNROLL, finish, 0)
+    finish_groups(shape, u2_ref, out_ref, out_sem)
 
 
 def empty_kernel(out_ref):
@@ -519,17 +572,6 @@
     size = lax.axis_size(axis)
     up = [(i, (i + 1) % size) for i in range(size - 1)]
     return lax.ppermute(high, axis, up), lax.ppermute(low, axis, [(b, a) for a, b in up])
-
-
-def diagonal(value, grp_step, dev_step):
-    groups, devices = lax.axis_size("grp"), lax.axis_size("dev")
-    pairs = []
-    for g in range(groups):
-        for d in range(devices):
-            to_g, to_d = g + grp_step, d + dev_step
-            if 0 <= to_g < groups and 0 <= to_d < devices:
-                pairs.append((g * devices + d, to_g * devices + to_d))
-    return lax.ppermute(value, ("grp", "dev"), pairs)
 
 
 def on_device(old_fine, old_ids, old_coarse, coarse_ids, velocity, diffusion):
@@ -680,40 +722,59 @@
         pltpu.VMEM((species, rows, lanes), f32),
         pltpu.SemaphoreType.DMA,
     ]
-    corner_shape = jax.ShapeDtypeStruct((16, lanes), f32)
-    ylow_own, yhigh_own, xlow_own, xhigh_own, *corners = pl.pallas_call(
+    ylow_own, yhigh_own, xlow_own, xhigh_own = pl.pallas_call(
         functools.partial(edges_kernel, old_fine.shape),
-        out_shape=edge_shapes(ITERS, species) + [corner_shape] * 4,
+        out_shape=edge_shapes(ITERS, species),
         in_specs=[SMEM] * 4 + [VMEM, ANY] + [VMEM] * 4,
-        out_specs=[VMEM] * 8,
+        out_specs=[VMEM] * 4,
         scratch_shapes=late_scratch,
         compiler_params=PARAMS,
         cost_estimate=cost(4),
         name="edges",
     )(late, left, fine_at, coarse_at, second, rest, *edges)
     ylow, yhigh = neighbours("grp", ylow_own, yhigh_own)
-    xlow, xhigh = neighbours("dev", xlow_own, xhigh_own)
-    low_low, low_high, high_low, high_high = corners
-    corners = [diagonal(high_high, 1, 1), diagonal(high_low, -1, 1), diagonal(low_high, 1, -1), diagonal(low_low, -1, -1)]
+    state_scratch = pltpu.VMEM(state_shape.shape, f32)
+    group_sems = pltpu.SemaphoreType.DMA((planes // UNROLL,))
+    stepped = pl.pallas_call(
+        functools.partial(first_step_kernel, old_fine.shape),
+        out_shape=state_shape,
+        in_specs=[SMEM] * 5 + [VMEM, ANY, ANY, VMEM],
+        out_specs=ANY,
+        scratch_shapes=[state_scratch] * 2 + late_scratch + [group_sems],
+        compiler_params=PARAMS,
+        cost_estimate=cost(10),
+        name="first_step",
+    )(late, left, fine_at, coarse_at, diffusion, second, rest, state, velocity)
+    ylow, yhigh, stepped = lax.optimization_barrier((ylow, yhigh, stepped))
+    message = jax.ShapeDtypeStruct((ITERS * size + 32, lanes), f32)
+    down, up = pl.pallas_call(
+        functools.partial(corners_kernel, planes, species),
+        out_shape=[message] * 2,
+        in_specs=[VMEM] * 4,
+        out_specs=[VMEM] * 2,
+        compiler_params=PARAMS,
+        name="corners",
+    )(ylow, yhigh, xlow_own, xhigh_own)
+    xlow, xhigh = neighbours("dev", down, up)
     grp, dev = lax.axis_index("grp"), lax.axis_index("dev")
     inside = jnp.stack([grp > 0, grp < lax.axis_size("grp") - 1, dev > 0, dev < devices - 1]).astype(f32)
     row_edge = pltpu.VMEM((species * planes, lanes), f32)
     plane_edge = pltpu.VMEM((size, lanes), f32)
     done = pl.pallas_call(
-        functools.partial(steps_kernel, old_fine.shape),
+        functools.partial(second_step_kernel, old_fine.shape),
         out_shape=state_shape,
-        in_specs=[SMEM] * 6 + [VMEM, ANY, ANY] + [VMEM] * 15,
+        in_specs=[SMEM] * 2 + [ANY] + [VMEM] * 15,
         out_specs=ANY,
-        scratch_shapes=[pltpu.VMEM(state_shape.shape, f32)] * 2
+        scratch_shapes=[state_scratch] * 2
         + [row_edge] * 2
         + [plane_edge] * 2
-        + late_scratch
-        + [pltpu.SemaphoreType.DMA((planes // UNROLL,))],
+        + [pltpu.SemaphoreType.DMA, group_sems],
         compiler_params=PARAMS,
-        name="steps",
+        cost_estimate=cost(10),
+        name="second_step",
     )(
-        late, left, fine_at, coarse_at, inside, diffusion, second, rest, state, velocity,
-        ylow_own, yhigh_own, ylow, yhigh, xlow, xhigh, *corners, *flow_edges,
+        inside, diffusion, stepped, velocity, ylow_own, yhigh_own, xlow_own, xhigh_own, ylow, yhigh, xlow, xhigh,
+        vylow, vyhigh, *flow_edges,
     )
     return done.reshape(old_fine.shape)
 

time: 283 us -> 270 us (0.954)
  waiting for transfers between devices: 146 us -> 133 us
  starting transfers between devices: 65.1 us -> 54.9 us
  Pallas kernels: 48.8 us -> 58 us
    ppermute x4 -> x0, waiting for transfers between devices: 15.8 us -> none  [diagonal(): return lax.ppermute(value, ('grp', 'dev'), pairs)]
    ppermute x4 -> x0, starting transfers between devices: 11.4 us -> none  [diagonal(): return lax.ppermute(value, ('grp', 'dev'), pairs)]
    pallas_call x1 -> x3, Pallas kernels: 16.7 us -> 24.6 us  [the longest x1 11.4 us: on_device(): pl.pallas_call(functools.partial(first_step_kernel, old_fine.shape), out_...]
  transfers between devices with their start and end apart: 15 -> 11, of which waited for: 7 -> 6; matrix products, arithmetic and copies ran while one was open for 4% -> 4% of each run, Pallas kernels for 4% -> 9%
where the time goes in v7:
time: 270 us; the launch traced here: 267 us
  waiting for transfers between devices  133 us (49%)
  Pallas kernels  58 us (21%)
  starting transfers between devices  54.9 us (20%)
  other arithmetic  15.6 us (6%)
  local copies, waits for them, and re-layouts  3.86 us (1%)
    ppermute x4, waiting for transfers between devices, neighbours(): lax.ppermute(high, axis, up)  110 us
    all_to_all x2, waiting for transfers between devices, exchange(): return lax.all_to_all(value, 'dev', split_axis=0, concat_axis=0, tiled=True)  17.5 us
    ppermute x4, starting transfers between devices, neighbours(): lax.ppermute(low, axis, [(b, a) for a, b in up])  16.6 us
    all_to_all x2, starting transfers between devices, exchange(): return lax.all_to_all(value, 'dev', split_axis=0, concat_axis=0, tiled=True)  16.3 us
    all_to_all x1, starting transfers between devices, on_device(): lax.all_to_all(labels, 'dev', split_axis=0, concat_axis=0, tiled=True)  11.6 us
    pallas_call x1, Pallas kernels, on_device(): pl.pallas_call(functools.partial(first_step_kernel, old_fine.shape), out_...  11.4 us
    pallas_call x1, Pallas kernels, on_device(): pl.pallas_call(functools.partial(second_step_kernel, old_fine.shape), out...  11.2 us
    ppermute x4, starting transfers between devices, neighbours(): lax.ppermute(high, axis, up)  10.4 us
  transfers between devices with their start and end apart: 11, of which 6 were waited for; matrix products, arithmetic and copies ran while one was open for 4% of the time, Pallas kernels for 9%

profile of v7, /device:TPU:22, one launch (start us, length us, event | category | flops | bytes accessed | tf_op | source)
XLA Modules:
  0.0 266.5 jit_solution(3040886717556798100)
XLA Ops:
  0.0 0.7 pad_add_fusion
  0.7 0.6 broadcast_in_dim.70
  1.4 11.6 %all-to-all-start.1 = ((s32[32,1,96]{2,1,0:T(1,128)}), s32[32,1,96]{2,1,0:T(1,128)S(1)}, u32[]{:S(2)}, u32[]{:S(2)}) async-start(s32[32,1,96]{2,1,0:T(1,128)} %broadcast_in_dim.70), calls=%async_computation.1 | async-start | bytes 32768 | tf_op jit(solution)/shard_map/all_to_all | solution.py:593
  13.0 0.7 fusion.17
  13.6 0.7 and_select_fusion.1
  14.3 0.7 compare_select_fusion.21
  15.0 0.7 fusion.16
  16.0 0.7 compare_select_fusion.20.fine_at_ref
  16.9 3.9 %all-to-all-done.1 = s32[32,1,96]{2,1,0:T(1,128)S(1)} async-done(((s32[32,1,96]{2,1,0:T(1,128)}), s32[32,1,96]{2,1,0:T(1,128)S(1)}, u32[]{:S(2)}, u32[]{:S(2)}) %all-to-all-start.1) | async-done | bytes 12320 | tf_op jit(solution)/shard_map/all_to_all | solution.py:593
  21.1 0.9 convert_reduce_fusion.5
  22.0 1.1 convert_reduce_fusion
  23.4 0.4 convert_reduce_fusion.4
  23.8 0.6 multiply_add_fusion.units_ref
  24.4 4.6 %plan.1 = (s32[8,128]{1,0:T(8,128)S(1)}, s32[32,128]{1,0:T(8,128)}) custom-call(s32[1]{0:T(128)} %bitcast.7.me_ref, s32[32,128]{1,0:T(8,128)} %multiply_add_fusion.units_ref), custom_call_target="tpu_custom_call" | custom-call | tf_op jit(solution)/shard_map/plan/pallas_call | solution.py:607
  29.0 0.7 slice_reduce_fusion
  29.6 0.7 compare_select_fusion.coarse_at_ref
  30.3 7.6 %pack.1 = f32[160,9,8,128]{3,2,1,0:T(8,128)} custom-call(s32[1]{0:T(128)} %bitcast.7.me_ref, s32[64]{0:T(128)S(1)} %compare_select_fusion.20.fine_at_ref, s32[32]{0:T(128)S(1)} %compare_select_fusion.coarse_at_ref, s32[8,128]{1,0:T(8,128)S(1)} %get-tuple-element.55.row_ref, f32[64,9,16,128]{3,2,1,0:T(8,128)} %fine_in_ref.1, f32[32,9,8,64]{3,2,1,0:T(8,128)} %coarse_ref.1), custom_call_target="tpu_custom_call" | custom-call | tf_op jit(solution)/shard_map/pack/pallas_call | solution.py:637
  38.6 6.5 %all-to-all-start.2 = ((f32[160,9,8,128]{3,2,1,0:T(8,128)}), f32[160,9,8,128]{3,2,1,0:T(8,128)}, u32[]{:S(2)}, u32[]{:S(2)}) async-start(f32[160,9,8,128]{3,2,1,0:T(8,128)} %pack.1), calls=%async_computation.2 | async-start | bytes 11796480 | tf_op jit(solution)/shard_map/all_to_all | solution.py:634
  45.3 0.9 convert_reduce_fusion.2
  46.3 1.3 select_reduce_fusion.fine_at_ref
  47.9 2.2 velocity_edges.1
  50.1 3.4 %collective-permute-start.2 = (f32[48,128]{1,0:T(8,128)}, f32[48,128]{1,0:T(8,128)S(1)}, u32[]{:S(2)}, u32[]{:S(2)}) collective-permute-start(f32[48,128]{1,0:T(8,128)} %get-tuple-element.60), channel_id=1, source_target_pairs={{0,1},{1,2},{2,3},{3,4},{4,5},{5,6},{6,7},{7,8},{8,9},{9,10},{10,1... | collective-permute-start | bytes 73736 | tf_op jit(solution)/shard_map/ppermute | solution.py:574
  53.4 4.6 %collective-permute-start.3 = (f32[48,128]{1,0:T(8,128)}, f32[48,128]{1,0:T(8,128)S(1)}, u32[]{:S(2)}, u32[]{:S(2)}) collective-permute-start(f32[48,128]{1,0:T(8,128)} %get-tuple-element.61), channel_id=1, source_target_pairs={{1,0},{2,1},{3,2},{4,3},{5,4},{6,5},{7,6},{8,7},{9,8},{10,9},{11,1... | collective-permute-start | bytes 73736 | tf_op jit(solution)/shard_map/ppermute | solution.py:574
  58.0 1.9 collective-permute-start
  59.9 3.6 %collective-permute-start.1 = (f32[192,128]{1,0:T(8,128)}, f32[192,128]{1,0:T(8,128)S(1)}, u32[]{:S(2)}, u32[]{:S(2)}) collective-permute-start(f32[192,128]{1,0:T(8,128)} %get-tuple-element.59.vylow_own_ref), channel_id=1, source_target_pairs={{32,0},{64,32},{96,64},{128,96},{160,128},{192,160},{224,192},{33,... | collective-permute-start | bytes 294920 | tf_op jit(solution)/shard_map/ppermute | solution.py:574
  63.8 0.8 convert_reduce_fusion.3
  64.6 109.0 %collective-permute-done.2.vxlow_ref = f32[48,128]{1,0:T(8,128)S(1)} collective-permute-done((f32[48,128]{1,0:T(8,128)}, f32[48,128]{1,0:T(8,128)S(1)}, u32[]{:S(2)}, u32[]{:S(2)}) %collective-permute-start.2) | collective-permute-done | bytes 24608 | tf_op jit(solution)/shard_map/ppermute | solution.py:574
  173.6 1.1 all-to-all-done.2.in_ref.first_ref
  174.7 3.6 %forward.1 = f32[32,9,8,128]{3,2,1,0:T(8,128)} custom-call(s32[1]{0:T(128)} %bitcast.7.me_ref, s32[32,128]{1,0:T(8,128)} %get-tuple-element.54.column_ref, f32[160,9,8,128]{3,2,1,0:T(8,128)} %all-to-all-done.2.in_ref.first_ref), custom_call_target="tpu_custom_call" | custom-call | bytes 10800000 | tf_op jit(solution)/shard_map/forward/pallas_call | solution.py:675
  178.3 9.8 %all-to-all-start.3 = ((f32[32,9,8,128]{3,2,1,0:T(8,128)}), f32[32,9,8,128]{3,2,1,0:T(8,128)S(1)}, u32[]{:S(2)}, u32[]{:S(2)}) async-start(f32[32,9,8,128]{3,2,1,0:T(8,128)} %forward.1), calls=%async_computation.3 | async-start | bytes 2359296 | tf_op jit(solution)/shard_map/all_to_all | solution.py:634
  188.6 0.7 select_reduce_fusion.1.coarse_at_ref
  189.8 0.6 pad_add_fusion.1.late_ref
  190.4 10.3 %build.1 = (f32[9216,128]{1,0:T(8,128)}, f32[1152,128]{1,0:T(8,128)}, f32[1152,128]{1,0:T(8,128)}, f32[288,128]{1,0:T(8,128)}, f32[288,128]{1,0:T(8,128)}) custom-call(s32[64]{0:T(128)} %copy-done.11, s32[32]{0:T(128)} %copy-done.12, f32[160,9,8,128]{3,2,1,0:T(8,128)} %all-to-all-done.2.in_ref.first_ref), custom_call_target="tpu_custom_call" | custom-call | bytes 36000000 | tf_op jit(solution)/shard_map/build/pallas_call | solution.py:689
  200.7 16.4 %all-to-all-done.3.second_ref = f32[32,9,8,128]{3,2,1,0:T(8,128)S(1)} async-done(((f32[32,9,8,128]{3,2,1,0:T(8,128)}), f32[32,9,8,128]{3,2,1,0:T(8,128)S(1)}, u32[]{:S(2)}, u32[]{:S(2)}) %all-to-all-start.3) | async-done | bytes 1179680 | tf_op jit(solution)/shard_map/all_to_all | solution.py:634
  217.1 1.1 copy-done
  218.2 5.1 %edges.1 = (f32[1152,128]{1,0:T(8,128)}, f32[1152,128]{1,0:T(8,128)}, f32[288,128]{1,0:T(8,128)}, f32[288,128]{1,0:T(8,128)}) custom-call(s32[96]{0:T(128)} %pad_add_fusion.1.late_ref, s32[1]{0:T(128)} %bitcast.8.left_ref, s32[64]{0:T(128)} %copy-done.11, s32[32]{0:T(128)} %copy-done.12, f32[32,9,8,128]{3,2,1,0:T(8,128)} %copy-done, ...), custom_call_target="tpu_custom_call" | custom-call | bytes 14400000 | tf_op jit(solution)/shard_map/edges/pallas_call | solution.py:725
  223.3 1.9 collective-permute-start.4
  225.2 3.6 %collective-permute-start.5 = (f32[1152,128]{1,0:T(8,128)}, f32[1152,128]{1,0:T(8,128)S(1)}, u32[]{:S(2)}, u32[]{:S(2)}) collective-permute-start(f32[1152,128]{1,0:T(8,128)} %get-tuple-element.69.ylow_own_ref), channel_id=1, source_target_pairs={{32,0},{64,32},{96,64},{128,96},{160,128},{192,160},{224,192},{33,... | collective-permute-start | bytes 1769480 | tf_op jit(solution)/shard_map/ppermute | solution.py:574
  228.9 11.4 %first_step.1.first_ref = f32[9216,128]{1,0:T(8,128)} custom-call(s32[96]{0:T(128)} %pad_add_fusion.1.late_ref, s32[1]{0:T(128)} %bitcast.8.left_ref, s32[64]{0:T(128)} %copy-done.11, s32[32]{0:T(128)} %copy-done.12, f32[9]{0:T(128)} %diff_ref.3, f32[32,9,8,128]{3,2,1,0:T(8,128)} %copy-done, f32[128,9,8,128]{3,2,1,0:T(8,128)} %get-tuple-element.97.rest_ref, ...), custom_call_target="tpu_custom_call" | custom-call | bytes 36000000 | tf_op jit(solution)/shard_map/first_step/pallas_call | solution.py:738
  240.3 0.8 copy-done.2
  241.3 2.1 corners.1
  243.4 3.2 %collective-permute-start.6 = (f32[320,128]{1,0:T(8,128)}, f32[320,128]{1,0:T(8,128)S(1)}, u32[]{:S(2)}, u32[]{:S(2)}) collective-permute-start(f32[320,128]{1,0:T(8,128)} %get-tuple-element.76), channel_id=1, source_target_pairs={{0,1},{1,2},{2,3},{3,4},{4,5},{5,6},{6,7},{7,8},{8,9},{9,10},{10,1... | collective-permute-start | bytes 491528 | tf_op jit(solution)/shard_map/ppermute | solution.py:574
  246.6 4.7 %collective-permute-start.7 = (f32[320,128]{1,0:T(8,128)}, f32[320,128]{1,0:T(8,128)S(1)}, u32[]{:S(2)}, u32[]{:S(2)}) collective-permute-start(f32[320,128]{1,0:T(8,128)} %get-tuple-element.77), channel_id=1, source_target_pairs={{1,0},{2,1},{3,2},{4,3},{5,4},{6,5},{7,6},{8,7},{9,8},{10,9},{11,1... | collective-permute-start | bytes 491528 | tf_op jit(solution)/shard_map/ppermute | solution.py:574
  251.3 0.7 add_convert_fusion.inside_ref
  252.0 1.1 collective-permute-done.6.xlow_ref
  253.1 1.4 collective-permute-done.7.xhigh_ref
  254.5 0.7 copy-done.5
  255.1 11.2 %second_step.1 = f32[9216,128]{1,0:T(8,128)} custom-call(f32[4]{0:T(128)} %add_convert_fusion.inside_ref, f32[9]{0:T(128)} %diff_ref.3, f32[9216,128]{1,0:T(8,128)} %first_step.1.first_ref, f32[64,3,16,128]{3,2,1,0:T(8,128)} %vel_ref.3, f32[1152,128]{1,0:T(8,128)} %get-tuple-element.69.ylow_own_ref, f32[1152,128]{1,0:T(8,128)} %get-tuple-element.68.yhigh_own_ref, ...), custom_call_target="tpu_custom_call" | custom-call | bytes 36000000 | tf_op jit(solution)/shard_map/second_step/pallas_call | solution.py:763
  (69 shorter events, 2.9 us)
Async XLA Ops:
  1.4 19.4 %all-to-all-start.1 = ((s32[32,1,96]{2,1,0:T(1,128)}), s32[32,1,96]{2,1,0:T(1,128)S(1)}, u32[]{:S(2)}, u32[]{:S(2)}) async-start(s32[32,1,96]{2,1,0:T(1,128)} %broadcast_in_dim.70), calls=%async_computation.1 | async-start | bytes 32768 | tf_op jit(solution)/shard_map/all_to_all | solution.py:593
  30.3 8.2 %copy-start.1 = (f32[32,9,8,64]{3,2,1,0:T(8,128)S(1)}, f32[32,9,8,64]{3,2,1,0:T(8,128)}, u32[]{:S(2)}) copy-start(f32[32,9,8,64]{3,2,1,0:T(8,128)} %coarse_ref.1) | copy-start | bytes 1769476
  38.6 6.6 %copy-start.8 = (s32[32,128]{1,0:T(8,128)S(1)}, s32[32,128]{1,0:T(8,128)}, u32[]{:S(2)}) copy-start(s32[32,128]{1,0:T(8,128)} %get-tuple-element.54.column_ref) | copy-start | bytes 49156
  38.6 136.1 %all-to-all-start.2 = ((f32[160,9,8,128]{3,2,1,0:T(8,128)}), f32[160,9,8,128]{3,2,1,0:T(8,128)}, u32[]{:S(2)}, u32[]{:S(2)}) async-start(f32[160,9,8,128]{3,2,1,0:T(8,128)} %pack.1), calls=%async_computation.2 | async-start | bytes 11796480 | tf_op jit(solution)/shard_map/all_to_all | solution.py:634
  47.7 140.6 %copy-start.11 = (s32[64]{0:T(128)}, s32[64]{0:T(128)S(1)}, u32[]{:S(2)}) copy-start(s32[64]{0:T(128)S(1)} %select_reduce_fusion.fine_at_ref) | copy-start | bytes 772
  50.1 123.5 %collective-permute-start.2 = (f32[48,128]{1,0:T(8,128)}, f32[48,128]{1,0:T(8,128)S(1)}, u32[]{:S(2)}, u32[]{:S(2)}) collective-permute-start(f32[48,128]{1,0:T(8,128)} %get-tuple-element.60), channel_id=1, source_target_pairs={{0,1},{1,2},{2,3},{3,4},{4,5},{5,6},{6,7},{7,8},{8,9},{9,10},{10,1... | collective-permute-start | bytes 73736 | tf_op jit(solution)/shard_map/ppermute | solution.py:574
  53.4 120.1 %collective-permute-start.3 = (f32[48,128]{1,0:T(8,128)}, f32[48,128]{1,0:T(8,128)S(1)}, u32[]{:S(2)}, u32[]{:S(2)}) collective-permute-start(f32[48,128]{1,0:T(8,128)} %get-tuple-element.61), channel_id=1, source_target_pairs={{1,0},{2,1},{3,2},{4,3},{5,4},{6,5},{7,6},{8,7},{9,8},{10,9},{11,1... | collective-permute-start | bytes 73736 | tf_op jit(solution)/shard_map/ppermute | solution.py:574
  58.0 115.6 %collective-permute-start = (f32[192,128]{1,0:T(8,128)}, f32[192,128]{1,0:T(8,128)S(1)}, u32[]{:S(2)}, u32[]{:S(2)}) collective-permute-start(f32[192,128]{1,0:T(8,128)} %get-tuple-element.58.vyhigh_own_ref), channel_id=1, source_target_pairs={{0,32},{32,64},{64,96},{96,128},{128,160},{160,192},{192,224},{1,3... | collective-permute-start | bytes 294920 | tf_op jit(solution)/shard_map/ppermute | solution.py:574
  59.9 113.6 %collective-permute-start.1 = (f32[192,128]{1,0:T(8,128)}, f32[192,128]{1,0:T(8,128)S(1)}, u32[]{:S(2)}, u32[]{:S(2)}) collective-permute-start(f32[192,128]{1,0:T(8,128)} %get-tuple-element.59.vylow_own_ref), channel_id=1, source_target_pairs={{32,0},{64,32},{96,64},{128,96},{160,128},{192,160},{224,192},{33,... | collective-permute-start | bytes 294920 | tf_op jit(solution)/shard_map/ppermute | solution.py:574
  173.6 4.7 %copy-start.9 = (f32[48,128]{1,0:T(8,128)}, f32[48,128]{1,0:T(8,128)S(1)}, u32[]{:S(2)}) copy-start(f32[48,128]{1,0:T(8,128)S(1)} %collective-permute-done.2.vxlow_ref) | copy-start | bytes 73732
  173.6 4.7 %copy-start.10 = (f32[48,128]{1,0:T(8,128)}, f32[48,128]{1,0:T(8,128)S(1)}, u32[]{:S(2)}) copy-start(f32[48,128]{1,0:T(8,128)S(1)} %collective-permute-done.3.vxhigh_ref) | copy-start | bytes 73732
  173.6 4.7 %copy-start.6 = (f32[192,128]{1,0:T(8,128)}, f32[192,128]{1,0:T(8,128)S(1)}, u32[]{:S(2)}) copy-start(f32[192,128]{1,0:T(8,128)S(1)} %collective-permute-done.vylow_ref) | copy-start | bytes 294916
  173.6 4.7 %copy-start.7 = (f32[192,128]{1,0:T(8,128)}, f32[192,128]{1,0:T(8,128)S(1)}, u32[]{:S(2)}) copy-start(f32[192,128]{1,0:T(8,128)S(1)} %collective-permute-done.1.vyhigh_ref) | copy-start | bytes 294916
  178.3 38.8 %all-to-all-start.3 = ((f32[32,9,8,128]{3,2,1,0:T(8,128)}), f32[32,9,8,128]{3,2,1,0:T(8,128)S(1)}, u32[]{:S(2)}, u32[]{:S(2)}) async-start(f32[32,9,8,128]{3,2,1,0:T(8,128)} %forward.1), calls=%async_computation.3 | async-start | bytes 2359296 | tf_op jit(solution)/shard_map/all_to_all | solution.py:634
  189.3 1.1 copy-start.12
  217.1 1.1 copy-start
  223.3 16.9 %collective-permute-start.4 = (f32[1152,128]{1,0:T(8,128)}, f32[1152,128]{1,0:T(8,128)S(1)}, u32[]{:S(2)}, u32[]{:S(2)}) collective-permute-start(f32[1152,128]{1,0:T(8,128)} %get-tuple-element.68.yhigh_own_ref), channel_id=1, source_target_pairs={{0,32},{32,64},{64,96},{96,128},{128,160},{160,192},{192,224},{1,3... | collective-permute-start | bytes 1769480 | tf_op jit(solution)/shard_map/ppermute | solution.py:574
  225.2 15.0 %collective-permute-start.5 = (f32[1152,128]{1,0:T(8,128)}, f32[1152,128]{1,0:T(8,128)S(1)}, u32[]{:S(2)}, u32[]{:S(2)}) collective-permute-start(f32[1152,128]{1,0:T(8,128)} %get-tuple-element.69.ylow_own_ref), channel_id=1, source_target_pairs={{32,0},{64,32},{96,64},{128,96},{160,128},{192,160},{224,192},{33,... | collective-permute-start | bytes 1769480 | tf_op jit(solution)/shard_map/ppermute | solution.py:574
  240.3 0.8 copy-start.2
  240.3 1.0 copy-start.3
  243.4 9.7 %collective-permute-start.6 = (f32[320,128]{1,0:T(8,128)}, f32[320,128]{1,0:T(8,128)S(1)}, u32[]{:S(2)}, u32[]{:S(2)}) collective-permute-start(f32[320,128]{1,0:T(8,128)} %get-tuple-element.76), channel_id=1, source_target_pairs={{0,1},{1,2},{2,3},{3,4},{4,5},{5,6},{6,7},{7,8},{8,9},{9,10},{10,1... | collective-permute-start | bytes 491528 | tf_op jit(solution)/shard_map/ppermute | solution.py:574
  246.6 7.8 %collective-permute-start.7 = (f32[320,128]{1,0:T(8,128)}, f32[320,128]{1,0:T(8,128)S(1)}, u32[]{:S(2)}, u32[]{:S(2)}) collective-permute-start(f32[320,128]{1,0:T(8,128)} %get-tuple-element.77), channel_id=1, source_target_pairs={{1,0},{2,1},{3,2},{4,3},{5,4},{6,5},{7,6},{8,7},{9,8},{10,9},{11,1... | collective-permute-start | bytes 491528 | tf_op jit(solution)/shard_map/ppermute | solution.py:574
  253.1 1.4 copy-start.4
  254.5 0.7 copy-start.5

commit v8 on v7

--- a/solution.py
+++ b/solution.py
@@ -441,39 +441,74 @@
     lax.fori_loop(0, shape[0] // UNROLL, finish, 0)
 
 
-def first_step_kernel(
-    shape, late_ref, left_ref, fine_at_ref, coarse_at_ref, diff_ref, second_ref, rest_ref, state_ref, vel_ref, out_ref,
-    u0_ref, u1_ref, held_ref, plane_ref, sem, out_sem,
-):
-    _, species, rows, _ = shape
-    half = rows // 2
-    size = species * rows
-    copy = pltpu.make_async_copy(state_ref, u0_ref, sem)
-    copy.start()
-    copy.wait()
-
-    def half_plane(x, h, ref, slot):
-        for s in range(species):
-            base = pl.multiple_of(x * size + s * rows + h * half, half)
-            u0_ref[pl.ds(base, half), :] = ref[slot, s]
-
-    def whole_plane(x):
-        for s in range(species):
-            u0_ref[pl.ds(pl.multiple_of(x * size + s * rows, rows), rows), :] = plane_ref[s]
-
-    late_units(
-        shape, late_ref, left_ref, fine_at_ref, coarse_at_ref, second_ref, rest_ref, held_ref, plane_ref,
-        sem, half_plane, whole_plane,
-    )
-
-    def nothing(s):
-        return 0.0
-
+def nothing(s):
+    return 0.0
+
+
+def first_step_kernel(shape, diff_ref, state_ref, vel_ref, out_ref, u0_ref, u1_ref, in_sem, out_sem):
+    for g in range(shape[0] // UNROLL):
+        send_group(shape, state_ref, u0_ref, in_sem, g).start()
+    finish_groups(shape, state_ref, u0_ref, in_sem)
     advance(
         shape, diff_ref, vel_ref, u0_ref, u1_ref, nothing, nothing, lambda x: nothing, lambda x: nothing,
         lambda g: send_group(shape, u1_ref, out_ref, out_sem, g).start(),
     )
     finish_groups(shape, u1_ref, out_ref, out_sem)
+
+
+def late_step_kernel(
+    shape, late_ref, left_ref, fine_at_ref, coarse_at_ref, again_ref, diff_ref, second_ref, rest_ref, state_ref, vel_ref, _,
+    out_ref, u0_ref, u1_ref, held_ref, plane_ref, sem, out_sem,
+):
+    planes, species, rows, lanes = shape
+    half = rows // 2
+    size = species * rows
+    copy = pltpu.make_async_copy(state_ref, u0_ref.at[size : size + planes * size], sem)
+    copy.start()
+    u0_ref[0:size] = jnp.zeros((size, lanes), jnp.float32)
+    u0_ref[size + planes * size : 2 * size + planes * size] = jnp.zeros((size, lanes), jnp.float32)
+    copy.wait()
+
+    def half_plane(x, h, ref, slot):
+        for s in range(species):
+            base = pl.multiple_of((x + 1) * size + s * rows + h * half, half)
+            u0_ref[pl.ds(base, half), :] = ref[slot, s]
+
+    def whole_plane(x):
+        for s in range(species):
+            u0_ref[pl.ds(pl.multiple_of((x + 1) * size + s * rows, rows), rows), :] = plane_ref[s]
+
+    late_units(
+        shape, late_ref, left_ref, fine_at_ref, coarse_at_ref, second_ref, rest_ref, held_ref, plane_ref,
+        sem, half_plane, whole_plane,
+    )
+
+    def send(x):
+        part = pl.ds(pl.multiple_of(x * size, size), size)
+        return pltpu.make_async_copy(u1_ref.at[part], out_ref.at[part], out_sem.at[x])
+
+    def take(x, carry):
+        @pl.when(again_ref[x] > 0)
+        def _():
+            def store(s, new):
+                u1_ref[pl.ds(pl.multiple_of(x * size + s * rows, rows), rows), :] = new
+
+            around = [planes_of(u0_ref, x + 1 + i, rows, size) for i in (0, -1, 1)]
+            advance_plane(diff_ref, [vel_ref[x, k] for k in range(3)], *around, nothing, nothing, store)
+            send(x).start()
+
+        return carry
+
+    lax.fori_loop(0, planes, take, 0)
+
+    def finish(x, carry):
+        @pl.when(again_ref[x] > 0)
+        def _():
+            send(x).wait()
+
+        return carry
+
+    lax.fori_loop(0, planes, finish, 0)
 
 
 def second_step_kernel(
@@ -717,11 +752,28 @@
         for j in range(COARSE_CAP)
     ]
     late = jnp.concatenate([late_fine, *late_parents])
+    late_child = jnp.repeat(fresh & (code % unit_count >= DIRECT), 2) & (fine_at < 0)
+    late_plane = late_child | ((fine_at >= 0) & (2 * (fine_at % FINE_CAP) + 1 >= DIRECT))
+    beside = jnp.pad(late_plane, 1)
+    again = (beside[:-2] | beside[1:-1] | beside[2:]).astype(i32)
     late_scratch = [
         pltpu.VMEM((1, species, half, lanes), f32),
         pltpu.VMEM((species, rows, lanes), f32),
         pltpu.SemaphoreType.DMA,
     ]
+    state_scratch = pltpu.VMEM(state_shape.shape, f32)
+    group_sems = pltpu.SemaphoreType.DMA((planes // UNROLL,))
+    stepped = pl.pallas_call(
+        functools.partial(first_step_kernel, old_fine.shape),
+        out_shape=state_shape,
+        in_specs=[SMEM, ANY, VMEM],
+        out_specs=ANY,
+        scratch_shapes=[state_scratch] * 2 + [group_sems] * 2,
+        compiler_params=PARAMS,
+        cost_estimate=cost(10),
+        name="first_step",
+    )(diffusion, state, velocity)
+    second, stepped = lax.optimization_barrier((second, stepped))
     ylow_own, yhigh_own, xlow_own, xhigh_own = pl.pallas_call(
         functools.partial(edges_kernel, old_fine.shape),
         out_shape=edge_shapes(ITERS, species),
@@ -733,18 +785,19 @@
         name="edges",
     )(late, left, fine_at, coarse_at, second, rest, *edges)
     ylow, yhigh = neighbours("grp", ylow_own, yhigh_own)
-    state_scratch = pltpu.VMEM(state_shape.shape, f32)
-    group_sems = pltpu.SemaphoreType.DMA((planes // UNROLL,))
     stepped = pl.pallas_call(
-        functools.partial(first_step_kernel, old_fine.shape),
+        functools.partial(late_step_kernel, old_fine.shape),
         out_shape=state_shape,
-        in_specs=[SMEM] * 5 + [VMEM, ANY, ANY, VMEM],
+        in_specs=[SMEM] * 6 + [VMEM, ANY, ANY, VMEM, ANY],
         out_specs=ANY,
-        scratch_shapes=[state_scratch] * 2 + late_scratch + [group_sems],
+        scratch_shapes=[pltpu.VMEM(((planes + 2) * size, lanes), f32), state_scratch]
+        + late_scratch
+        + [pltpu.SemaphoreType.DMA((planes,))],
+        input_output_aliases={10: 0},
         compiler_params=PARAMS,
-        cost_estimate=cost(10),
-        name="first_step",
-    )(late, left, fine_at, coarse_at, diffusion, second, rest, state, velocity)
+        cost_estimate=cost(7),
+        name="late_step",
+    )(late, left, fine_at, coarse_at, again, diffusion, second, rest, state, velocity, stepped)
     ylow, yhigh, stepped = lax.optimization_barrier((ylow, yhigh, stepped))
     message = jax.ShapeDtypeStruct((ITERS * size + 32, lanes), f32)
     down, up = pl.pallas_call(

time: 270 us -> 271 us (level)
  waiting for transfers between devices: 133 us -> 125 us
  Pallas kernels: 58 us -> 65.3 us
    pallas_call x0 -> x1, Pallas kernels: none -> 10.2 us  [on_device(): pl.pallas_call(functools.partial(late_step_kernel, old_fine.shape), out_s...]
    all_to_all x2, waiting for transfers between devices: 17.5 us -> 8.42 us  [exchange(): return lax.all_to_all(value, 'dev', split_axis=0, concat_axis=0, tiled=True)]
  transfers between devices with their start and end apart: 11 -> 11, of which waited for: 6 -> 6; matrix products, arithmetic and copies ran while one was open for 4% -> 4% of each run, Pallas kernels for 9% -> 12%
where the time goes in v8:
time: 271 us; the launch traced here: 267 us
  waiting for transfers between devices  125 us (46%)
  Pallas kernels  65.3 us (24%)
  starting transfers between devices  55.4 us (20%)
  other arithmetic  16.3 us (6%)
  local copies, waits for them, and re-layouts  4.05 us (1%)
    ppermute x4, waiting for transfers between devices, neighbours(): lax.ppermute(high, axis, up)  110 us
    all_to_all x2, starting transfers between devices, exchange(): return lax.all_to_all(value, 'dev', split_axis=0, concat_axis=0, tiled=True)  16.8 us
    ppermute x4, starting transfers between devices, neighbours(): lax.ppermute(low, axis, [(b, a) for a, b in up])  15 us
    ppermute x4, starting transfers between devices, neighbours(): lax.ppermute(high, axis, up)  12 us
    all_to_all x1, starting transfers between devices, on_device(): lax.all_to_all(labels, 'dev', split_axis=0, concat_axis=0, tiled=True)  11.6 us
    pallas_call x1, Pallas kernels, on_device(): pl.pallas_call(functools.partial(second_step_kernel, old_fine.shape), out...  11.2 us
    pallas_call x1, Pallas kernels, on_device(): pl.pallas_call(functools.partial(late_step_kernel, old_fine.shape), out_s...  10.2 us
    pallas_call x1, Pallas kernels, on_device(): pl.pallas_call(functools.partial(build_kernel, old_fine.shape), out_shape...  9.59 us
  transfers between devices with their start and end apart: 11, of which 6 were waited for; matrix products, arithmetic and copies ran while one was open for 4% of the time, Pallas kernels for 12%

profile of v8, /device:TPU:22, one launch (start us, length us, event | category | flops | bytes accessed | tf_op | source)
XLA Modules:
  0.0 267.4 jit_solution(18291817301569775343)
XLA Ops:
  0.0 0.7 pad_add_fusion
  0.7 0.6 broadcast_in_dim.76
  1.4 11.6 %all-to-all-start.1 = ((s32[32,1,96]{2,1,0:T(1,128)}), s32[32,1,96]{2,1,0:T(1,128)S(1)}, u32[]{:S(2)}, u32[]{:S(2)}) async-start(s32[32,1,96]{2,1,0:T(1,128)} %broadcast_in_dim.76), calls=%async_computation.1 | async-start | bytes 32768 | tf_op jit(solution)/shard_map/all_to_all | solution.py:628
  13.0 0.7 fusion.20
  13.6 0.7 and_select_fusion.2
  14.3 0.7 compare_select_fusion.23
  15.0 0.7 fusion.19
  16.0 0.7 compare_select_fusion.22.fine_at_ref
  16.9 3.9 %all-to-all-done.1 = s32[32,1,96]{2,1,0:T(1,128)S(1)} async-done(((s32[32,1,96]{2,1,0:T(1,128)}), s32[32,1,96]{2,1,0:T(1,128)S(1)}, u32[]{:S(2)}, u32[]{:S(2)}) %all-to-all-start.1) | async-done | bytes 12320 | tf_op jit(solution)/shard_map/all_to_all | solution.py:628
  21.1 0.9 convert_reduce_fusion.5
  22.0 1.1 convert_reduce_fusion
  24.4 4.6 %plan.1 = (s32[8,128]{1,0:T(8,128)S(1)}, s32[32,128]{1,0:T(8,128)}) custom-call(s32[1]{0:T(128)} %bitcast.7.me_ref, s32[32,128]{1,0:T(8,128)} %multiply_add_fusion.units_ref), custom_call_target="tpu_custom_call" | custom-call | tf_op jit(solution)/shard_map/plan/pallas_call | solution.py:642
  29.0 0.7 slice_reduce_fusion
  29.6 0.7 compare_select_fusion.coarse_at_ref
  30.3 7.3 %pack.1 = f32[160,9,8,128]{3,2,1,0:T(8,128)} custom-call(s32[1]{0:T(128)} %bitcast.7.me_ref, s32[64]{0:T(128)S(1)} %compare_select_fusion.22.fine_at_ref, s32[32]{0:T(128)S(1)} %compare_select_fusion.coarse_at_ref, s32[8,128]{1,0:T(8,128)S(1)} %get-tuple-element.57.row_ref, f32[64,9,16,128]{3,2,1,0:T(8,128)} %fine_in_ref.1, f32[32,9,8,64]{3,2,1,0:T(8,128)} %coarse_ref.1), custom_call_target="tpu_custom_call" | custom-call | tf_op jit(solution)/shard_map/pack/pallas_call | solution.py:672
  38.3 6.9 %all-to-all-start.2 = ((f32[160,9,8,128]{3,2,1,0:T(8,128)}), f32[160,9,8,128]{3,2,1,0:T(8,128)}, u32[]{:S(2)}, u32[]{:S(2)}) async-start(f32[160,9,8,128]{3,2,1,0:T(8,128)} %pack.1), calls=%async_computation.2 | async-start | bytes 11796480 | tf_op jit(solution)/shard_map/all_to_all | solution.py:669
  45.4 0.9 convert_reduce_fusion.2
  46.4 1.3 select_reduce_fusion.fine_at_ref
  48.0 2.2 velocity_edges.1
  50.2 3.4 %collective-permute-start.2 = (f32[48,128]{1,0:T(8,128)}, f32[48,128]{1,0:T(8,128)S(1)}, u32[]{:S(2)}, u32[]{:S(2)}) collective-permute-start(f32[48,128]{1,0:T(8,128)} %get-tuple-element.62), channel_id=1, source_target_pairs={{0,1},{1,2},{2,3},{3,4},{4,5},{5,6},{6,7},{7,8},{8,9},{9,10},{10,1... | collective-permute-start | bytes 73736 | tf_op jit(solution)/shard_map/ppermute | solution.py:609
  53.5 4.6 %collective-permute-start.3 = (f32[48,128]{1,0:T(8,128)}, f32[48,128]{1,0:T(8,128)S(1)}, u32[]{:S(2)}, u32[]{:S(2)}) collective-permute-start(f32[48,128]{1,0:T(8,128)} %get-tuple-element.63), channel_id=1, source_target_pairs={{1,0},{2,1},{3,2},{4,3},{5,4},{6,5},{7,6},{8,7},{9,8},{10,9},{11,1... | collective-permute-start | bytes 73736 | tf_op jit(solution)/shard_map/ppermute | solution.py:609
  58.1 1.9 collective-permute-start
  60.0 3.6 %collective-permute-start.1 = (f32[192,128]{1,0:T(8,128)}, f32[192,128]{1,0:T(8,128)S(1)}, u32[]{:S(2)}, u32[]{:S(2)}) collective-permute-start(f32[192,128]{1,0:T(8,128)} %get-tuple-element.61.vylow_own_ref), channel_id=1, source_target_pairs={{32,0},{64,32},{96,64},{128,96},{160,128},{192,160},{224,192},{33,... | collective-permute-start | bytes 294920 | tf_op jit(solution)/shard_map/ppermute | solution.py:609
  63.9 0.8 convert_reduce_fusion.3
  64.7 109.0 %collective-permute-done.2.vxlow_ref = f32[48,128]{1,0:T(8,128)S(1)} collective-permute-done((f32[48,128]{1,0:T(8,128)}, f32[48,128]{1,0:T(8,128)S(1)}, u32[]{:S(2)}, u32[]{:S(2)}) %collective-permute-start.2) | collective-permute-done | bytes 24608 | tf_op jit(solution)/shard_map/ppermute | solution.py:609
  173.7 1.1 all-to-all-done.2.in_ref.first_ref
  174.8 3.6 %forward.1 = f32[32,9,8,128]{3,2,1,0:T(8,128)} custom-call(s32[1]{0:T(128)} %bitcast.7.me_ref, s32[32,128]{1,0:T(8,128)} %get-tuple-element.56.column_ref, f32[160,9,8,128]{3,2,1,0:T(8,128)} %all-to-all-done.2.in_ref.first_ref), custom_call_target="tpu_custom_call" | custom-call | bytes 10800000 | tf_op jit(solution)/shard_map/forward/pallas_call | solution.py:710
  178.4 10.0 %all-to-all-start.3 = ((f32[32,9,8,128]{3,2,1,0:T(8,128)}), f32[32,9,8,128]{3,2,1,0:T(8,128)S(1)}, u32[]{:S(2)}, u32[]{:S(2)}) async-start(f32[32,9,8,128]{3,2,1,0:T(8,128)} %forward.1), calls=%async_computation.3 | async-start | bytes 2359296 | tf_op jit(solution)/shard_map/all_to_all | solution.py:669
  188.8 0.7 select_reduce_fusion.1.coarse_at_ref
  190.0 0.6 pad_add_fusion.1.late_ref
  190.6 9.6 %build.1 = (f32[9216,128]{1,0:T(8,128)}, f32[1152,128]{1,0:T(8,128)}, f32[1152,128]{1,0:T(8,128)}, f32[288,128]{1,0:T(8,128)}, f32[288,128]{1,0:T(8,128)}) custom-call(s32[64]{0:T(128)} %copy-done.11, s32[32]{0:T(128)} %copy-done.13, f32[160,9,8,128]{3,2,1,0:T(8,128)} %all-to-all-done.2.in_ref.first_ref), custom_call_target="tpu_custom_call" | custom-call | bytes 36000000 | tf_op jit(solution)/shard_map/build/pallas_call | solution.py:724
  200.2 9.4 %first_step.1._ = f32[9216,128]{1,0:T(8,128)} custom-call(f32[9]{0:T(128)} %diff_ref.5, f32[9216,128]{1,0:T(8,128)} %get-tuple-element.65.state_ref, f32[64,3,16,128]{3,2,1,0:T(8,128)} %vel_ref.5), custom_call_target="tpu_custom_call" | custom-call | bytes 36000000 | tf_op jit(solution)/shard_map/first_step/pallas_call | solution.py:766
  209.6 7.3 %all-to-all-done.3.second_ref = f32[32,9,8,128]{3,2,1,0:T(8,128)S(1)} async-done(((f32[32,9,8,128]{3,2,1,0:T(8,128)}), f32[32,9,8,128]{3,2,1,0:T(8,128)S(1)}, u32[]{:S(2)}, u32[]{:S(2)}) %all-to-all-start.3) | async-done | bytes 1179680 | tf_op jit(solution)/shard_map/all_to_all | solution.py:669
  216.9 1.1 copy-done
  218.0 5.3 %edges.1 = (f32[1152,128]{1,0:T(8,128)}, f32[1152,128]{1,0:T(8,128)}, f32[288,128]{1,0:T(8,128)}, f32[288,128]{1,0:T(8,128)}) custom-call(s32[96]{0:T(128)} %pad_add_fusion.1.late_ref, s32[1]{0:T(128)} %bitcast.8.left_ref, s32[64]{0:T(128)} %copy-done.11, s32[32]{0:T(128)} %copy-done.13, f32[32,9,8,128]{3,2,1,0:T(8,128)} %copy-done, ...), custom_call_target="tpu_custom_call" | custom-call | bytes 14400000 | tf_op jit(solution)/shard_map/edges/pallas_call | solution.py:777
  223.3 1.9 collective-permute-start.4
  225.2 3.6 %collective-permute-start.5 = (f32[1152,128]{1,0:T(8,128)}, f32[1152,128]{1,0:T(8,128)S(1)}, u32[]{:S(2)}, u32[]{:S(2)}) collective-permute-start(f32[1152,128]{1,0:T(8,128)} %get-tuple-element.73.ylow_own_ref), channel_id=1, source_target_pairs={{32,0},{64,32},{96,64},{128,96},{160,128},{192,160},{224,192},{33,... | collective-permute-start | bytes 1769480 | tf_op jit(solution)/shard_map/ppermute | solution.py:609
  229.1 0.7 or_convert_fusion.again_ref
  229.8 10.2 %late_step.1.first_ref = f32[9216,128]{1,0:T(8,128)} custom-call(s32[96]{0:T(128)} %pad_add_fusion.1.late_ref, s32[1]{0:T(128)} %bitcast.8.left_ref, s32[64]{0:T(128)} %copy-done.11, s32[32]{0:T(128)} %copy-done.13, s32[64]{0:T(128)} %or_convert_fusion.again_ref, f32[9]{0:T(128)} %diff_ref.5, ...), custom_call_target="tpu_custom_call", output_to_operand_aliasing={{}: (10, {})} | custom-call | bytes 25200000 | tf_op jit(solution)/shard_map/late_step/pallas_call | solution.py:788
  240.0 0.8 copy-done.2
  241.0 2.1 corners.1
  243.1 4.8 %collective-permute-start.6 = (f32[320,128]{1,0:T(8,128)}, f32[320,128]{1,0:T(8,128)S(1)}, u32[]{:S(2)}, u32[]{:S(2)}) collective-permute-start(f32[320,128]{1,0:T(8,128)} %get-tuple-element.80), channel_id=1, source_target_pairs={{0,1},{1,2},{2,3},{3,4},{4,5},{5,6},{6,7},{7,8},{8,9},{9,10},{10,1... | collective-permute-start | bytes 491528 | tf_op jit(solution)/shard_map/ppermute | solution.py:609
  247.9 3.1 %collective-permute-start.7 = (f32[320,128]{1,0:T(8,128)}, f32[320,128]{1,0:T(8,128)S(1)}, u32[]{:S(2)}, u32[]{:S(2)}) collective-permute-start(f32[320,128]{1,0:T(8,128)} %get-tuple-element.81), channel_id=1, source_target_pairs={{1,0},{2,1},{3,2},{4,3},{5,4},{6,5},{7,6},{8,7},{9,8},{10,9},{11,1... | collective-permute-start | bytes 491528 | tf_op jit(solution)/shard_map/ppermute | solution.py:609
  251.0 0.7 add_convert_fusion.inside_ref
  251.7 0.9 collective-permute-done.6.xlow_ref
  252.6 2.7 %collective-permute-done.7.xhigh_ref = f32[320,128]{1,0:T(8,128)S(1)} collective-permute-done((f32[320,128]{1,0:T(8,128)}, f32[320,128]{1,0:T(8,128)S(1)}, u32[]{:S(2)}, u32[]{:S(2)}) %collective-permute-start.7) | collective-permute-done | bytes 163872 | tf_op jit(solution)/shard_map/ppermute | solution.py:609
  255.3 0.7 copy-done.5
  256.0 11.2 %second_step.1 = f32[9216,128]{1,0:T(8,128)} custom-call(f32[4]{0:T(128)} %add_convert_fusion.inside_ref, f32[9]{0:T(128)} %diff_ref.5, f32[9216,128]{1,0:T(8,128)} %late_step.1.first_ref, f32[64,3,16,128]{3,2,1,0:T(8,128)} %vel_ref.5, f32[1152,128]{1,0:T(8,128)} %get-tuple-element.73.ylow_own_ref, f32[1152,128]{1,0:T(8,128)} %get-tuple-element.72.yhigh_own_ref, ...), custom_call_target="tpu_custom_call" | custom-call | bytes 36000000 | tf_op jit(solution)/shard_map/second_step/pallas_call | solution.py:816
  (76 shorter events, 4.1 us)
Async XLA Ops:
  1.4 19.4 %all-to-all-start.1 = ((s32[32,1,96]{2,1,0:T(1,128)}), s32[32,1,96]{2,1,0:T(1,128)S(1)}, u32[]{:S(2)}, u32[]{:S(2)}) async-start(s32[32,1,96]{2,1,0:T(1,128)} %broadcast_in_dim.76), calls=%async_computation.1 | async-start | bytes 32768 | tf_op jit(solution)/shard_map/all_to_all | solution.py:628
  30.3 7.9 %copy-start.1 = (f32[32,9,8,64]{3,2,1,0:T(8,128)S(1)}, f32[32,9,8,64]{3,2,1,0:T(8,128)}, u32[]{:S(2)}) copy-start(f32[32,9,8,64]{3,2,1,0:T(8,128)} %coarse_ref.1) | copy-start | bytes 1769476
  38.3 7.0 %copy-start.8 = (s32[32,128]{1,0:T(8,128)S(1)}, s32[32,128]{1,0:T(8,128)}, u32[]{:S(2)}) copy-start(s32[32,128]{1,0:T(8,128)} %get-tuple-element.56.column_ref) | copy-start | bytes 49156
  38.3 136.5 %all-to-all-start.2 = ((f32[160,9,8,128]{3,2,1,0:T(8,128)}), f32[160,9,8,128]{3,2,1,0:T(8,128)}, u32[]{:S(2)}, u32[]{:S(2)}) async-start(f32[160,9,8,128]{3,2,1,0:T(8,128)} %pack.1), calls=%async_computation.2 | async-start | bytes 11796480 | tf_op jit(solution)/shard_map/all_to_all | solution.py:669
  47.8 140.7 %copy-start.11 = (s32[64]{0:T(128)}, s32[64]{0:T(128)S(1)}, u32[]{:S(2)}) copy-start(s32[64]{0:T(128)S(1)} %select_reduce_fusion.fine_at_ref) | copy-start | bytes 772
  50.2 123.5 %collective-permute-start.2 = (f32[48,128]{1,0:T(8,128)}, f32[48,128]{1,0:T(8,128)S(1)}, u32[]{:S(2)}, u32[]{:S(2)}) collective-permute-start(f32[48,128]{1,0:T(8,128)} %get-tuple-element.62), channel_id=1, source_target_pairs={{0,1},{1,2},{2,3},{3,4},{4,5},{5,6},{6,7},{7,8},{8,9},{9,10},{10,1... | collective-permute-start | bytes 73736 | tf_op jit(solution)/shard_map/ppermute | solution.py:609
  53.5 120.1 %collective-permute-start.3 = (f32[48,128]{1,0:T(8,128)}, f32[48,128]{1,0:T(8,128)S(1)}, u32[]{:S(2)}, u32[]{:S(2)}) collective-permute-start(f32[48,128]{1,0:T(8,128)} %get-tuple-element.63), channel_id=1, source_target_pairs={{1,0},{2,1},{3,2},{4,3},{5,4},{6,5},{7,6},{8,7},{9,8},{10,9},{11,1... | collective-permute-start | bytes 73736 | tf_op jit(solution)/shard_map/ppermute | solution.py:609
  58.1 115.5 %collective-permute-start = (f32[192,128]{1,0:T(8,128)}, f32[192,128]{1,0:T(8,128)S(1)}, u32[]{:S(2)}, u32[]{:S(2)}) collective-permute-start(f32[192,128]{1,0:T(8,128)} %get-tuple-element.60.vyhigh_own_ref), channel_id=1, source_target_pairs={{0,32},{32,64},{64,96},{96,128},{128,160},{160,192},{192,224},{1,3... | collective-permute-start | bytes 294920 | tf_op jit(solution)/shard_map/ppermute | solution.py:609
  60.0 113.6 %collective-permute-start.1 = (f32[192,128]{1,0:T(8,128)}, f32[192,128]{1,0:T(8,128)S(1)}, u32[]{:S(2)}, u32[]{:S(2)}) collective-permute-start(f32[192,128]{1,0:T(8,128)} %get-tuple-element.61.vylow_own_ref), channel_id=1, source_target_pairs={{32,0},{64,32},{96,64},{128,96},{160,128},{192,160},{224,192},{33,... | collective-permute-start | bytes 294920 | tf_op jit(solution)/shard_map/ppermute | solution.py:609
  173.6 4.7 %copy-start.9 = (f32[48,128]{1,0:T(8,128)}, f32[48,128]{1,0:T(8,128)S(1)}, u32[]{:S(2)}) copy-start(f32[48,128]{1,0:T(8,128)S(1)} %collective-permute-done.2.vxlow_ref) | copy-start | bytes 73732
  173.6 4.7 %copy-start.10 = (f32[48,128]{1,0:T(8,128)}, f32[48,128]{1,0:T(8,128)S(1)}, u32[]{:S(2)}) copy-start(f32[48,128]{1,0:T(8,128)S(1)} %collective-permute-done.3.vxhigh_ref) | copy-start | bytes 73732
  173.6 4.7 %copy-start.6 = (f32[192,128]{1,0:T(8,128)}, f32[192,128]{1,0:T(8,128)S(1)}, u32[]{:S(2)}) copy-start(f32[192,128]{1,0:T(8,128)S(1)} %collective-permute-done.vylow_ref) | copy-start | bytes 294916
  173.7 4.7 %copy-start.7 = (f32[192,128]{1,0:T(8,128)}, f32[192,128]{1,0:T(8,128)S(1)}, u32[]{:S(2)}) copy-start(f32[192,128]{1,0:T(8,128)S(1)} %collective-permute-done.1.vyhigh_ref) | copy-start | bytes 294916
  178.4 38.5 %all-to-all-start.3 = ((f32[32,9,8,128]{3,2,1,0:T(8,128)}), f32[32,9,8,128]{3,2,1,0:T(8,128)S(1)}, u32[]{:S(2)}, u32[]{:S(2)}) async-start(f32[32,9,8,128]{3,2,1,0:T(8,128)} %forward.1), calls=%async_computation.3 | async-start | bytes 2359296 | tf_op jit(solution)/shard_map/all_to_all | solution.py:669
  189.5 1.1 copy-start.13
  209.6 19.5 %copy-start.12 = (s32[64]{0:T(128)S(1)}, s32[64]{0:T(128)}, u32[]{:S(2)}) copy-start(s32[64]{0:T(128)} %copy-done.11) | copy-start | bytes 772
  216.9 1.1 copy-start
  223.3 16.6 %collective-permute-start.4 = (f32[1152,128]{1,0:T(8,128)}, f32[1152,128]{1,0:T(8,128)S(1)}, u32[]{:S(2)}, u32[]{:S(2)}) collective-permute-start(f32[1152,128]{1,0:T(8,128)} %get-tuple-element.72.yhigh_own_ref), channel_id=1, source_target_pairs={{0,32},{32,64},{64,96},{96,128},{128,160},{160,192},{192,224},{1,3... | collective-permute-start | bytes 1769480 | tf_op jit(solution)/shard_map/ppermute | solution.py:609
  225.2 14.7 %collective-permute-start.5 = (f32[1152,128]{1,0:T(8,128)}, f32[1152,128]{1,0:T(8,128)S(1)}, u32[]{:S(2)}, u32[]{:S(2)}) collective-permute-start(f32[1152,128]{1,0:T(8,128)} %get-tuple-element.73.ylow_own_ref), channel_id=1, source_target_pairs={{32,0},{64,32},{96,64},{128,96},{160,128},{192,160},{224,192},{33,... | collective-permute-start | bytes 1769480 | tf_op jit(solution)/shard_map/ppermute | solution.py:609
  239.9 0.8 copy-start.2
  240.0 1.0 copy-start.3
  243.1 9.5 %collective-permute-start.6 = (f32[320,128]{1,0:T(8,128)}, f32[320,128]{1,0:T(8,128)S(1)}, u32[]{:S(2)}, u32[]{:S(2)}) collective-permute-start(f32[320,128]{1,0:T(8,128)} %get-tuple-element.80), channel_id=1, source_target_pairs={{0,1},{1,2},{2,3},{3,4},{4,5},{5,6},{6,7},{7,8},{8,9},{9,10},{10,1... | collective-permute-start | bytes 491528 | tf_op jit(solution)/shard_map/ppermute | solution.py:609
  247.9 7.4 %collective-permute-start.7 = (f32[320,128]{1,0:T(8,128)}, f32[320,128]{1,0:T(8,128)S(1)}, u32[]{:S(2)}, u32[]{:S(2)}) collective-permute-start(f32[320,128]{1,0:T(8,128)} %get-tuple-element.81), channel_id=1, source_target_pairs={{1,0},{2,1},{3,2},{4,3},{5,4},{6,5},{7,6},{8,7},{9,8},{10,9},{11,1... | collective-permute-start | bytes 491528 | tf_op jit(solution)/shard_map/ppermute | solution.py:609
  252.6 2.7 %copy-start.4 = (f32[320,128]{1,0:T(8,128)}, f32[320,128]{1,0:T(8,128)S(1)}, u32[]{:S(2)}) copy-start(f32[320,128]{1,0:T(8,128)S(1)} %collective-permute-done.6.xlow_ref) | copy-start | bytes 491524
  255.3 0.7 copy-start.5

commit v9 on v8

--- a/solution.py
+++ b/solution.py
@@ -26,41 +26,45 @@
     return jnp.sum((same & earlier).astype(jnp.int32), axis=-1)
 
 
-def plan_kernel(me_ref, units_ref, row_ref, column_ref):
+def plan_kernel(me_ref, units_ref, row_ref, column_ref, left_ref):
     devices, lanes = units_ref.shape
     me = me_ref[0]
     units = units_ref[...]
     source = lax.broadcasted_iota(jnp.int32, units.shape, 0)
     lane = lax.broadcasted_iota(jnp.int32, units.shape, 1)
-    surplus = pltpu.roll(jnp.maximum(units - DIRECT, 0), 0, 1, stride=1, stride_axis=0)
     none = jnp.full(units.shape, -1, jnp.int32)
 
     def one_round(r, carry):
-        left, free, second, through, *chosen = carry
+        left, codes, free, second, through = carry
         ok = (left > 0) & (free > 0) & (second > 0)
         position = DIRECT - free
-        item = surplus - left
-        chosen = [jnp.where(ok & (item == i), r * 8 + position, table) for i, table in enumerate(chosen)]
+        code = jnp.left_shift(r * 8 + position, 8 * jnp.maximum(left - 1, 0))
+        codes = jnp.where(ok, codes | code, codes)
         through = jnp.where(ok, source * 8 + position, through)
         used = ok.astype(jnp.int32)
         left, free, second = left - used, free - used, second - used
-        free = pltpu.roll(free, lanes - 1, 1)
-        second = pltpu.roll(pltpu.roll(second, devices - 1, 0), lanes - 1, 1)
-        through = pltpu.roll(pltpu.roll(through, devices - 1, 0), lanes - 1, 1)
-        return (left, free, second, through, *chosen)
-
-    init = (surplus, jnp.maximum(DIRECT - units, 0), jnp.ones(units.shape, jnp.int32), none) + (none,) * EXTRA
-    left, _, _, through, *chosen = lax.fori_loop(0, devices, one_round, init)
-    for i in range(EXTRA):
-        row_ref[i : i + 1] = jnp.max(jnp.where(source == me, chosen[i], -1), axis=0, keepdims=True)
-    row_ref[EXTRA : EXTRA + 1] = jnp.max(left, axis=0, keepdims=True)
+        return (
+            pltpu.roll(left, 1, 1),
+            pltpu.roll(codes, 1, 1),
+            free,
+            pltpu.roll(second, devices - 1, 0),
+            pltpu.roll(through, devices - 1, 0),
+        )
+
+    surplus = pltpu.roll(jnp.maximum(units - DIRECT, 0), 0, 1, stride=1, stride_axis=0)
+    free = jnp.maximum(DIRECT - units, 0)
+    init = (surplus, jnp.zeros_like(units), free, jnp.ones_like(units), none)
+    left, codes, _, _, through = lax.fori_loop(0, devices, one_round, init)
     column = none
     for i in range(EXTRA):
+        chosen = jnp.where(left <= i, lax.shift_right_logical(codes, jnp.full_like(codes, 8 * i)) & 255, -1)
+        row_ref[i : i + 1] = jnp.max(jnp.where(source == me, chosen, -1), axis=0, keepdims=True)
         mine = (lane < devices) & (lane == (source + me) % devices)
-        found = jnp.max(jnp.where(mine, chosen[i], -1), axis=1, keepdims=True)
+        found = jnp.max(jnp.where(mine, chosen, -1), axis=1, keepdims=True)
         column = jnp.where(lane == i, found, column)
     found = jnp.max(jnp.where(lane == me, through, -1), axis=1, keepdims=True)
     column_ref[...] = jnp.where(lane == EXTRA, found, column)
+    left_ref[0] = jnp.max(left.astype(jnp.float32)).astype(jnp.int32)
 
 
 def pack_kernel(
@@ -487,28 +491,28 @@
         part = pl.ds(pl.multiple_of(x * size, size), size)
         return pltpu.make_async_copy(u1_ref.at[part], out_ref.at[part], out_sem.at[x])
 
-    def take(x, carry):
-        @pl.when(again_ref[x] > 0)
-        def _():
+    def take(i, carry):
+        for x in (again_ref[2 * i], again_ref[2 * i + 1]):
+            read, write = jnp.maximum(x, 0), jnp.where(x < 0, planes, x)
+
             def store(s, new):
-                u1_ref[pl.ds(pl.multiple_of(x * size + s * rows, rows), rows), :] = new
-
-            around = [planes_of(u0_ref, x + 1 + i, rows, size) for i in (0, -1, 1)]
-            advance_plane(diff_ref, [vel_ref[x, k] for k in range(3)], *around, nothing, nothing, store)
-            send(x).start()
-
+                u1_ref[pl.ds(pl.multiple_of(write * size + s * rows, rows), rows), :] = new
+
+            around = [planes_of(u0_ref, read + 1 + j, rows, size) for j in (0, -1, 1)]
+            advance_plane(diff_ref, [vel_ref[read, k] for k in range(3)], *around, nothing, nothing, store)
         return carry
 
-    lax.fori_loop(0, planes, take, 0)
-
-    def finish(x, carry):
-        @pl.when(again_ref[x] > 0)
-        def _():
-            send(x).wait()
-
-        return carry
-
-    lax.fori_loop(0, planes, finish, 0)
+    def each(act):
+        def body(i, carry):
+            act(send(again_ref[i]))
+            return carry
+
+        lax.fori_loop(0, count, body, 0)
+
+    count = again_ref[planes]
+    lax.fori_loop(0, (count + 1) // 2, take, 0)
+    each(lambda copy: copy.start())
+    each(lambda copy: copy.wait())
 
 
 def second_step_kernel(
@@ -639,15 +643,17 @@
     fine_units = jnp.sum((all_box[:, None, :] == box[None, :, None]).astype(i32), axis=-1)
     asked = needed(all_coarse)[:, None, :] & (all_coarse_box[:, None, :] == box[None, :, None])
     units = 2 * fine_units + jnp.max(asked.astype(i32), axis=-1)
-    row, column = pl.pallas_call(
+    row, column, left = pl.pallas_call(
         plan_kernel,
-        out_shape=[jax.ShapeDtypeStruct((8, lanes), i32), jax.ShapeDtypeStruct((devices, lanes), i32)],
+        out_shape=[
+            jax.ShapeDtypeStruct((EXTRA, lanes), i32),
+            jax.ShapeDtypeStruct((devices, lanes), i32),
+            jax.ShapeDtypeStruct((1,), i32),
+        ],
         in_specs=[SMEM, VMEM],
-        out_specs=[VMEM] * 2,
+        out_specs=[VMEM, VMEM, SMEM],
         name="plan",
     )(me_ref, units)
-    left = jnp.max(row[EXTRA, :devices]).reshape(1)
-
     own_box = jnp.where(own >= 0, own // planes, -1)
     send_fine = jnp.where(own >= 0, own_box * FINE_CAP + ranks(own_box), -1)
     own_coarse_box = own_coarse // coarse_planes
@@ -755,7 +761,13 @@
     late_child = jnp.repeat(fresh & (code % unit_count >= DIRECT), 2) & (fine_at < 0)
     late_plane = late_child | ((fine_at >= 0) & (2 * (fine_at % FINE_CAP) + 1 >= DIRECT))
     beside = jnp.pad(late_plane, 1)
-    again = (beside[:-2] | beside[1:-1] | beside[2:]).astype(i32)
+    new_plane = jnp.arange(planes)
+    again = beside[:-2] | beside[1:-1] | beside[2:]
+    place = jnp.sum((again[None, :] & (new_plane[None, :] < new_plane[:, None])).astype(i32), axis=1)
+    listed = again[None, :] & (place[None, :] == new_plane[:, None])
+    again = jnp.concatenate(
+        [jnp.max(jnp.where(listed, new_plane[None, :], -1), axis=1), jnp.sum(again.astype(i32)).reshape(1)]
+    )
     late_scratch = [
         pltpu.VMEM((1, species, half, lanes), f32),
         pltpu.VMEM((species, rows, lanes), f32),
@@ -790,7 +802,7 @@
         out_shape=state_shape,
         in_specs=[SMEM] * 6 + [VMEM, ANY, ANY, VMEM, ANY],
         out_specs=ANY,
-        scratch_shapes=[pltpu.VMEM(((planes + 2) * size, lanes), f32), state_scratch]
+        scratch_shapes=[pltpu.VMEM(((planes + 2) * size, lanes), f32), pltpu.VMEM(((planes + 1) * size, lanes), f32)]
         + late_scratch
         + [pltpu.SemaphoreType.DMA((planes,))],
         input_output_aliases={10: 0},

time: 271 us -> 271 us (level)
    ppermute x4, starting transfers between devices: 12 us -> 9.11 us  [neighbours(): lax.ppermute(high, axis, up)]
    ppermute x4, starting transfers between devices: 15 us -> 17.9 us  [neighbours(): lax.ppermute(low, axis, [(b, a) for a, b in up])]
  transfers between devices with their start and end apart: 11 -> 11, of which waited for: 6 -> 6; matrix products, arithmetic and copies ran while one was open for 4% -> 5% of each run, Pallas kernels for 12% -> 11%
where the time goes in v9:
time: 271 us; the launch traced here: 267 us
  waiting for transfers between devices  125 us (46%)
  Pallas kernels  64.3 us (24%)
  starting transfers between devices  55.2 us (20%)
  other arithmetic  17.1 us (6%)
  local copies, waits for them, and re-layouts  4.07 us (2%)
    ppermute x4, waiting for transfers between devices, neighbours(): lax.ppermute(high, axis, up)  110 us
    ppermute x4, starting transfers between devices, neighbours(): lax.ppermute(low, axis, [(b, a) for a, b in up])  17.9 us
    all_to_all x2, starting transfers between devices, exchange(): return lax.all_to_all(value, 'dev', split_axis=0, concat_axis=0, tiled=True)  16.6 us
    all_to_all x1, starting transfers between devices, on_device(): lax.all_to_all(labels, 'dev', split_axis=0, concat_axis=0, tiled=True)  11.6 us
    pallas_call x1, Pallas kernels, on_device(): pl.pallas_call(functools.partial(second_step_kernel, old_fine.shape), out...  11.2 us
    all_to_all x2, waiting for transfers between devices, exchange(): return lax.all_to_all(value, 'dev', split_axis=0, concat_axis=0, tiled=True)  9.44 us
    pallas_call x1, Pallas kernels, on_device(): pl.pallas_call(functools.partial(first_step_kernel, old_fine.shape), out_...  9.37 us
    pallas_call x1, Pallas kernels, on_device(): pl.pallas_call(functools.partial(build_kernel, old_fine.shape), out_shape...  9.14 us
  transfers between devices with their start and end apart: 11, of which 6 were waited for; matrix products, arithmetic and copies ran while one was open for 5% of the time, Pallas kernels for 11%

profile of v9, /device:TPU:22, one launch (start us, length us, event | category | flops | bytes accessed | tf_op | source)
XLA Modules:
  0.0 266.8 jit_solution(192311727673879401)
XLA Ops:
  0.0 0.7 pad_add_fusion
  0.7 0.6 broadcast_in_dim.83
  1.4 11.6 %all-to-all-start.1 = ((s32[32,1,96]{2,1,0:T(1,128)}), s32[32,1,96]{2,1,0:T(1,128)S(1)}, u32[]{:S(2)}, u32[]{:S(2)}) async-start(s32[32,1,96]{2,1,0:T(1,128)} %broadcast_in_dim.83), calls=%async_computation.1 | async-start | bytes 32768 | tf_op jit(solution)/shard_map/all_to_all | solution.py:632
  13.0 0.7 fusion.21
  13.6 0.7 and_select_fusion.2
  14.3 0.7 compare_select_fusion.23
  15.0 0.7 fusion.20
  16.0 0.7 compare_select_fusion.22.fine_at_ref
  16.9 3.9 %all-to-all-done.1 = s32[32,1,96]{2,1,0:T(1,128)S(1)} async-done(((s32[32,1,96]{2,1,0:T(1,128)}), s32[32,1,96]{2,1,0:T(1,128)S(1)}, u32[]{:S(2)}, u32[]{:S(2)}) %all-to-all-start.1) | async-done | bytes 12320 | tf_op jit(solution)/shard_map/all_to_all | solution.py:632
  21.1 0.9 convert_reduce_fusion.5
  22.0 1.1 convert_reduce_fusion
  24.4 4.3 %plan.1 = (s32[4,128]{1,0:T(4,128)S(1)}, s32[32,128]{1,0:T(8,128)}, s32[1]{0:T(128)}) custom-call(s32[1]{0:T(128)} %bitcast.7.me_ref, s32[32,128]{1,0:T(8,128)} %multiply_add_fusion.units_ref), custom_call_target="tpu_custom_call" | custom-call | tf_op jit(solution)/shard_map/plan/pallas_call | solution.py:646
  28.7 0.7 compare_select_fusion.coarse_at_ref
  29.4 8.1 %pack.1 = f32[160,9,8,128]{3,2,1,0:T(8,128)} custom-call(s32[1]{0:T(128)} %bitcast.7.me_ref, s32[64]{0:T(128)S(1)} %compare_select_fusion.22.fine_at_ref, s32[32]{0:T(128)S(1)} %compare_select_fusion.coarse_at_ref, s32[4,128]{1,0:T(4,128)S(1)} %get-tuple-element.59.row_ref, f32[64,9,16,128]{3,2,1,0:T(8,128)} %fine_in_ref.1, f32[32,9,8,64]{3,2,1,0:T(8,128)} %coarse_ref.1), custom_call_target="tpu_custom_call" | custom-call | tf_op jit(solution)/shard_map/pack/pallas_call | solution.py:678
  38.2 6.5 %all-to-all-start.2 = ((f32[160,9,8,128]{3,2,1,0:T(8,128)}), f32[160,9,8,128]{3,2,1,0:T(8,128)}, u32[]{:S(2)}, u32[]{:S(2)}) async-start(f32[160,9,8,128]{3,2,1,0:T(8,128)} %pack.1), calls=%async_computation.2 | async-start | bytes 11796480 | tf_op jit(solution)/shard_map/all_to_all | solution.py:675
  44.8 2.2 velocity_edges.1
  47.0 3.4 %collective-permute-start.2 = (f32[48,128]{1,0:T(8,128)}, f32[48,128]{1,0:T(8,128)S(1)}, u32[]{:S(2)}, u32[]{:S(2)}) collective-permute-start(f32[48,128]{1,0:T(8,128)} %get-tuple-element.64), channel_id=1, source_target_pairs={{0,1},{1,2},{2,3},{3,4},{4,5},{5,6},{6,7},{7,8},{8,9},{9,10},{10,1... | collective-permute-start | bytes 73736 | tf_op jit(solution)/shard_map/ppermute | solution.py:613
  50.4 4.6 %collective-permute-start.3 = (f32[48,128]{1,0:T(8,128)}, f32[48,128]{1,0:T(8,128)S(1)}, u32[]{:S(2)}, u32[]{:S(2)}) collective-permute-start(f32[48,128]{1,0:T(8,128)} %get-tuple-element.65), channel_id=1, source_target_pairs={{1,0},{2,1},{3,2},{4,3},{5,4},{6,5},{7,6},{8,7},{9,8},{10,9},{11,1... | collective-permute-start | bytes 73736 | tf_op jit(solution)/shard_map/ppermute | solution.py:613
  54.9 1.9 collective-permute-start
  56.9 3.6 %collective-permute-start.1 = (f32[192,128]{1,0:T(8,128)}, f32[192,128]{1,0:T(8,128)S(1)}, u32[]{:S(2)}, u32[]{:S(2)}) collective-permute-start(f32[192,128]{1,0:T(8,128)} %get-tuple-element.63.vylow_own_ref), channel_id=1, source_target_pairs={{32,0},{64,32},{96,64},{128,96},{160,128},{192,160},{224,192},{33,... | collective-permute-start | bytes 294920 | tf_op jit(solution)/shard_map/ppermute | solution.py:613
  60.5 0.8 convert_reduce_fusion.3
  61.4 0.7 select_reduce_fusion.1.coarse_at_ref
  62.1 0.9 convert_reduce_fusion.2
  63.3 1.3 select_reduce_fusion.fine_at_ref
  64.9 108.3 %collective-permute-done.2.vxlow_ref = f32[48,128]{1,0:T(8,128)S(1)} collective-permute-done((f32[48,128]{1,0:T(8,128)}, f32[48,128]{1,0:T(8,128)S(1)}, u32[]{:S(2)}, u32[]{:S(2)}) %collective-permute-start.2) | collective-permute-done | bytes 24608 | tf_op jit(solution)/shard_map/ppermute | solution.py:613
  173.3 1.1 all-to-all-done.2.in_ref.first_ref
  174.4 3.5 %forward.1 = f32[32,9,8,128]{3,2,1,0:T(8,128)} custom-call(s32[1]{0:T(128)} %bitcast.7.me_ref, s32[32,128]{1,0:T(8,128)} %get-tuple-element.57.column_ref, f32[160,9,8,128]{3,2,1,0:T(8,128)} %all-to-all-done.2.in_ref.first_ref), custom_call_target="tpu_custom_call" | custom-call | bytes 10800000 | tf_op jit(solution)/shard_map/forward/pallas_call | solution.py:716
  177.9 10.1 %all-to-all-start.3 = ((f32[32,9,8,128]{3,2,1,0:T(8,128)}), f32[32,9,8,128]{3,2,1,0:T(8,128)S(1)}, u32[]{:S(2)}, u32[]{:S(2)}) async-start(f32[32,9,8,128]{3,2,1,0:T(8,128)} %forward.1), calls=%async_computation.3 | async-start | bytes 2359296 | tf_op jit(solution)/shard_map/all_to_all | solution.py:675
  189.1 0.6 pad_add_fusion.1.late_ref
  189.8 9.1 %build.1 = (f32[9216,128]{1,0:T(8,128)}, f32[1152,128]{1,0:T(8,128)}, f32[1152,128]{1,0:T(8,128)}, f32[288,128]{1,0:T(8,128)}, f32[288,128]{1,0:T(8,128)}) custom-call(s32[64]{0:T(128)} %copy-done.11, s32[32]{0:T(128)} %copy-done.13, f32[160,9,8,128]{3,2,1,0:T(8,128)} %all-to-all-done.2.in_ref.first_ref), custom_call_target="tpu_custom_call" | custom-call | bytes 36000000 | tf_op jit(solution)/shard_map/build/pallas_call | solution.py:730
  198.9 9.4 %first_step.1._ = f32[9216,128]{1,0:T(8,128)} custom-call(f32[9]{0:T(128)} %diff_ref.5, f32[9216,128]{1,0:T(8,128)} %get-tuple-element.67.state_ref, f32[64,3,16,128]{3,2,1,0:T(8,128)} %vel_ref.5), custom_call_target="tpu_custom_call" | custom-call | bytes 36000000 | tf_op jit(solution)/shard_map/first_step/pallas_call | solution.py:778
  208.3 8.3 %all-to-all-done.3.second_ref = f32[32,9,8,128]{3,2,1,0:T(8,128)S(1)} async-done(((f32[32,9,8,128]{3,2,1,0:T(8,128)}), f32[32,9,8,128]{3,2,1,0:T(8,128)S(1)}, u32[]{:S(2)}, u32[]{:S(2)}) %all-to-all-start.3) | async-done | bytes 1179680 | tf_op jit(solution)/shard_map/all_to_all | solution.py:675
  216.6 1.1 copy-done
  217.7 5.3 %edges.1 = (f32[1152,128]{1,0:T(8,128)}, f32[1152,128]{1,0:T(8,128)}, f32[288,128]{1,0:T(8,128)}, f32[288,128]{1,0:T(8,128)}) custom-call(s32[96]{0:T(128)} %pad_add_fusion.1.late_ref, s32[1]{0:T(128)} %get-tuple-element.58.left_ref, s32[64]{0:T(128)} %copy-done.11, s32[32]{0:T(128)} %copy-done.13, f32[32,9,8,128]{3,2,1,0:T(8,128)} %copy-done, ...), custom_call_target="tpu_custom_call" | custom-call | bytes 14400000 | tf_op jit(solution)/shard_map/edges/pallas_call | solution.py:789
  222.9 1.9 collective-permute-start.4
  224.9 3.6 %collective-permute-start.5 = (f32[1152,128]{1,0:T(8,128)}, f32[1152,128]{1,0:T(8,128)S(1)}, u32[]{:S(2)}, u32[]{:S(2)}) collective-permute-start(f32[1152,128]{1,0:T(8,128)} %get-tuple-element.75.ylow_own_ref), channel_id=1, source_target_pairs={{32,0},{64,32},{96,64},{128,96},{160,128},{192,160},{224,192},{33,... | collective-permute-start | bytes 1769480 | tf_op jit(solution)/shard_map/ppermute | solution.py:613
  228.6 0.7 convert_reduce_fusion.11
  229.5 1.2 pad_add_fusion.2.again_ref
  230.8 9.1 %late_step.1.first_ref = f32[9216,128]{1,0:T(8,128)} custom-call(s32[96]{0:T(128)} %pad_add_fusion.1.late_ref, s32[1]{0:T(128)} %get-tuple-element.58.left_ref, s32[64]{0:T(128)} %copy-done.11, s32[32]{0:T(128)} %copy-done.13, s32[65]{0:T(128)} %pad_add_fusion.2.again_ref, f32[9]{0:T(128)} %diff_ref.5, ...), custom_call_target="tpu_custom_call", output_to_operand_aliasing={{}: (10, {})} | custom-call | bytes 25200000 | tf_op jit(solution)/shard_map/late_step/pallas_call | solution.py:800
  239.9 0.8 copy-done.2
  240.9 2.1 corners.1
  243.0 1.9 collective-permute-start.6
  244.9 6.0 %collective-permute-start.7 = (f32[320,128]{1,0:T(8,128)}, f32[320,128]{1,0:T(8,128)S(1)}, u32[]{:S(2)}, u32[]{:S(2)}) collective-permute-start(f32[320,128]{1,0:T(8,128)} %get-tuple-element.83), channel_id=1, source_target_pairs={{1,0},{2,1},{3,2},{4,3},{5,4},{6,5},{7,6},{8,7},{9,8},{10,9},{11,1... | collective-permute-start | bytes 491528 | tf_op jit(solution)/shard_map/ppermute | solution.py:613
  250.9 0.7 add_convert_fusion.inside_ref
  251.6 1.3 collective-permute-done.6.xlow_ref
  252.9 1.9 collective-permute-done.7.xhigh_ref
  254.8 0.7 copy-done.5
  255.4 11.2 %second_step.1 = f32[9216,128]{1,0:T(8,128)} custom-call(f32[4]{0:T(128)} %add_convert_fusion.inside_ref, f32[9]{0:T(128)} %diff_ref.5, f32[9216,128]{1,0:T(8,128)} %late_step.1.first_ref, f32[64,3,16,128]{3,2,1,0:T(8,128)} %vel_ref.5, f32[1152,128]{1,0:T(8,128)} %get-tuple-element.75.ylow_own_ref, f32[1152,128]{1,0:T(8,128)} %get-tuple-element.74.yhigh_own_ref, ...), custom_call_target="tpu_custom_call" | custom-call | bytes 36000000 | tf_op jit(solution)/shard_map/second_step/pallas_call | solution.py:828
  (83 shorter events, 4.4 us)
Async XLA Ops:
  1.4 19.4 %all-to-all-start.1 = ((s32[32,1,96]{2,1,0:T(1,128)}), s32[32,1,96]{2,1,0:T(1,128)S(1)}, u32[]{:S(2)}, u32[]{:S(2)}) async-start(s32[32,1,96]{2,1,0:T(1,128)} %broadcast_in_dim.83), calls=%async_computation.1 | async-start | bytes 32768 | tf_op jit(solution)/shard_map/all_to_all | solution.py:632
  23.1 15.1 %slice-start = ((s8[4718592]{0:T(1024)(128)(4,1)}), s8[524288]{0:T(1024)(128)(4,1)S(1)}, s32[]{:S(2)}) async-start(s8[4718592]{0:T(1024)(128)(4,1)} %bitcast.24), calls=%async_computation.4 | async-start | bytes 1048576
  29.4 8.8 %slice-start.1 = ((s8[4718592]{0:T(1024)(128)(4,1)}), s8[4194304]{0:T(1024)(128)(4,1)S(1)}, s32[]{:S(2)}) async-start(s8[4718592]{0:T(1024)(128)(4,1)} %bitcast.24), calls=%async_computation.5 | async-start | bytes 8388608
  29.4 8.8 %copy-start.1 = (f32[32,9,8,64]{3,2,1,0:T(8,128)S(1)}, f32[32,9,8,64]{3,2,1,0:T(8,128)}, u32[]{:S(2)}) copy-start(f32[32,9,8,64]{3,2,1,0:T(8,128)} %coarse_ref.1) | copy-start | bytes 1769476
  38.2 25.0 %copy-start.8 = (s32[32,128]{1,0:T(8,128)S(1)}, s32[32,128]{1,0:T(8,128)}, u32[]{:S(2)}) copy-start(s32[32,128]{1,0:T(8,128)} %get-tuple-element.57.column_ref) | copy-start | bytes 49156
  38.2 136.1 %all-to-all-start.2 = ((f32[160,9,8,128]{3,2,1,0:T(8,128)}), f32[160,9,8,128]{3,2,1,0:T(8,128)}, u32[]{:S(2)}, u32[]{:S(2)}) async-start(f32[160,9,8,128]{3,2,1,0:T(8,128)} %pack.1), calls=%async_computation.2 | async-start | bytes 11796480 | tf_op jit(solution)/shard_map/all_to_all | solution.py:675
  47.0 126.2 %collective-permute-start.2 = (f32[48,128]{1,0:T(8,128)}, f32[48,128]{1,0:T(8,128)S(1)}, u32[]{:S(2)}, u32[]{:S(2)}) collective-permute-start(f32[48,128]{1,0:T(8,128)} %get-tuple-element.64), channel_id=1, source_target_pairs={{0,1},{1,2},{2,3},{3,4},{4,5},{5,6},{6,7},{7,8},{8,9},{9,10},{10,1... | collective-permute-start | bytes 73736 | tf_op jit(solution)/shard_map/ppermute | solution.py:613
  50.4 122.9 %collective-permute-start.3 = (f32[48,128]{1,0:T(8,128)}, f32[48,128]{1,0:T(8,128)S(1)}, u32[]{:S(2)}, u32[]{:S(2)}) collective-permute-start(f32[48,128]{1,0:T(8,128)} %get-tuple-element.65), channel_id=1, source_target_pairs={{1,0},{2,1},{3,2},{4,3},{5,4},{6,5},{7,6},{8,7},{9,8},{10,9},{11,1... | collective-permute-start | bytes 73736 | tf_op jit(solution)/shard_map/ppermute | solution.py:613
  54.9 118.3 %collective-permute-start = (f32[192,128]{1,0:T(8,128)}, f32[192,128]{1,0:T(8,128)S(1)}, u32[]{:S(2)}, u32[]{:S(2)}) collective-permute-start(f32[192,128]{1,0:T(8,128)} %get-tuple-element.62.vyhigh_own_ref), channel_id=1, source_target_pairs={{0,32},{32,64},{64,96},{96,128},{128,160},{160,192},{192,224},{1,3... | collective-permute-start | bytes 294920 | tf_op jit(solution)/shard_map/ppermute | solution.py:613
  56.9 116.4 %collective-permute-start.1 = (f32[192,128]{1,0:T(8,128)}, f32[192,128]{1,0:T(8,128)S(1)}, u32[]{:S(2)}, u32[]{:S(2)}) collective-permute-start(f32[192,128]{1,0:T(8,128)} %get-tuple-element.63.vylow_own_ref), channel_id=1, source_target_pairs={{32,0},{64,32},{96,64},{128,96},{160,128},{192,160},{224,192},{33,... | collective-permute-start | bytes 294920 | tf_op jit(solution)/shard_map/ppermute | solution.py:613
  62.1 115.8 %copy-start.13 = (s32[32]{0:T(128)}, s32[32]{0:T(128)S(1)}, u32[]{:S(2)}) copy-start(s32[32]{0:T(128)S(1)} %select_reduce_fusion.1.coarse_at_ref) | copy-start | bytes 388
  64.6 123.9 %copy-start.11 = (s32[64]{0:T(128)}, s32[64]{0:T(128)S(1)}, u32[]{:S(2)}) copy-start(s32[64]{0:T(128)S(1)} %select_reduce_fusion.fine_at_ref) | copy-start | bytes 772
  173.2 4.7 %copy-start.9 = (f32[48,128]{1,0:T(8,128)}, f32[48,128]{1,0:T(8,128)S(1)}, u32[]{:S(2)}) copy-start(f32[48,128]{1,0:T(8,128)S(1)} %collective-permute-done.2.vxlow_ref) | copy-start | bytes 73732
  173.2 4.7 %copy-start.10 = (f32[48,128]{1,0:T(8,128)}, f32[48,128]{1,0:T(8,128)S(1)}, u32[]{:S(2)}) copy-start(f32[48,128]{1,0:T(8,128)S(1)} %collective-permute-done.3.vxhigh_ref) | copy-start | bytes 73732
  173.2 4.7 %copy-start.6 = (f32[192,128]{1,0:T(8,128)}, f32[192,128]{1,0:T(8,128)S(1)}, u32[]{:S(2)}) copy-start(f32[192,128]{1,0:T(8,128)S(1)} %collective-permute-done.vylow_ref) | copy-start | bytes 294916
  173.2 4.7 %copy-start.7 = (f32[192,128]{1,0:T(8,128)}, f32[192,128]{1,0:T(8,128)S(1)}, u32[]{:S(2)}) copy-start(f32[192,128]{1,0:T(8,128)S(1)} %collective-permute-done.1.vyhigh_ref) | copy-start | bytes 294916
  177.9 38.7 %all-to-all-start.3 = ((f32[32,9,8,128]{3,2,1,0:T(8,128)}), f32[32,9,8,128]{3,2,1,0:T(8,128)S(1)}, u32[]{:S(2)}, u32[]{:S(2)}) async-start(f32[32,9,8,128]{3,2,1,0:T(8,128)} %forward.1), calls=%async_computation.3 | async-start | bytes 2359296 | tf_op jit(solution)/shard_map/all_to_all | solution.py:675
  208.3 20.3 %copy-start.12 = (s32[64]{0:T(128)S(1)}, s32[64]{0:T(128)}, u32[]{:S(2)}) copy-start(s32[64]{0:T(128)} %copy-done.11) | copy-start | bytes 772
  216.6 1.1 copy-start
  222.9 16.9 %collective-permute-start.4 = (f32[1152,128]{1,0:T(8,128)}, f32[1152,128]{1,0:T(8,128)S(1)}, u32[]{:S(2)}, u32[]{:S(2)}) collective-permute-start(f32[1152,128]{1,0:T(8,128)} %get-tuple-element.74.yhigh_own_ref), channel_id=1, source_target_pairs={{0,32},{32,64},{64,96},{96,128},{128,160},{160,192},{192,224},{1,3... | collective-permute-start | bytes 1769480 | tf_op jit(solution)/shard_map/ppermute | solution.py:613
  224.9 15.0 %collective-permute-start.5 = (f32[1152,128]{1,0:T(8,128)}, f32[1152,128]{1,0:T(8,128)S(1)}, u32[]{:S(2)}, u32[]{:S(2)}) collective-permute-start(f32[1152,128]{1,0:T(8,128)} %get-tuple-element.75.ylow_own_ref), channel_id=1, source_target_pairs={{32,0},{64,32},{96,64},{128,96},{160,128},{192,160},{224,192},{33,... | collective-permute-start | bytes 1769480 | tf_op jit(solution)/shard_map/ppermute | solution.py:613
  239.9 0.8 copy-start.2
  239.9 1.0 copy-start.3
  243.0 9.9 %collective-permute-start.6 = (f32[320,128]{1,0:T(8,128)}, f32[320,128]{1,0:T(8,128)S(1)}, u32[]{:S(2)}, u32[]{:S(2)}) collective-permute-start(f32[320,128]{1,0:T(8,128)} %get-tuple-element.82), channel_id=1, source_target_pairs={{0,1},{1,2},{2,3},{3,4},{4,5},{5,6},{6,7},{7,8},{8,9},{9,10},{10,1... | collective-permute-start | bytes 491528 | tf_op jit(solution)/shard_map/ppermute | solution.py:613
  244.9 9.9 %collective-permute-start.7 = (f32[320,128]{1,0:T(8,128)}, f32[320,128]{1,0:T(8,128)S(1)}, u32[]{:S(2)}, u32[]{:S(2)}) collective-permute-start(f32[320,128]{1,0:T(8,128)} %get-tuple-element.83), channel_id=1, source_target_pairs={{1,0},{2,1},{3,2},{4,3},{5,4},{6,5},{7,6},{8,7},{9,8},{10,9},{11,1... | collective-permute-start | bytes 491528 | tf_op jit(solution)/shard_map/ppermute | solution.py:613
  252.9 1.9 copy-start.4
  254.8 0.7 copy-start.5

commit v10 on v9

--- a/solution.py
+++ b/solution.py
@@ -17,6 +17,10 @@
 ANY = pl.BlockSpec(memory_space=pl.ANY)
 PARAMS = pltpu.CompilerParams(vmem_limit_bytes=56 * 1024 * 1024)
 UNROLL = 4
+
+
+def room(mib):
+    return pltpu.CompilerParams(vmem_limit_bytes=mib * 1024 * 1024)
 
 
 def ranks(boxes):
@@ -303,18 +307,33 @@
         lax.fori_loop(0, planes // 2, direct, 0)
 
 
+def load_all(pairs, sem):
+    copies = [pltpu.make_async_copy(source, target, sem.at[i]) for i, (source, target) in enumerate(pairs)]
+    for copy in copies:
+        copy.start()
+    return copies
+
+
 def edges_kernel(
-    shape, late_ref, left_ref, fine_at_ref, coarse_at_ref, second_ref, rest_ref,
+    shape, late_ref, left_ref, fine_at_ref, coarse_at_ref, second_in_ref, rest_ref,
     ylow_in_ref, yhigh_in_ref, xlow_in_ref, xhigh_in_ref,
-    ylow_ref, yhigh_ref, xlow_ref, xhigh_ref, held_ref, plane_ref, sem,
+    ylow_ref, yhigh_ref, xlow_ref, xhigh_ref, held_ref, plane_ref, sem, second_ref, load_sem,
 ):
     planes, species, rows, _ = shape
     half = rows // 2
     size = species * rows
-    ylow_ref[...] = ylow_in_ref[...]
-    yhigh_ref[...] = yhigh_in_ref[...]
-    xlow_ref[...] = xlow_in_ref[...]
-    xhigh_ref[...] = xhigh_in_ref[...]
+    loads = load_all(
+        [
+            (second_in_ref, second_ref),
+            (ylow_in_ref, ylow_ref),
+            (yhigh_in_ref, yhigh_ref),
+            (xlow_in_ref, xlow_ref),
+            (xhigh_in_ref, xhigh_ref),
+        ],
+        load_sem,
+    )
+    for load in loads:
+        load.wait()
 
     def half_edges(x, h, value):
         edge_ref, first = ((ylow_ref, 0), (yhigh_ref, half - ITERS))[h]
@@ -461,17 +480,19 @@
 
 
 def late_step_kernel(
-    shape, late_ref, left_ref, fine_at_ref, coarse_at_ref, again_ref, diff_ref, second_ref, rest_ref, state_ref, vel_ref, _,
-    out_ref, u0_ref, u1_ref, held_ref, plane_ref, sem, out_sem,
+    shape, late_ref, left_ref, fine_at_ref, coarse_at_ref, again_ref, diff_ref, second_in_ref, rest_ref, state_ref,
+    vel_in_ref, _, out_ref, u0_ref, u1_ref, held_ref, plane_ref, sem, second_ref, vel_ref, load_sem, out_sem,
 ):
     planes, species, rows, lanes = shape
     half = rows // 2
     size = species * rows
-    copy = pltpu.make_async_copy(state_ref, u0_ref.at[size : size + planes * size], sem)
-    copy.start()
+    loads = load_all(
+        [(second_in_ref, second_ref), (state_ref, u0_ref.at[size : size + planes * size]), (vel_in_ref, vel_ref)], load_sem
+    )
     u0_ref[0:size] = jnp.zeros((size, lanes), jnp.float32)
     u0_ref[size + planes * size : 2 * size + planes * size] = jnp.zeros((size, lanes), jnp.float32)
-    copy.wait()
+    for load in loads[:2]:
+        load.wait()
 
     def half_plane(x, h, ref, slot):
         for s in range(species):
@@ -509,6 +530,7 @@
 
         lax.fori_loop(0, count, body, 0)
 
+    loads[2].wait()
     count = again_ref[planes]
     lax.fori_loop(0, (count + 1) // 2, take, 0)
     each(lambda copy: copy.start())
@@ -516,15 +538,14 @@
 
 
 def second_step_kernel(
-    shape, inside_ref, diff_ref, first_ref, vel_ref, ylow_own_ref, yhigh_own_ref, xlow_own_ref, xhigh_own_ref, ylow_ref,
+    shape, inside_ref, diff_ref, first_ref, vel_in_ref, ylow_own_ref, yhigh_own_ref, xlow_own_ref, xhigh_own_ref, ylow_ref,
     yhigh_ref, xlow_ref, xhigh_ref, vylow_own_ref, vyhigh_own_ref, vylow_ref, vyhigh_ref, vxlow_ref, vxhigh_ref,
-    out_ref, u1_ref, u2_ref, row_low_ref, row_high_ref, plane_low_ref, plane_high_ref, sem, out_sem,
+    out_ref, u1_ref, u2_ref, row_low_ref, row_high_ref, plane_low_ref, plane_high_ref, vel_ref, load_sem, out_sem,
 ):
     planes, species, rows, lanes = shape
     size = species * rows
     deep = ITERS * size
-    copy = pltpu.make_async_copy(first_ref, u1_ref, sem)
-    copy.start()
+    loads = load_all([(first_ref, u1_ref), (vel_in_ref, vel_ref)], load_sem)
 
     for (near_ref, near, far, own_ref, own, v_ref, corner, target_ref, inside) in (
         (ylow_ref, 1, 0, ylow_own_ref, 0, vylow_ref, deep, row_low_ref, 0),
@@ -570,7 +591,8 @@
         velocity = [v_ref[k * rows : (k + 1) * rows] for k in range(3)]
         advance_plane(diff_ref, velocity, at(halo_ref, near), below, above, corner(0), corner(16), store)
 
-    copy.wait()
+    for load in loads:
+        load.wait()
     for x in range(0, planes, 8):
         up = jnp.maximum(vylow_own_ref[planes + x : planes + x + 8], 0.0)
         down = jnp.minimum(vyhigh_own_ref[planes + x : planes + x + 8], 0.0)
@@ -789,10 +811,10 @@
     ylow_own, yhigh_own, xlow_own, xhigh_own = pl.pallas_call(
         functools.partial(edges_kernel, old_fine.shape),
         out_shape=edge_shapes(ITERS, species),
-        in_specs=[SMEM] * 4 + [VMEM, ANY] + [VMEM] * 4,
+        in_specs=[SMEM] * 4 + [ANY] * 6,
         out_specs=[VMEM] * 4,
-        scratch_shapes=late_scratch,
-        compiler_params=PARAMS,
+        scratch_shapes=late_scratch + [pltpu.VMEM(second.shape, f32), pltpu.SemaphoreType.DMA((5,))],
+        compiler_params=room(12),
         cost_estimate=cost(4),
         name="edges",
     )(late, left, fine_at, coarse_at, second, rest, *edges)
@@ -800,13 +822,14 @@
     stepped = pl.pallas_call(
         functools.partial(late_step_kernel, old_fine.shape),
         out_shape=state_shape,
-        in_specs=[SMEM] * 6 + [VMEM, ANY, ANY, VMEM, ANY],
+        in_specs=[SMEM] * 6 + [ANY] * 5,
         out_specs=ANY,
         scratch_shapes=[pltpu.VMEM(((planes + 2) * size, lanes), f32), pltpu.VMEM(((planes + 1) * size, lanes), f32)]
         + late_scratch
+        + [pltpu.VMEM(second.shape, f32), pltpu.VMEM(velocity.shape, f32), pltpu.SemaphoreType.DMA((3,))]
         + [pltpu.SemaphoreType.DMA((planes,))],
         input_output_aliases={10: 0},
-        compiler_params=PARAMS,
+        compiler_params=room(24),
         cost_estimate=cost(7),
         name="late_step",
     )(late, left, fine_at, coarse_at, again, diffusion, second, rest, state, velocity, stepped)
@@ -817,7 +840,7 @@
         out_shape=[message] * 2,
         in_specs=[VMEM] * 4,
         out_specs=[VMEM] * 2,
-        compiler_params=PARAMS,
+        compiler_params=room(8),
         name="corners",
     )(ylow, yhigh, xlow_own, xhigh_own)
     xlow, xhigh = neighbours("dev", down, up)
@@ -828,13 +851,13 @@
     done = pl.pallas_call(
         functools.partial(second_step_kernel, old_fine.shape),
         out_shape=state_shape,
-        in_specs=[SMEM] * 2 + [ANY] + [VMEM] * 15,
+        in_specs=[SMEM] * 2 + [ANY] * 2 + [VMEM] * 14,
         out_specs=ANY,
         scratch_shapes=[state_scratch] * 2
         + [row_edge] * 2
         + [plane_edge] * 2
-        + [pltpu.SemaphoreType.DMA, group_sems],
-        compiler_params=PARAMS,
+        + [pltpu.VMEM(velocity.shape, f32), pltpu.SemaphoreType.DMA((2,)), group_sems],
+        compiler_params=room(28),
         cost_estimate=cost(10),
         name="second_step",
     )(

time: 271 us -> 278 us (1.026)
  local copies, waits for them, and re-layouts: 4.07 us -> 20.5 us
  Pallas kernels: 64.3 us -> 57.8 us
    unnamed x32 -> x64, local copies, waits for them, and re-layouts: 2.81 us -> 18.7 us
    pallas_call x1, Pallas kernels: 11.2 us -> 7.68 us  [on_device(): pl.pallas_call(functools.partial(second_step_kernel, old_fine.shape), out...]
  transfers between devices with their start and end apart: 11 -> 11, of which waited for: 6 -> 5; matrix products, arithmetic and copies ran while one was open for 5% -> 4% of each run, Pallas kernels for 11% -> 11%
where the time goes in v10:
time: 278 us; the launch traced here: 275 us
  waiting for transfers between devices  124 us (45%)
  Pallas kernels  57.8 us (21%)
  starting transfers between devices  54.9 us (20%)
  local copies, waits for them, and re-layouts  20.5 us (7%)
  other arithmetic  15.9 us (6%)
    ppermute x4, waiting for transfers between devices, neighbours(): lax.ppermute(high, axis, up)  111 us
    unnamed x64, local copies, waits for them, and re-layouts  18.7 us
    all_to_all x2, starting transfers between devices, exchange(): return lax.all_to_all(value, 'dev', split_axis=0, concat_axis=0, tiled=True)  16.3 us
    ppermute x4, starting transfers between devices, neighbours(): lax.ppermute(low, axis, [(b, a) for a, b in up])  15.7 us
    all_to_all x1, starting transfers between devices, on_device(): lax.all_to_all(labels, 'dev', split_axis=0, concat_axis=0, tiled=True)  11.6 us
    ppermute x4, starting transfers between devices, neighbours(): lax.ppermute(high, axis, up)  11.3 us
    pallas_call x1, Pallas kernels, on_device(): pl.pallas_call(functools.partial(build_kernel, old_fine.shape), out_shape...  10.6 us
    pallas_call x1, Pallas kernels, on_device(): pl.pallas_call(functools.partial(first_step_kernel, old_fine.shape), out_...  9.43 us
  transfers between devices with their start and end apart: 11, of which 5 were waited for; matrix products, arithmetic and copies ran while one was open for 4% of the time, Pallas kernels for 11%

profile of v10, /device:TPU:22, one launch (start us, length us, event | category | flops | bytes accessed | tf_op | source)
XLA Modules:
  0.0 274.7 jit_solution(6857435075949126127)
XLA Ops:
  0.0 0.7 pad_add_fusion
  1.4 11.6 %all-to-all-start.1 = ((s32[32,1,96]{2,1,0:T(1,128)}), s32[32,1,96]{2,1,0:T(1,128)S(1)}, u32[]{:S(2)}, u32[]{:S(2)}) async-start(s32[32,1,96]{2,1,0:T(1,128)} %broadcast_in_dim.83), calls=%async_computation.1 | async-start | bytes 32768 | tf_op jit(solution)/shard_map/all_to_all | solution.py:654
  16.9 3.9 %all-to-all-done.1 = s32[32,1,96]{2,1,0:T(1,128)S(1)} async-done(((s32[32,1,96]{2,1,0:T(1,128)}), s32[32,1,96]{2,1,0:T(1,128)S(1)}, u32[]{:S(2)}, u32[]{:S(2)}) %all-to-all-start.1) | async-done | bytes 12320 | tf_op jit(solution)/shard_map/all_to_all | solution.py:654
  21.1 0.9 convert_reduce_fusion.5
  22.0 1.1 convert_reduce_fusion
  24.4 4.3 %plan.1 = (s32[4,128]{1,0:T(4,128)S(1)}, s32[32,128]{1,0:T(8,128)}, s32[1]{0:T(128)}) custom-call(s32[1]{0:T(128)} %bitcast.7.me_ref, s32[32,128]{1,0:T(8,128)} %multiply_add_fusion.units_ref), custom_call_target="tpu_custom_call" | custom-call | tf_op jit(solution)/shard_map/plan/pallas_call | solution.py:668
  29.4 8.0 %pack.1 = f32[160,9,8,128]{3,2,1,0:T(8,128)} custom-call(s32[1]{0:T(128)} %bitcast.7.me_ref, s32[64]{0:T(128)S(1)} %compare_select_fusion.22.fine_at_ref, s32[32]{0:T(128)S(1)} %compare_select_fusion.coarse_at_ref, s32[4,128]{1,0:T(4,128)S(1)} %get-tuple-element.59.row_ref, f32[64,9,16,128]{3,2,1,0:T(8,128)} %fine_in_ref.1, f32[32,9,8,64]{3,2,1,0:T(8,128)} %coarse_ref.1), custom_call_target="tpu_custom_call" | custom-call | tf_op jit(solution)/shard_map/pack/pallas_call | solution.py:700
  38.1 6.9 %all-to-all-start.2 = ((f32[160,9,8,128]{3,2,1,0:T(8,128)}), f32[160,9,8,128]{3,2,1,0:T(8,128)}, u32[]{:S(2)}, u32[]{:S(2)}) async-start(f32[160,9,8,128]{3,2,1,0:T(8,128)} %pack.1), calls=%async_computation.2 | async-start | bytes 11796480 | tf_op jit(solution)/shard_map/all_to_all | solution.py:697
  45.1 2.1 velocity_edges.1
  47.3 3.4 %collective-permute-start.2 = (f32[48,128]{1,0:T(8,128)}, f32[48,128]{1,0:T(8,128)S(1)}, u32[]{:S(2)}, u32[]{:S(2)}) collective-permute-start(f32[48,128]{1,0:T(8,128)} %get-tuple-element.64), channel_id=1, source_target_pairs={{0,1},{1,2},{2,3},{3,4},{4,5},{5,6},{6,7},{7,8},{8,9},{9,10},{10,1... | collective-permute-start | bytes 73736 | tf_op jit(solution)/shard_map/ppermute | solution.py:635
  50.6 4.6 %collective-permute-start.3 = (f32[48,128]{1,0:T(8,128)}, f32[48,128]{1,0:T(8,128)S(1)}, u32[]{:S(2)}, u32[]{:S(2)}) collective-permute-start(f32[48,128]{1,0:T(8,128)} %get-tuple-element.65), channel_id=1, source_target_pairs={{1,0},{2,1},{3,2},{4,3},{5,4},{6,5},{7,6},{8,7},{9,8},{10,9},{11,1... | collective-permute-start | bytes 73736 | tf_op jit(solution)/shard_map/ppermute | solution.py:635
  55.2 1.9 collective-permute-start
  57.2 3.6 %collective-permute-start.1 = (f32[192,128]{1,0:T(8,128)}, f32[192,128]{1,0:T(8,128)S(1)}, u32[]{:S(2)}, u32[]{:S(2)}) collective-permute-start(f32[192,128]{1,0:T(8,128)} %get-tuple-element.63.vylow_own_ref), channel_id=1, source_target_pairs={{32,0},{64,32},{96,64},{128,96},{160,128},{192,160},{224,192},{33,... | collective-permute-start | bytes 294920 | tf_op jit(solution)/shard_map/ppermute | solution.py:635
  60.8 0.8 convert_reduce_fusion.3
  61.7 0.7 select_reduce_fusion.1.coarse_at_ref
  62.4 0.9 convert_reduce_fusion.2
  63.6 1.3 select_reduce_fusion.fine_at_ref
  65.2 108.6 %collective-permute-done.2.vxlow_ref = f32[48,128]{1,0:T(8,128)S(1)} collective-permute-done((f32[48,128]{1,0:T(8,128)}, f32[48,128]{1,0:T(8,128)S(1)}, u32[]{:S(2)}, u32[]{:S(2)}) %collective-permute-start.2) | collective-permute-done | bytes 24608 | tf_op jit(solution)/shard_map/ppermute | solution.py:635
  173.9 3.6 %forward.1 = f32[32,9,8,128]{3,2,1,0:T(8,128)} custom-call(s32[1]{0:T(128)} %bitcast.7.me_ref, s32[32,128]{1,0:T(8,128)} %get-tuple-element.57.column_ref, f32[160,9,8,128]{3,2,1,0:T(8,128)} %all-to-all-done.2.in_ref.first_ref), custom_call_target="tpu_custom_call" | custom-call | bytes 10800000 | tf_op jit(solution)/shard_map/forward/pallas_call | solution.py:738
  177.5 9.4 %all-to-all-start.3 = ((f32[32,9,8,128]{3,2,1,0:T(8,128)}), f32[32,9,8,128]{3,2,1,0:T(8,128)S(1)}, u32[]{:S(2)}, u32[]{:S(2)}) async-start(f32[32,9,8,128]{3,2,1,0:T(8,128)} %forward.1), calls=%async_computation.3 | async-start | bytes 2359296 | tf_op jit(solution)/shard_map/all_to_all | solution.py:697
  188.6 10.6 %build.1 = (f32[9216,128]{1,0:T(8,128)}, f32[1152,128]{1,0:T(8,128)}, f32[1152,128]{1,0:T(8,128)}, f32[288,128]{1,0:T(8,128)}, f32[288,128]{1,0:T(8,128)}) custom-call(s32[64]{0:T(128)} %copy-done.23, s32[32]{0:T(128)} %copy-done.25, f32[160,9,8,128]{3,2,1,0:T(8,128)} %all-to-all-done.2.in_ref.first_ref), custom_call_target="tpu_custom_call" | custom-call | bytes 36000000 | tf_op jit(solution)/shard_map/build/pallas_call | solution.py:752
  199.3 9.4 %first_step.1._ = f32[9216,128]{1,0:T(8,128)} custom-call(f32[9]{0:T(128)} %diff_ref.5, f32[9216,128]{1,0:T(8,128)} %get-tuple-element.67.state_ref, f32[64,3,16,128]{3,2,1,0:T(8,128)} %vel_in_ref.3), custom_call_target="tpu_custom_call" | custom-call | bytes 36000000 | tf_op jit(solution)/shard_map/first_step/pallas_call | solution.py:800
  208.8 7.2 %all-to-all-done.3.second_in_ref = f32[32,9,8,128]{3,2,1,0:T(8,128)S(1)} async-done(((f32[32,9,8,128]{3,2,1,0:T(8,128)}), f32[32,9,8,128]{3,2,1,0:T(8,128)S(1)}, u32[]{:S(2)}, u32[]{:S(2)}) %all-to-all-start.3) | async-done | bytes 1179680 | tf_op jit(solution)/shard_map/all_to_all | solution.py:697
  216.0 1.2 copy-done.12
  217.2 1.2 copy-done.15
  218.4 0.9 copy-done.16
  219.3 3.8 %edges.1 = (f32[1152,128]{1,0:T(8,128)S(1)}, f32[1152,128]{1,0:T(8,128)S(1)}, f32[288,128]{1,0:T(8,128)S(1)}, f32[288,128]{1,0:T(8,128)S(1)}) custom-call(s32[96]{0:T(128)S(1)} %pad_add_fusion.1.late_ref, s32[1]{0:T(128)} %get-tuple-element.58.left_ref, s32[64]{0:T(128)S(1)} %copy-done.24, s32[32]{0:T(128)S(1)} %copy-done.26, ...), custom_call_target="tpu_custom_call" | custom-call | bytes 14400000 | tf_op jit(solution)/shard_map/edges/pallas_call | solution.py:811
  223.2 1.9 collective-permute-start.4
  225.1 3.6 %collective-permute-start.5 = (f32[1152,128]{1,0:T(8,128)S(1)}, f32[1152,128]{1,0:T(8,128)S(1)}, u32[]{:S(2)}, u32[]{:S(2)}) collective-permute-start(f32[1152,128]{1,0:T(8,128)S(1)} %get-tuple-element.75.ylow_own_ref), channel_id=1, source_target_pairs={{32,0},{64,32},{96,64},{128,96},{160,128},{192,160},{224,192},{33,... | collective-permute-start | bytes 1769480 | tf_op jit(solution)/shard_map/ppermute | solution.py:635
  229.4 0.7 convert_reduce_fusion.11
  230.9 2.3 copy-done.4
  233.2 8.1 %late_step.1.first_ref = f32[9216,128]{1,0:T(8,128)S(1)} custom-call(s32[96]{0:T(128)S(1)} %pad_add_fusion.1.late_ref, s32[1]{0:T(128)} %get-tuple-element.58.left_ref, s32[64]{0:T(128)S(1)} %copy-done.24, s32[32]{0:T(128)S(1)} %copy-done.26, s32[65]{0:T(128)S(1)} %pad_add_fusion.2.again_ref, f32[9]{0:T(128)S(1)} %copy-done.27, ...), custom_call_target="tpu_custom_call", output_to_operand_aliasing={{}: (10, {})} | custom-call | bytes 25200000 | tf_op jit(solution)/shard_map/late_step/pallas_call | solution.py:822
  241.3 2.2 copy-done.1
  243.6 0.8 copy-done.5
  244.4 4.1 %collective-permute-start.6 = (f32[320,128]{1,0:T(8,128)S(1)}, f32[320,128]{1,0:T(8,128)S(1)}, u32[]{:S(2)}, u32[]{:S(2)}) collective-permute-start(f32[320,128]{1,0:T(8,128)S(1)} %get-tuple-element.82), channel_id=1, source_target_pairs={{0,1},{1,2},{2,3},{3,4},{4,5},{5,6},{6,7},{7,8},{8,9},{9,10},{10,1... | collective-permute-start | bytes 491528 | tf_op jit(solution)/shard_map/ppermute | solution.py:635
  248.5 3.9 %collective-permute-start.7 = (f32[320,128]{1,0:T(8,128)S(1)}, f32[320,128]{1,0:T(8,128)S(1)}, u32[]{:S(2)}, u32[]{:S(2)}) collective-permute-start(f32[320,128]{1,0:T(8,128)S(1)} %get-tuple-element.83), channel_id=1, source_target_pairs={{1,0},{2,1},{3,2},{4,3},{5,4},{6,5},{7,6},{8,7},{9,8},{10,9},{11,1... | collective-permute-start | bytes 491528 | tf_op jit(solution)/shard_map/ppermute | solution.py:635
  252.4 2.7 collective-permute-done.6.xlow_ref
  255.1 1.8 collective-permute-done.7.xhigh_ref
  256.9 2.3 copy-done.2
  259.2 1.1 copy-done.6
  260.3 1.1 copy-done.8
  261.3 1.1 copy-done.10
  262.4 0.9 copy-done.14
  263.3 0.9 copy-done.17
  264.2 0.9 copy-done.18
  265.1 0.9 copy-done.20
  266.0 0.9 copy-done.22
  266.9 7.7 %second_step.1 = f32[9216,128]{1,0:T(8,128)} custom-call(f32[4]{0:T(128)S(1)} %add_convert_fusion.inside_ref, f32[9]{0:T(128)S(1)} %copy-done.27, f32[9216,128]{1,0:T(8,128)S(1)} %copy-done.2, f32[64,3,16,128]{3,2,1,0:T(8,128)S(1)} %copy-done.3, f32[1152,128]{1,0:T(8,128)S(1)} %copy-done.8, f32[1152,128]{1,0:T(8,128)S(1)} %copy-done.10, ...), custom_call_target="tpu_custom_call" | custom-call | bytes 36000000 | tf_op jit(solution)/shard_map/second_step/pallas_call | solution.py:851
  (115 shorter events, 10.7 us)
Async XLA Ops:
  1.4 19.4 %all-to-all-start.1 = ((s32[32,1,96]{2,1,0:T(1,128)}), s32[32,1,96]{2,1,0:T(1,128)S(1)}, u32[]{:S(2)}, u32[]{:S(2)}) async-start(s32[32,1,96]{2,1,0:T(1,128)} %broadcast_in_dim.83), calls=%async_computation.1 | async-start | bytes 32768 | tf_op jit(solution)/shard_map/all_to_all | solution.py:654
  23.1 15.0 %slice-start = ((s8[4718592]{0:T(1024)(128)(4,1)}), s8[524288]{0:T(1024)(128)(4,1)S(1)}, s32[]{:S(2)}) async-start(s8[4718592]{0:T(1024)(128)(4,1)} %bitcast.24), calls=%async_computation.4 | async-start | bytes 1048576
  29.4 8.7 %slice-start.1 = ((s8[4718592]{0:T(1024)(128)(4,1)}), s8[4194304]{0:T(1024)(128)(4,1)S(1)}, s32[]{:S(2)}) async-start(s8[4718592]{0:T(1024)(128)(4,1)} %bitcast.24), calls=%async_computation.5 | async-start | bytes 8388608
  29.4 8.7 %copy-start.28 = (f32[32,9,8,64]{3,2,1,0:T(8,128)S(1)}, f32[32,9,8,64]{3,2,1,0:T(8,128)}, u32[]{:S(2)}) copy-start(f32[32,9,8,64]{3,2,1,0:T(8,128)} %coarse_ref.1) | copy-start | bytes 1769476
  38.1 25.4 %copy-start.29 = (s32[32,128]{1,0:T(8,128)S(1)}, s32[32,128]{1,0:T(8,128)}, u32[]{:S(2)}) copy-start(s32[32,128]{1,0:T(8,128)} %get-tuple-element.57.column_ref) | copy-start | bytes 49156
  38.1 135.7 %all-to-all-start.2 = ((f32[160,9,8,128]{3,2,1,0:T(8,128)}), f32[160,9,8,128]{3,2,1,0:T(8,128)}, u32[]{:S(2)}, u32[]{:S(2)}) async-start(f32[160,9,8,128]{3,2,1,0:T(8,128)} %pack.1), calls=%async_computation.2 | async-start | bytes 11796480 | tf_op jit(solution)/shard_map/all_to_all | solution.py:697
  47.3 126.6 %collective-permute-start.2 = (f32[48,128]{1,0:T(8,128)}, f32[48,128]{1,0:T(8,128)S(1)}, u32[]{:S(2)}, u32[]{:S(2)}) collective-permute-start(f32[48,128]{1,0:T(8,128)} %get-tuple-element.64), channel_id=1, source_target_pairs={{0,1},{1,2},{2,3},{3,4},{4,5},{5,6},{6,7},{7,8},{8,9},{9,10},{10,1... | collective-permute-start | bytes 73736 | tf_op jit(solution)/shard_map/ppermute | solution.py:635
  50.6 123.2 %collective-permute-start.3 = (f32[48,128]{1,0:T(8,128)}, f32[48,128]{1,0:T(8,128)S(1)}, u32[]{:S(2)}, u32[]{:S(2)}) collective-permute-start(f32[48,128]{1,0:T(8,128)} %get-tuple-element.65), channel_id=1, source_target_pairs={{1,0},{2,1},{3,2},{4,3},{5,4},{6,5},{7,6},{8,7},{9,8},{10,9},{11,1... | collective-permute-start | bytes 73736 | tf_op jit(solution)/shard_map/ppermute | solution.py:635
  55.2 118.6 %collective-permute-start = (f32[192,128]{1,0:T(8,128)}, f32[192,128]{1,0:T(8,128)S(1)}, u32[]{:S(2)}, u32[]{:S(2)}) collective-permute-start(f32[192,128]{1,0:T(8,128)} %get-tuple-element.62.vyhigh_own_ref), channel_id=1, source_target_pairs={{0,32},{32,64},{64,96},{96,128},{128,160},{160,192},{192,224},{1,3... | collective-permute-start | bytes 294920 | tf_op jit(solution)/shard_map/ppermute | solution.py:635
  57.2 116.7 %collective-permute-start.1 = (f32[192,128]{1,0:T(8,128)}, f32[192,128]{1,0:T(8,128)S(1)}, u32[]{:S(2)}, u32[]{:S(2)}) collective-permute-start(f32[192,128]{1,0:T(8,128)} %get-tuple-element.63.vylow_own_ref), channel_id=1, source_target_pairs={{32,0},{64,32},{96,64},{128,96},{160,128},{192,160},{224,192},{33,... | collective-permute-start | bytes 294920 | tf_op jit(solution)/shard_map/ppermute | solution.py:635
  62.4 115.1 %copy-start.25 = (s32[32]{0:T(128)}, s32[32]{0:T(128)S(1)}, u32[]{:S(2)}) copy-start(s32[32]{0:T(128)S(1)} %select_reduce_fusion.1.coarse_at_ref) | copy-start | bytes 388
  64.9 123.0 %copy-start.23 = (s32[64]{0:T(128)}, s32[64]{0:T(128)S(1)}, u32[]{:S(2)}) copy-start(s32[64]{0:T(128)S(1)} %select_reduce_fusion.fine_at_ref) | copy-start | bytes 772
  173.8 3.7 %copy-start.19 = (f32[192,128]{1,0:T(8,128)}, f32[192,128]{1,0:T(8,128)S(1)}, u32[]{:S(2)}) copy-start(f32[192,128]{1,0:T(8,128)S(1)} %collective-permute-done.vylow_ref) | copy-start | bytes 294916
  173.9 3.7 %copy-start.21 = (f32[192,128]{1,0:T(8,128)}, f32[192,128]{1,0:T(8,128)S(1)}, u32[]{:S(2)}) copy-start(f32[192,128]{1,0:T(8,128)S(1)} %collective-permute-done.1.vyhigh_ref) | copy-start | bytes 294916
  177.5 38.5 %all-to-all-start.3 = ((f32[32,9,8,128]{3,2,1,0:T(8,128)}), f32[32,9,8,128]{3,2,1,0:T(8,128)S(1)}, u32[]{:S(2)}, u32[]{:S(2)}) async-start(f32[32,9,8,128]{3,2,1,0:T(8,128)} %forward.1), calls=%async_computation.3 | async-start | bytes 2359296 | tf_op jit(solution)/shard_map/all_to_all | solution.py:697
  199.3 16.7 %copy-start.11 = (f32[1152,128]{1,0:T(8,128)S(1)}, f32[1152,128]{1,0:T(8,128)}, u32[]{:S(2)}) copy-start(f32[1152,128]{1,0:T(8,128)} %get-tuple-element.70.ylow_in_ref) | copy-start | bytes 1769476
  199.3 16.7 %copy-start.24 = (s32[64]{0:T(128)S(1)}, s32[64]{0:T(128)}, u32[]{:S(2)}) copy-start(s32[64]{0:T(128)} %copy-done.23) | copy-start | bytes 772
  199.3 16.7 %copy-start.26 = (s32[32]{0:T(128)S(1)}, s32[32]{0:T(128)}, u32[]{:S(2)}) copy-start(s32[32]{0:T(128)} %copy-done.25) | copy-start | bytes 388
  199.3 31.6 %copy-start.27 = (f32[9]{0:T(128)S(1)}, f32[9]{0:T(128)}, u32[]{:S(2)}) copy-start(f32[9]{0:T(128)} %diff_ref.5) | copy-start | bytes 112
  208.7 22.2 %copy-start.3 = (f32[64,3,16,128]{3,2,1,0:T(8,128)S(1)}, f32[64,3,16,128]{3,2,1,0:T(8,128)}, u32[]{:S(2)}) copy-start(f32[64,3,16,128]{3,2,1,0:T(8,128)} %vel_in_ref.3) | copy-start | bytes 4718596
  216.0 14.9 %copy-start = (f32[9216,128]{1,0:T(8,128)S(1)}, f32[9216,128]{1,0:T(8,128)}, u32[]{:S(2)}) copy-start(f32[9216,128]{1,0:T(8,128)} %first_step.1._) | copy-start | bytes 14155780
  216.0 1.2 copy-start.12
  217.2 1.2 copy-start.15
  218.4 0.9 copy-start.16
  223.2 18.2 %copy-start.7 = (f32[1152,128]{1,0:T(8,128)}, f32[1152,128]{1,0:T(8,128)S(1)}, u32[]{:S(2)}) copy-start(f32[1152,128]{1,0:T(8,128)S(1)} %get-tuple-element.75.ylow_own_ref) | copy-start | bytes 1769476
  223.2 18.2 %copy-start.9 = (f32[1152,128]{1,0:T(8,128)}, f32[1152,128]{1,0:T(8,128)S(1)}, u32[]{:S(2)}) copy-start(f32[1152,128]{1,0:T(8,128)S(1)} %get-tuple-element.74.yhigh_own_ref) | copy-start | bytes 1769476
  223.2 20.3 %copy-start.13 = (f32[288,128]{1,0:T(8,128)}, f32[288,128]{1,0:T(8,128)S(1)}, u32[]{:S(2)}) copy-start(f32[288,128]{1,0:T(8,128)S(1)} %get-tuple-element.79.xhigh_ref.xhigh_own_ref) | copy-start | bytes 442372
  223.2 20.3 %collective-permute-start.4 = (f32[1152,128]{1,0:T(8,128)S(1)}, f32[1152,128]{1,0:T(8,128)S(1)}, u32[]{:S(2)}, u32[]{:S(2)}) collective-permute-start(f32[1152,128]{1,0:T(8,128)S(1)} %get-tuple-element.74.yhigh_own_ref), channel_id=1, source_target_pairs={{0,32},{32,64},{64,96},{96,128},{128,160},{160,192},{192,224},{1,3... | collective-permute-start | bytes 1769480 | tf_op jit(solution)/shard_map/ppermute | solution.py:635
  225.1 18.4 %collective-permute-start.5 = (f32[1152,128]{1,0:T(8,128)S(1)}, f32[1152,128]{1,0:T(8,128)S(1)}, u32[]{:S(2)}, u32[]{:S(2)}) collective-permute-start(f32[1152,128]{1,0:T(8,128)S(1)} %get-tuple-element.75.ylow_own_ref), channel_id=1, source_target_pairs={{32,0},{64,32},{96,64},{128,96},{160,128},{192,160},{224,192},{33,... | collective-permute-start | bytes 1769480 | tf_op jit(solution)/shard_map/ppermute | solution.py:635
  230.9 2.3 copy-start.4
  241.3 2.2 copy-start.1
  243.6 0.8 copy-start.5
  244.4 10.7 %collective-permute-start.6 = (f32[320,128]{1,0:T(8,128)S(1)}, f32[320,128]{1,0:T(8,128)S(1)}, u32[]{:S(2)}, u32[]{:S(2)}) collective-permute-start(f32[320,128]{1,0:T(8,128)S(1)} %get-tuple-element.82), channel_id=1, source_target_pairs={{0,1},{1,2},{2,3},{3,4},{4,5},{5,6},{6,7},{7,8},{8,9},{9,10},{10,1... | collective-permute-start | bytes 491528 | tf_op jit(solution)/shard_map/ppermute | solution.py:635
  248.5 8.4 %collective-permute-start.7 = (f32[320,128]{1,0:T(8,128)S(1)}, f32[320,128]{1,0:T(8,128)S(1)}, u32[]{:S(2)}, u32[]{:S(2)}) collective-permute-start(f32[320,128]{1,0:T(8,128)S(1)} %get-tuple-element.83), channel_id=1, source_target_pairs={{1,0},{2,1},{3,2},{4,3},{5,4},{6,5},{7,6},{8,7},{9,8},{10,9},{11,1... | collective-permute-start | bytes 491528 | tf_op jit(solution)/shard_map/ppermute | solution.py:635
  256.9 2.3 copy-start.2
  259.2 1.1 copy-start.6
  260.3 1.1 copy-start.8
  261.3 1.1 copy-start.10
  262.4 0.9 copy-start.14
  263.3 0.9 copy-start.17
  264.2 0.9 copy-start.18
  265.1 0.9 copy-start.20
  266.0 0.9 copy-start.22

commit v11 on v10

--- a/solution.py
+++ b/solution.py
@@ -15,12 +15,8 @@
 VMEM = pl.BlockSpec(memory_space=pltpu.VMEM)
 SMEM = pl.BlockSpec(memory_space=pltpu.SMEM)
 ANY = pl.BlockSpec(memory_space=pl.ANY)
-PARAMS = pltpu.CompilerParams(vmem_limit_bytes=56 * 1024 * 1024)
+PARAMS = pltpu.CompilerParams(vmem_limit_bytes=58 * 1024 * 1024)
 UNROLL = 4
-
-
-def room(mib):
-    return pltpu.CompilerParams(vmem_limit_bytes=mib * 1024 * 1024)
 
 
 def ranks(boxes):
@@ -814,7 +810,7 @@
         in_specs=[SMEM] * 4 + [ANY] * 6,
         out_specs=[VMEM] * 4,
         scratch_shapes=late_scratch + [pltpu.VMEM(second.shape, f32), pltpu.SemaphoreType.DMA((5,))],
-        compiler_params=room(12),
+        compiler_params=PARAMS,
         cost_estimate=cost(4),
         name="edges",
     )(late, left, fine_at, coarse_at, second, rest, *edges)
@@ -829,7 +825,7 @@
         + [pltpu.VMEM(second.shape, f32), pltpu.VMEM(velocity.shape, f32), pltpu.SemaphoreType.DMA((3,))]
         + [pltpu.SemaphoreType.DMA((planes,))],
         input_output_aliases={10: 0},
-        compiler_params=room(24),
+        compiler_params=PARAMS,
         cost_estimate=cost(7),
         name="late_step",
     )(late, left, fine_at, coarse_at, again, diffusion, second, rest, state, velocity, stepped)
@@ -840,7 +836,7 @@
         out_shape=[message] * 2,
         in_specs=[VMEM] * 4,
         out_specs=[VMEM] * 2,
-        compiler_params=room(8),
+        compiler_params=PARAMS,
         name="corners",
     )(ylow, yhigh, xlow_own, xhigh_own)
     xlow, xhigh = neighbours("dev", down, up)
@@ -857,7 +853,7 @@
         + [row_edge] * 2
         + [plane_edge] * 2
         + [pltpu.VMEM(velocity.shape, f32), pltpu.SemaphoreType.DMA((2,)), group_sems],
-        compiler_params=room(28),
+        compiler_params=PARAMS,
         cost_estimate=cost(10),
         name="second_step",
     )(

time: 278 us -> 271 us (0.975)
  local copies, waits for them, and re-layouts: 20.5 us -> 4.07 us
  Pallas kernels: 57.8 us -> 66 us
    unnamed x64 -> x32, local copies, waits for them, and re-layouts: 18.7 us -> 2.81 us
    pallas_call x1, Pallas kernels: 7.68 us -> 11.3 us  [on_device(): pl.pallas_call(functools.partial(second_step_kernel, old_fine.shape), out...]
  transfers between devices with their start and end apart: 11 -> 11, of which waited for: 5 -> 5; matrix products, arithmetic and copies ran while one was open for 4% -> 5% of each run, Pallas kernels for 11% -> 11%
where the time goes in v11:
time: 271 us; the launch traced here: 270 us
  waiting for transfers between devices  126 us (46%)
  Pallas kernels  66 us (24%)
  starting transfers between devices  54.8 us (20%)
  other arithmetic  17.1 us (6%)
  local copies, waits for them, and re-layouts  4.07 us (2%)
    ppermute x4, waiting for transfers between devices, neighbours(): lax.ppermute(high, axis, up)  109 us
    all_to_all x2, starting transfers between devices, exchange(): return lax.all_to_all(value, 'dev', split_axis=0, concat_axis=0, tiled=True)  16 us
    ppermute x4, starting transfers between devices, neighbours(): lax.ppermute(low, axis, [(b, a) for a, b in up])  13.8 us
    ppermute x4, starting transfers between devices, neighbours(): lax.ppermute(high, axis, up)  13.5 us
    all_to_all x1, starting transfers between devices, on_device(): lax.all_to_all(labels, 'dev', split_axis=0, concat_axis=0, tiled=True)  11.6 us
    pallas_call x1, Pallas kernels, on_device(): pl.pallas_call(functools.partial(second_step_kernel, old_fine.shape), out...  11.3 us
    pallas_call x1, Pallas kernels, on_device(): pl.pallas_call(functools.partial(late_step_kernel, old_fine.shape), out_s...  9.59 us
    pallas_call x1, Pallas kernels, on_device(): pl.pallas_call(functools.partial(first_step_kernel, old_fine.shape), out_...  9.37 us
  transfers between devices with their start and end apart: 11, of which 5 were waited for; matrix products, arithmetic and copies ran while one was open for 5% of the time, Pallas kernels for 11%

profile of v11, /device:TPU:22, one launch (start us, length us, event | category | flops | bytes accessed | tf_op | source)
XLA Modules:
  0.0 269.6 jit_solution(18230982255187520499)
XLA Ops:
  0.0 0.7 pad_add_fusion
  0.7 0.6 broadcast_in_dim.83
  1.4 11.6 %all-to-all-start.1 = ((s32[32,1,96]{2,1,0:T(1,128)}), s32[32,1,96]{2,1,0:T(1,128)S(1)}, u32[]{:S(2)}, u32[]{:S(2)}) async-start(s32[32,1,96]{2,1,0:T(1,128)} %broadcast_in_dim.83), calls=%async_computation.1 | async-start | bytes 32768 | tf_op jit(solution)/shard_map/all_to_all | solution.py:650
  13.0 0.7 fusion.21
  13.6 0.7 and_select_fusion.2
  14.3 0.7 compare_select_fusion.23
  15.0 0.7 fusion.20
  16.0 0.7 compare_select_fusion.22.fine_at_ref
  16.9 3.9 %all-to-all-done.1 = s32[32,1,96]{2,1,0:T(1,128)S(1)} async-done(((s32[32,1,96]{2,1,0:T(1,128)}), s32[32,1,96]{2,1,0:T(1,128)S(1)}, u32[]{:S(2)}, u32[]{:S(2)}) %all-to-all-start.1) | async-done | bytes 12320 | tf_op jit(solution)/shard_map/all_to_all | solution.py:650
  21.1 0.9 convert_reduce_fusion.5
  22.0 1.1 convert_reduce_fusion
  23.8 0.6 multiply_add_fusion.units_ref
  24.4 4.3 %plan.1 = (s32[4,128]{1,0:T(4,128)S(1)}, s32[32,128]{1,0:T(8,128)}, s32[1]{0:T(128)}) custom-call(s32[1]{0:T(128)} %bitcast.7.me_ref, s32[32,128]{1,0:T(8,128)} %multiply_add_fusion.units_ref), custom_call_target="tpu_custom_call" | custom-call | tf_op jit(solution)/shard_map/plan/pallas_call | solution.py:664
  28.7 0.7 compare_select_fusion.coarse_at_ref
  29.4 8.1 %pack.1 = f32[160,9,8,128]{3,2,1,0:T(8,128)} custom-call(s32[1]{0:T(128)} %bitcast.7.me_ref, s32[64]{0:T(128)S(1)} %compare_select_fusion.22.fine_at_ref, s32[32]{0:T(128)S(1)} %compare_select_fusion.coarse_at_ref, s32[4,128]{1,0:T(4,128)S(1)} %get-tuple-element.59.row_ref, f32[64,9,16,128]{3,2,1,0:T(8,128)} %fine_in_ref.1, f32[32,9,8,64]{3,2,1,0:T(8,128)} %coarse_ref.1), custom_call_target="tpu_custom_call" | custom-call | tf_op jit(solution)/shard_map/pack/pallas_call | solution.py:696
  38.3 6.7 %all-to-all-start.2 = ((f32[160,9,8,128]{3,2,1,0:T(8,128)}), f32[160,9,8,128]{3,2,1,0:T(8,128)}, u32[]{:S(2)}, u32[]{:S(2)}) async-start(f32[160,9,8,128]{3,2,1,0:T(8,128)} %pack.1), calls=%async_computation.2 | async-start | bytes 11796480 | tf_op jit(solution)/shard_map/all_to_all | solution.py:693
  45.0 2.2 velocity_edges.1
  47.2 3.4 %collective-permute-start.2 = (f32[48,128]{1,0:T(8,128)}, f32[48,128]{1,0:T(8,128)S(1)}, u32[]{:S(2)}, u32[]{:S(2)}) collective-permute-start(f32[48,128]{1,0:T(8,128)} %get-tuple-element.64), channel_id=1, source_target_pairs={{0,1},{1,2},{2,3},{3,4},{4,5},{5,6},{6,7},{7,8},{8,9},{9,10},{10,1... | collective-permute-start | bytes 73736 | tf_op jit(solution)/shard_map/ppermute | solution.py:631
  50.6 4.6 %collective-permute-start.3 = (f32[48,128]{1,0:T(8,128)}, f32[48,128]{1,0:T(8,128)S(1)}, u32[]{:S(2)}, u32[]{:S(2)}) collective-permute-start(f32[48,128]{1,0:T(8,128)} %get-tuple-element.65), channel_id=1, source_target_pairs={{1,0},{2,1},{3,2},{4,3},{5,4},{6,5},{7,6},{8,7},{9,8},{10,9},{11,1... | collective-permute-start | bytes 73736 | tf_op jit(solution)/shard_map/ppermute | solution.py:631
  55.1 1.9 collective-permute-start
  57.1 3.6 %collective-permute-start.1 = (f32[192,128]{1,0:T(8,128)}, f32[192,128]{1,0:T(8,128)S(1)}, u32[]{:S(2)}, u32[]{:S(2)}) collective-permute-start(f32[192,128]{1,0:T(8,128)} %get-tuple-element.63.vylow_own_ref), channel_id=1, source_target_pairs={{32,0},{64,32},{96,64},{128,96},{160,128},{192,160},{224,192},{33,... | collective-permute-start | bytes 294920 | tf_op jit(solution)/shard_map/ppermute | solution.py:631
  60.7 0.8 convert_reduce_fusion.3
  61.6 0.7 select_reduce_fusion.1.coarse_at_ref
  62.3 0.9 convert_reduce_fusion.2
  63.5 1.3 select_reduce_fusion.fine_at_ref
  65.1 108.5 %collective-permute-done.2.vxlow_ref = f32[48,128]{1,0:T(8,128)S(1)} collective-permute-done((f32[48,128]{1,0:T(8,128)}, f32[48,128]{1,0:T(8,128)S(1)}, u32[]{:S(2)}, u32[]{:S(2)}) %collective-permute-start.2) | collective-permute-done | bytes 24608 | tf_op jit(solution)/shard_map/ppermute | solution.py:631
  173.7 3.6 %forward.1 = f32[32,9,8,128]{3,2,1,0:T(8,128)} custom-call(s32[1]{0:T(128)} %bitcast.7.me_ref, s32[32,128]{1,0:T(8,128)} %get-tuple-element.57.column_ref, f32[160,9,8,128]{3,2,1,0:T(8,128)} %all-to-all-done.2.in_ref.first_ref), custom_call_target="tpu_custom_call" | custom-call | bytes 10800000 | tf_op jit(solution)/shard_map/forward/pallas_call | solution.py:734
  177.3 9.3 %all-to-all-start.3 = ((f32[32,9,8,128]{3,2,1,0:T(8,128)}), f32[32,9,8,128]{3,2,1,0:T(8,128)S(1)}, u32[]{:S(2)}, u32[]{:S(2)}) async-start(f32[32,9,8,128]{3,2,1,0:T(8,128)} %forward.1), calls=%async_computation.3 | async-start | bytes 2359296 | tf_op jit(solution)/shard_map/all_to_all | solution.py:693
  187.8 0.6 pad_add_fusion.1.late_ref
  188.4 9.3 %build.1 = (f32[9216,128]{1,0:T(8,128)}, f32[1152,128]{1,0:T(8,128)}, f32[1152,128]{1,0:T(8,128)}, f32[288,128]{1,0:T(8,128)}, f32[288,128]{1,0:T(8,128)}) custom-call(s32[64]{0:T(128)} %copy-done.11, s32[32]{0:T(128)} %copy-done.13, f32[160,9,8,128]{3,2,1,0:T(8,128)} %all-to-all-done.2.in_ref.first_ref), custom_call_target="tpu_custom_call" | custom-call | bytes 36000000 | tf_op jit(solution)/shard_map/build/pallas_call | solution.py:748
  197.6 9.4 %first_step.1._ = f32[9216,128]{1,0:T(8,128)} custom-call(f32[9]{0:T(128)} %diff_ref.5, f32[9216,128]{1,0:T(8,128)} %get-tuple-element.67.state_ref, f32[64,3,16,128]{3,2,1,0:T(8,128)} %vel_in_ref.3), custom_call_target="tpu_custom_call" | custom-call | bytes 36000000 | tf_op jit(solution)/shard_map/first_step/pallas_call | solution.py:796
  207.0 8.9 %all-to-all-done.3.second_in_ref = f32[32,9,8,128]{3,2,1,0:T(8,128)S(1)} async-done(((f32[32,9,8,128]{3,2,1,0:T(8,128)}), f32[32,9,8,128]{3,2,1,0:T(8,128)S(1)}, u32[]{:S(2)}, u32[]{:S(2)}) %all-to-all-start.3) | async-done | bytes 1179680 | tf_op jit(solution)/shard_map/all_to_all | solution.py:693
  216.0 1.1 copy-done
  217.0 6.3 %edges.1 = (f32[1152,128]{1,0:T(8,128)}, f32[1152,128]{1,0:T(8,128)}, f32[288,128]{1,0:T(8,128)}, f32[288,128]{1,0:T(8,128)}) custom-call(s32[96]{0:T(128)} %pad_add_fusion.1.late_ref, s32[1]{0:T(128)} %get-tuple-element.58.left_ref, s32[64]{0:T(128)} %copy-done.11, s32[32]{0:T(128)} %copy-done.13, f32[32,9,8,128]{3,2,1,0:T(8,128)} %copy-done, ...), custom_call_target="tpu_custom_call" | custom-call | bytes 14400000 | tf_op jit(solution)/shard_map/edges/pallas_call | solution.py:807
  223.3 1.9 collective-permute-start.4
  225.2 3.6 %collective-permute-start.5 = (f32[1152,128]{1,0:T(8,128)}, f32[1152,128]{1,0:T(8,128)S(1)}, u32[]{:S(2)}, u32[]{:S(2)}) collective-permute-start(f32[1152,128]{1,0:T(8,128)} %get-tuple-element.75.ylow_own_ref), channel_id=1, source_target_pairs={{32,0},{64,32},{96,64},{128,96},{160,128},{192,160},{224,192},{33,... | collective-permute-start | bytes 1769480 | tf_op jit(solution)/shard_map/ppermute | solution.py:631
  228.9 0.7 convert_reduce_fusion.11
  229.9 1.2 pad_add_fusion.2.again_ref
  231.1 9.6 %late_step.1.first_ref = f32[9216,128]{1,0:T(8,128)} custom-call(s32[96]{0:T(128)} %pad_add_fusion.1.late_ref, s32[1]{0:T(128)} %get-tuple-element.58.left_ref, s32[64]{0:T(128)} %copy-done.11, s32[32]{0:T(128)} %copy-done.13, s32[65]{0:T(128)} %pad_add_fusion.2.again_ref, f32[9]{0:T(128)} %diff_ref.5, ...), custom_call_target="tpu_custom_call", output_to_operand_aliasing={{}: (10, {})} | custom-call | bytes 25200000 | tf_op jit(solution)/shard_map/late_step/pallas_call | solution.py:818
  240.8 0.8 copy-done.2
  241.8 2.1 corners.1
  243.8 6.3 %collective-permute-start.6 = (f32[320,128]{1,0:T(8,128)}, f32[320,128]{1,0:T(8,128)S(1)}, u32[]{:S(2)}, u32[]{:S(2)}) collective-permute-start(f32[320,128]{1,0:T(8,128)} %get-tuple-element.82), channel_id=1, source_target_pairs={{0,1},{1,2},{2,3},{3,4},{4,5},{5,6},{6,7},{7,8},{8,9},{9,10},{10,1... | collective-permute-start | bytes 491528 | tf_op jit(solution)/shard_map/ppermute | solution.py:631
  250.1 1.9 collective-permute-start.7
  252.1 0.7 add_convert_fusion.inside_ref
  252.7 0.6 collective-permute-done.6.xlow_ref
  253.4 4.2 %collective-permute-done.7.xhigh_ref = f32[320,128]{1,0:T(8,128)S(1)} collective-permute-done((f32[320,128]{1,0:T(8,128)}, f32[320,128]{1,0:T(8,128)S(1)}, u32[]{:S(2)}, u32[]{:S(2)}) %collective-permute-start.7) | collective-permute-done | bytes 163872 | tf_op jit(solution)/shard_map/ppermute | solution.py:631
  257.5 0.7 copy-done.5
  258.2 11.3 %second_step.1 = f32[9216,128]{1,0:T(8,128)} custom-call(f32[4]{0:T(128)} %add_convert_fusion.inside_ref, f32[9]{0:T(128)} %diff_ref.5, f32[9216,128]{1,0:T(8,128)} %late_step.1.first_ref, f32[64,3,16,128]{3,2,1,0:T(8,128)} %vel_in_ref.3, f32[1152,128]{1,0:T(8,128)} %get-tuple-element.75.ylow_own_ref, f32[1152,128]{1,0:T(8,128)} %get-tuple-element.74.yhigh_own_ref, ...), custom_call_target="tpu_custom_call" | custom-call | bytes 36000000 | tf_op jit(solution)/shard_map/second_step/pallas_call | solution.py:847
  (83 shorter events, 3.8 us)
Async XLA Ops:
  1.4 19.4 %all-to-all-start.1 = ((s32[32,1,96]{2,1,0:T(1,128)}), s32[32,1,96]{2,1,0:T(1,128)S(1)}, u32[]{:S(2)}, u32[]{:S(2)}) async-start(s32[32,1,96]{2,1,0:T(1,128)} %broadcast_in_dim.83), calls=%async_computation.1 | async-start | bytes 32768 | tf_op jit(solution)/shard_map/all_to_all | solution.py:650
  23.1 15.1 %slice-start = ((s8[4718592]{0:T(1024)(128)(4,1)}), s8[524288]{0:T(1024)(128)(4,1)S(1)}, s32[]{:S(2)}) async-start(s8[4718592]{0:T(1024)(128)(4,1)} %bitcast.24), calls=%async_computation.4 | async-start | bytes 1048576
  29.4 8.8 %slice-start.1 = ((s8[4718592]{0:T(1024)(128)(4,1)}), s8[4194304]{0:T(1024)(128)(4,1)S(1)}, s32[]{:S(2)}) async-start(s8[4718592]{0:T(1024)(128)(4,1)} %bitcast.24), calls=%async_computation.5 | async-start | bytes 8388608
  29.4 8.8 %copy-start.1 = (f32[32,9,8,64]{3,2,1,0:T(8,128)S(1)}, f32[32,9,8,64]{3,2,1,0:T(8,128)}, u32[]{:S(2)}) copy-start(f32[32,9,8,64]{3,2,1,0:T(8,128)} %coarse_ref.1) | copy-start | bytes 1769476
  38.3 25.2 %copy-start.8 = (s32[32,128]{1,0:T(8,128)S(1)}, s32[32,128]{1,0:T(8,128)}, u32[]{:S(2)}) copy-start(s32[32,128]{1,0:T(8,128)} %get-tuple-element.57.column_ref) | copy-start | bytes 49156
  38.3 135.4 %all-to-all-start.2 = ((f32[160,9,8,128]{3,2,1,0:T(8,128)}), f32[160,9,8,128]{3,2,1,0:T(8,128)}, u32[]{:S(2)}, u32[]{:S(2)}) async-start(f32[160,9,8,128]{3,2,1,0:T(8,128)} %pack.1), calls=%async_computation.2 | async-start | bytes 11796480 | tf_op jit(solution)/shard_map/all_to_all | solution.py:693
  47.2 126.5 %collective-permute-start.2 = (f32[48,128]{1,0:T(8,128)}, f32[48,128]{1,0:T(8,128)S(1)}, u32[]{:S(2)}, u32[]{:S(2)}) collective-permute-start(f32[48,128]{1,0:T(8,128)} %get-tuple-element.64), channel_id=1, source_target_pairs={{0,1},{1,2},{2,3},{3,4},{4,5},{5,6},{6,7},{7,8},{8,9},{9,10},{10,1... | collective-permute-start | bytes 73736 | tf_op jit(solution)/shard_map/ppermute | solution.py:631
  50.6 123.1 %collective-permute-start.3 = (f32[48,128]{1,0:T(8,128)}, f32[48,128]{1,0:T(8,128)S(1)}, u32[]{:S(2)}, u32[]{:S(2)}) collective-permute-start(f32[48,128]{1,0:T(8,128)} %get-tuple-element.65), channel_id=1, source_target_pairs={{1,0},{2,1},{3,2},{4,3},{5,4},{6,5},{7,6},{8,7},{9,8},{10,9},{11,1... | collective-permute-start | bytes 73736 | tf_op jit(solution)/shard_map/ppermute | solution.py:631
  55.1 118.5 %collective-permute-start = (f32[192,128]{1,0:T(8,128)}, f32[192,128]{1,0:T(8,128)S(1)}, u32[]{:S(2)}, u32[]{:S(2)}) collective-permute-start(f32[192,128]{1,0:T(8,128)} %get-tuple-element.62.vyhigh_own_ref), channel_id=1, source_target_pairs={{0,32},{32,64},{64,96},{96,128},{128,160},{160,192},{192,224},{1,3... | collective-permute-start | bytes 294920 | tf_op jit(solution)/shard_map/ppermute | solution.py:631
  57.1 116.6 %collective-permute-start.1 = (f32[192,128]{1,0:T(8,128)}, f32[192,128]{1,0:T(8,128)S(1)}, u32[]{:S(2)}, u32[]{:S(2)}) collective-permute-start(f32[192,128]{1,0:T(8,128)} %get-tuple-element.63.vylow_own_ref), channel_id=1, source_target_pairs={{32,0},{64,32},{96,64},{128,96},{160,128},{192,160},{224,192},{33,... | collective-permute-start | bytes 294920 | tf_op jit(solution)/shard_map/ppermute | solution.py:631
  62.3 115.0 %copy-start.13 = (s32[32]{0:T(128)}, s32[32]{0:T(128)S(1)}, u32[]{:S(2)}) copy-start(s32[32]{0:T(128)S(1)} %select_reduce_fusion.1.coarse_at_ref) | copy-start | bytes 388
  64.8 122.3 %copy-start.11 = (s32[64]{0:T(128)}, s32[64]{0:T(128)S(1)}, u32[]{:S(2)}) copy-start(s32[64]{0:T(128)S(1)} %select_reduce_fusion.fine_at_ref) | copy-start | bytes 772
  173.6 3.7 %copy-start.9 = (f32[48,128]{1,0:T(8,128)}, f32[48,128]{1,0:T(8,128)S(1)}, u32[]{:S(2)}) copy-start(f32[48,128]{1,0:T(8,128)S(1)} %collective-permute-done.2.vxlow_ref) | copy-start | bytes 73732
  173.6 3.7 %copy-start.10 = (f32[48,128]{1,0:T(8,128)}, f32[48,128]{1,0:T(8,128)S(1)}, u32[]{:S(2)}) copy-start(f32[48,128]{1,0:T(8,128)S(1)} %collective-permute-done.3.vxhigh_ref) | copy-start | bytes 73732
  173.7 3.7 %copy-start.6 = (f32[192,128]{1,0:T(8,128)}, f32[192,128]{1,0:T(8,128)S(1)}, u32[]{:S(2)}) copy-start(f32[192,128]{1,0:T(8,128)S(1)} %collective-permute-done.vylow_ref) | copy-start | bytes 294916
  173.7 3.6 %copy-start.7 = (f32[192,128]{1,0:T(8,128)}, f32[192,128]{1,0:T(8,128)S(1)}, u32[]{:S(2)}) copy-start(f32[192,128]{1,0:T(8,128)S(1)} %collective-permute-done.1.vyhigh_ref) | copy-start | bytes 294916
  177.3 38.6 %all-to-all-start.3 = ((f32[32,9,8,128]{3,2,1,0:T(8,128)}), f32[32,9,8,128]{3,2,1,0:T(8,128)S(1)}, u32[]{:S(2)}, u32[]{:S(2)}) async-start(f32[32,9,8,128]{3,2,1,0:T(8,128)} %forward.1), calls=%async_computation.3 | async-start | bytes 2359296 | tf_op jit(solution)/shard_map/all_to_all | solution.py:693
  207.0 21.9 %copy-start.12 = (s32[64]{0:T(128)S(1)}, s32[64]{0:T(128)}, u32[]{:S(2)}) copy-start(s32[64]{0:T(128)} %copy-done.11) | copy-start | bytes 772
  216.0 1.1 copy-start
  223.3 17.4 %collective-permute-start.4 = (f32[1152,128]{1,0:T(8,128)}, f32[1152,128]{1,0:T(8,128)S(1)}, u32[]{:S(2)}, u32[]{:S(2)}) collective-permute-start(f32[1152,128]{1,0:T(8,128)} %get-tuple-element.74.yhigh_own_ref), channel_id=1, source_target_pairs={{0,32},{32,64},{64,96},{96,128},{128,160},{160,192},{192,224},{1,3... | collective-permute-start | bytes 1769480 | tf_op jit(solution)/shard_map/ppermute | solution.py:631
  225.2 15.5 %collective-permute-start.5 = (f32[1152,128]{1,0:T(8,128)}, f32[1152,128]{1,0:T(8,128)S(1)}, u32[]{:S(2)}, u32[]{:S(2)}) collective-permute-start(f32[1152,128]{1,0:T(8,128)} %get-tuple-element.75.ylow_own_ref), channel_id=1, source_target_pairs={{32,0},{64,32},{96,64},{128,96},{160,128},{192,160},{224,192},{33,... | collective-permute-start | bytes 1769480 | tf_op jit(solution)/shard_map/ppermute | solution.py:631
  240.7 0.8 copy-start.2
  240.7 1.0 copy-start.3
  243.8 9.5 %collective-permute-start.6 = (f32[320,128]{1,0:T(8,128)}, f32[320,128]{1,0:T(8,128)S(1)}, u32[]{:S(2)}, u32[]{:S(2)}) collective-permute-start(f32[320,128]{1,0:T(8,128)} %get-tuple-element.82), channel_id=1, source_target_pairs={{0,1},{1,2},{2,3},{3,4},{4,5},{5,6},{6,7},{7,8},{8,9},{9,10},{10,1... | collective-permute-start | bytes 491528 | tf_op jit(solution)/shard_map/ppermute | solution.py:631
  250.1 7.4 %collective-permute-start.7 = (f32[320,128]{1,0:T(8,128)}, f32[320,128]{1,0:T(8,128)S(1)}, u32[]{:S(2)}, u32[]{:S(2)}) collective-permute-start(f32[320,128]{1,0:T(8,128)} %get-tuple-element.83), channel_id=1, source_target_pairs={{1,0},{2,1},{3,2},{4,3},{5,4},{6,5},{7,6},{8,7},{9,8},{10,9},{11,1... | collective-permute-start | bytes 491528 | tf_op jit(solution)/shard_map/ppermute | solution.py:631
  253.4 4.2 %copy-start.4 = (f32[320,128]{1,0:T(8,128)}, f32[320,128]{1,0:T(8,128)S(1)}, u32[]{:S(2)}) copy-start(f32[320,128]{1,0:T(8,128)S(1)} %collective-permute-done.6.xlow_ref) | copy-start | bytes 491524
  257.5 0.7 copy-start.5
